TPU v7x, 128 devices: a whole 4x4x4 slice. The times are simulated.
128 devices in a mesh: seq: 16 (over z, y), head: 8 (over x, core).
Axes of the slice: x: 4, y: 4, z: 4, core: 2. Of those that a mesh axis runs over, the one named last changes fastest.
Arguments:
- video_query: bfloat16 [4096, 3072], P(('seq', 'head')), may hold values from -5 to 5
- video_key: bfloat16 [4096, 3072], P(('seq', 'head')), may hold values from -5 to 5
- video_value: bfloat16 [4096, 3072], P(('seq', 'head')), may hold values from -6 to 6
- video_grad: bfloat16 [4096, 3072], P(('seq', 'head')), may hold values from -6 to 6
- text_query: bfloat16 [2048, 3072], P('seq', 'head'), may hold values from -5 to 5
- text_key: bfloat16 [2048, 3072], P('seq', 'head'), may hold values from -5 to 5
- text_value: bfloat16 [2048, 3072], P('seq', 'head'), may hold values from -6 to 6
- text_grad: bfloat16 [2048, 3072], P('seq', 'head'), may hold values from -6 to 6
- shot_length: int32 [8], replicated, may hold values from 1 to 2048, 4096 in all
- caption_length: int32 [8], replicated, may hold values from 64 to 256, as said below
Outputs:
- video_query_grad: bfloat16 [4096, 3072], P(('seq', 'head'))
- video_key_grad: bfloat16 [4096, 3072], P(('seq', 'head'))
- video_value_grad: bfloat16 [4096, 3072], P(('seq', 'head'))
- text_query_grad: bfloat16 [2048, 3072], P('seq', 'head')
- text_key_grad: bfloat16 [2048, 3072], P('seq', 'head')
- text_value_grad: bfloat16 [2048, 3072], P('seq', 'head')
Inputs may be any that keep to these rules, and one draw needn't show every extreme that they name: `shot_length`: the shots cover the video in order; exactly one length equals 2048. `caption_length`: some shot has all 256 caption tokens live.
All inputs are finite; a program needn't handle non-finite values.
Results may differ from a plain program's by a relative error of at most 0.012.
The roundings to bfloat16 on the way count: a program that leaves them out, or rounds other values in their place, can miss the bound.
Values may be sent and summed in bfloat16 or wider, within the bound.
No kernel may reach another device: no remote copies, remote signals or barrier semaphores. Data moves between devices by JAX's collectives and lax.ppermute only.
A program may use at most 128 MiB of HBM per device.

v0:
```python
import jax
import jax.numpy as jnp
from jax import lax
from jax.sharding import PartitionSpec as P

HDIM = 128
CAP = 256


def row_labels(rows_index, shard, text_rows, ends, caption_length):
    block_rows = shard + text_rows
    device = rows_index // block_rows
    local_row = rows_index % block_rows
    is_text = local_row >= shard
    video_index = device * shard + local_row
    text_index = device * text_rows + local_row - shard
    video_shot = jnp.sum((video_index[:, None] >= ends[None, :]).astype(jnp.int32), axis=1)
    text_shot = text_index // CAP
    shot_id = jnp.where(is_text, text_shot, video_shot)
    shot_table = jnp.arange(ends.shape[0], dtype=jnp.int32)
    limits = jnp.sum(
        jnp.where(shot_id[:, None] == shot_table[None, :], caption_length[None, :], 0), axis=1
    )
    is_live = jnp.logical_or(jnp.logical_not(is_text), text_index % CAP < limits)
    return (shot_id, is_text, is_live)


def allowed_pairs(query_labels, key_labels):
    both_video = jnp.logical_and(
        jnp.logical_not(query_labels[1])[:, None], jnp.logical_not(key_labels[1])[None, :]
    )
    same_shot = query_labels[0][:, None] == key_labels[0][None, :]
    return jnp.logical_and(key_labels[2][None, :], jnp.logical_or(both_video, same_shot))


def masked_scores(queries, keys, allowed, scale):
    raw = jnp.einsum("qhd,khd->hqk", queries, keys, preferred_element_type=jnp.float32) * scale
    return jnp.where(allowed[None, :, :], raw, -jnp.inf)


def score_grads(probs, grads, values, delta):
    dprob = jnp.einsum("qhd,khd->hqk", grads, values, preferred_element_type=jnp.float32)
    return (probs * (dprob - delta[:, :, None])).astype(jnp.bfloat16)


def on_device(
    video_query,
    video_key,
    video_value,
    video_grad,
    text_query,
    text_key,
    text_value,
    text_grad,
    shot_length,
    caption_length,
):
    scale = HDIM ** (-0.5)
    seq_count = lax.axis_size("seq")
    seq_index = lax.axis_index("seq")
    queries_video, keys_video, values_video, grads_video = (
        lax.all_to_all(video_query, "head", split_axis=1, concat_axis=0, tiled=True),
        lax.all_to_all(video_key, "head", split_axis=1, concat_axis=0, tiled=True),
        lax.all_to_all(video_value, "head", split_axis=1, concat_axis=0, tiled=True),
        lax.all_to_all(video_grad, "head", split_axis=1, concat_axis=0, tiled=True),
    )
    shard = queries_video.shape[0]
    text_rows = text_query.shape[0]
    width = text_query.shape[1]
    heads_local = width // HDIM
    block_rows = shard + text_rows
    ends = jnp.cumsum(shot_length)

    def labels_of(rows_index):
        return row_labels(rows_index, shard, text_rows, ends, caption_length)

    def heads_view(array):
        return array.reshape(array.shape[0], heads_local, HDIM)

    own_index = seq_index * block_rows + jnp.arange(block_rows, dtype=jnp.int32)
    own_labels = labels_of(own_index)
    text_live = own_labels[2][shard:]
    grads_text = jnp.where(text_live[:, None], text_grad, jnp.zeros_like(text_grad))
    queries = jnp.concatenate([queries_video, text_query], 0)
    keys_own = jnp.concatenate([keys_video, text_key], 0)
    values_own = jnp.concatenate([values_video, text_value], 0)
    grads_own = jnp.concatenate([grads_video, grads_text], 0)
    keys_all, values_all = (
        lax.all_gather(keys_own, "seq", axis=0, tiled=True),
        lax.all_gather(values_own, "seq", axis=0, tiled=True),
    )
    total_rows = keys_all.shape[0]
    group = 1
    while group * 2 * block_rows <= 1024 and seq_count % (group * 2) == 0:
        group = group * 2
    span_rows = group * block_rows
    block_count = total_rows // span_rows
    queries_heads = heads_view(queries)
    grads_heads = heads_view(grads_own)
    keys_blocks = keys_all.reshape(block_count, span_rows, heads_local, HDIM)
    values_blocks = values_all.reshape(block_count, span_rows, heads_local, HDIM)
    block_ids = jnp.arange(block_count, dtype=jnp.int32)

    def block_allowed(index):
        key_index = index * span_rows + jnp.arange(span_rows, dtype=jnp.int32)
        return allowed_pairs(own_labels, labels_of(key_index))

    def stats_step(carry, inputs):
        running_max, running_sum = carry
        index, keys_block = inputs
        scores = masked_scores(queries_heads, keys_block, block_allowed(index), scale)
        new_max = jnp.maximum(running_max, jnp.max(scores, axis=2))
        safe_max = jnp.where(new_max == -jnp.inf, 0.0, new_max)
        running_sum = running_sum * jnp.exp(running_max - safe_max) + jnp.sum(
            jnp.exp(scores - safe_max[:, :, None]), axis=2
        )
        return ((new_max, running_sum), None)

    start_max = jnp.full((heads_local, block_rows), -jnp.inf, jnp.float32)
    start_sum = jnp.zeros((heads_local, block_rows), jnp.float32)
    (row_max, row_sum), _ = lax.scan(stats_step, (start_max, start_sum), (block_ids, keys_blocks))
    log_total = row_max + jnp.log(row_sum)

    def output_step(output, inputs):
        index, keys_block, values_block = inputs
        scores = masked_scores(queries_heads, keys_block, block_allowed(index), scale)
        probs_low = jnp.exp(scores - log_total[:, :, None]).astype(jnp.bfloat16)
        output = output + jnp.einsum(
            "hqk,khd->qhd", probs_low, values_block, preferred_element_type=jnp.float32
        )
        return (output, None)

    zero_rows = jnp.zeros((block_rows, heads_local, HDIM), jnp.float32)
    output, _ = lax.scan(output_step, zero_rows, (block_ids, keys_blocks, values_blocks))
    delta = jnp.transpose(jnp.sum(grads_heads.astype(jnp.float32) * output, axis=2))

    def key_step(accum, inputs):
        index, keys_block, values_block = inputs
        scores = masked_scores(queries_heads, keys_block, block_allowed(index), scale)
        probs = jnp.exp(scores - log_total[:, :, None])
        probs_low = probs.astype(jnp.bfloat16)
        dscore = score_grads(probs, grads_heads, values_block, delta)
        accum = accum + jnp.einsum(
            "hqk,khd->qhd", dscore, keys_block, preferred_element_type=jnp.float32
        )
        key_part = (
            jnp.einsum("hqk,qhd->khd", dscore, queries_heads, preferred_element_type=jnp.float32)
            * scale
        )
        value_part = jnp.einsum(
            "hqk,qhd->khd", probs_low, grads_heads, preferred_element_type=jnp.float32
        )
        terms = jnp.concatenate(
            [key_part.reshape(span_rows, width), value_part.reshape(span_rows, width)], axis=1
        )
        return (accum, terms)

    query_accum, key_value_terms = lax.scan(
        key_step, zero_rows, (block_ids, keys_blocks, values_blocks)
    )
    summed = lax.psum_scatter(
        key_value_terms.reshape(total_rows, 2 * width), "seq", scatter_dimension=0, tiled=True
    )
    key_grad = summed[:, :width].astype(jnp.bfloat16)
    value_grad = summed[:, width:].astype(jnp.bfloat16)
    query_grad = (query_accum * scale).reshape(block_rows, width).astype(jnp.bfloat16)
    video_back = (
        lax.all_to_all(query_grad[:shard], "head", split_axis=0, concat_axis=1, tiled=True),
        lax.all_to_all(key_grad[:shard], "head", split_axis=0, concat_axis=1, tiled=True),
        lax.all_to_all(value_grad[:shard], "head", split_axis=0, concat_axis=1, tiled=True),
    )
    return (
        video_back[0],
        video_back[1],
        video_back[2],
        query_grad[shard:],
        key_grad[shard:],
        value_grad[shard:],
    )


def solution(mesh):
    in_specs = (
        P(("seq", "head"), None),
        P(("seq", "head"), None),
        P(("seq", "head"), None),
        P(("seq", "head"), None),
        P("seq", "head"),
        P("seq", "head"),
        P("seq", "head"),
        P("seq", "head"),
        P(),
        P(),
    )
    out_specs = (
        P(("seq", "head"), None),
        P(("seq", "head"), None),
        P(("seq", "head"), None),
        P("seq", "head"),
        P("seq", "head"),
        P("seq", "head"),
    )
    return jax.shard_map(
        on_device, mesh=mesh, in_specs=in_specs, out_specs=out_specs, check_vma=False
    )
```

profile of v0, /device:TPU:1, one launch (start us, length us, event | category | flops | bytes accessed | tf_op | source)
XLA Modules:
  0.0 509.0 jit_solution(7523882014536161291)
XLA Ops:
  8.3 11.5 %all_to_all.127 = bf16[32,8,384]{2,0,1:T(8,128)(2,1)S(1)} all-to-all(bf16[32,8,384]{2,0,1:T(8,128)(2,1)S(1)} %bitcast.196), channel_id=1, replica_groups=mesh['seq'=16,'head'=8] {'head'}, dimensions={1} | all-to-all | bytes 393216 | tf_op jit(solution)/shard_map/all_to_all | solution.py:64
  22.5 9.2 %all_to_all.128 = bf16[32,8,384]{2,0,1:T(8,128)(2,1)S(1)} all-to-all(bf16[32,8,384]{2,0,1:T(8,128)(2,1)S(1)} %bitcast.197), channel_id=1, replica_groups=mesh['seq'=16,'head'=8] {'head'}, dimensions={1} | all-to-all | bytes 393216 | tf_op jit(solution)/shard_map/all_to_all | solution.py:63
  35.0 4.2 all-to-all-start.1
  40.5 4.6 all-to-all-done.1
  45.1 4.2 all-to-all-start.3
  50.6 4.7 all-to-all-done.3
  55.9 20.6 %all-gather.5.cloned.1.call-done = bf16[6144,384]{1,0:T(8,128)(2,1)} async-done(((bf16[384,384]{1,0:T(8,128)(2,1)}), bf16[6144,384]{1,0:T(8,128)(2,1)}) %all-gather.5.cloned.1.call-update) | async-done | bytes 4718608 | tf_op jit(solution)/shard_map/all_gather | solution.py:90
  76.5 6.7 %copy.141 = bf16[6144,384]{0,1:T(8,128)(2,1)} copy(bf16[6144,384]{1,0:T(8,128)(2,1)} %all-gather.5.cloned.1.call-done) | data formatting | bytes 9437184 | tf_op jit(solution)/shard_map/all_gather | solution.py:90
  83.2 3.8 copy.179
  87.0 2.2 copy-done
  89.2 3.2 copy.145
  92.4 7.0 %copy.151 = bf16[8,768,3,128]{3,1,2,0:T(8,128)(2,1)} copy(bf16[8,768,3,128]{1,0,3,2:T(8,128)(2,1)} %bitcast.187) | data formatting | bytes 9437184
  99.4 33.0 %all-gather.3.cloned.1.call-done = bf16[6144,384]{1,0:T(8,128)(2,1)} async-done(((bf16[384,384]{1,0:T(8,128)(2,1)}), bf16[6144,384]{1,0:T(8,128)(2,1)}) %all-gather.3.cloned.1.call-update) | async-done | bytes 4718608 | tf_op jit(solution)/shard_map/all_gather | solution.py:89
  132.4 13.0 %reshape.727 = bf16[8,768,3,128]{3,2,1,0:T(4,128)(2,1)} reshape(bf16[6144,384]{1,0:T(8,128)(2,1)} %all-gather.3.cloned.1.call-done) | data formatting | bytes 9437184 | tf_op jit(solution)/shard_map/reshape | solution.py:100
  145.4 6.1 %copy.149 = bf16[8,768,3,128]{3,1,2,0:T(8,128)(2,1)} copy(bf16[8,768,3,128]{3,2,1,0:T(4,128)(2,1)} %reshape.727) | data formatting | bytes 9437184
  151.5 39.5 %while.46 = (s32[]{:T(128)}, f32[3,384]{1,0:T(4,128)S(1)}, f32[3,384]{1,0:T(4,128)S(1)}, s32[8]{0:T(128)S(1)}, s32[8]{0:T(128)S(1)}, /*index=5*/s32[8]{0:T(128)S...) while((s32[]{:T(128)}, f32[3,384]{1,0:T(4,128)S(1)}, ...), condition=%wide.region_7.8_spmd.clone, body=%wide.region_2.7_spmd.clone.sunk | while | flops 233975040 | bytes 8945148 | solution.py:121
  153.7 1.8 fusion.136
  158.7 1.9 fusion.136
  163.6 1.8 fusion.136
  168.6 1.9 fusion.136
  173.5 1.8 fusion.136
  178.4 1.9 fusion.136
  183.4 1.8 fusion.136
  188.3 1.9 fusion.136
  191.6 39.6 %while.47 = (s32[]{:T(128)}, f32[384,3,128]{0,2,1:T(8,128)S(1)}, bf16[8,768,3,128]{1,3,2,0:T(8,128)(2,1)}, s32[8]{0:T(128)S(1)}, s32[8]{0:T(128)S(1)}, /*index=5...) while((s32[]{:T(128)}, f32[384,3,128]{0,2,1:T(8,128)S(1)}, ...), condition=%wide.region_12.13_spmd.clone, body=%wide.region_9.12_spmd.clone.sunk | while | flops 458097792 | bytes 3284990 | solution.py:134
  193.9 2.7 fusion.143
  198.8 2.7 fusion.143
  203.8 2.7 fusion.143
  208.7 2.7 fusion.143
  213.7 2.7 fusion.143
  218.6 2.7 fusion.143
  223.6 2.7 fusion.143
  228.5 2.7 fusion.143
  232.8 124.9 %while.48 = (s32[]{:T(128)}, f32[384,3,128]{0,2,1:T(8,128)S(1)}, f32[8,768,768]{2,1,0:T(8,128)}, bf16[8,768,3,128]{3,1,2,0:T(8,128)(2,1)}, s32[8]{0:T(128)S(1)},...) while((s32[]{:T(128)}, f32[384,3,128]{0,2,1:T(8,128)S(1)}, ...), condition=%wide.region_17.18_spmd.clone, body=%wide.region_14.17_spmd.clone.sunk | while | flops 1143768192 | bytes 37504040 | solution.py:158
  236.7 1.8 fusion.159
  238.5 2.3 fusion.157
  244.8 2.0 copy.189
  252.3 1.8 fusion.159
  254.1 2.3 fusion.157
  260.4 2.0 copy.189
  267.9 1.8 fusion.159
  269.7 2.3 fusion.157
  275.9 2.0 copy.189
  283.5 1.8 fusion.159
  285.3 2.3 fusion.157
  291.6 2.0 copy.189
  299.1 1.8 fusion.159
  301.0 2.4 fusion.157
  307.2 2.0 copy.189
  314.7 1.8 fusion.159
  316.6 2.3 fusion.157
  322.8 2.0 copy.189
  330.4 1.8 fusion.159
  332.2 2.4 fusion.157
  338.5 2.0 copy.189
  346.0 1.8 fusion.159
  347.8 2.3 fusion.157
  354.1 2.0 copy.189
  358.8 4.9 all-to-all-start.4
  363.7 114.8 %reduce-scatter.2.cloned.1.call-done = f32[384,768]{1,0:T(8,128)} async-done(((f32[6144,768]{1,0:T(8,128)}), f32[384,768]{1,0:T(8,128)}) %reduce-scatter.2.cloned.1.call-update) | async-done | bytes 1179664 | tf_op jit(solution)/shard_map/reduce_scatter | solution.py:161
  480.7 5.0 all-to-all-start.5
  487.2 4.4 all-to-all-done.5
  491.6 4.2 all-to-all-start.6
  497.2 4.5 all-to-all-done.6
  (331 shorter events, 119.9 us)
Async XLA Ops:
  7.2 32.1 %copy-start.5 = (s32[8]{0:T(128)S(1)}, s32[8]{0:T(128)}, u32[]{:S(2)}) copy-start(s32[8]{0:T(128)} %param.24) | copy-start | bytes 100
  7.2 32.4 %copy-start.2 = (s32[8]{0:T(128)S(1)}, s32[8]{0:T(128)}, u32[]{:S(2)}) copy-start(s32[8]{0:T(128)} %param.25) | copy-start | bytes 100
  7.2 32.5 %copy-start.3 = (bf16[128,384]{1,0:T(8,128)(2,1)S(1)}, bf16[128,384]{1,0:T(8,128)(2,1)}, u32[]{:S(2)}) copy-start(bf16[128,384]{1,0:T(8,128)(2,1)} %param.23) | copy-start | bytes 294916
  7.2 32.6 %copy-start.1 = (bf16[32,3072]{1,0:T(8,128)(2,1)S(1)}, bf16[32,3072]{1,0:T(8,128)(2,1)}, u32[]{:S(2)}) copy-start(bf16[32,3072]{1,0:T(8,128)(2,1)} %param.19) | copy-start | bytes 589828
  7.2 42.2 %copy-start.4 = (bf16[128,384]{1,0:T(8,128)(2,1)S(1)}, bf16[128,384]{1,0:T(8,128)(2,1)}, u32[]{:S(2)}) copy-start(bf16[128,384]{1,0:T(8,128)(2,1)} %param.20) | copy-start | bytes 294916
  7.2 69.3 %all-gather.5.cloned.1.call-start = ((), (), s32[]{:S(2)}) async-start(), calls=%async_computation.9 | async-start | bytes 5013504 | tf_op jit(solution)/shard_map/all_gather | solution.py:90
  21.5 111.0 %all-gather.3.cloned.1.call-start = ((), (), s32[]{:S(2)}) async-start(), calls=%async_computation.8 | async-start | bytes 5013504 | tf_op jit(solution)/shard_map/all_gather | solution.py:89
  35.0 10.2 %all-to-all-start.1 = ((bf16[32,8,384]{2,0,1:T(8,128)(2,1)}), bf16[32,8,384]{2,0,1:T(8,128)(2,1)S(1)}, u32[]{:S(2)}, u32[]{:S(2)}) async-start(bf16[32,8,384]{2,0,1:T(8,128)(2,1)} %bitcast.127), calls=%async_computation.1 | async-start | bytes 393216 | tf_op jit(solution)/shard_map/all_to_all | solution.py:62
  45.1 10.2 %all-to-all-start.3 = ((bf16[32,8,384]{2,0,1:T(8,128)(2,1)}), bf16[32,8,384]{2,0,1:T(8,128)(2,1)S(1)}, u32[]{:S(2)}, u32[]{:S(2)}) async-start(bf16[32,8,384]{2,0,1:T(8,128)(2,1)} %bitcast.125), calls=%async_computation.3 | async-start | bytes 393216 | tf_op jit(solution)/shard_map/all_to_all | solution.py:65
  49.4 429.2 %reduce-scatter.2.cloned.1.call-start = ((), (), s32[]{:S(2)}) async-start(), calls=%async_computation.10 | async-start | bytes 20054016 | tf_op jit(solution)/shard_map/reduce_scatter | solution.py:161
  87.0 2.2 copy-start
  358.8 121.9 %all-to-all-start.4 = ((bf16[8,32,384]{2,1,0:T(8,128)(2,1)}), bf16[8,32,384]{2,1,0:T(8,128)(2,1)S(1)}, u32[]{:S(2)}, u32[]{:S(2)}) async-start(bf16[8,32,384]{2,1,0:T(8,128)(2,1)} %all_to_all.108), calls=%async_computation.4 | async-start | bytes 393216 | tf_op jit(solution)/shard_map/all_to_all | solution.py:168
  480.7 10.9 %all-to-all-start.5 = ((bf16[8,32,384]{2,1,0:T(8,128)(2,1)}), bf16[8,32,384]{2,1,0:T(8,128)(2,1)S(1)}, u32[]{:S(2)}, u32[]{:S(2)}) async-start(bf16[8,32,384]{2,1,0:T(8,128)(2,1)} %bitcast.13), calls=%async_computation.6 | async-start | bytes 393216 | tf_op jit(solution)/shard_map/all_to_all | solution.py:169
  491.6 10.2 %all-to-all-start.6 = ((bf16[8,32,384]{2,1,0:T(8,128)(2,1)}), bf16[8,32,384]{2,1,0:T(8,128)(2,1)S(1)}, u32[]{:S(2)}, u32[]{:S(2)}) async-start(bf16[8,32,384]{2,1,0:T(8,128)(2,1)} %bitcast.15), calls=%async_computation.7 | async-start | bytes 393216 | tf_op jit(solution)/shard_map/all_to_all | solution.py:170
Sparse Core Ops, SparseCore 0:
  21.6 54.9 all-gather.4
  78.7 53.6 all-gather.2
  357.8 120.7 reduce-scatter.1
where the time goes:
time: 513 us; the launch traced here: 509 us
  waiting for transfers between devices  187 us (36%)
  matrix products  102 us (20%)
  local copies, waits for them, and re-layouts  97 us (19%)
  other arithmetic  49.1 us (10%)
  starting transfers between devices  22.7 us (4%)
  blocking collectives  20.7 us (4%)
  loops' own time  16.9 us (3%)
  between operations  14 us (3%)
    reduce_scatter x1, waiting for transfers between devices, on_device(): lax.psum_scatter(key_value_terms.reshape(total_rows, 2 * width), 'seq', s...  115 us
    all_gather x1, waiting for transfers between devices, on_device(): lax.all_gather(keys_own, 'seq', axis=0, tiled=True)  33 us
    dynamic_update_slice x16, local copies, waits for them, and re-layouts, on_device(): lax.scan(key_step, zero_rows, (block_ids, keys_blocks, values_blocks))  29 us
    dot_general x16, matrix products, masked_scores(): jnp.einsum('qhd,khd->hqk', queries, keys, preferred_element_type=jnp.floa...  28.2 us
    unnamed x23, local copies, waits for them, and re-layouts  24.6 us
    dot_general x8, matrix products, output_step(): jnp.einsum('hqk,khd->qhd', probs_low, values_block, preferred_element_typ...  21.5 us
    all_gather x1, waiting for transfers between devices, on_device(): lax.all_gather(values_own, 'seq', axis=0, tiled=True)  20.6 us
    dot_general x8, matrix products, score_grads(): jnp.einsum('qhd,khd->hqk', grads, values, preferred_element_type=jnp.floa...  18.8 us
  transfers between devices with their start and end apart: 8, of which 7 were waited for; matrix products, arithmetic and copies ran while one was open for 6% of the time, Pallas kernels for 0%

commit v1 on v0

v1 whole, which is shorter than its diff:
```python
import functools

import jax
import jax.numpy as jnp
from jax import lax
from jax.experimental import pallas as pl
from jax.experimental.pallas import tpu as pltpu
from jax.sharding import PartitionSpec as P

HDIM = 128
CAP = 256
NSHOT = 8
HEADS_LOCAL = 3
WIDTH = HEADS_LOCAL * HDIM
GROUP = 8
SIDE = 4
OWN = 32
BLOCK = GROUP * OWN
HALF = 128
VIDEO_ROWS = SIDE * BLOCK
TEXT_ROWS = SIDE * HALF
ROWS = VIDEO_ROWS + TEXT_ROWS
SCALE = HDIM ** (-0.5)
LOG2E = 1.4426950408889634
TO_LOG2 = SCALE * LOG2E
LOW = -1e30
F32 = jnp.float32
BF16 = jnp.bfloat16
VMEM_LIMIT = 24 * 1024 * 1024


def dot_nt(a, b):
    return lax.dot_general(a, b, (((1,), (1,)), ((), ())), preferred_element_type=F32)


def dot_nn(a, b):
    return lax.dot_general(a, b, (((1,), (0,)), ((), ())), preferred_element_type=F32)


def pack_kernel(q_ref, k_ref, v_ref, g_ref, tq_ref, tg_ref, out_ref, text_qg_ref):
    for d in range(GROUP):
        cols = slice(d * WIDTH, (d + 1) * WIDTH)
        for n, ref in enumerate((q_ref, g_ref, k_ref, v_ref)):
            out_ref[d, n] = ref[:, cols]
    text_qg_ref[0] = tq_ref[...]
    text_qg_ref[1] = tg_ref[...]


def pack(*arrays):
    video = jax.ShapeDtypeStruct((GROUP, 4, OWN, WIDTH), BF16)
    text = jax.ShapeDtypeStruct((2, HALF, WIDTH), BF16)
    return pl.pallas_call(pack_kernel, out_shape=(video, text), name="pack_inputs")(*arrays)


def assemble_kernel(in_ref, tk_ref, tv_ref, qg_ref, kv_ref):
    for n in range(2):
        qg_ref[n] = in_ref[:, n].reshape(BLOCK, WIDTH)
        kv_ref[n, :BLOCK] = in_ref[:, 2 + n].reshape(BLOCK, WIDTH)
    kv_ref[0, BLOCK:] = tk_ref[...]
    kv_ref[1, BLOCK:] = tv_ref[...]


def assemble(arrived, text_key, text_value):
    return pl.pallas_call(
        assemble_kernel,
        out_shape=(QUERY_MESSAGE, KEY_MESSAGE),
        name="assemble_blocks",
    )(*placed([arrived]), text_key, text_value)


def unpack_kernel(in_ref, q_ref, k_ref, v_ref):
    for d in range(GROUP):
        cols = slice(d * WIDTH, (d + 1) * WIDTH)
        q_ref[:, cols] = in_ref[d, 0]
        k_ref[:, cols] = in_ref[d, 1]
        v_ref[:, cols] = in_ref[d, 2]


def unpack(arrived):
    shape = jax.ShapeDtypeStruct((OWN, GROUP * WIDTH), BF16)
    return pl.pallas_call(unpack_kernel, out_shape=(shape, shape, shape), name="unpack_video")(*placed([arrived]))


def head_cols(h):
    return slice(h * HDIM, (h + 1) * HDIM)


def sum_kernel(*refs):
    dq, dkv = refs[:SIDE], refs[SIDE : 2 * SIDE]
    out, *text_out = refs[2 * SIDE :]
    for h in range(HEADS_LOCAL):
        total = jnp.transpose(sum(r[h].astype(F32) for r in dq).astype(BF16))
        out[:, 0, :, head_cols(h)] = total[:BLOCK].reshape(GROUP, OWN, HDIM)
        text_out[0][:, head_cols(h)] = total[BLOCK:]
    for n in range(2):
        total = sum(r[n].astype(F32) for r in dkv).astype(BF16)
        out[:, 1 + n] = total[:BLOCK].reshape(GROUP, OWN, WIDTH)
        text_out[1 + n][...] = total[BLOCK:]


def sum_terms(dq, dkv):
    return pl.pallas_call(
        sum_kernel,
        out_shape=[jax.ShapeDtypeStruct((GROUP, 3, OWN, WIDTH), BF16)]
        + [jax.ShapeDtypeStruct((HALF, WIDTH), BF16)] * 3,
        name="sum_terms",
    )(*placed([*dq, *dkv]))


class Labels:
    def __init__(self, length_ref, caption_ref, place_ref):
        place = place_ref[0]
        self.z = place // SIDE
        self.y = place % SIDE
        self.caption_ref = caption_ref
        starts = [jnp.int32(0)]
        for s in range(NSHOT):
            starts.append(starts[-1] + length_ref[s])
        self.starts = starts

    def span(self, shot):
        begin = jnp.int32(0)
        end = jnp.int32(0)
        for s in range(NSHOT):
            begin = jnp.where(shot == s, self.starts[s], begin)
            end = jnp.where(shot == s, self.starts[s + 1], end)
        return begin, end

    def query_base(self, j):
        return (self.z * SIDE + (self.y ^ j)) * BLOCK

    def key_base(self, i):
        return ((self.z ^ i) * SIDE + self.y) * BLOCK

    def query_shot(self, p):
        return self.z * 2 + (self.y ^ (2 * p)) // 2

    def key_shot(self, t):
        return (self.z ^ t) * 2 + self.y // 2

    def live(self, shot, half):
        row = half * HALF + lax.broadcasted_iota(jnp.int32, (HALF, 1), 0)
        return row < self.caption_ref[shot]


def stage_queries(labels, qg, text_qg, q_all, g_all):
    for j in range(SIDE):
        q_all[j] = qg[j][0]
        g_all[j] = qg[j][1]
    for u in range(SIDE):
        p, rows = u // 2, slice(u % 2 * HALF, (u % 2 + 1) * HALF)
        q_all[SIDE + p, rows] = text_qg[u][0]
        live = labels.live(labels.query_shot(p), (labels.y ^ u) % 2)
        g_all[SIDE + p, rows] = jnp.where(live, text_qg[u][1], jnp.zeros((HALF, WIDTH), BF16))


def stage_keys(kv, k_all, v_all, tk_all, tv_all):
    for i, ref in enumerate(kv):
        k_all[i] = ref[0, :BLOCK]
        v_all[i] = ref[1, :BLOCK]
        tk_all[i] = ref[0, BLOCK:]
        tv_all[i] = ref[1, BLOCK:]


def loop(count, step):
    lax.fori_loop(0, count, lambda n, c: (step(n), c)[1], 0)


def text_keys(labels, first, count, visit):
    def step(n):
        t, j = first + n // SIDE, n % SIDE
        shot, base = labels.key_shot(t), labels.query_base(j)
        begin, end = labels.span(shot)

        @pl.when(jnp.logical_and(begin < base + BLOCK, end > base))
        def _():
            row = base + lax.broadcasted_iota(jnp.int32, (1, BLOCK), 1)
            same = jnp.logical_and(row >= begin, row < end)
            visit(t - first, j, jnp.logical_and(labels.live(shot, labels.y % 2), same))

    loop(count * SIDE, step)
    if first == 0:
        live = labels.live(labels.key_shot(0), labels.y % 2)
        visit(0, SIDE, jnp.broadcast_to(live, (HALF, BLOCK)))


def text_queries(labels, first, count, visit):
    def step(n):
        i, p = first + n // 2, n % 2
        base = labels.key_base(i)
        begin, end = labels.span(labels.query_shot(p))

        @pl.when(jnp.logical_and(begin < base + BLOCK, end > base))
        def _():
            row = base + lax.broadcasted_iota(jnp.int32, (BLOCK, 1), 0)
            same = jnp.logical_and(row >= begin, row < end)
            visit(i - first, p, jnp.broadcast_to(same, (BLOCK, BLOCK)))

    loop(2 * count, step)


def head_ds(h):
    return pl.ds(pl.multiple_of(h * HDIM, HDIM), HDIM)


def rows_ds(j):
    return pl.ds(pl.multiple_of(j * BLOCK, BLOCK), BLOCK)


def query_cols(j):
    return slice(j * BLOCK, (j + 1) * BLOCK)


def stats_kernel(first, length_ref, caption_ref, place_ref, *refs):
    acc_in, refs = (refs[:1], refs[1:]) if first else ((), refs)
    qg, kv, text_qg = refs[:SIDE], refs[SIDE : SIDE + 2], refs[SIDE + 2 : 2 * SIDE + 2]
    out_ref, q_all, g_all, k_all, v_all, tk_all, tv_all, *scratch = refs[2 * SIDE + 2 :]
    labels = Labels(length_ref, caption_ref, place_ref)
    stage_queries(labels, qg, text_qg, q_all, g_all)
    stage_keys(kv, k_all, v_all, tk_all, tv_all)
    if first:
        acc = scratch[0]
        acc[...] = acc_in[0][...]
    else:
        acc = out_ref
        acc[0] = jnp.full((HEADS_LOCAL, ROWS), LOW, F32)
        acc[1:3] = jnp.zeros((2, HEADS_LOCAL, ROWS), F32)

    def head(h):
        c, row = head_ds(h), pl.ds(h, 1)
        keys = k_all[:, :, c].reshape(2 * BLOCK, HDIM)
        values = v_all[:, :, c].reshape(2 * BLOCK, HDIM)
        for j in range(SIDE):
            cols = query_cols(j)
            scores = dot_nt(keys, q_all[j, :, c])
            dprob = dot_nt(values, g_all[j, :, c])
            top = jnp.max(scores, axis=0, keepdims=True) * TO_LOG2
            if first:
                before = acc[0, row, cols]
                top = jnp.maximum(before, top)
                shrink = jnp.exp2(before - top)
            weight = jnp.exp2(scores * TO_LOG2 - top)
            total = jnp.sum(weight, axis=0, keepdims=True)
            weighted = jnp.sum(weight * dprob, axis=0, keepdims=True)
            if first:
                total += acc[1, row, cols] * shrink
                weighted += acc[2, row, cols] * shrink
            acc[0, row, cols] = top
            acc[1, row, cols] = total
            acc[2, row, cols] = weighted

    loop(HEADS_LOCAL, head)

    def visit(keys_ref, values_ref, n, j, mask):
        cols = rows_ds(j)
        results = []
        for h in range(HEADS_LOCAL):
            c = head_cols(h)
            scores = jnp.where(mask, dot_nt(keys_ref[n, :, c], q_all[j, :, c]) * TO_LOG2, LOW)
            dprob = dot_nt(values_ref[n, :, c], g_all[j, :, c])
            before = acc[0, h : h + 1, cols]
            top = jnp.maximum(before, jnp.max(scores, axis=0, keepdims=True))
            weight = jnp.where(mask, jnp.exp2(scores - top), 0.0)
            shrink = jnp.exp2(before - top)
            results.append(
                (
                    top,
                    acc[1, h : h + 1, cols] * shrink + jnp.sum(weight, axis=0, keepdims=True),
                    acc[2, h : h + 1, cols] * shrink + jnp.sum(weight * dprob, axis=0, keepdims=True),
                )
            )
        for h in range(HEADS_LOCAL):
            for n in range(3):
                acc[n, h : h + 1, cols] = results[h][n]

    text_keys(labels, first, 2, lambda t, j, mask: visit(tk_all, tv_all, t, j, mask))
    text_queries(labels, first, 2, lambda i, p, mask: visit(k_all, v_all, i, SIDE + p, mask))
    if first:
        total = acc[1]
        some = total > 0.0
        total = jnp.where(some, total, 1.0)
        out_ref[0] = jnp.where(some, acc[0] + jnp.log2(total), LOW)
        out_ref[1] = acc[2] / total


def normalize(stats, norm):
    for j in range(SIDE + 2):
        parts = []
        for e in range(SIDE):
            if j < SIDE:
                parts.append([stats[e][n, :, query_cols(j ^ e)] for n in range(2)])
            else:
                halves = []
                for u in (2 * (j - SIDE), 2 * (j - SIDE) + 1):
                    at = VIDEO_ROWS + (u ^ e) * HALF
                    halves.append([stats[e][n, :, at : at + HALF] for n in range(2)])
                parts.append([jnp.concatenate([halves[0][n], halves[1][n]], 1) for n in range(2)])
        top = functools.reduce(jnp.maximum, [p[0] for p in parts])
        share = [jnp.exp2(p[0] - top) for p in parts]
        total = sum(share)
        delta = sum(p[1] * s for p, s in zip(parts, share)) / total
        norm[0, :, query_cols(j)] = top + jnp.log2(total)
        norm[1, :, query_cols(j)] = delta


def key_grads(labels, first, count, kv, dkv_out, norm, dq_t, scratch):
    q_all, g_all, k_all, v_all, tk_all, tv_all, dk, dv, text_dk, text_dv, p_all, ds_all = scratch
    stage_keys(kv, k_all, v_all, tk_all, tv_all)
    text_dk[...] = jnp.zeros((count, HEADS_LOCAL, HALF, HDIM), F32)
    text_dv[...] = jnp.zeros((count, HEADS_LOCAL, HALF, HDIM), F32)
    rows = count * BLOCK

    def head(h):
        c, row = head_ds(h), pl.ds(h, 1)
        keys = k_all[:, :, c].reshape(rows, HDIM)
        values = v_all[:, :, c].reshape(rows, HDIM)
        keys_t = jnp.transpose(keys)
        for j in range(SIDE):
            cols = query_cols(j)
            scores = dot_nt(keys, q_all[j, :, c])
            dprob = dot_nt(values, g_all[j, :, c])
            probs = jnp.exp2(scores * TO_LOG2 - norm[0, row, cols])
            dscore = (probs * (dprob - norm[1, row, cols])).astype(BF16)
            p_all[:, cols] = probs.astype(BF16)
            ds_all[:, cols] = dscore
            part = dot_nn(keys_t, dscore)
            if first:
                dq_t[h, :, cols] = part
            else:
                dq_t[h, :, cols] += part
        dv[h] = dot_nn(p_all[...], g_all[:SIDE, :, c].reshape(VIDEO_ROWS, HDIM))
        dk[h] = dot_nn(ds_all[...], q_all[:SIDE, :, c].reshape(VIDEO_ROWS, HDIM))

    loop(HEADS_LOCAL, head)

    def visit(keys_ref, values_ref, n, j, mask, add):
        cols = rows_ds(j)
        results = []
        for h in range(HEADS_LOCAL):
            c = head_cols(h)
            keys, queries, grads = keys_ref[n, :, c], q_all[j, :, c], g_all[j, :, c]
            scores = dot_nt(keys, queries) * TO_LOG2
            dprob = dot_nt(values_ref[n, :, c], grads)
            probs = jnp.where(mask, jnp.exp2(jnp.where(mask, scores, LOW) - norm[0, h : h + 1, cols]), 0.0)
            low = probs.astype(BF16)
            dscore = (probs * (dprob - norm[1, h : h + 1, cols])).astype(BF16)
            results.append((dot_nn(dscore, queries), dot_nn(low, grads), dot_nn(jnp.transpose(keys), dscore)))
        for h in range(HEADS_LOCAL):
            add(n, h, results[h][0], results[h][1])
            dq_t[h, :, cols] += results[h][2]

    def add_text(n, h, key_part, value_part):
        text_dk[n, h] += key_part
        text_dv[n, h] += value_part

    def add_video(n, h, key_part, value_part):
        dk[h, rows_ds(n)] += key_part
        dv[h, rows_ds(n)] += value_part

    text_keys(labels, first, count, lambda t, j, mask: visit(tk_all, tv_all, t, j, mask, add_text))
    text_queries(labels, first, count, lambda i, p, mask: visit(k_all, v_all, i, SIDE + p, mask, add_video))

    for i in range(count):
        for h in range(HEADS_LOCAL):
            c = head_cols(h)
            dkv_out[i][0, :BLOCK, c] = (dk[h, query_cols(i)] * SCALE).astype(BF16)
            dkv_out[i][1, :BLOCK, c] = dv[h, query_cols(i)].astype(BF16)
            dkv_out[i][0, BLOCK:, c] = (text_dk[i, h] * SCALE).astype(BF16)
            dkv_out[i][1, BLOCK:, c] = text_dv[i, h].astype(BF16)


def others_kernel(length_ref, caption_ref, place_ref, *refs):
    qg, kv, stats = refs[:SIDE], refs[SIDE : 2 * SIDE - 1], refs[2 * SIDE - 1 : 3 * SIDE - 1]
    text_qg, refs = refs[3 * SIDE - 1 : 4 * SIDE - 1], refs[4 * SIDE - 1 :]
    dkv_out, (dq_t, norm, *scratch) = refs[: SIDE - 1], refs[SIDE - 1 :]
    labels = Labels(length_ref, caption_ref, place_ref)
    stage_queries(labels, qg, text_qg, scratch[0], scratch[1])
    normalize(stats, norm)
    dq_t[:, :, VIDEO_ROWS:] = jnp.zeros((HEADS_LOCAL, HDIM, TEXT_ROWS), F32)
    key_grads(labels, 1, SIDE - 1, kv, dkv_out, norm, dq_t, scratch)


def own_kernel(length_ref, caption_ref, place_ref, *refs):
    norm, dq_in, qg, kv = refs[0], refs[1], refs[2 : SIDE + 2], refs[SIDE + 2 : SIDE + 3]
    text_qg, refs = refs[SIDE + 3 : 2 * SIDE + 3], refs[2 * SIDE + 3 :]
    dq_out, dkv_out, (dq_t, *scratch) = refs[:SIDE], refs[SIDE : SIDE + 1], refs[SIDE + 1 :]
    labels = Labels(length_ref, caption_ref, place_ref)
    stage_queries(labels, qg, text_qg, scratch[0], scratch[1])
    dq_t[...] = dq_in[...]
    key_grads(labels, 0, 1, kv, dkv_out, norm, dq_t, scratch)
    for n in range(SIDE):
        dq_out[n][:, :, :BLOCK] = (dq_t[:, :, query_cols(n)] * SCALE).astype(BF16)
        dq_out[n][:, :, BLOCK:] = (dq_t[:, :, VIDEO_ROWS + n * HALF : VIDEO_ROWS + (n + 1) * HALF] * SCALE).astype(BF16)


SMEM_SPEC = pl.BlockSpec(memory_space=pltpu.SMEM)
VMEM_SPEC = pl.BlockSpec(memory_space=pltpu.VMEM)
PARAMS = pltpu.CompilerParams(vmem_limit_bytes=VMEM_LIMIT)
DQ_T = (HEADS_LOCAL, HDIM, ROWS)
STATS = (3, HEADS_LOCAL, ROWS)
QUERY_MESSAGE = jax.ShapeDtypeStruct((2, BLOCK, WIDTH), BF16)
KEY_MESSAGE = jax.ShapeDtypeStruct((2, BLOCK + HALF, WIDTH), BF16)


def staged(count):
    return (
        [pltpu.VMEM((SIDE + 2, BLOCK, WIDTH), BF16)] * 2
        + [pltpu.VMEM((count, BLOCK, WIDTH), BF16)] * 2
        + [pltpu.VMEM((count, HALF, WIDTH), BF16)] * 2
    )


def grads_scratch(count):
    return (
        staged(count)
        + [pltpu.VMEM((HEADS_LOCAL, count * BLOCK, HDIM), F32)] * 2
        + [pltpu.VMEM((count, HEADS_LOCAL, HALF, HDIM), F32)] * 2
        + [pltpu.VMEM((count * BLOCK, VIDEO_ROWS), BF16)] * 2
    )


def placed(arrays, space=pltpu.VMEM):
    return [pltpu.with_memory_space_constraint(a, space) for a in arrays]


def cost(blocks, matmuls):
    pairs = HEADS_LOCAL * VIDEO_ROWS * BLOCK * blocks
    return pl.CostEstimate(flops=2 * HDIM * matmuls * pairs, bytes_accessed=8 * 1024 * 1024, transcendentals=pairs)


def stats_call(first, scalars, acc, qg, kv, text_qg):
    return pl.pallas_call(
        functools.partial(stats_kernel, first),
        in_specs=[SMEM_SPEC] * 3 + [VMEM_SPEC] * (len(acc) + 2 * SIDE + 2),
        out_specs=VMEM_SPEC,
        out_shape=jax.ShapeDtypeStruct((2, HEADS_LOCAL, ROWS) if first else STATS, F32),
        scratch_shapes=staged(2) + ([pltpu.VMEM(STATS, F32)] if first else []),
        compiler_params=PARAMS,
        cost_estimate=cost(2, 2),
        name="stats_last" if first else "stats_first",
    )(*scalars, *placed([*acc, *qg, *kv[first : first + 2]]), *placed(text_qg, pltpu.HBM))


def others_call(scalars, qg, kv, text_qg, stats):
    *dkv, dq_t, norm = pl.pallas_call(
        others_kernel,
        in_specs=[SMEM_SPEC] * 3 + [VMEM_SPEC] * (4 * SIDE - 1),
        out_specs=[VMEM_SPEC] * (SIDE + 1),
        out_shape=[KEY_MESSAGE] * (SIDE - 1)
        + [jax.ShapeDtypeStruct(DQ_T, F32), jax.ShapeDtypeStruct((2, HEADS_LOCAL, ROWS), F32)],
        scratch_shapes=grads_scratch(SIDE - 1),
        compiler_params=PARAMS,
        cost_estimate=cost(SIDE - 1, 5),
        name="grads_others",
    )(*scalars, *placed([*qg, *kv[1:], *stats]), *placed(text_qg, pltpu.HBM))
    return dkv, dq_t, norm


def own_call(scalars, qg, kv, text_qg, dq_t, norm):
    *dq, dkv = pl.pallas_call(
        own_kernel,
        in_specs=[SMEM_SPEC] * 3 + [VMEM_SPEC] * (2 * SIDE + 3),
        out_specs=[VMEM_SPEC] * (SIDE + 1),
        out_shape=[jax.ShapeDtypeStruct((HEADS_LOCAL, HDIM, BLOCK + HALF), BF16)] * SIDE + [KEY_MESSAGE],
        scratch_shapes=[pltpu.VMEM(DQ_T, F32)] + grads_scratch(1),
        compiler_params=PARAMS,
        cost_estimate=cost(1, 5),
        name="grads_own",
    )(*scalars, *placed([norm]), dq_t, *placed(qg, pltpu.HBM), *placed(kv[:1]), *placed(text_qg, pltpu.HBM))
    return dq, dkv


def swap(array, axis, step):
    shift = step if axis == "y" else step * SIDE
    return lax.ppermute(array, "seq", [(i, i ^ shift) for i in range(SIDE * SIDE)])


def gathered(array, axis):
    return [array] + [swap(array, axis, step) for step in range(1, SIDE)]


def on_device(
    video_query,
    video_key,
    video_value,
    video_grad,
    text_query,
    text_key,
    text_value,
    text_grad,
    shot_length,
    caption_length,
):
    place = lax.axis_index("seq").astype(jnp.int32)
    scalars = (shot_length, caption_length, place.reshape(1))
    packed, text_qg = pack(video_query, video_key, video_value, video_grad, text_query, text_grad)
    text_qg = gathered(text_qg, "y")
    arrived = lax.all_to_all(packed, "head", split_axis=0, concat_axis=0)
    arrived, text_qg = lax.optimization_barrier((arrived, text_qg))
    qg, kv = assemble(arrived, text_key, text_value)
    qg, kv = gathered(qg, "y"), gathered(kv, "z")

    acc = stats_call(0, scalars, [], qg, kv, text_qg)
    stats = gathered(stats_call(2, scalars, [acc], qg, kv, text_qg), "y")
    dkv, dq_t, norm = others_call(scalars, qg, kv, text_qg, stats)
    dq, dkv_own = own_call(scalars, qg, kv, text_qg, dq_t, norm)

    first = swap(dkv[0], "z", 1)
    dq, first = lax.optimization_barrier((dq, first))
    dkv = [dkv_own, first, swap(dkv[1], "z", 2), swap(dkv[2], "z", 3)]
    dq = [dq[0]] + [swap(dq[step], "y", step) for step in range(1, SIDE)]
    video, *text = sum_terms(dq, dkv)
    video_back = unpack(lax.all_to_all(video, "head", split_axis=0, concat_axis=0))
    return (*video_back, *text)


def solution(mesh):
    video = P(("seq", "head"), None)
    text = P("seq", "head")
    return jax.shard_map(
        on_device,
        mesh=mesh,
        in_specs=(video,) * 4 + (text,) * 4 + (P(), P()),
        out_specs=(video,) * 3 + (text,) * 3,
        check_vma=False,
    )
```

time: 513 us -> 147 us (0.29)
  waiting for transfers between devices: 187 us -> 38.3 us
  matrix products: 102 us -> 0 us
  local copies, waits for them, and re-layouts: 97 us -> 12.9 us
  other arithmetic: 49.1 us -> 0 us
  Pallas kernels: 0 us -> 42.6 us
  loops' own time: 16.9 us -> 0 us
  between operations: 14 us -> 0.82 us
  starting transfers between devices: 22.7 us -> 29.6 us
    reduce_scatter x1 -> x0, waiting for transfers between devices: 115 us -> none  [on_device(): lax.psum_scatter(key_value_terms.reshape(total_rows, 2 * width), 'seq', s...]
    dot_general x56 -> x0, matrix products: 102 us -> none  [the longest x16 28.2 us: masked_scores(): jnp.einsum('qhd,khd->hqk', queries, keys, preferred_element_type=jnp.floa...]
    all_gather x2 -> x0, waiting for transfers between devices: 53.6 us -> none  [the longest x1 33 us: on_device(): lax.all_gather(keys_own, 'seq', axis=0, tiled=True)]
    pallas_call x0 -> x8, Pallas kernels: none -> 42.6 us  [the longest x2 13.1 us: stats_call(): pl.pallas_call(functools.partial(stats_kernel, first), in_specs=[SMEM_SPE...]
    ppermute x0 -> x18, waiting for transfers between devices: none -> 38.3 us  [swap(): lax.ppermute(array, 'seq', [(i, i ^ shift) for i in range(SIDE * SIDE)])]
    dynamic_update_slice x16 -> x0, local copies, waits for them, and re-layouts: 29 us -> none  [on_device(): lax.scan(key_step, zero_rows, (block_ids, keys_blocks, values_blocks))]
    ppermute x0 -> x18, starting transfers between devices: none -> 23.8 us  [swap(): lax.ppermute(array, 'seq', [(i, i ^ shift) for i in range(SIDE * SIDE)])]
    all_to_all x5 -> x1, waiting for transfers between devices: 18.3 us -> 0.01 us  [on_device(): arrived = lax.all_to_all(packed, 'head', split_axis=0, concat_axis=0)]
  transfers between devices with their start and end apart: 8 -> 19, of which waited for: 7 -> 7; matrix products, arithmetic and copies ran while one was open for 6% -> 0% of each run, Pallas kernels for 0% -> 12%
where the time goes in v1:
time: 147 us; the launch traced here: 146 us
  Pallas kernels  42.6 us (29%)
  waiting for transfers between devices  38.3 us (26%)
  starting transfers between devices  29.6 us (20%)
  blocking collectives  21.5 us (15%)
  local copies, waits for them, and re-layouts  12.9 us (9%)
    ppermute x18, waiting for transfers between devices, swap(): lax.ppermute(array, 'seq', [(i, i ^ shift) for i in range(SIDE * SIDE)])  38.3 us
    ppermute x18, starting transfers between devices, swap(): lax.ppermute(array, 'seq', [(i, i ^ shift) for i in range(SIDE * SIDE)])  23.8 us
    all_to_all x1, blocking collectives, on_device(): lax.all_to_all(video, 'head', split_axis=0, concat_axis=0)  21.5 us
    pallas_call x2, Pallas kernels, stats_call(): pl.pallas_call(functools.partial(stats_kernel, first), in_specs=[SMEM_SPE...  13.1 us
    pallas_call x1, Pallas kernels, others_call(): pl.pallas_call(others_kernel, in_specs=[SMEM_SPEC] * 3 + [VMEM_SPEC] * (4...  13.1 us
    unnamed x46, local copies, waits for them, and re-layouts  12.9 us
    pallas_call x1, Pallas kernels, own_call(): pl.pallas_call(own_kernel, in_specs=[SMEM_SPEC] * 3 + [VMEM_SPEC] * (2 *...  9.81 us
    all_to_all x1, starting transfers between devices, on_device(): arrived = lax.all_to_all(packed, 'head', split_axis=0, concat_axis=0)  5.8 us
  transfers between devices with their start and end apart: 19, of which 7 were waited for; matrix products, arithmetic and copies ran while one was open for 0% of the time, Pallas kernels for 12%

profile of v1, /device:TPU:1, one launch (start us, length us, event | category | flops | bytes accessed | tf_op | source)
XLA Modules:
  0.0 145.7 jit_solution(14213960027373130858)
XLA Ops:
  0.6 0.0 copy-start.19
  0.6 0.0 copy-start.18
  0.7 2.3 %pack_inputs.1 = (bf16[8,4,32,384]{3,2,1,0:T(8,128)(2,1)}, bf16[2,128,384]{2,1,0:T(8,128)(2,1)}) custom-call(bf16[32,3072]{1,0:T(8,128)(2,1)} %q_ref.1, bf16[32,3072]{1,0:T(8,128)(2,1)} %k_ref.1, bf16[32,3072]{1,0:T(8,128)(2,1)} %v_ref.1, bf16[32,3072]{1,0:T(8,128)(2,1)} %g_ref.1, bf16[128,384]{1,0:T(8,128)(2,1)} %tq_ref.1, bf16[128,384]{1,0:T(8,128)(2,1)} %tg_ref.1), custom_call_target="tpu_custom_call" | custom-call | tf_op jit(solution)/shard_map/pack_inputs/pallas_call | solution.py:52
  2.9 5.8 %all-to-all-start = ((bf16[8,4,32,384]{3,2,1,0:T(8,128)(2,1)}), bf16[8,4,32,384]{3,2,1,0:T(8,128)(2,1)S(1)}, u32[]{:S(2)}, u32[]{:S(2)}) async-start(bf16[8,4,32,384]{3,2,1,0:T(8,128)(2,1)} %get-tuple-element.37), calls=%async_computation | async-start | bytes 1572864 | tf_op jit(solution)/shard_map/all_to_all | solution.py:498
  8.7 2.7 %collective-permute-start.2 = (bf16[2,128,384]{2,1,0:T(8,128)(2,1)}, bf16[2,128,384]{2,1,0:T(8,128)(2,1)S(1)}, u32[]{:S(2)}, u32[]{:S(2)}) collective-permute-start(bf16[2,128,384]{2,1,0:T(8,128)(2,1)} %get-tuple-element.42.refs_6_.refs_7_.refs_11_), channel_id=1, source_target_pairs={{0,24},{8,16},{16,8},{24,0},{32,56},{40,48},{48,40},{56,32},{64,88... | collective-permute-start | bytes 589832 | tf_op jit(solution)/shard_map/ppermute | solution.py:475
  11.5 0.3 collective-permute-start.1
  11.8 0.2 collective-permute-start
  12.1 9.0 %collective-permute-done.2.refs_9_.refs_10_.refs_14_ = bf16[2,128,384]{2,1,0:T(8,128)(2,1)S(1)} collective-permute-done((bf16[2,128,384]{2,1,0:T(8,128)(2,1)}, bf16[2,128,384]{2,1,0:T(8,128)(2,1)S(1)}, u32[]{:S(2)}, u32[]{:S(2)}) %collective-permute-start.2) | collective-permute-done | bytes 196640 | tf_op jit(solution)/shard_map/ppermute | solution.py:475
  21.0 0.0 collective-permute-done.1.refs_8_.refs_9_.refs_13_
  21.0 0.3 collective-permute-done.refs_7_.refs_8_.refs_12_
  21.3 0.0 all-to-all-done.in_ref
  21.3 2.0 %assemble_blocks.1 = (bf16[2,256,384]{2,1,0:T(8,128)(2,1)}, bf16[2,384,384]{2,1,0:T(8,128)(2,1)}) custom-call(bf16[8,4,32,384]{3,2,1,0:T(8,128)(2,1)S(1)} %all-to-all-done.in_ref, bf16[128,384]{1,0:T(8,128)(2,1)} %tk_ref.1, bf16[128,384]{1,0:T(8,128)(2,1)} %tv_ref.1), custom_call_target="tpu_custom_call" | custom-call | tf_op jit(solution)/shard_map/assemble_blocks/pallas_call | solution.py:64
  23.4 2.6 %collective-permute-start.5 = (bf16[2,256,384]{2,1,0:T(8,128)(2,1)}, bf16[2,256,384]{2,1,0:T(8,128)(2,1)S(1)}, u32[]{:S(2)}, u32[]{:S(2)}) collective-permute-start(bf16[2,256,384]{2,1,0:T(8,128)(2,1)} %get-tuple-element.40.refs_0_.refs_1_.refs_2_), channel_id=1, source_target_pairs={{0,24},{8,16},{16,8},{24,0},{32,56},{40,48},{48,40},{56,32},{64,88... | collective-permute-start | bytes 1179656 | tf_op jit(solution)/shard_map/ppermute | solution.py:475
  26.0 1.6 %collective-permute-start.6 = (bf16[2,384,384]{2,1,0:T(8,128)(2,1)}, bf16[2,384,384]{2,1,0:T(8,128)(2,1)S(1)}, u32[]{:S(2)}, u32[]{:S(2)}) collective-permute-start(bf16[2,384,384]{2,1,0:T(8,128)(2,1)} %get-tuple-element.41.refs_4_.refs_6_), channel_id=1, source_target_pairs={{0,32},{8,40},{16,48},{24,56},{32,0},{40,8},{48,16},{56,24},{64,96... | collective-permute-start | bytes 1769480 | tf_op jit(solution)/shard_map/ppermute | solution.py:475
  27.6 2.2 %collective-permute-start.8 = (bf16[2,384,384]{2,1,0:T(8,128)(2,1)}, bf16[2,384,384]{2,1,0:T(8,128)(2,1)S(1)}, u32[]{:S(2)}, u32[]{:S(2)}) collective-permute-start(bf16[2,384,384]{2,1,0:T(8,128)(2,1)} %get-tuple-element.41.refs_4_.refs_6_), channel_id=1, source_target_pairs={{0,96},{8,104},{16,112},{24,120},{32,64},{40,72},{48,80},{56,88},{... | collective-permute-start | bytes 1769480 | tf_op jit(solution)/shard_map/ppermute | solution.py:475
  29.9 1.1 collective-permute-start.7
  30.9 0.4 collective-permute-start.4
  31.3 10.6 %collective-permute-done.5.refs_3_.refs_4_.refs_5_ = bf16[2,256,384]{2,1,0:T(8,128)(2,1)S(1)} collective-permute-done((bf16[2,256,384]{2,1,0:T(8,128)(2,1)}, bf16[2,256,384]{2,1,0:T(8,128)(2,1)S(1)}, u32[]{:S(2)}, u32[]{:S(2)}) %collective-permute-start.5) | collective-permute-done | bytes 393248 | tf_op jit(solution)/shard_map/ppermute | solution.py:475
  41.9 0.0 collective-permute-start.3
  41.9 0.0 collective-permute-done.4.refs_2_.refs_3_.refs_4_
  41.9 7.9 %collective-permute-done.3.refs_1_.refs_2_.refs_3_ = bf16[2,256,384]{2,1,0:T(8,128)(2,1)S(1)} collective-permute-done((bf16[2,256,384]{2,1,0:T(8,128)(2,1)}, bf16[2,256,384]{2,1,0:T(8,128)(2,1)S(1)}, u32[]{:S(2)}, u32[]{:S(2)}) %collective-permute-start.3) | collective-permute-done | bytes 393248 | tf_op jit(solution)/shard_map/ppermute | solution.py:475
  49.8 0.0 collective-permute-done.6.refs_5_.refs_4_
  49.9 1.1 copy-done
  51.0 1.1 copy-done.4
  52.1 7.4 %stats_first.1.refs_0_ = f32[3,3,1536]{2,1,0:T(4,128)S(1)} custom-call(s32[8]{0:T(128)S(1)} %copy-done.18, s32[8]{0:T(128)S(1)} %copy-done.19, s32[1]{0:T(128)} %bitcast.place_ref, bf16[2,256,384]{2,1,0:T(8,128)(2,1)S(1)} %copy-done, bf16[2,256,384]{2,1,0:T(8,128)(2,1)S(1)} %collective-permute-done.3.refs_1_.refs_2_.refs_3_, ...), custom_call_target="tpu_custom_call" | custom-call | flops 805306368 | bytes 8388608 | tf_op jit(solution)/shard_map/stats_first/pallas_call | solution.py:432
  59.5 0.0 collective-permute-done.8.refs_6_
  59.5 0.0 collective-permute-done.7.refs_5_
  59.5 5.8 %stats_last.1.refs_7_ = f32[2,3,1536]{2,1,0:T(4,128)S(1)} custom-call(s32[8]{0:T(128)S(1)} %copy-done.18, s32[8]{0:T(128)S(1)} %copy-done.19, s32[1]{0:T(128)} %bitcast.place_ref, f32[3,3,1536]{2,1,0:T(4,128)S(1)} %stats_first.1.refs_0_, bf16[2,256,384]{2,1,0:T(8,128)(2,1)S(1)} %copy-done, ...), custom_call_target="tpu_custom_call" | custom-call | flops 805306368 | bytes 8388608 | tf_op jit(solution)/shard_map/stats_last/pallas_call | solution.py:432
  65.2 2.4 %collective-permute-start.11 = (f32[2,3,1536]{2,1,0:T(4,128)S(1)}, f32[2,3,1536]{2,1,0:T(4,128)S(1)}, u32[]{:S(2)}, u32[]{:S(2)}) collective-permute-start(f32[2,3,1536]{2,1,0:T(4,128)S(1)} %stats_last.1.refs_7_), channel_id=1, source_target_pairs={{0,24},{8,16},{16,8},{24,0},{32,56},{40,48},{48,40},{56,32},{64,88... | collective-permute-start | bytes 110600 | tf_op jit(solution)/shard_map/ppermute | solution.py:475
  67.7 0.1 collective-permute-start.10
  67.8 0.8 collective-permute-start.9
  68.6 0.9 collective-permute-done.11.refs_10_
  69.5 2.7 %collective-permute-done.10.refs_9_ = f32[2,3,1536]{2,1,0:T(4,128)S(1)} collective-permute-done((f32[2,3,1536]{2,1,0:T(4,128)S(1)}, f32[2,3,1536]{2,1,0:T(4,128)S(1)}, u32[]{:S(2)}, u32[]{:S(2)}) %collective-permute-start.10) | collective-permute-done | bytes 36896 | tf_op jit(solution)/shard_map/ppermute | solution.py:475
  72.1 0.0 collective-permute-done.9.refs_8_
  72.1 0.0 copy-done.2
  72.1 13.1 %grads_others.1 = (bf16[2,384,384]{2,1,0:T(8,128)(2,1)S(1)}, bf16[2,384,384]{2,1,0:T(8,128)(2,1)S(1)}, bf16[2,384,384]{2,1,0:T(8,128)(2,1)S(1)}, f32[3,128,1536]{2,1,0:T(8,128)S(1)}, f32[2,3,1536]{2,1,0:T(4,128)S(1)}) custom-call(s32[8]{0:T(128)S(1)} %copy-done.18, s32[8]{0:T(128)S(1)} %copy-done.19, s32[1]{0:T(128)} %bitcast.place_ref, ...), custom_call_target="tpu_custom_call" | custom-call | flops 3019898880 | bytes 8388608 | tf_op jit(solution)/shard_map/grads_others/pallas_call | solution.py:445
  85.2 1.7 %collective-permute-start.12 = (bf16[2,384,384]{2,1,0:T(8,128)(2,1)S(1)}, bf16[2,384,384]{2,1,0:T(8,128)(2,1)S(1)}, u32[]{:S(2)}, u32[]{:S(2)}) collective-permute-start(bf16[2,384,384]{2,1,0:T(8,128)(2,1)S(1)} %get-tuple-element.52), channel_id=1, source_target_pairs={{0,32},{8,40},{16,48},{24,56},{32,0},{40,8},{48,16},{56,24},{64,96... | collective-permute-start | bytes 1769480 | tf_op jit(solution)/shard_map/ppermute | solution.py:475
  86.9 3.4 %collective-permute-start.16 = (bf16[2,384,384]{2,1,0:T(8,128)(2,1)S(1)}, bf16[2,384,384]{2,1,0:T(8,128)(2,1)S(1)}, u32[]{:S(2)}, u32[]{:S(2)}) collective-permute-start(bf16[2,384,384]{2,1,0:T(8,128)(2,1)S(1)} %get-tuple-element.59), channel_id=1, source_target_pairs={{0,64},{8,72},{16,80},{24,88},{32,96},{40,104},{48,112},{56,120},{... | collective-permute-start | bytes 1769480 | tf_op jit(solution)/shard_map/ppermute | solution.py:475
  90.4 0.0 collective-permute-start.17
  90.4 9.8 %grads_own.1 = (bf16[3,128,384]{2,1,0:T(8,128)(2,1)S(1)}, bf16[3,128,384]{2,1,0:T(8,128)(2,1)S(1)}, bf16[3,128,384]{2,1,0:T(8,128)(2,1)S(1)}, bf16[3,128,384]{2,1,0:T(8,128)(2,1)S(1)}, bf16[2,384,384]{2,1,0:T(8,128)(2,1)S(1)}) custom-call(s32[8]{0:T(128)S(1)} %copy-done.18, s32[8]{0:T(128)S(1)} %copy-done.19, s32[1]{0:T(128)} %bitcast.place_ref, ...), custom_call_target="tpu_custom_call" | custom-call | flops 1006632960 | bytes 8388608 | tf_op jit(solution)/shard_map/grads_own/pallas_call | solution.py:460
  100.2 0.0 collective-permute-done.12.refs_5_
  100.2 0.8 copy-done.6
  101.0 1.7 %collective-permute-start.13 = (bf16[3,128,384]{2,1,0:T(8,128)(2,1)S(1)}, bf16[3,128,384]{2,1,0:T(8,128)(2,1)S(1)}, u32[]{:S(2)}, u32[]{:S(2)}) collective-permute-start(bf16[3,128,384]{2,1,0:T(8,128)(2,1)S(1)} %get-tuple-element.54), channel_id=1, source_target_pairs={{0,8},{8,0},{16,24},{24,16},{32,40},{40,32},{48,56},{56,48},{64,72... | collective-permute-start | bytes 884744 | tf_op jit(solution)/shard_map/ppermute | solution.py:475
  102.7 0.0 collective-permute-start.14
  102.7 2.4 %collective-permute-start.15 = (bf16[3,128,384]{2,1,0:T(8,128)(2,1)S(1)}, bf16[3,128,384]{2,1,0:T(8,128)(2,1)S(1)}, u32[]{:S(2)}, u32[]{:S(2)}) collective-permute-start(bf16[3,128,384]{2,1,0:T(8,128)(2,1)S(1)} %get-tuple-element.56), channel_id=1, source_target_pairs={{0,24},{8,16},{16,8},{24,0},{32,56},{40,48},{48,40},{56,32},{64,88... | collective-permute-start | bytes 884744 | tf_op jit(solution)/shard_map/ppermute | solution.py:475
  105.1 6.9 %collective-permute-done.16.refs_6_ = bf16[2,384,384]{2,1,0:T(8,128)(2,1)S(1)} collective-permute-done((bf16[2,384,384]{2,1,0:T(8,128)(2,1)S(1)}, bf16[2,384,384]{2,1,0:T(8,128)(2,1)S(1)}, u32[]{:S(2)}, u32[]{:S(2)}) %collective-permute-start.16) | collective-permute-done | bytes 589856 | tf_op jit(solution)/shard_map/ppermute | solution.py:475
  112.1 0.8 copy-done.8
  112.9 0.0 collective-permute-done.17.refs_7_
  112.9 0.8 copy-done.10
  113.7 0.0 collective-permute-done.13.refs_1_
  113.7 0.7 copy-done.12
  114.4 0.0 collective-permute-done.14.refs_2_
  114.4 0.7 copy-done.14
  115.2 0.0 collective-permute-done.15.refs_3_
  115.2 0.7 copy-done.16
  115.9 1.1 copy-done.7
  117.0 1.1 copy-done.9
  118.0 1.1 copy-done.11
  119.1 1.0 copy-done.13
  120.1 1.0 copy-done.15
  121.0 1.0 copy-done.17
  122.0 1.4 sum_terms.1
  123.3 21.5 %all_to_all.10.in_ref = bf16[8,3,32,384]{3,2,1,0:T(8,128)(2,1)S(1)} all-to-all(bf16[8,3,32,384]{3,2,1,0:T(8,128)(2,1)} %get-tuple-element.61), channel_id=1, replica_groups=mesh['seq'=16,'head'=8] {'head'}, dimensions={0} | all-to-all | bytes 1179648 | tf_op jit(solution)/shard_map/all_to_all | solution.py:513
  144.8 0.9 unpack_video.1
  (29 shorter events, 0.1 us)
Async XLA Ops:
  0.6 49.2 %copy-start.19 = (s32[8]{0:T(128)S(1)}, s32[8]{0:T(128)}, u32[]{:S(2)}) copy-start(s32[8]{0:T(128)} %caption_ref.7) | copy-start | bytes 100
  0.6 49.2 %copy-start.18 = (s32[8]{0:T(128)S(1)}, s32[8]{0:T(128)}, u32[]{:S(2)}) copy-start(s32[8]{0:T(128)} %length_ref.7) | copy-start | bytes 100
  2.9 18.4 %all-to-all-start = ((bf16[8,4,32,384]{3,2,1,0:T(8,128)(2,1)}), bf16[8,4,32,384]{3,2,1,0:T(8,128)(2,1)S(1)}, u32[]{:S(2)}, u32[]{:S(2)}) async-start(bf16[8,4,32,384]{3,2,1,0:T(8,128)(2,1)} %get-tuple-element.37), calls=%async_computation | async-start | bytes 1572864 | tf_op jit(solution)/shard_map/all_to_all | solution.py:498
  8.7 12.3 %collective-permute-start.2 = (bf16[2,128,384]{2,1,0:T(8,128)(2,1)}, bf16[2,128,384]{2,1,0:T(8,128)(2,1)S(1)}, u32[]{:S(2)}, u32[]{:S(2)}) collective-permute-start(bf16[2,128,384]{2,1,0:T(8,128)(2,1)} %get-tuple-element.42.refs_6_.refs_7_.refs_11_), channel_id=1, source_target_pairs={{0,24},{8,16},{16,8},{24,0},{32,56},{40,48},{48,40},{56,32},{64,88... | collective-permute-start | bytes 589832 | tf_op jit(solution)/shard_map/ppermute | solution.py:475
  11.5 9.6 %collective-permute-start.1 = (bf16[2,128,384]{2,1,0:T(8,128)(2,1)}, bf16[2,128,384]{2,1,0:T(8,128)(2,1)S(1)}, u32[]{:S(2)}, u32[]{:S(2)}) collective-permute-start(bf16[2,128,384]{2,1,0:T(8,128)(2,1)} %get-tuple-element.42.refs_6_.refs_7_.refs_11_), channel_id=1, source_target_pairs={{0,16},{8,24},{16,0},{24,8},{32,48},{40,56},{48,32},{56,40},{64,80... | collective-permute-start | bytes 589832 | tf_op jit(solution)/shard_map/ppermute | solution.py:475
  11.8 9.5 %collective-permute-start = (bf16[2,128,384]{2,1,0:T(8,128)(2,1)}, bf16[2,128,384]{2,1,0:T(8,128)(2,1)S(1)}, u32[]{:S(2)}, u32[]{:S(2)}) collective-permute-start(bf16[2,128,384]{2,1,0:T(8,128)(2,1)} %get-tuple-element.42.refs_6_.refs_7_.refs_11_), channel_id=1, source_target_pairs={{0,8},{8,0},{16,24},{24,16},{32,40},{40,32},{48,56},{56,48},{64,72... | collective-permute-start | bytes 589832 | tf_op jit(solution)/shard_map/ppermute | solution.py:475
  21.0 28.8 %copy-start.20 = (bf16[2,128,384]{2,1,0:T(8,128)(2,1)}, bf16[2,128,384]{2,1,0:T(8,128)(2,1)S(1)}, u32[]{:S(2)}) copy-start(bf16[2,128,384]{2,1,0:T(8,128)(2,1)S(1)} %collective-permute-done.2.refs_9_.refs_10_.refs_14_) | copy-start | bytes 589828
  21.0 28.8 %copy-start.21 = (bf16[2,128,384]{2,1,0:T(8,128)(2,1)}, bf16[2,128,384]{2,1,0:T(8,128)(2,1)S(1)}, u32[]{:S(2)}) copy-start(bf16[2,128,384]{2,1,0:T(8,128)(2,1)S(1)} %collective-permute-done.1.refs_8_.refs_9_.refs_13_) | copy-start | bytes 589828
  21.3 28.5 %copy-start.22 = (bf16[2,128,384]{2,1,0:T(8,128)(2,1)}, bf16[2,128,384]{2,1,0:T(8,128)(2,1)S(1)}, u32[]{:S(2)}) copy-start(bf16[2,128,384]{2,1,0:T(8,128)(2,1)S(1)} %collective-permute-done.refs_7_.refs_8_.refs_12_) | copy-start | bytes 589828
  23.4 18.5 %collective-permute-start.5 = (bf16[2,256,384]{2,1,0:T(8,128)(2,1)}, bf16[2,256,384]{2,1,0:T(8,128)(2,1)S(1)}, u32[]{:S(2)}, u32[]{:S(2)}) collective-permute-start(bf16[2,256,384]{2,1,0:T(8,128)(2,1)} %get-tuple-element.40.refs_0_.refs_1_.refs_2_), channel_id=1, source_target_pairs={{0,24},{8,16},{16,8},{24,0},{32,56},{40,48},{48,40},{56,32},{64,88... | collective-permute-start | bytes 1179656 | tf_op jit(solution)/shard_map/ppermute | solution.py:475
  26.0 23.9 %collective-permute-start.6 = (bf16[2,384,384]{2,1,0:T(8,128)(2,1)}, bf16[2,384,384]{2,1,0:T(8,128)(2,1)S(1)}, u32[]{:S(2)}, u32[]{:S(2)}) collective-permute-start(bf16[2,384,384]{2,1,0:T(8,128)(2,1)} %get-tuple-element.41.refs_4_.refs_6_), channel_id=1, source_target_pairs={{0,32},{8,40},{16,48},{24,56},{32,0},{40,8},{48,16},{56,24},{64,96... | collective-permute-start | bytes 1769480 | tf_op jit(solution)/shard_map/ppermute | solution.py:475
  27.6 31.8 %collective-permute-start.8 = (bf16[2,384,384]{2,1,0:T(8,128)(2,1)}, bf16[2,384,384]{2,1,0:T(8,128)(2,1)S(1)}, u32[]{:S(2)}, u32[]{:S(2)}) collective-permute-start(bf16[2,384,384]{2,1,0:T(8,128)(2,1)} %get-tuple-element.41.refs_4_.refs_6_), channel_id=1, source_target_pairs={{0,96},{8,104},{16,112},{24,120},{32,64},{40,72},{48,80},{56,88},{... | collective-permute-start | bytes 1769480 | tf_op jit(solution)/shard_map/ppermute | solution.py:475
  29.9 29.6 %collective-permute-start.7 = (bf16[2,384,384]{2,1,0:T(8,128)(2,1)}, bf16[2,384,384]{2,1,0:T(8,128)(2,1)S(1)}, u32[]{:S(2)}, u32[]{:S(2)}) collective-permute-start(bf16[2,384,384]{2,1,0:T(8,128)(2,1)} %get-tuple-element.41.refs_4_.refs_6_), channel_id=1, source_target_pairs={{0,64},{8,72},{16,80},{24,88},{32,96},{40,104},{48,112},{56,120},{... | collective-permute-start | bytes 1769480 | tf_op jit(solution)/shard_map/ppermute | solution.py:475
  30.9 11.0 %collective-permute-start.4 = (bf16[2,256,384]{2,1,0:T(8,128)(2,1)}, bf16[2,256,384]{2,1,0:T(8,128)(2,1)S(1)}, u32[]{:S(2)}, u32[]{:S(2)}) collective-permute-start(bf16[2,256,384]{2,1,0:T(8,128)(2,1)} %get-tuple-element.40.refs_0_.refs_1_.refs_2_), channel_id=1, source_target_pairs={{0,16},{8,24},{16,0},{24,8},{32,48},{40,56},{48,32},{56,40},{64,80... | collective-permute-start | bytes 1179656 | tf_op jit(solution)/shard_map/ppermute | solution.py:475
  41.9 30.2 %copy-start.1 = (bf16[2,256,384]{2,1,0:T(8,128)(2,1)}, bf16[2,256,384]{2,1,0:T(8,128)(2,1)S(1)}, u32[]{:S(2)}) copy-start(bf16[2,256,384]{2,1,0:T(8,128)(2,1)S(1)} %collective-permute-done.5.refs_3_.refs_4_.refs_5_) | copy-start | bytes 1179652
  41.9 8.0 %collective-permute-start.3 = (bf16[2,256,384]{2,1,0:T(8,128)(2,1)}, bf16[2,256,384]{2,1,0:T(8,128)(2,1)S(1)}, u32[]{:S(2)}, u32[]{:S(2)}) collective-permute-start(bf16[2,256,384]{2,1,0:T(8,128)(2,1)} %get-tuple-element.40.refs_0_.refs_1_.refs_2_), channel_id=1, source_target_pairs={{0,8},{8,0},{16,24},{24,16},{32,40},{40,32},{48,56},{56,48},{64,72... | collective-permute-start | bytes 1179656 | tf_op jit(solution)/shard_map/ppermute | solution.py:475
  41.9 30.2 %copy-start.2 = (bf16[2,256,384]{2,1,0:T(8,128)(2,1)}, bf16[2,256,384]{2,1,0:T(8,128)(2,1)S(1)}, u32[]{:S(2)}) copy-start(bf16[2,256,384]{2,1,0:T(8,128)(2,1)S(1)} %collective-permute-done.4.refs_2_.refs_3_.refs_4_) | copy-start | bytes 1179652
  49.8 22.3 %copy-start.3 = (bf16[2,256,384]{2,1,0:T(8,128)(2,1)}, bf16[2,256,384]{2,1,0:T(8,128)(2,1)S(1)}, u32[]{:S(2)}) copy-start(bf16[2,256,384]{2,1,0:T(8,128)(2,1)S(1)} %collective-permute-done.3.refs_1_.refs_2_.refs_3_) | copy-start | bytes 1179652
  49.9 1.1 copy-start
  51.0 1.1 copy-start.4
  65.2 25.1 %copy-start.5 = (bf16[2,384,384]{2,1,0:T(8,128)(2,1)S(1)}, bf16[2,384,384]{2,1,0:T(8,128)(2,1)}, u32[]{:S(2)}) copy-start(bf16[2,384,384]{2,1,0:T(8,128)(2,1)} %get-tuple-element.41.refs_4_.refs_6_) | copy-start | bytes 1769476
  65.2 4.2 %collective-permute-start.11 = (f32[2,3,1536]{2,1,0:T(4,128)S(1)}, f32[2,3,1536]{2,1,0:T(4,128)S(1)}, u32[]{:S(2)}, u32[]{:S(2)}) collective-permute-start(f32[2,3,1536]{2,1,0:T(4,128)S(1)} %stats_last.1.refs_7_), channel_id=1, source_target_pairs={{0,24},{8,16},{16,8},{24,0},{32,56},{40,48},{48,40},{56,32},{64,88... | collective-permute-start | bytes 110600 | tf_op jit(solution)/shard_map/ppermute | solution.py:475
  67.7 4.4 %collective-permute-start.10 = (f32[2,3,1536]{2,1,0:T(4,128)S(1)}, f32[2,3,1536]{2,1,0:T(4,128)S(1)}, u32[]{:S(2)}, u32[]{:S(2)}) collective-permute-start(f32[2,3,1536]{2,1,0:T(4,128)S(1)} %stats_last.1.refs_7_), channel_id=1, source_target_pairs={{0,16},{8,24},{16,0},{24,8},{32,48},{40,56},{48,32},{56,40},{64,80... | collective-permute-start | bytes 110600 | tf_op jit(solution)/shard_map/ppermute | solution.py:475
  67.8 4.4 %collective-permute-start.9 = (f32[2,3,1536]{2,1,0:T(4,128)S(1)}, f32[2,3,1536]{2,1,0:T(4,128)S(1)}, u32[]{:S(2)}, u32[]{:S(2)}) collective-permute-start(f32[2,3,1536]{2,1,0:T(4,128)S(1)} %stats_last.1.refs_7_), channel_id=1, source_target_pairs={{0,8},{8,0},{16,24},{24,16},{32,40},{40,32},{48,56},{56,48},{64,72... | collective-permute-start | bytes 110600 | tf_op jit(solution)/shard_map/ppermute | solution.py:475
  85.2 15.0 %collective-permute-start.12 = (bf16[2,384,384]{2,1,0:T(8,128)(2,1)S(1)}, bf16[2,384,384]{2,1,0:T(8,128)(2,1)S(1)}, u32[]{:S(2)}, u32[]{:S(2)}) collective-permute-start(bf16[2,384,384]{2,1,0:T(8,128)(2,1)S(1)} %get-tuple-element.52), channel_id=1, source_target_pairs={{0,32},{8,40},{16,48},{24,56},{32,0},{40,8},{48,16},{56,24},{64,96... | collective-permute-start | bytes 1769480 | tf_op jit(solution)/shard_map/ppermute | solution.py:475
  86.9 25.1 %collective-permute-start.16 = (bf16[2,384,384]{2,1,0:T(8,128)(2,1)S(1)}, bf16[2,384,384]{2,1,0:T(8,128)(2,1)S(1)}, u32[]{:S(2)}, u32[]{:S(2)}) collective-permute-start(bf16[2,384,384]{2,1,0:T(8,128)(2,1)S(1)} %get-tuple-element.59), channel_id=1, source_target_pairs={{0,64},{8,72},{16,80},{24,88},{32,96},{40,104},{48,112},{56,120},{... | collective-permute-start | bytes 1769480 | tf_op jit(solution)/shard_map/ppermute | solution.py:475
  90.4 22.5 %collective-permute-start.17 = (bf16[2,384,384]{2,1,0:T(8,128)(2,1)S(1)}, bf16[2,384,384]{2,1,0:T(8,128)(2,1)S(1)}, u32[]{:S(2)}, u32[]{:S(2)}) collective-permute-start(bf16[2,384,384]{2,1,0:T(8,128)(2,1)S(1)} %get-tuple-element.60), channel_id=1, source_target_pairs={{0,96},{8,104},{16,112},{24,120},{32,64},{40,72},{48,80},{56,88},{... | collective-permute-start | bytes 1769480 | tf_op jit(solution)/shard_map/ppermute | solution.py:475
  100.2 0.8 copy-start.6
  101.0 12.7 %collective-permute-start.13 = (bf16[3,128,384]{2,1,0:T(8,128)(2,1)S(1)}, bf16[3,128,384]{2,1,0:T(8,128)(2,1)S(1)}, u32[]{:S(2)}, u32[]{:S(2)}) collective-permute-start(bf16[3,128,384]{2,1,0:T(8,128)(2,1)S(1)} %get-tuple-element.54), channel_id=1, source_target_pairs={{0,8},{8,0},{16,24},{24,16},{32,40},{40,32},{48,56},{56,48},{64,72... | collective-permute-start | bytes 884744 | tf_op jit(solution)/shard_map/ppermute | solution.py:475
  102.7 11.7 %collective-permute-start.14 = (bf16[3,128,384]{2,1,0:T(8,128)(2,1)S(1)}, bf16[3,128,384]{2,1,0:T(8,128)(2,1)S(1)}, u32[]{:S(2)}, u32[]{:S(2)}) collective-permute-start(bf16[3,128,384]{2,1,0:T(8,128)(2,1)S(1)} %get-tuple-element.55), channel_id=1, source_target_pairs={{0,16},{8,24},{16,0},{24,8},{32,48},{40,56},{48,32},{56,40},{64,80... | collective-permute-start | bytes 884744 | tf_op jit(solution)/shard_map/ppermute | solution.py:475
  102.7 12.4 %collective-permute-start.15 = (bf16[3,128,384]{2,1,0:T(8,128)(2,1)S(1)}, bf16[3,128,384]{2,1,0:T(8,128)(2,1)S(1)}, u32[]{:S(2)}, u32[]{:S(2)}) collective-permute-start(bf16[3,128,384]{2,1,0:T(8,128)(2,1)S(1)} %get-tuple-element.56), channel_id=1, source_target_pairs={{0,24},{8,16},{16,8},{24,0},{32,56},{40,48},{48,40},{56,32},{64,88... | collective-permute-start | bytes 884744 | tf_op jit(solution)/shard_map/ppermute | solution.py:475
  112.1 0.8 copy-start.8
  112.9 0.8 copy-start.10
  113.7 0.7 copy-start.12
  114.4 0.7 copy-start.14
  115.2 0.7 copy-start.16
  115.9 1.1 copy-start.7
  117.0 1.1 copy-start.9
  118.0 1.1 copy-start.11
  119.1 1.0 copy-start.13
  120.1 1.0 copy-start.15
  121.0 1.0 copy-start.17

commit v2 on v1

--- a/solution.py
+++ b/solution.py
@@ -64,6 +64,7 @@
     return pl.pallas_call(
         assemble_kernel,
         out_shape=(QUERY_MESSAGE, KEY_MESSAGE),
+        compiler_params=SMALL,
         name="assemble_blocks",
     )(*placed([arrived]), text_key, text_value)
 
@@ -78,7 +79,7 @@
 
 def unpack(arrived):
     shape = jax.ShapeDtypeStruct((OWN, GROUP * WIDTH), BF16)
-    return pl.pallas_call(unpack_kernel, out_shape=(shape, shape, shape), name="unpack_video")(*placed([arrived]))
+    return pl.pallas_call(unpack_kernel, out_shape=(shape, shape, shape), compiler_params=SMALL, name="unpack_video")(*placed([arrived]))
 
 
 def head_cols(h):
@@ -103,6 +104,7 @@
         sum_kernel,
         out_shape=[jax.ShapeDtypeStruct((GROUP, 3, OWN, WIDTH), BF16)]
         + [jax.ShapeDtypeStruct((HALF, WIDTH), BF16)] * 3,
+        compiler_params=SMALL,
         name="sum_terms",
     )(*placed([*dq, *dkv]))
 
@@ -166,37 +168,41 @@
     lax.fori_loop(0, count, lambda n, c: (step(n), c)[1], 0)
 
 
-def text_keys(labels, first, count, visit):
+def chosen(blocks, n):
+    return sum(jnp.where(n == m, block, 0) for m, block in enumerate(blocks))
+
+
+def text_keys(labels, blocks, visit):
     def step(n):
-        t, j = first + n // SIDE, n % SIDE
-        shot, base = labels.key_shot(t), labels.query_base(j)
+        t, j = n // SIDE, n % SIDE
+        shot, base = labels.key_shot(chosen(blocks, t)), labels.query_base(j)
         begin, end = labels.span(shot)
 
         @pl.when(jnp.logical_and(begin < base + BLOCK, end > base))
         def _():
             row = base + lax.broadcasted_iota(jnp.int32, (1, BLOCK), 1)
             same = jnp.logical_and(row >= begin, row < end)
-            visit(t - first, j, jnp.logical_and(labels.live(shot, labels.y % 2), same))
-
-    loop(count * SIDE, step)
-    if first == 0:
+            visit(t, j, jnp.logical_and(labels.live(shot, labels.y % 2), same))
+
+    loop(len(blocks) * SIDE, step)
+    if 0 in blocks:
         live = labels.live(labels.key_shot(0), labels.y % 2)
-        visit(0, SIDE, jnp.broadcast_to(live, (HALF, BLOCK)))
-
-
-def text_queries(labels, first, count, visit):
+        visit(blocks.index(0), SIDE, jnp.broadcast_to(live, (HALF, BLOCK)))
+
+
+def text_queries(labels, blocks, visit):
     def step(n):
-        i, p = first + n // 2, n % 2
-        base = labels.key_base(i)
+        i, p = n // 2, n % 2
+        base = labels.key_base(chosen(blocks, i))
         begin, end = labels.span(labels.query_shot(p))
 
         @pl.when(jnp.logical_and(begin < base + BLOCK, end > base))
         def _():
             row = base + lax.broadcasted_iota(jnp.int32, (BLOCK, 1), 0)
             same = jnp.logical_and(row >= begin, row < end)
-            visit(i - first, p, jnp.broadcast_to(same, (BLOCK, BLOCK)))
-
-    loop(2 * count, step)
+            visit(i, p, jnp.broadcast_to(same, (BLOCK, BLOCK)))
+
+    loop(2 * len(blocks), step)
 
 
 def head_ds(h):
@@ -211,14 +217,15 @@
     return slice(j * BLOCK, (j + 1) * BLOCK)
 
 
-def stats_kernel(first, length_ref, caption_ref, place_ref, *refs):
-    acc_in, refs = (refs[:1], refs[1:]) if first else ((), refs)
-    qg, kv, text_qg = refs[:SIDE], refs[SIDE : SIDE + 2], refs[SIDE + 2 : 2 * SIDE + 2]
-    out_ref, q_all, g_all, k_all, v_all, tk_all, tv_all, *scratch = refs[2 * SIDE + 2 :]
+def stats_kernel(blocks, last, length_ref, caption_ref, place_ref, *refs):
+    count = len(blocks)
+    acc_in, refs = (refs[:1], refs[1:]) if last else ((), refs)
+    qg, kv, text_qg = refs[:SIDE], refs[SIDE : SIDE + count], refs[SIDE + count : 2 * SIDE + count]
+    out_ref, q_all, g_all, k_all, v_all, tk_all, tv_all, *scratch = refs[2 * SIDE + count :]
     labels = Labels(length_ref, caption_ref, place_ref)
     stage_queries(labels, qg, text_qg, q_all, g_all)
     stage_keys(kv, k_all, v_all, tk_all, tv_all)
-    if first:
+    if last:
         acc = scratch[0]
         acc[...] = acc_in[0][...]
     else:
@@ -228,21 +235,21 @@
 
     def head(h):
         c, row = head_ds(h), pl.ds(h, 1)
-        keys = k_all[:, :, c].reshape(2 * BLOCK, HDIM)
-        values = v_all[:, :, c].reshape(2 * BLOCK, HDIM)
+        keys = k_all[:, :, c].reshape(count * BLOCK, HDIM)
+        values = v_all[:, :, c].reshape(count * BLOCK, HDIM)
         for j in range(SIDE):
             cols = query_cols(j)
             scores = dot_nt(keys, q_all[j, :, c])
             dprob = dot_nt(values, g_all[j, :, c])
             top = jnp.max(scores, axis=0, keepdims=True) * TO_LOG2
-            if first:
+            if last:
                 before = acc[0, row, cols]
                 top = jnp.maximum(before, top)
                 shrink = jnp.exp2(before - top)
             weight = jnp.exp2(scores * TO_LOG2 - top)
             total = jnp.sum(weight, axis=0, keepdims=True)
             weighted = jnp.sum(weight * dprob, axis=0, keepdims=True)
-            if first:
+            if last:
                 total += acc[1, row, cols] * shrink
                 weighted += acc[2, row, cols] * shrink
             acc[0, row, cols] = top
@@ -273,9 +280,9 @@
             for n in range(3):
                 acc[n, h : h + 1, cols] = results[h][n]
 
-    text_keys(labels, first, 2, lambda t, j, mask: visit(tk_all, tv_all, t, j, mask))
-    text_queries(labels, first, 2, lambda i, p, mask: visit(k_all, v_all, i, SIDE + p, mask))
-    if first:
+    text_keys(labels, blocks, lambda t, j, mask: visit(tk_all, tv_all, t, j, mask))
+    text_queries(labels, blocks, lambda i, p, mask: visit(k_all, v_all, i, SIDE + p, mask))
+    if last:
         total = acc[1]
         some = total > 0.0
         total = jnp.where(some, total, 1.0)
@@ -303,7 +310,8 @@
         norm[1, :, query_cols(j)] = delta
 
 
-def key_grads(labels, first, count, kv, dkv_out, norm, dq_t, scratch):
+def key_grads(labels, blocks, fresh, kv, dkv_out, norm, dq_t, scratch):
+    count = len(blocks)
     q_all, g_all, k_all, v_all, tk_all, tv_all, dk, dv, text_dk, text_dv, p_all, ds_all = scratch
     stage_keys(kv, k_all, v_all, tk_all, tv_all)
     text_dk[...] = jnp.zeros((count, HEADS_LOCAL, HALF, HDIM), F32)
@@ -324,7 +332,7 @@
             p_all[:, cols] = probs.astype(BF16)
             ds_all[:, cols] = dscore
             part = dot_nn(keys_t, dscore)
-            if first:
+            if fresh:
                 dq_t[h, :, cols] = part
             else:
                 dq_t[h, :, cols] += part
@@ -357,8 +365,8 @@
         dk[h, rows_ds(n)] += key_part
         dv[h, rows_ds(n)] += value_part
 
-    text_keys(labels, first, count, lambda t, j, mask: visit(tk_all, tv_all, t, j, mask, add_text))
-    text_queries(labels, first, count, lambda i, p, mask: visit(k_all, v_all, i, SIDE + p, mask, add_video))
+    text_keys(labels, blocks, lambda t, j, mask: visit(tk_all, tv_all, t, j, mask, add_text))
+    text_queries(labels, blocks, lambda i, p, mask: visit(k_all, v_all, i, SIDE + p, mask, add_video))
 
     for i in range(count):
         for h in range(HEADS_LOCAL):
@@ -369,25 +377,27 @@
             dkv_out[i][1, BLOCK:, c] = text_dv[i, h].astype(BF16)
 
 
-def others_kernel(length_ref, caption_ref, place_ref, *refs):
-    qg, kv, stats = refs[:SIDE], refs[SIDE : 2 * SIDE - 1], refs[2 * SIDE - 1 : 3 * SIDE - 1]
-    text_qg, refs = refs[3 * SIDE - 1 : 4 * SIDE - 1], refs[4 * SIDE - 1 :]
-    dkv_out, (dq_t, norm, *scratch) = refs[: SIDE - 1], refs[SIDE - 1 :]
+def grads_first_kernel(blocks, length_ref, caption_ref, place_ref, *refs):
+    count = len(blocks)
+    qg, kv, refs = refs[:SIDE], refs[SIDE : SIDE + count], refs[SIDE + count :]
+    stats, text_qg, refs = refs[:SIDE], refs[SIDE : 2 * SIDE], refs[2 * SIDE :]
+    dkv_out, (dq_t, norm, *scratch) = refs[:count], refs[count:]
     labels = Labels(length_ref, caption_ref, place_ref)
     stage_queries(labels, qg, text_qg, scratch[0], scratch[1])
     normalize(stats, norm)
     dq_t[:, :, VIDEO_ROWS:] = jnp.zeros((HEADS_LOCAL, HDIM, TEXT_ROWS), F32)
-    key_grads(labels, 1, SIDE - 1, kv, dkv_out, norm, dq_t, scratch)
-
-
-def own_kernel(length_ref, caption_ref, place_ref, *refs):
-    norm, dq_in, qg, kv = refs[0], refs[1], refs[2 : SIDE + 2], refs[SIDE + 2 : SIDE + 3]
-    text_qg, refs = refs[SIDE + 3 : 2 * SIDE + 3], refs[2 * SIDE + 3 :]
-    dq_out, dkv_out, (dq_t, *scratch) = refs[:SIDE], refs[SIDE : SIDE + 1], refs[SIDE + 1 :]
+    key_grads(labels, blocks, True, kv, dkv_out, norm, dq_t, scratch)
+
+
+def grads_last_kernel(blocks, length_ref, caption_ref, place_ref, *refs):
+    count = len(blocks)
+    norm, dq_in, qg, refs = refs[0], refs[1], refs[2 : SIDE + 2], refs[SIDE + 2 :]
+    kv, text_qg, refs = refs[:count], refs[count : SIDE + count], refs[SIDE + count :]
+    dq_out, dkv_out, (dq_t, *scratch) = refs[:SIDE], refs[SIDE : SIDE + count], refs[SIDE + count :]
     labels = Labels(length_ref, caption_ref, place_ref)
     stage_queries(labels, qg, text_qg, scratch[0], scratch[1])
     dq_t[...] = dq_in[...]
-    key_grads(labels, 0, 1, kv, dkv_out, norm, dq_t, scratch)
+    key_grads(labels, blocks, False, kv, dkv_out, norm, dq_t, scratch)
     for n in range(SIDE):
         dq_out[n][:, :, :BLOCK] = (dq_t[:, :, query_cols(n)] * SCALE).astype(BF16)
         dq_out[n][:, :, BLOCK:] = (dq_t[:, :, VIDEO_ROWS + n * HALF : VIDEO_ROWS + (n + 1) * HALF] * SCALE).astype(BF16)
@@ -396,6 +406,7 @@
 SMEM_SPEC = pl.BlockSpec(memory_space=pltpu.SMEM)
 VMEM_SPEC = pl.BlockSpec(memory_space=pltpu.VMEM)
 PARAMS = pltpu.CompilerParams(vmem_limit_bytes=VMEM_LIMIT)
+SMALL = pltpu.CompilerParams(vmem_limit_bytes=8 * 1024 * 1024)
 DQ_T = (HEADS_LOCAL, HDIM, ROWS)
 STATS = (3, HEADS_LOCAL, ROWS)
 QUERY_MESSAGE = jax.ShapeDtypeStruct((2, BLOCK, WIDTH), BF16)
@@ -428,46 +439,49 @@
     return pl.CostEstimate(flops=2 * HDIM * matmuls * pairs, bytes_accessed=8 * 1024 * 1024, transcendentals=pairs)
 
 
-def stats_call(first, scalars, acc, qg, kv, text_qg):
+def stats_call(blocks, scalars, acc, qg, kv, text_qg):
+    last = len(acc)
     return pl.pallas_call(
-        functools.partial(stats_kernel, first),
-        in_specs=[SMEM_SPEC] * 3 + [VMEM_SPEC] * (len(acc) + 2 * SIDE + 2),
+        functools.partial(stats_kernel, blocks, last),
+        in_specs=[SMEM_SPEC] * 3 + [VMEM_SPEC] * (last + 2 * SIDE + len(blocks)),
         out_specs=VMEM_SPEC,
-        out_shape=jax.ShapeDtypeStruct((2, HEADS_LOCAL, ROWS) if first else STATS, F32),
-        scratch_shapes=staged(2) + ([pltpu.VMEM(STATS, F32)] if first else []),
+        out_shape=jax.ShapeDtypeStruct((2, HEADS_LOCAL, ROWS) if last else STATS, F32),
+        scratch_shapes=staged(len(blocks)) + [pltpu.VMEM(STATS, F32)] * last,
         compiler_params=PARAMS,
-        cost_estimate=cost(2, 2),
-        name="stats_last" if first else "stats_first",
-    )(*scalars, *placed([*acc, *qg, *kv[first : first + 2]]), *placed(text_qg, pltpu.HBM))
-
-
-def others_call(scalars, qg, kv, text_qg, stats):
+        cost_estimate=cost(len(blocks), 2),
+        name="stats_last" if last else "stats_first",
+    )(*scalars, *placed([*acc, *qg, *[kv[i] for i in blocks]]), *placed(text_qg, pltpu.HBM))
+
+
+def grads_first_call(blocks, scalars, qg, kv, text_qg, stats):
+    count = len(blocks)
     *dkv, dq_t, norm = pl.pallas_call(
-        others_kernel,
-        in_specs=[SMEM_SPEC] * 3 + [VMEM_SPEC] * (4 * SIDE - 1),
-        out_specs=[VMEM_SPEC] * (SIDE + 1),
-        out_shape=[KEY_MESSAGE] * (SIDE - 1)
+        functools.partial(grads_first_kernel, blocks),
+        in_specs=[SMEM_SPEC] * 3 + [VMEM_SPEC] * (3 * SIDE + count),
+        out_specs=[VMEM_SPEC] * (count + 2),
+        out_shape=[KEY_MESSAGE] * count
         + [jax.ShapeDtypeStruct(DQ_T, F32), jax.ShapeDtypeStruct((2, HEADS_LOCAL, ROWS), F32)],
-        scratch_shapes=grads_scratch(SIDE - 1),
+        scratch_shapes=grads_scratch(count),
         compiler_params=PARAMS,
-        cost_estimate=cost(SIDE - 1, 5),
-        name="grads_others",
-    )(*scalars, *placed([*qg, *kv[1:], *stats]), *placed(text_qg, pltpu.HBM))
+        cost_estimate=cost(count, 5),
+        name="grads_first",
+    )(*scalars, *placed([*qg, *[kv[i] for i in blocks], *stats]), *placed(text_qg, pltpu.HBM))
     return dkv, dq_t, norm
 
 
-def own_call(scalars, qg, kv, text_qg, dq_t, norm):
-    *dq, dkv = pl.pallas_call(
-        own_kernel,
-        in_specs=[SMEM_SPEC] * 3 + [VMEM_SPEC] * (2 * SIDE + 3),
-        out_specs=[VMEM_SPEC] * (SIDE + 1),
-        out_shape=[jax.ShapeDtypeStruct((HEADS_LOCAL, HDIM, BLOCK + HALF), BF16)] * SIDE + [KEY_MESSAGE],
-        scratch_shapes=[pltpu.VMEM(DQ_T, F32)] + grads_scratch(1),
+def grads_last_call(blocks, scalars, qg, kv, text_qg, dq_t, norm):
+    count = len(blocks)
+    out = pl.pallas_call(
+        functools.partial(grads_last_kernel, blocks),
+        in_specs=[SMEM_SPEC] * 3 + [VMEM_SPEC] * (2 * SIDE + count + 2),
+        out_specs=[VMEM_SPEC] * (SIDE + count),
+        out_shape=[jax.ShapeDtypeStruct((HEADS_LOCAL, HDIM, BLOCK + HALF), BF16)] * SIDE + [KEY_MESSAGE] * count,
+        scratch_shapes=[pltpu.VMEM(DQ_T, F32)] + grads_scratch(count),
         compiler_params=PARAMS,
-        cost_estimate=cost(1, 5),
-        name="grads_own",
-    )(*scalars, *placed([norm]), dq_t, *placed(qg, pltpu.HBM), *placed(kv[:1]), *placed(text_qg, pltpu.HBM))
-    return dq, dkv
+        cost_estimate=cost(count, 5),
+        name="grads_last",
+    )(*scalars, *placed([norm]), dq_t, *placed(qg, pltpu.HBM), *placed([kv[i] for i in blocks]), *placed(text_qg, pltpu.HBM))
+    return out[:SIDE], out[SIDE:]
 
 
 def swap(array, axis, step):
@@ -498,17 +512,20 @@
     arrived = lax.all_to_all(packed, "head", split_axis=0, concat_axis=0)
     arrived, text_qg = lax.optimization_barrier((arrived, text_qg))
     qg, kv = assemble(arrived, text_key, text_value)
-    qg, kv = gathered(qg, "y"), gathered(kv, "z")
-
-    acc = stats_call(0, scalars, [], qg, kv, text_qg)
-    stats = gathered(stats_call(2, scalars, [acc], qg, kv, text_qg), "y")
-    dkv, dq_t, norm = others_call(scalars, qg, kv, text_qg, stats)
-    dq, dkv_own = own_call(scalars, qg, kv, text_qg, dq_t, norm)
-
-    first = swap(dkv[0], "z", 1)
-    dq, first = lax.optimization_barrier((dq, first))
-    dkv = [dkv_own, first, swap(dkv[1], "z", 2), swap(dkv[2], "z", 3)]
+    qg = gathered(qg, "y")
+    kv1, kv3 = swap(kv, "z", 1), swap(kv, "z", 3)
+    later, qg = lax.optimization_barrier((kv, qg))
+    kv = [kv, kv1, swap(later, "z", 2), kv3]
+
+    acc = stats_call((0, 1, 3), scalars, [], qg, kv, text_qg)
+    stats = gathered(stats_call((2,), scalars, [acc], qg, kv, text_qg), "y")
+    (dkv1, dkv3), dq_t, norm = grads_first_call((1, 3), scalars, qg, kv, text_qg, stats)
+    dq, (dkv2, dkv0) = grads_last_call((2, 0), scalars, qg, kv, text_qg, dq_t, norm)
+
+    dkv1, dkv3 = swap(dkv1, "z", 1), swap(dkv3, "z", 3)
+    dq, dkv1, dkv2 = lax.optimization_barrier((dq, dkv1, dkv2))
     dq = [dq[0]] + [swap(dq[step], "y", step) for step in range(1, SIDE)]
+    dkv = [dkv0, dkv1, swap(dkv2, "z", 2), dkv3]
     video, *text = sum_terms(dq, dkv)
     video_back = unpack(lax.all_to_all(video, "head", split_axis=0, concat_axis=0))
     return (*video_back, *text)

time: 147 us -> 132 us (0.90)
  local copies, waits for them, and re-layouts: 12.9 us -> 0.04 us
  blocking collectives: 21.5 us -> 17 us
  waiting for transfers between devices: 38.3 us -> 41.9 us
  Pallas kernels: 42.6 us -> 39.2 us
  starting transfers between devices: 29.6 us -> 32.9 us
    unnamed x46 -> x22, local copies, waits for them, and re-layouts: 12.9 us -> 0.04 us
    all_to_all x1, blocking collectives: 21.5 us -> 17 us  [on_device(): lax.all_to_all(video, 'head', split_axis=0, concat_axis=0)]
    ppermute x18, waiting for transfers between devices: 38.3 us -> 41.9 us  [swap(): lax.ppermute(array, 'seq', [(i, i ^ shift) for i in range(SIDE * SIDE)])]
    pallas_call x6, Pallas kernels: 38.9 us -> 35.5 us  [the longest x2 12.9 us: stats_call(): pl.pallas_call(functools.partial(stats_kernel, blocks, last), in_specs=[S...]
    ppermute x18, starting transfers between devices: 23.8 us -> 27.1 us  [swap(): lax.ppermute(array, 'seq', [(i, i ^ shift) for i in range(SIDE * SIDE)])]
  transfers between devices with their start and end apart: 19 -> 19, of which waited for: 7 -> 9; matrix products, arithmetic and copies ran while one was open for 0% -> 0% of each run, Pallas kernels for 12% -> 16%
where the time goes in v2:
time: 132 us
  waiting for transfers between devices  41.9 us (32%)
  Pallas kernels  39.2 us (30%)
  starting transfers between devices  32.9 us (25%)
  blocking collectives  17 us (13%)
    ppermute x18, waiting for transfers between devices, swap(): lax.ppermute(array, 'seq', [(i, i ^ shift) for i in range(SIDE * SIDE)])  41.9 us
    ppermute x18, starting transfers between devices, swap(): lax.ppermute(array, 'seq', [(i, i ^ shift) for i in range(SIDE * SIDE)])  27.1 us
    all_to_all x1, blocking collectives, on_device(): lax.all_to_all(video, 'head', split_axis=0, concat_axis=0)  17 us
    pallas_call x2, Pallas kernels, stats_call(): pl.pallas_call(functools.partial(stats_kernel, blocks, last), in_specs=[S...  12.9 us
    pallas_call x1, Pallas kernels, grads_last_call(): pl.pallas_call(functools.partial(grads_last_kernel, blocks), in_specs=[SM...  12 us
    pallas_call x1, Pallas kernels, grads_first_call(): pl.pallas_call(functools.partial(grads_first_kernel, blocks), in_specs=[S...  9.67 us
    all_to_all x1, starting transfers between devices, on_device(): arrived = lax.all_to_all(packed, 'head', split_axis=0, concat_axis=0)  5.8 us
  transfers between devices with their start and end apart: 19, of which 9 were waited for; matrix products, arithmetic and copies ran while one was open for 0% of the time, Pallas kernels for 16%

profile of v2, /device:TPU:1, one launch (start us, length us, event | category | flops | bytes accessed | tf_op | source)
XLA Modules:
  0.0 131.8 jit_solution(8639733889175705012)
XLA Ops:
  0.6 0.0 copy-start.5
  0.6 0.0 copy-start.4
  0.7 0.0 copy-start.7
  0.7 0.0 copy-start.6
  0.7 2.4 %pack_inputs.1 = (bf16[8,4,32,384]{3,2,1,0:T(8,128)(2,1)}, bf16[2,128,384]{2,1,0:T(8,128)(2,1)}) custom-call(bf16[32,3072]{1,0:T(8,128)(2,1)} %q_ref.1, bf16[32,3072]{1,0:T(8,128)(2,1)} %k_ref.1, bf16[32,3072]{1,0:T(8,128)(2,1)} %v_ref.1, bf16[32,3072]{1,0:T(8,128)(2,1)} %g_ref.1, bf16[128,384]{1,0:T(8,128)(2,1)} %tq_ref.1, bf16[128,384]{1,0:T(8,128)(2,1)} %tg_ref.1), custom_call_target="tpu_custom_call" | custom-call | tf_op jit(solution)/shard_map/pack_inputs/pallas_call | solution.py:52
  3.0 5.8 %all-to-all-start = ((bf16[8,4,32,384]{3,2,1,0:T(8,128)(2,1)}), bf16[8,4,32,384]{3,2,1,0:T(8,128)(2,1)S(1)}, u32[]{:S(2)}, u32[]{:S(2)}) async-start(bf16[8,4,32,384]{3,2,1,0:T(8,128)(2,1)} %get-tuple-element.43), calls=%async_computation | async-start | bytes 1572864 | tf_op jit(solution)/shard_map/all_to_all | solution.py:512
  8.8 2.7 %collective-permute-start.2 = (bf16[2,128,384]{2,1,0:T(8,128)(2,1)}, bf16[2,128,384]{2,1,0:T(8,128)(2,1)S(1)}, u32[]{:S(2)}, u32[]{:S(2)}) collective-permute-start(bf16[2,128,384]{2,1,0:T(8,128)(2,1)} %get-tuple-element.52.refs_7_.refs_6_.refs_10_.refs_8_), channel_id=1, source_target_pairs={{0,24},{8,16},{16,8},{24,0},{32,56},{40,48},{48,40},{56,32},{64,88... | collective-permute-start | bytes 589832 | tf_op jit(solution)/shard_map/ppermute | solution.py:489
  11.6 0.3 collective-permute-start.1
  11.9 0.2 collective-permute-start
  12.1 9.0 %collective-permute-done.2.refs_10_.refs_9_.refs_13_.refs_11_ = bf16[2,128,384]{2,1,0:T(8,128)(2,1)S(1)} collective-permute-done((bf16[2,128,384]{2,1,0:T(8,128)(2,1)}, bf16[2,128,384]{2,1,0:T(8,128)(2,1)S(1)}, u32[]{:S(2)}, u32[]{:S(2)}) %collective-permute-start.2) | collective-permute-done | bytes 196640 | tf_op jit(solution)/shard_map/ppermute | solution.py:489
  21.1 0.0 collective-permute-done.1.refs_9_.refs_8_.refs_12_.refs_10_
  21.1 0.3 collective-permute-done.refs_8_.refs_7_.refs_11_.refs_9_
  21.4 0.0 all-to-all-done.in_ref
  21.4 0.0 copy-done.5
  21.4 0.0 copy-done.4
  21.5 0.1 assemble_blocks.1
  21.5 0.0 copy-start
  21.6 2.7 %collective-permute-start.5 = (bf16[2,256,384]{2,1,0:T(8,128)(2,1)S(1)}, bf16[2,256,384]{2,1,0:T(8,128)(2,1)S(1)}, u32[]{:S(2)}, u32[]{:S(2)}) collective-permute-start(bf16[2,256,384]{2,1,0:T(8,128)(2,1)S(1)} %get-tuple-element.48.refs_0_.refs_1_.refs_2_), channel_id=1, source_target_pairs={{0,24},{8,16},{16,8},{24,0},{32,56},{40,48},{48,40},{56,32},{64,88... | collective-permute-start | bytes 1179656 | tf_op jit(solution)/shard_map/ppermute | solution.py:489
  24.2 0.4 collective-permute-start.4
  24.6 0.3 collective-permute-start.3
  24.9 3.8 %collective-permute-start.7 = (bf16[2,384,384]{2,1,0:T(8,128)(2,1)S(1)}, bf16[2,384,384]{2,1,0:T(8,128)(2,1)S(1)}, u32[]{:S(2)}, u32[]{:S(2)}) collective-permute-start(bf16[2,384,384]{2,1,0:T(8,128)(2,1)S(1)} %get-tuple-element.56.refs_4_.refs_7_), channel_id=1, source_target_pairs={{0,96},{8,104},{16,112},{24,120},{32,64},{40,72},{48,80},{56,88},{... | collective-permute-start | bytes 1769480 | tf_op jit(solution)/shard_map/ppermute | solution.py:489
  28.7 0.0 collective-permute-start.6
  28.7 12.4 %collective-permute-done.5.refs_3_.refs_4_.refs_5_ = bf16[2,256,384]{2,1,0:T(8,128)(2,1)S(1)} collective-permute-done((bf16[2,256,384]{2,1,0:T(8,128)(2,1)S(1)}, bf16[2,256,384]{2,1,0:T(8,128)(2,1)S(1)}, u32[]{:S(2)}, u32[]{:S(2)}) %collective-permute-start.5) | collective-permute-done | bytes 393248 | tf_op jit(solution)/shard_map/ppermute | solution.py:489
  41.0 0.0 collective-permute-done.4.refs_2_.refs_3_.refs_4_
  41.1 0.0 copy-done.9
  41.1 0.0 copy-done.10
  41.1 0.0 copy-start.2
  41.1 0.3 collective-permute-done.3.refs_1_.refs_2_.refs_3_
  41.4 3.5 %collective-permute-start.8 = (bf16[2,384,384]{2,1,0:T(8,128)(2,1)S(1)}, bf16[2,384,384]{2,1,0:T(8,128)(2,1)S(1)}, u32[]{:S(2)}, u32[]{:S(2)}) collective-permute-start(bf16[2,384,384]{2,1,0:T(8,128)(2,1)S(1)} %get-tuple-element.56.refs_4_.refs_7_), channel_id=1, source_target_pairs={{0,64},{8,72},{16,80},{24,88},{32,96},{40,104},{48,112},{56,120},{... | collective-permute-start | bytes 1769480 | tf_op jit(solution)/shard_map/ppermute | solution.py:489
  44.9 0.0 collective-permute-done.7.refs_6_.refs_5_
  44.9 0.0 collective-permute-done.6.refs_5_.refs_4_
  44.9 0.0 copy-done.8
  44.9 0.0 copy-done.7
  44.9 0.0 copy-done.6
  44.9 9.5 %stats_first.1.refs_0_ = f32[3,3,1536]{2,1,0:T(4,128)S(1)} custom-call(s32[8]{0:T(128)S(1)} %copy-done.6, s32[8]{0:T(128)S(1)} %copy-done.7, s32[1]{0:T(128)} %bitcast.place_ref, bf16[2,256,384]{2,1,0:T(8,128)(2,1)S(1)} %get-tuple-element.48.refs_0_.refs_1_.refs_2_, bf16[2,256,384]{2,1,0:T(8,128)(2,1)S(1)} %collective-permute-done.3.refs_1_.refs_2_.refs_3_, ...), custom_call_target="tpu_custom_call" | custom-call | flops 1207959552 | bytes 8388608 | tf_op jit(solution)/shard_map/stats_first/pallas_call | solution.py:444
  54.4 1.9 %collective-permute-done.8.refs_5_.refs_6_ = bf16[2,384,384]{2,1,0:T(8,128)(2,1)S(1)} collective-permute-done((bf16[2,384,384]{2,1,0:T(8,128)(2,1)S(1)}, bf16[2,384,384]{2,1,0:T(8,128)(2,1)S(1)}, u32[]{:S(2)}, u32[]{:S(2)}) %collective-permute-start.8) | collective-permute-done | bytes 589856 | tf_op jit(solution)/shard_map/ppermute | solution.py:489
  56.3 3.4 %stats_last.1.refs_6_ = f32[2,3,1536]{2,1,0:T(4,128)S(1)} custom-call(s32[8]{0:T(128)S(1)} %copy-done.6, s32[8]{0:T(128)S(1)} %copy-done.7, s32[1]{0:T(128)} %bitcast.place_ref, f32[3,3,1536]{2,1,0:T(4,128)S(1)} %stats_first.1.refs_0_, bf16[2,256,384]{2,1,0:T(8,128)(2,1)S(1)} %get-tuple-element.48.refs_0_.refs_1_.refs_2_, ...), custom_call_target="tpu_custom_call" | custom-call | flops 402653184 | bytes 8388608 | tf_op jit(solution)/shard_map/stats_last/pallas_call | solution.py:444
  59.7 4.1 %collective-permute-start.11 = (f32[2,3,1536]{2,1,0:T(4,128)S(1)}, f32[2,3,1536]{2,1,0:T(4,128)S(1)}, u32[]{:S(2)}, u32[]{:S(2)}) collective-permute-start(f32[2,3,1536]{2,1,0:T(4,128)S(1)} %stats_last.1.refs_6_), channel_id=1, source_target_pairs={{0,24},{8,16},{16,8},{24,0},{32,56},{40,48},{48,40},{56,32},{64,88... | collective-permute-start | bytes 110600 | tf_op jit(solution)/shard_map/ppermute | solution.py:489
  63.9 0.0 collective-permute-start.10
  63.9 0.7 collective-permute-start.9
  64.5 0.8 collective-permute-done.11.refs_9_
  65.3 3.0 %collective-permute-done.10.refs_8_ = f32[2,3,1536]{2,1,0:T(4,128)S(1)} collective-permute-done((f32[2,3,1536]{2,1,0:T(4,128)S(1)}, f32[2,3,1536]{2,1,0:T(4,128)S(1)}, u32[]{:S(2)}, u32[]{:S(2)}) %collective-permute-start.10) | collective-permute-done | bytes 36896 | tf_op jit(solution)/shard_map/ppermute | solution.py:489
  68.3 0.0 collective-permute-done.9.refs_7_
  68.3 0.0 copy-done
  68.3 0.0 copy-done.1
  68.3 0.0 copy-done.2
  68.3 0.0 copy-done.3
  68.3 9.7 %grads_first.1 = (bf16[2,384,384]{2,1,0:T(8,128)(2,1)S(1)}, bf16[2,384,384]{2,1,0:T(8,128)(2,1)S(1)}, f32[3,128,1536]{2,1,0:T(8,128)S(1)}, f32[2,3,1536]{2,1,0:T(4,128)S(1)}) custom-call(s32[8]{0:T(128)S(1)} %copy-done.6, s32[8]{0:T(128)S(1)} %copy-done.7, s32[1]{0:T(128)} %bitcast.place_ref, ...), custom_call_target="tpu_custom_call" | custom-call | flops 2013265920 | bytes 8388608 | tf_op jit(solution)/shard_map/grads_first/pallas_call | solution.py:458
  78.0 1.8 %collective-permute-start.12 = (bf16[2,384,384]{2,1,0:T(8,128)(2,1)S(1)}, bf16[2,384,384]{2,1,0:T(8,128)(2,1)S(1)}, u32[]{:S(2)}, u32[]{:S(2)}) collective-permute-start(bf16[2,384,384]{2,1,0:T(8,128)(2,1)S(1)} %get-tuple-element.63), channel_id=1, source_target_pairs={{0,32},{8,40},{16,48},{24,56},{32,0},{40,8},{48,16},{56,24},{64,96... | collective-permute-start | bytes 1769480 | tf_op jit(solution)/shard_map/ppermute | solution.py:489
  79.8 0.7 collective-permute-start.17
  80.5 12.0 %grads_last.1 = (bf16[3,128,384]{2,1,0:T(8,128)(2,1)S(1)}, bf16[3,128,384]{2,1,0:T(8,128)(2,1)S(1)}, bf16[3,128,384]{2,1,0:T(8,128)(2,1)S(1)}, bf16[3,128,384]{2...) custom-call(s32[8]{0:T(128)S(1)} %copy-done.6, s32[8]{0:T(128)S(1)} %copy-done.7, ...), custom_call_target="tpu_custom_call" | custom-call | flops 2013265920 | bytes 8388608 | tf_op jit(solution)/shard_map/grads_last/pallas_call | solution.py:474
  92.6 0.0 collective-permute-done.12.refs_5_
  92.6 0.1 collective-permute-start.16
  92.7 0.1 collective-permute-start.13
  92.8 5.6 %collective-permute-start.14 = (bf16[3,128,384]{2,1,0:T(8,128)(2,1)S(1)}, bf16[3,128,384]{2,1,0:T(8,128)(2,1)S(1)}, u32[]{:S(2)}, u32[]{:S(2)}) collective-permute-start(bf16[3,128,384]{2,1,0:T(8,128)(2,1)S(1)} %get-tuple-element.67), channel_id=1, source_target_pairs={{0,16},{8,24},{16,0},{24,8},{32,48},{40,56},{48,32},{56,40},{64,80... | collective-permute-start | bytes 884744 | tf_op jit(solution)/shard_map/ppermute | solution.py:489
  98.4 0.0 collective-permute-start.15
  98.4 0.0 collective-permute-done.17.refs_7_
  98.4 0.0 collective-permute-done.13.refs_1_
  98.4 9.1 %collective-permute-done.14.refs_2_ = bf16[3,128,384]{2,1,0:T(8,128)(2,1)S(1)} collective-permute-done((bf16[3,128,384]{2,1,0:T(8,128)(2,1)S(1)}, bf16[3,128,384]{2,1,0:T(8,128)(2,1)S(1)}, u32[]{:S(2)}, u32[]{:S(2)}) %collective-permute-start.14) | collective-permute-done | bytes 294944 | tf_op jit(solution)/shard_map/ppermute | solution.py:489
  107.5 5.2 %collective-permute-done.15.refs_3_ = bf16[3,128,384]{2,1,0:T(8,128)(2,1)S(1)} collective-permute-done((bf16[3,128,384]{2,1,0:T(8,128)(2,1)S(1)}, bf16[3,128,384]{2,1,0:T(8,128)(2,1)S(1)}, u32[]{:S(2)}, u32[]{:S(2)}) %collective-permute-start.15) | collective-permute-done | bytes 294944 | tf_op jit(solution)/shard_map/ppermute | solution.py:489
  112.7 0.0 collective-permute-done.16.refs_6_
  112.7 1.3 sum_terms.1
  113.9 17.0 %all_to_all.10.in_ref = bf16[8,3,32,384]{3,2,1,0:T(8,128)(2,1)S(1)} all-to-all(bf16[8,3,32,384]{3,2,1,0:T(8,128)(2,1)S(1)} %get-tuple-element.73), channel_id=1, replica_groups=mesh['seq'=16,'head'=8] {'head'}, dimensions={0} | all-to-all | bytes 1179648 | tf_op jit(solution)/shard_map/all_to_all | solution.py:530
  131.0 0.9 unpack_video.1
  (5 shorter events, 0.0 us)
Async XLA Ops:
  0.6 20.8 %copy-start.5 = (bf16[128,384]{1,0:T(8,128)(2,1)S(1)}, bf16[128,384]{1,0:T(8,128)(2,1)}, u32[]{:S(2)}) copy-start(bf16[128,384]{1,0:T(8,128)(2,1)} %tv_ref.1) | copy-start | bytes 294916
  0.6 20.8 %copy-start.4 = (bf16[128,384]{1,0:T(8,128)(2,1)S(1)}, bf16[128,384]{1,0:T(8,128)(2,1)}, u32[]{:S(2)}) copy-start(bf16[128,384]{1,0:T(8,128)(2,1)} %tk_ref.1) | copy-start | bytes 294916
  0.7 44.2 %copy-start.7 = (s32[8]{0:T(128)S(1)}, s32[8]{0:T(128)}, u32[]{:S(2)}) copy-start(s32[8]{0:T(128)} %caption_ref.7) | copy-start | bytes 100
  0.7 44.2 %copy-start.6 = (s32[8]{0:T(128)S(1)}, s32[8]{0:T(128)}, u32[]{:S(2)}) copy-start(s32[8]{0:T(128)} %length_ref.7) | copy-start | bytes 100
  3.0 18.4 %all-to-all-start = ((bf16[8,4,32,384]{3,2,1,0:T(8,128)(2,1)}), bf16[8,4,32,384]{3,2,1,0:T(8,128)(2,1)S(1)}, u32[]{:S(2)}, u32[]{:S(2)}) async-start(bf16[8,4,32,384]{3,2,1,0:T(8,128)(2,1)} %get-tuple-element.43), calls=%async_computation | async-start | bytes 1572864 | tf_op jit(solution)/shard_map/all_to_all | solution.py:512
  8.8 12.3 %collective-permute-start.2 = (bf16[2,128,384]{2,1,0:T(8,128)(2,1)}, bf16[2,128,384]{2,1,0:T(8,128)(2,1)S(1)}, u32[]{:S(2)}, u32[]{:S(2)}) collective-permute-start(bf16[2,128,384]{2,1,0:T(8,128)(2,1)} %get-tuple-element.52.refs_7_.refs_6_.refs_10_.refs_8_), channel_id=1, source_target_pairs={{0,24},{8,16},{16,8},{24,0},{32,56},{40,48},{48,40},{56,32},{64,88... | collective-permute-start | bytes 589832 | tf_op jit(solution)/shard_map/ppermute | solution.py:489
  11.6 9.6 %collective-permute-start.1 = (bf16[2,128,384]{2,1,0:T(8,128)(2,1)}, bf16[2,128,384]{2,1,0:T(8,128)(2,1)S(1)}, u32[]{:S(2)}, u32[]{:S(2)}) collective-permute-start(bf16[2,128,384]{2,1,0:T(8,128)(2,1)} %get-tuple-element.52.refs_7_.refs_6_.refs_10_.refs_8_), channel_id=1, source_target_pairs={{0,16},{8,24},{16,0},{24,8},{32,48},{40,56},{48,32},{56,40},{64,80... | collective-permute-start | bytes 589832 | tf_op jit(solution)/shard_map/ppermute | solution.py:489
  11.9 9.5 %collective-permute-start = (bf16[2,128,384]{2,1,0:T(8,128)(2,1)}, bf16[2,128,384]{2,1,0:T(8,128)(2,1)S(1)}, u32[]{:S(2)}, u32[]{:S(2)}) collective-permute-start(bf16[2,128,384]{2,1,0:T(8,128)(2,1)} %get-tuple-element.52.refs_7_.refs_6_.refs_10_.refs_8_), channel_id=1, source_target_pairs={{0,8},{8,0},{16,24},{24,16},{32,40},{40,32},{48,56},{56,48},{64,72... | collective-permute-start | bytes 589832 | tf_op jit(solution)/shard_map/ppermute | solution.py:489
  21.1 23.7 %copy-start.8 = (bf16[2,128,384]{2,1,0:T(8,128)(2,1)}, bf16[2,128,384]{2,1,0:T(8,128)(2,1)S(1)}, u32[]{:S(2)}) copy-start(bf16[2,128,384]{2,1,0:T(8,128)(2,1)S(1)} %collective-permute-done.2.refs_10_.refs_9_.refs_13_.refs_11_) | copy-start | bytes 589828
  21.1 19.9 %copy-start.9 = (bf16[2,128,384]{2,1,0:T(8,128)(2,1)}, bf16[2,128,384]{2,1,0:T(8,128)(2,1)S(1)}, u32[]{:S(2)}) copy-start(bf16[2,128,384]{2,1,0:T(8,128)(2,1)S(1)} %collective-permute-done.1.refs_9_.refs_8_.refs_12_.refs_10_) | copy-start | bytes 589828
  21.4 19.6 %copy-start.10 = (bf16[2,128,384]{2,1,0:T(8,128)(2,1)}, bf16[2,128,384]{2,1,0:T(8,128)(2,1)S(1)}, u32[]{:S(2)}) copy-start(bf16[2,128,384]{2,1,0:T(8,128)(2,1)S(1)} %collective-permute-done.refs_8_.refs_7_.refs_11_.refs_9_) | copy-start | bytes 589828
  21.5 46.8 %copy-start = (bf16[2,256,384]{2,1,0:T(8,128)(2,1)}, bf16[2,256,384]{2,1,0:T(8,128)(2,1)S(1)}, u32[]{:S(2)}) copy-start(bf16[2,256,384]{2,1,0:T(8,128)(2,1)S(1)} %get-tuple-element.48.refs_0_.refs_1_.refs_2_) | copy-start | bytes 1179652
  21.6 19.5 %collective-permute-start.5 = (bf16[2,256,384]{2,1,0:T(8,128)(2,1)S(1)}, bf16[2,256,384]{2,1,0:T(8,128)(2,1)S(1)}, u32[]{:S(2)}, u32[]{:S(2)}) collective-permute-start(bf16[2,256,384]{2,1,0:T(8,128)(2,1)S(1)} %get-tuple-element.48.refs_0_.refs_1_.refs_2_), channel_id=1, source_target_pairs={{0,24},{8,16},{16,8},{24,0},{32,56},{40,48},{48,40},{56,32},{64,88... | collective-permute-start | bytes 1179656 | tf_op jit(solution)/shard_map/ppermute | solution.py:489
  24.2 16.8 %collective-permute-start.4 = (bf16[2,256,384]{2,1,0:T(8,128)(2,1)S(1)}, bf16[2,256,384]{2,1,0:T(8,128)(2,1)S(1)}, u32[]{:S(2)}, u32[]{:S(2)}) collective-permute-start(bf16[2,256,384]{2,1,0:T(8,128)(2,1)S(1)} %get-tuple-element.48.refs_0_.refs_1_.refs_2_), channel_id=1, source_target_pairs={{0,16},{8,24},{16,0},{24,8},{32,48},{40,56},{48,32},{56,40},{64,80... | collective-permute-start | bytes 1179656 | tf_op jit(solution)/shard_map/ppermute | solution.py:489
  24.6 16.8 %collective-permute-start.3 = (bf16[2,256,384]{2,1,0:T(8,128)(2,1)S(1)}, bf16[2,256,384]{2,1,0:T(8,128)(2,1)S(1)}, u32[]{:S(2)}, u32[]{:S(2)}) collective-permute-start(bf16[2,256,384]{2,1,0:T(8,128)(2,1)S(1)} %get-tuple-element.48.refs_0_.refs_1_.refs_2_), channel_id=1, source_target_pairs={{0,8},{8,0},{16,24},{24,16},{32,40},{40,32},{48,56},{56,48},{64,72... | collective-permute-start | bytes 1179656 | tf_op jit(solution)/shard_map/ppermute | solution.py:489
  24.9 20.0 %collective-permute-start.7 = (bf16[2,384,384]{2,1,0:T(8,128)(2,1)S(1)}, bf16[2,384,384]{2,1,0:T(8,128)(2,1)S(1)}, u32[]{:S(2)}, u32[]{:S(2)}) collective-permute-start(bf16[2,384,384]{2,1,0:T(8,128)(2,1)S(1)} %get-tuple-element.56.refs_4_.refs_7_), channel_id=1, source_target_pairs={{0,96},{8,104},{16,112},{24,120},{32,64},{40,72},{48,80},{56,88},{... | collective-permute-start | bytes 1769480 | tf_op jit(solution)/shard_map/ppermute | solution.py:489
  28.7 16.2 %collective-permute-start.6 = (bf16[2,384,384]{2,1,0:T(8,128)(2,1)S(1)}, bf16[2,384,384]{2,1,0:T(8,128)(2,1)}, u32[]{:S(2)}, u32[]{:S(2)}) collective-permute-start(bf16[2,384,384]{2,1,0:T(8,128)(2,1)S(1)} %get-tuple-element.56.refs_4_.refs_7_), channel_id=1, source_target_pairs={{0,32},{8,40},{16,48},{24,56},{32,0},{40,8},{48,16},{56,24},{64,96... | collective-permute-start | bytes 1769480 | tf_op jit(solution)/shard_map/ppermute | solution.py:489
  41.0 27.3 %copy-start.1 = (bf16[2,256,384]{2,1,0:T(8,128)(2,1)}, bf16[2,256,384]{2,1,0:T(8,128)(2,1)S(1)}, u32[]{:S(2)}) copy-start(bf16[2,256,384]{2,1,0:T(8,128)(2,1)S(1)} %collective-permute-done.5.refs_3_.refs_4_.refs_5_) | copy-start | bytes 1179652
  41.1 27.3 %copy-start.2 = (bf16[2,256,384]{2,1,0:T(8,128)(2,1)}, bf16[2,256,384]{2,1,0:T(8,128)(2,1)S(1)}, u32[]{:S(2)}) copy-start(bf16[2,256,384]{2,1,0:T(8,128)(2,1)S(1)} %collective-permute-done.4.refs_2_.refs_3_.refs_4_) | copy-start | bytes 1179652
  41.4 27.0 %copy-start.3 = (bf16[2,256,384]{2,1,0:T(8,128)(2,1)}, bf16[2,256,384]{2,1,0:T(8,128)(2,1)S(1)}, u32[]{:S(2)}) copy-start(bf16[2,256,384]{2,1,0:T(8,128)(2,1)S(1)} %collective-permute-done.3.refs_1_.refs_2_.refs_3_) | copy-start | bytes 1179652
  41.4 15.0 %collective-permute-start.8 = (bf16[2,384,384]{2,1,0:T(8,128)(2,1)S(1)}, bf16[2,384,384]{2,1,0:T(8,128)(2,1)S(1)}, u32[]{:S(2)}, u32[]{:S(2)}) collective-permute-start(bf16[2,384,384]{2,1,0:T(8,128)(2,1)S(1)} %get-tuple-element.56.refs_4_.refs_7_), channel_id=1, source_target_pairs={{0,64},{8,72},{16,80},{24,88},{32,96},{40,104},{48,112},{56,120},{... | collective-permute-start | bytes 1769480 | tf_op jit(solution)/shard_map/ppermute | solution.py:489
  59.7 5.6 %collective-permute-start.11 = (f32[2,3,1536]{2,1,0:T(4,128)S(1)}, f32[2,3,1536]{2,1,0:T(4,128)S(1)}, u32[]{:S(2)}, u32[]{:S(2)}) collective-permute-start(f32[2,3,1536]{2,1,0:T(4,128)S(1)} %stats_last.1.refs_6_), channel_id=1, source_target_pairs={{0,24},{8,16},{16,8},{24,0},{32,56},{40,48},{48,40},{56,32},{64,88... | collective-permute-start | bytes 110600 | tf_op jit(solution)/shard_map/ppermute | solution.py:489
  63.9 4.4 %collective-permute-start.10 = (f32[2,3,1536]{2,1,0:T(4,128)S(1)}, f32[2,3,1536]{2,1,0:T(4,128)S(1)}, u32[]{:S(2)}, u32[]{:S(2)}) collective-permute-start(f32[2,3,1536]{2,1,0:T(4,128)S(1)} %stats_last.1.refs_6_), channel_id=1, source_target_pairs={{0,16},{8,24},{16,0},{24,8},{32,48},{40,56},{48,32},{56,40},{64,80... | collective-permute-start | bytes 110600 | tf_op jit(solution)/shard_map/ppermute | solution.py:489
  63.9 4.4 %collective-permute-start.9 = (f32[2,3,1536]{2,1,0:T(4,128)S(1)}, f32[2,3,1536]{2,1,0:T(4,128)S(1)}, u32[]{:S(2)}, u32[]{:S(2)}) collective-permute-start(f32[2,3,1536]{2,1,0:T(4,128)S(1)} %stats_last.1.refs_6_), channel_id=1, source_target_pairs={{0,8},{8,0},{16,24},{24,16},{32,40},{40,32},{48,56},{56,48},{64,72... | collective-permute-start | bytes 110600 | tf_op jit(solution)/shard_map/ppermute | solution.py:489
  78.0 14.6 %collective-permute-start.12 = (bf16[2,384,384]{2,1,0:T(8,128)(2,1)S(1)}, bf16[2,384,384]{2,1,0:T(8,128)(2,1)S(1)}, u32[]{:S(2)}, u32[]{:S(2)}) collective-permute-start(bf16[2,384,384]{2,1,0:T(8,128)(2,1)S(1)} %get-tuple-element.63), channel_id=1, source_target_pairs={{0,32},{8,40},{16,48},{24,56},{32,0},{40,8},{48,16},{56,24},{64,96... | collective-permute-start | bytes 1769480 | tf_op jit(solution)/shard_map/ppermute | solution.py:489
  79.8 18.6 %collective-permute-start.17 = (bf16[2,384,384]{2,1,0:T(8,128)(2,1)S(1)}, bf16[2,384,384]{2,1,0:T(8,128)(2,1)S(1)}, u32[]{:S(2)}, u32[]{:S(2)}) collective-permute-start(bf16[2,384,384]{2,1,0:T(8,128)(2,1)S(1)} %get-tuple-element.72), channel_id=1, source_target_pairs={{0,96},{8,104},{16,112},{24,120},{32,64},{40,72},{48,80},{56,88},{... | collective-permute-start | bytes 1769480 | tf_op jit(solution)/shard_map/ppermute | solution.py:489
  92.6 20.1 %collective-permute-start.16 = (bf16[2,384,384]{2,1,0:T(8,128)(2,1)S(1)}, bf16[2,384,384]{2,1,0:T(8,128)(2,1)S(1)}, u32[]{:S(2)}, u32[]{:S(2)}) collective-permute-start(bf16[2,384,384]{2,1,0:T(8,128)(2,1)S(1)} %get-tuple-element.71), channel_id=1, source_target_pairs={{0,64},{8,72},{16,80},{24,88},{32,96},{40,104},{48,112},{56,120},{... | collective-permute-start | bytes 1769480 | tf_op jit(solution)/shard_map/ppermute | solution.py:489
  92.7 5.7 %collective-permute-start.13 = (bf16[3,128,384]{2,1,0:T(8,128)(2,1)S(1)}, bf16[3,128,384]{2,1,0:T(8,128)(2,1)S(1)}, u32[]{:S(2)}, u32[]{:S(2)}) collective-permute-start(bf16[3,128,384]{2,1,0:T(8,128)(2,1)S(1)} %get-tuple-element.66), channel_id=1, source_target_pairs={{0,8},{8,0},{16,24},{24,16},{32,40},{40,32},{48,56},{56,48},{64,72... | collective-permute-start | bytes 884744 | tf_op jit(solution)/shard_map/ppermute | solution.py:489
  92.8 14.7 %collective-permute-start.14 = (bf16[3,128,384]{2,1,0:T(8,128)(2,1)S(1)}, bf16[3,128,384]{2,1,0:T(8,128)(2,1)S(1)}, u32[]{:S(2)}, u32[]{:S(2)}) collective-permute-start(bf16[3,128,384]{2,1,0:T(8,128)(2,1)S(1)} %get-tuple-element.67), channel_id=1, source_target_pairs={{0,16},{8,24},{16,0},{24,8},{32,48},{40,56},{48,32},{56,40},{64,80... | collective-permute-start | bytes 884744 | tf_op jit(solution)/shard_map/ppermute | solution.py:489
  98.4 14.3 %collective-permute-start.15 = (bf16[3,128,384]{2,1,0:T(8,128)(2,1)S(1)}, bf16[3,128,384]{2,1,0:T(8,128)(2,1)S(1)}, u32[]{:S(2)}, u32[]{:S(2)}) collective-permute-start(bf16[3,128,384]{2,1,0:T(8,128)(2,1)S(1)} %get-tuple-element.68), channel_id=1, source_target_pairs={{0,24},{8,16},{16,8},{24,0},{32,56},{40,48},{48,40},{56,32},{64,88... | collective-permute-start | bytes 884744 | tf_op jit(solution)/shard_map/ppermute | solution.py:489

commit v3 on v2

--- a/solution.py
+++ b/solution.py
@@ -49,7 +49,8 @@
 def pack(*arrays):
     video = jax.ShapeDtypeStruct((GROUP, 4, OWN, WIDTH), BF16)
     text = jax.ShapeDtypeStruct((2, HALF, WIDTH), BF16)
-    return pl.pallas_call(pack_kernel, out_shape=(video, text), name="pack_inputs")(*arrays)
+    call = pl.pallas_call(pack_kernel, out_shape=(video, text), compiler_params=SMALL, name="pack_inputs")
+    return call(*placed(arrays, pltpu.HBM))
 
 
 def assemble_kernel(in_ref, tk_ref, tv_ref, qg_ref, kv_ref):
@@ -218,16 +219,18 @@
 
 
 def stats_kernel(blocks, last, length_ref, caption_ref, place_ref, *refs):
-    count = len(blocks)
-    acc_in, refs = (refs[:1], refs[1:]) if last else ((), refs)
-    qg, kv, text_qg = refs[:SIDE], refs[SIDE : SIDE + count], refs[SIDE + count : 2 * SIDE + count]
-    out_ref, q_all, g_all, k_all, v_all, tk_all, tv_all, *scratch = refs[2 * SIDE + count :]
+    kv, refs = refs[: len(blocks)], refs[len(blocks) :]
     labels = Labels(length_ref, caption_ref, place_ref)
-    stage_queries(labels, qg, text_qg, q_all, g_all)
+    if last:
+        acc_in, q_all, g_all, out_ref, k_all, v_all, tk_all, tv_all, *scratch = refs
+    else:
+        qg, text_qg = refs[:SIDE], refs[SIDE : 2 * SIDE]
+        out_ref, q_all, g_all, k_all, v_all, tk_all, tv_all, *scratch = refs[2 * SIDE :]
+        stage_queries(labels, qg, text_qg, q_all, g_all)
     stage_keys(kv, k_all, v_all, tk_all, tv_all)
     if last:
         acc = scratch[0]
-        acc[...] = acc_in[0][...]
+        acc[...] = acc_in[...]
     else:
         acc = out_ref
         acc[0] = jnp.full((HEADS_LOCAL, ROWS), LOW, F32)
@@ -235,8 +238,8 @@
 
     def head(h):
         c, row = head_ds(h), pl.ds(h, 1)
-        keys = k_all[:, :, c].reshape(count * BLOCK, HDIM)
-        values = v_all[:, :, c].reshape(count * BLOCK, HDIM)
+        keys = k_all[:, :, c].reshape(len(blocks) * BLOCK, HDIM)
+        values = v_all[:, :, c].reshape(len(blocks) * BLOCK, HDIM)
         for j in range(SIDE):
             cols = query_cols(j)
             scores = dot_nt(keys, q_all[j, :, c])
@@ -310,9 +313,9 @@
         norm[1, :, query_cols(j)] = delta
 
 
-def key_grads(labels, blocks, fresh, kv, dkv_out, norm, dq_t, scratch):
+def key_grads(labels, blocks, fresh, q_all, g_all, kv, dkv_out, norm, dq_t, scratch):
     count = len(blocks)
-    q_all, g_all, k_all, v_all, tk_all, tv_all, dk, dv, text_dk, text_dv, p_all, ds_all = scratch
+    k_all, v_all, tk_all, tv_all, dk, dv, text_dk, text_dv, p_all, ds_all = scratch
     stage_keys(kv, k_all, v_all, tk_all, tv_all)
     text_dk[...] = jnp.zeros((count, HEADS_LOCAL, HALF, HDIM), F32)
     text_dv[...] = jnp.zeros((count, HEADS_LOCAL, HALF, HDIM), F32)
@@ -379,25 +382,21 @@
 
 def grads_first_kernel(blocks, length_ref, caption_ref, place_ref, *refs):
     count = len(blocks)
-    qg, kv, refs = refs[:SIDE], refs[SIDE : SIDE + count], refs[SIDE + count :]
-    stats, text_qg, refs = refs[:SIDE], refs[SIDE : 2 * SIDE], refs[2 * SIDE :]
-    dkv_out, (dq_t, norm, *scratch) = refs[:count], refs[count:]
+    q_all, g_all, kv, refs = refs[0], refs[1], refs[2 : 2 + count], refs[2 + count :]
+    stats, dkv_out, (dq_t, norm, *scratch) = refs[:SIDE], refs[SIDE : SIDE + count], refs[SIDE + count :]
     labels = Labels(length_ref, caption_ref, place_ref)
-    stage_queries(labels, qg, text_qg, scratch[0], scratch[1])
     normalize(stats, norm)
     dq_t[:, :, VIDEO_ROWS:] = jnp.zeros((HEADS_LOCAL, HDIM, TEXT_ROWS), F32)
-    key_grads(labels, blocks, True, kv, dkv_out, norm, dq_t, scratch)
+    key_grads(labels, blocks, True, q_all, g_all, kv, dkv_out, norm, dq_t, scratch)
 
 
 def grads_last_kernel(blocks, length_ref, caption_ref, place_ref, *refs):
     count = len(blocks)
-    norm, dq_in, qg, refs = refs[0], refs[1], refs[2 : SIDE + 2], refs[SIDE + 2 :]
-    kv, text_qg, refs = refs[:count], refs[count : SIDE + count], refs[SIDE + count :]
+    norm, dq_in, q_all, g_all, kv, refs = *refs[:4], refs[4 : 4 + count], refs[4 + count :]
     dq_out, dkv_out, (dq_t, *scratch) = refs[:SIDE], refs[SIDE : SIDE + count], refs[SIDE + count :]
     labels = Labels(length_ref, caption_ref, place_ref)
-    stage_queries(labels, qg, text_qg, scratch[0], scratch[1])
     dq_t[...] = dq_in[...]
-    key_grads(labels, blocks, False, kv, dkv_out, norm, dq_t, scratch)
+    key_grads(labels, blocks, False, q_all, g_all, kv, dkv_out, norm, dq_t, scratch)
     for n in range(SIDE):
         dq_out[n][:, :, :BLOCK] = (dq_t[:, :, query_cols(n)] * SCALE).astype(BF16)
         dq_out[n][:, :, BLOCK:] = (dq_t[:, :, VIDEO_ROWS + n * HALF : VIDEO_ROWS + (n + 1) * HALF] * SCALE).astype(BF16)
@@ -409,16 +408,13 @@
 SMALL = pltpu.CompilerParams(vmem_limit_bytes=8 * 1024 * 1024)
 DQ_T = (HEADS_LOCAL, HDIM, ROWS)
 STATS = (3, HEADS_LOCAL, ROWS)
+STAGED_QUERIES = jax.ShapeDtypeStruct((SIDE + 2, BLOCK, WIDTH), BF16)
 QUERY_MESSAGE = jax.ShapeDtypeStruct((2, BLOCK, WIDTH), BF16)
 KEY_MESSAGE = jax.ShapeDtypeStruct((2, BLOCK + HALF, WIDTH), BF16)
 
 
 def staged(count):
-    return (
-        [pltpu.VMEM((SIDE + 2, BLOCK, WIDTH), BF16)] * 2
-        + [pltpu.VMEM((count, BLOCK, WIDTH), BF16)] * 2
-        + [pltpu.VMEM((count, HALF, WIDTH), BF16)] * 2
-    )
+    return [pltpu.VMEM((count, BLOCK, WIDTH), BF16)] * 2 + [pltpu.VMEM((count, HALF, WIDTH), BF16)] * 2
 
 
 def grads_scratch(count):
@@ -439,25 +435,37 @@
     return pl.CostEstimate(flops=2 * HDIM * matmuls * pairs, bytes_accessed=8 * 1024 * 1024, transcendentals=pairs)
 
 
-def stats_call(blocks, scalars, acc, qg, kv, text_qg):
-    last = len(acc)
+def stats_first_call(blocks, scalars, qg, kv, text_qg):
     return pl.pallas_call(
-        functools.partial(stats_kernel, blocks, last),
-        in_specs=[SMEM_SPEC] * 3 + [VMEM_SPEC] * (last + 2 * SIDE + len(blocks)),
-        out_specs=VMEM_SPEC,
-        out_shape=jax.ShapeDtypeStruct((2, HEADS_LOCAL, ROWS) if last else STATS, F32),
-        scratch_shapes=staged(len(blocks)) + [pltpu.VMEM(STATS, F32)] * last,
+        functools.partial(stats_kernel, blocks, False),
+        in_specs=[SMEM_SPEC] * 3 + [VMEM_SPEC] * (2 * SIDE + len(blocks)),
+        out_specs=[VMEM_SPEC] * 3,
+        out_shape=[jax.ShapeDtypeStruct(STATS, F32), STAGED_QUERIES, STAGED_QUERIES],
+        scratch_shapes=staged(len(blocks)),
         compiler_params=PARAMS,
         cost_estimate=cost(len(blocks), 2),
-        name="stats_last" if last else "stats_first",
-    )(*scalars, *placed([*acc, *qg, *[kv[i] for i in blocks]]), *placed(text_qg, pltpu.HBM))
-
-
-def grads_first_call(blocks, scalars, qg, kv, text_qg, stats):
+        name="stats_first",
+    )(*scalars, *placed([kv[i] for i in blocks] + qg), *placed(text_qg, pltpu.HBM))
+
+
+def stats_last_call(blocks, scalars, acc, queries, kv):
+    return pl.pallas_call(
+        functools.partial(stats_kernel, blocks, True),
+        in_specs=[SMEM_SPEC] * 3 + [VMEM_SPEC] * (3 + len(blocks)),
+        out_specs=VMEM_SPEC,
+        out_shape=jax.ShapeDtypeStruct((2, HEADS_LOCAL, ROWS), F32),
+        scratch_shapes=staged(len(blocks)) + [pltpu.VMEM(STATS, F32)],
+        compiler_params=PARAMS,
+        cost_estimate=cost(len(blocks), 2),
+        name="stats_last",
+    )(*scalars, *placed([*[kv[i] for i in blocks], acc, *queries]))
+
+
+def grads_first_call(blocks, scalars, queries, kv, stats):
     count = len(blocks)
     *dkv, dq_t, norm = pl.pallas_call(
         functools.partial(grads_first_kernel, blocks),
-        in_specs=[SMEM_SPEC] * 3 + [VMEM_SPEC] * (3 * SIDE + count),
+        in_specs=[SMEM_SPEC] * 3 + [VMEM_SPEC] * (2 + SIDE + count),
         out_specs=[VMEM_SPEC] * (count + 2),
         out_shape=[KEY_MESSAGE] * count
         + [jax.ShapeDtypeStruct(DQ_T, F32), jax.ShapeDtypeStruct((2, HEADS_LOCAL, ROWS), F32)],
@@ -465,22 +473,22 @@
         compiler_params=PARAMS,
         cost_estimate=cost(count, 5),
         name="grads_first",
-    )(*scalars, *placed([*qg, *[kv[i] for i in blocks], *stats]), *placed(text_qg, pltpu.HBM))
+    )(*scalars, *placed([*queries, *[kv[i] for i in blocks], *stats]))
     return dkv, dq_t, norm
 
 
-def grads_last_call(blocks, scalars, qg, kv, text_qg, dq_t, norm):
+def grads_last_call(blocks, scalars, queries, kv, dq_t, norm):
     count = len(blocks)
     out = pl.pallas_call(
         functools.partial(grads_last_kernel, blocks),
-        in_specs=[SMEM_SPEC] * 3 + [VMEM_SPEC] * (2 * SIDE + count + 2),
+        in_specs=[SMEM_SPEC] * 3 + [VMEM_SPEC] * (4 + count),
         out_specs=[VMEM_SPEC] * (SIDE + count),
         out_shape=[jax.ShapeDtypeStruct((HEADS_LOCAL, HDIM, BLOCK + HALF), BF16)] * SIDE + [KEY_MESSAGE] * count,
         scratch_shapes=[pltpu.VMEM(DQ_T, F32)] + grads_scratch(count),
         compiler_params=PARAMS,
         cost_estimate=cost(count, 5),
         name="grads_last",
-    )(*scalars, *placed([norm]), dq_t, *placed(qg, pltpu.HBM), *placed([kv[i] for i in blocks]), *placed(text_qg, pltpu.HBM))
+    )(*scalars, *placed([norm]), dq_t, *placed([*queries, *[kv[i] for i in blocks]]))
     return out[:SIDE], out[SIDE:]
 
 
@@ -514,13 +522,13 @@
     qg, kv = assemble(arrived, text_key, text_value)
     qg = gathered(qg, "y")
     kv1, kv3 = swap(kv, "z", 1), swap(kv, "z", 3)
-    later, qg = lax.optimization_barrier((kv, qg))
+    later, qg[1], qg[3] = lax.optimization_barrier((kv, qg[1], qg[3]))
     kv = [kv, kv1, swap(later, "z", 2), kv3]
 
-    acc = stats_call((0, 1, 3), scalars, [], qg, kv, text_qg)
-    stats = gathered(stats_call((2,), scalars, [acc], qg, kv, text_qg), "y")
-    (dkv1, dkv3), dq_t, norm = grads_first_call((1, 3), scalars, qg, kv, text_qg, stats)
-    dq, (dkv2, dkv0) = grads_last_call((2, 0), scalars, qg, kv, text_qg, dq_t, norm)
+    acc, *queries = stats_first_call((0, 1, 3), scalars, qg, kv, text_qg)
+    stats = gathered(stats_last_call((2,), scalars, acc, queries, kv), "y")
+    (dkv1, dkv3), dq_t, norm = grads_first_call((1, 3), scalars, queries, kv, stats)
+    dq, (dkv2, dkv0) = grads_last_call((2, 0), scalars, queries, kv, dq_t, norm)
 
     dkv1, dkv3 = swap(dkv1, "z", 1), swap(dkv3, "z", 3)
     dq, dkv1, dkv2 = lax.optimization_barrier((dq, dkv1, dkv2))

time: 132 us -> 127 us (0.962)
  waiting for transfers between devices: 41.9 us -> 34.2 us
  blocking collectives: 17 us -> 21.2 us
  starting transfers between devices: 32.9 us -> 30.2 us
  local copies, waits for them, and re-layouts: 0.04 us -> 1.37 us
    ppermute x18, waiting for transfers between devices: 41.9 us -> 34.2 us  [swap(): lax.ppermute(array, 'seq', [(i, i ^ shift) for i in range(SIDE * SIDE)])]
    all_to_all x1, blocking collectives: 17 us -> 21.2 us  [on_device(): lax.all_to_all(video, 'head', split_axis=0, concat_axis=0)]
    ppermute x18, starting transfers between devices: 27.1 us -> 24.3 us  [swap(): lax.ppermute(array, 'seq', [(i, i ^ shift) for i in range(SIDE * SIDE)])]
    pallas_call x1, Pallas kernels: 9.67 us -> 8.01 us  [grads_first_call(): pl.pallas_call(functools.partial(grads_first_kernel, blocks), in_specs=[S...]
    unnamed x22 -> x14, local copies, waits for them, and re-layouts: 0.04 us -> 1.37 us
  transfers between devices with their start and end apart: 19 -> 19, of which waited for: 9 -> 9; matrix products, arithmetic and copies ran while one was open for 0% -> 0% of each run, Pallas kernels for 16% -> 18%
where the time goes in v3:
time: 127 us; the launch traced here: 126 us
  Pallas kernels  38.4 us (30%)
  waiting for transfers between devices  34.2 us (27%)
  starting transfers between devices  30.2 us (24%)
  blocking collectives  21.2 us (17%)
  local copies, waits for them, and re-layouts  1.37 us (1%)
    ppermute x18, waiting for transfers between devices, swap(): lax.ppermute(array, 'seq', [(i, i ^ shift) for i in range(SIDE * SIDE)])  34.2 us
    ppermute x18, starting transfers between devices, swap(): lax.ppermute(array, 'seq', [(i, i ^ shift) for i in range(SIDE * SIDE)])  24.3 us
    all_to_all x1, blocking collectives, on_device(): lax.all_to_all(video, 'head', split_axis=0, concat_axis=0)  21.2 us
    pallas_call x1, Pallas kernels, grads_last_call(): pl.pallas_call(functools.partial(grads_last_kernel, blocks), in_specs=[SM...  13.1 us
    pallas_call x1, Pallas kernels, stats_first_call(): pl.pallas_call(functools.partial(stats_kernel, blocks, False), in_specs=[...  9.74 us
    pallas_call x1, Pallas kernels, grads_first_call(): pl.pallas_call(functools.partial(grads_first_kernel, blocks), in_specs=[S...  8.01 us
    all_to_all x1, starting transfers between devices, on_device(): arrived = lax.all_to_all(packed, 'head', split_axis=0, concat_axis=0)  5.94 us
    pallas_call x1, Pallas kernels, stats_last_call(): pl.pallas_call(functools.partial(stats_kernel, blocks, True), in_specs=[S...  3.03 us
  transfers between devices with their start and end apart: 19, of which 9 were waited for; matrix products, arithmetic and copies ran while one was open for 0% of the time, Pallas kernels for 18%

profile of v3, /device:TPU:1, one launch (start us, length us, event | category | flops | bytes accessed | tf_op | source)
XLA Modules:
  0.0 126.2 jit_solution(2366589134473052098)
XLA Ops:
  0.6 0.0 copy-start.1
  0.6 0.0 copy-start
  0.7 2.3 %pack_inputs.1 = (bf16[8,4,32,384]{3,2,1,0:T(8,128)(2,1)}, bf16[2,128,384]{2,1,0:T(8,128)(2,1)S(1)}) custom-call(bf16[32,3072]{1,0:T(8,128)(2,1)} %q_ref.1, bf16[32,3072]{1,0:T(8,128)(2,1)} %k_ref.1, bf16[32,3072]{1,0:T(8,128)(2,1)} %v_ref.1, bf16[32,3072]{1,0:T(8,128)(2,1)} %g_ref.1, bf16[128,384]{1,0:T(8,128)(2,1)} %tq_ref.1, bf16[128,384]{1,0:T(8,128)(2,1)} %tg_ref.1), custom_call_target="tpu_custom_call" | custom-call | tf_op jit(solution)/shard_map/pack_inputs/pallas_call | solution.py:53
  2.9 0.0 copy-start.4
  2.9 0.0 copy-start.2
  2.9 0.0 copy-start.3
  2.9 5.9 %all-to-all-start = ((bf16[8,4,32,384]{3,2,1,0:T(8,128)(2,1)}), bf16[8,4,32,384]{3,2,1,0:T(8,128)(2,1)S(1)}, u32[]{:S(2)}, u32[]{:S(2)}) async-start(bf16[8,4,32,384]{3,2,1,0:T(8,128)(2,1)} %get-tuple-element.44), calls=%async_computation | async-start | bytes 1572864 | tf_op jit(solution)/shard_map/all_to_all | solution.py:520
  8.9 2.7 %collective-permute-start.2 = (bf16[2,128,384]{2,1,0:T(8,128)(2,1)S(1)}, bf16[2,128,384]{2,1,0:T(8,128)(2,1)S(1)}, u32[]{:S(2)}, u32[]{:S(2)}) collective-permute-start(bf16[2,128,384]{2,1,0:T(8,128)(2,1)S(1)} %get-tuple-element.51.refs_7_), channel_id=1, source_target_pairs={{0,24},{8,16},{16,8},{24,0},{32,56},{40,48},{48,40},{56,32},{64,88... | collective-permute-start | bytes 589832 | tf_op jit(solution)/shard_map/ppermute | solution.py:497
  11.6 0.3 collective-permute-start.1
  12.0 0.2 collective-permute-start
  12.2 8.8 %collective-permute-done.2.refs_10_ = bf16[2,128,384]{2,1,0:T(8,128)(2,1)S(1)} collective-permute-done((bf16[2,128,384]{2,1,0:T(8,128)(2,1)S(1)}, bf16[2,128,384]{2,1,0:T(8,128)(2,1)S(1)}, u32[]{:S(2)}, u32[]{:S(2)}) %collective-permute-start.2) | collective-permute-done | bytes 196640 | tf_op jit(solution)/shard_map/ppermute | solution.py:497
  21.0 0.0 copy-start.5
  21.0 0.0 collective-permute-done.1.refs_9_
  21.0 0.7 copy-done.5
  21.7 0.0 copy-start.6
  21.7 0.7 copy-done.6
  22.3 0.0 collective-permute-done.refs_8_
  22.3 0.0 copy-done.4
  22.3 0.0 all-to-all-done.in_ref
  22.3 0.0 copy-done.1
  22.4 0.0 copy-done
  22.4 0.1 assemble_blocks.1
  22.5 2.7 %collective-permute-start.6 = (bf16[2,256,384]{2,1,0:T(8,128)(2,1)S(1)}, bf16[2,256,384]{2,1,0:T(8,128)(2,1)S(1)}, u32[]{:S(2)}, u32[]{:S(2)}) collective-permute-start(bf16[2,256,384]{2,1,0:T(8,128)(2,1)S(1)} %get-tuple-element.48.refs_3_), channel_id=1, source_target_pairs={{0,24},{8,16},{16,8},{24,0},{32,56},{40,48},{48,40},{56,32},{64,88... | collective-permute-start | bytes 1179656 | tf_op jit(solution)/shard_map/ppermute | solution.py:497
  25.2 0.0 collective-permute-start.5
  25.2 3.8 %collective-permute-start.4 = (bf16[2,384,384]{2,1,0:T(8,128)(2,1)S(1)}, bf16[2,384,384]{2,1,0:T(8,128)(2,1)S(1)}, u32[]{:S(2)}, u32[]{:S(2)}) collective-permute-start(bf16[2,384,384]{2,1,0:T(8,128)(2,1)S(1)} %get-tuple-element.57.refs_0_.refs_5_), channel_id=1, source_target_pairs={{0,96},{8,104},{16,112},{24,120},{32,64},{40,72},{48,80},{56,88},{... | collective-permute-start | bytes 1769480 | tf_op jit(solution)/shard_map/ppermute | solution.py:497
  29.0 0.0 collective-permute-start.3
  29.0 4.7 %collective-permute-done.6.refs_6_ = bf16[2,256,384]{2,1,0:T(8,128)(2,1)S(1)} collective-permute-done((bf16[2,256,384]{2,1,0:T(8,128)(2,1)S(1)}, bf16[2,256,384]{2,1,0:T(8,128)(2,1)S(1)}, u32[]{:S(2)}, u32[]{:S(2)}) %collective-permute-start.6) | collective-permute-done | bytes 393248 | tf_op jit(solution)/shard_map/ppermute | solution.py:497
  33.7 1.1 collective-permute-done.5.refs_4_
  34.8 3.6 %collective-permute-start.8 = (bf16[2,384,384]{2,1,0:T(8,128)(2,1)S(1)}, bf16[2,384,384]{2,1,0:T(8,128)(2,1)S(1)}, u32[]{:S(2)}, u32[]{:S(2)}) collective-permute-start(bf16[2,384,384]{2,1,0:T(8,128)(2,1)S(1)} %get-tuple-element.57.refs_0_.refs_5_), channel_id=1, source_target_pairs={{0,64},{8,72},{16,80},{24,88},{32,96},{40,104},{48,112},{56,120},{... | collective-permute-start | bytes 1769480 | tf_op jit(solution)/shard_map/ppermute | solution.py:497
  38.4 0.0 collective-permute-start.7
  38.4 10.0 %collective-permute-done.7.refs_5_ = bf16[2,256,384]{2,1,0:T(8,128)(2,1)} collective-permute-done((bf16[2,256,384]{2,1,0:T(8,128)(2,1)S(1)}, bf16[2,256,384]{2,1,0:T(8,128)(2,1)}, u32[]{:S(2)}, u32[]{:S(2)}) %collective-permute-start.7) | collective-permute-done | bytes 393248 | tf_op jit(solution)/shard_map/ppermute | solution.py:497
  48.4 0.0 collective-permute-done.4.refs_2_.refs_3_
  48.4 0.0 collective-permute-done.3.refs_1_.refs_2_
  48.5 0.0 copy-done.2
  48.5 0.0 copy-done.3
  48.5 9.7 %stats_first.1 = (f32[3,3,1536]{2,1,0:T(4,128)S(1)}, bf16[6,256,384]{2,1,0:T(8,128)(2,1)S(1)}, bf16[6,256,384]{2,1,0:T(8,128)(2,1)S(1)}) custom-call(s32[8]{0:T(128)S(1)} %copy-done.2, s32[8]{0:T(128)S(1)} %copy-done.3, s32[1]{0:T(128)} %bitcast.place_ref, bf16[2,384,384]{2,1,0:T(8,128)(2,1)S(1)} %get-tuple-element.57.refs_0_.refs_5_, ...), custom_call_target="tpu_custom_call" | custom-call | flops 1207959552 | bytes 8388608 | tf_op jit(solution)/shard_map/stats_first/pallas_call | solution.py:439
  58.2 0.0 collective-permute-done.8.refs_0_.refs_4_
  58.2 3.0 %stats_last.1.refs_4_ = f32[2,3,1536]{2,1,0:T(4,128)S(1)} custom-call(s32[8]{0:T(128)S(1)} %copy-done.2, s32[8]{0:T(128)S(1)} %copy-done.3, s32[1]{0:T(128)} %bitcast.place_ref, bf16[2,384,384]{2,1,0:T(8,128)(2,1)S(1)} %collective-permute-done.8.refs_0_.refs_4_, f32[3,3,1536]{2,1,0:T(4,128)S(1)} %get-tuple-element.58.refs_1_, ...), custom_call_target="tpu_custom_call" | custom-call | flops 402653184 | bytes 8388608 | tf_op jit(solution)/shard_map/stats_last/pallas_call | solution.py:452
  61.3 0.1 collective-permute-start.11
  61.4 1.9 %collective-permute-start.10 = (f32[2,3,1536]{2,1,0:T(4,128)S(1)}, f32[2,3,1536]{2,1,0:T(4,128)S(1)}, u32[]{:S(2)}, u32[]{:S(2)}) collective-permute-start(f32[2,3,1536]{2,1,0:T(4,128)S(1)} %stats_last.1.refs_4_), channel_id=1, source_target_pairs={{0,16},{8,24},{16,0},{24,8},{32,48},{40,56},{48,32},{56,40},{64,80... | collective-permute-start | bytes 110600 | tf_op jit(solution)/shard_map/ppermute | solution.py:497
  63.3 1.3 %collective-permute-start.9 = (f32[2,3,1536]{2,1,0:T(4,128)S(1)}, f32[2,3,1536]{2,1,0:T(4,128)S(1)}, u32[]{:S(2)}, u32[]{:S(2)}) collective-permute-start(f32[2,3,1536]{2,1,0:T(4,128)S(1)} %stats_last.1.refs_4_), channel_id=1, source_target_pairs={{0,8},{8,0},{16,24},{24,16},{32,40},{40,32},{48,56},{56,48},{64,72... | collective-permute-start | bytes 110600 | tf_op jit(solution)/shard_map/ppermute | solution.py:497
  64.6 1.4 %collective-permute-done.11.refs_7_ = f32[2,3,1536]{2,1,0:T(4,128)S(1)} collective-permute-done((f32[2,3,1536]{2,1,0:T(4,128)S(1)}, f32[2,3,1536]{2,1,0:T(4,128)S(1)}, u32[]{:S(2)}, u32[]{:S(2)}) %collective-permute-start.11) | collective-permute-done | bytes 36896 | tf_op jit(solution)/shard_map/ppermute | solution.py:497
  66.0 0.0 collective-permute-done.10.refs_6_
  66.0 0.6 collective-permute-done.9.refs_5_
  66.6 8.0 %grads_first.1 = (bf16[2,384,384]{2,1,0:T(8,128)(2,1)S(1)}, bf16[2,384,384]{2,1,0:T(8,128)(2,1)S(1)}, f32[3,128,1536]{2,1,0:T(8,128)S(1)}, f32[2,3,1536]{2,1,0:T(4,128)S(1)}) custom-call(s32[8]{0:T(128)S(1)} %copy-done.2, s32[8]{0:T(128)S(1)} %copy-done.3, s32[1]{0:T(128)} %bitcast.place_ref, bf16[6,256,384]{2,1,0:T(8,128)(2,1)S(1)} %get-tuple-element.55.refs_2_.refs_0_, ...), custom_call_target="tpu_custom_call" | custom-call | flops 2013265920 | bytes 8388608 | tf_op jit(solution)/shard_map/grads_first/pallas_call | solution.py:466
  74.6 3.5 %collective-permute-start.12 = (bf16[2,384,384]{2,1,0:T(8,128)(2,1)S(1)}, bf16[2,384,384]{2,1,0:T(8,128)(2,1)S(1)}, u32[]{:S(2)}, u32[]{:S(2)}) collective-permute-start(bf16[2,384,384]{2,1,0:T(8,128)(2,1)S(1)} %get-tuple-element.65), channel_id=1, source_target_pairs={{0,32},{8,40},{16,48},{24,56},{32,0},{40,8},{48,16},{56,24},{64,96... | collective-permute-start | bytes 1769480 | tf_op jit(solution)/shard_map/ppermute | solution.py:497
  78.1 0.0 collective-permute-start.17
  78.1 13.1 %grads_last.1 = (bf16[3,128,384]{2,1,0:T(8,128)(2,1)S(1)}, bf16[3,128,384]{2,1,0:T(8,128)(2,1)S(1)}, bf16[3,128,384]{2,1,0:T(8,128)(2,1)S(1)}, bf16[3,128,384]{2...) custom-call(s32[8]{0:T(128)S(1)} %copy-done.2, s32[8]{0:T(128)S(1)} %copy-done.3, ...), custom_call_target="tpu_custom_call" | custom-call | flops 2013265920 | bytes 8388608 | tf_op jit(solution)/shard_map/grads_last/pallas_call | solution.py:482
  91.2 0.0 collective-permute-done.12.refs_5_
  91.2 0.1 collective-permute-start.16
  91.3 1.0 collective-permute-start.13
  92.4 0.2 collective-permute-start.14
  92.6 2.7 %collective-permute-start.15 = (bf16[3,128,384]{2,1,0:T(8,128)(2,1)S(1)}, bf16[3,128,384]{2,1,0:T(8,128)(2,1)S(1)}, u32[]{:S(2)}, u32[]{:S(2)}) collective-permute-start(bf16[3,128,384]{2,1,0:T(8,128)(2,1)S(1)} %get-tuple-element.70), channel_id=1, source_target_pairs={{0,24},{8,16},{16,8},{24,0},{32,56},{40,48},{48,40},{56,32},{64,88... | collective-permute-start | bytes 884744 | tf_op jit(solution)/shard_map/ppermute | solution.py:497
  95.3 0.0 collective-permute-done.17.refs_7_
  95.3 1.7 %collective-permute-done.13.refs_1_ = bf16[3,128,384]{2,1,0:T(8,128)(2,1)S(1)} collective-permute-done((bf16[3,128,384]{2,1,0:T(8,128)(2,1)S(1)}, bf16[3,128,384]{2,1,0:T(8,128)(2,1)S(1)}, u32[]{:S(2)}, u32[]{:S(2)}) %collective-permute-start.13) | collective-permute-done | bytes 294944 | tf_op jit(solution)/shard_map/ppermute | solution.py:497
  97.0 3.3 %collective-permute-done.14.refs_2_ = bf16[3,128,384]{2,1,0:T(8,128)(2,1)S(1)} collective-permute-done((bf16[3,128,384]{2,1,0:T(8,128)(2,1)S(1)}, bf16[3,128,384]{2,1,0:T(8,128)(2,1)S(1)}, u32[]{:S(2)}, u32[]{:S(2)}) %collective-permute-start.14) | collective-permute-done | bytes 294944 | tf_op jit(solution)/shard_map/ppermute | solution.py:497
  100.3 2.5 %collective-permute-done.15.refs_3_ = bf16[3,128,384]{2,1,0:T(8,128)(2,1)S(1)} collective-permute-done((bf16[3,128,384]{2,1,0:T(8,128)(2,1)S(1)}, bf16[3,128,384]{2,1,0:T(8,128)(2,1)S(1)}, u32[]{:S(2)}, u32[]{:S(2)}) %collective-permute-start.15) | collective-permute-done | bytes 294944 | tf_op jit(solution)/shard_map/ppermute | solution.py:497
  102.8 0.0 collective-permute-done.16.refs_6_
  102.9 1.2 sum_terms.1
  104.1 21.2 %all_to_all.10.in_ref = bf16[8,3,32,384]{3,2,1,0:T(8,128)(2,1)S(1)} all-to-all(bf16[8,3,32,384]{3,2,1,0:T(8,128)(2,1)S(1)} %get-tuple-element.75), channel_id=1, replica_groups=mesh['seq'=16,'head'=8] {'head'}, dimensions={0} | all-to-all | bytes 1179648 | tf_op jit(solution)/shard_map/all_to_all | solution.py:538
  125.3 0.9 unpack_video.1
Async XLA Ops:
  0.6 21.7 %copy-start.1 = (bf16[128,384]{1,0:T(8,128)(2,1)S(1)}, bf16[128,384]{1,0:T(8,128)(2,1)}, u32[]{:S(2)}) copy-start(bf16[128,384]{1,0:T(8,128)(2,1)} %tv_ref.1) | copy-start | bytes 294916
  0.6 21.7 %copy-start = (bf16[128,384]{1,0:T(8,128)(2,1)S(1)}, bf16[128,384]{1,0:T(8,128)(2,1)}, u32[]{:S(2)}) copy-start(bf16[128,384]{1,0:T(8,128)(2,1)} %tk_ref.1) | copy-start | bytes 294916
  2.9 19.4 %copy-start.4 = (bf16[2,128,384]{2,1,0:T(8,128)(2,1)}, bf16[2,128,384]{2,1,0:T(8,128)(2,1)S(1)}, u32[]{:S(2)}) copy-start(bf16[2,128,384]{2,1,0:T(8,128)(2,1)S(1)} %get-tuple-element.51.refs_7_) | copy-start | bytes 589828
  2.9 45.5 %copy-start.2 = (s32[8]{0:T(128)S(1)}, s32[8]{0:T(128)}, u32[]{:S(2)}) copy-start(s32[8]{0:T(128)} %length_ref.7) | copy-start | bytes 100
  2.9 45.5 %copy-start.3 = (s32[8]{0:T(128)S(1)}, s32[8]{0:T(128)}, u32[]{:S(2)}) copy-start(s32[8]{0:T(128)} %caption_ref.7) | copy-start | bytes 100
  2.9 19.4 %all-to-all-start = ((bf16[8,4,32,384]{3,2,1,0:T(8,128)(2,1)}), bf16[8,4,32,384]{3,2,1,0:T(8,128)(2,1)S(1)}, u32[]{:S(2)}, u32[]{:S(2)}) async-start(bf16[8,4,32,384]{3,2,1,0:T(8,128)(2,1)} %get-tuple-element.44), calls=%async_computation | async-start | bytes 1572864 | tf_op jit(solution)/shard_map/all_to_all | solution.py:520
  8.9 12.1 %collective-permute-start.2 = (bf16[2,128,384]{2,1,0:T(8,128)(2,1)S(1)}, bf16[2,128,384]{2,1,0:T(8,128)(2,1)S(1)}, u32[]{:S(2)}, u32[]{:S(2)}) collective-permute-start(bf16[2,128,384]{2,1,0:T(8,128)(2,1)S(1)} %get-tuple-element.51.refs_7_), channel_id=1, source_target_pairs={{0,24},{8,16},{16,8},{24,0},{32,56},{40,48},{48,40},{56,32},{64,88... | collective-permute-start | bytes 589832 | tf_op jit(solution)/shard_map/ppermute | solution.py:497
  11.6 9.4 %collective-permute-start.1 = (bf16[2,128,384]{2,1,0:T(8,128)(2,1)S(1)}, bf16[2,128,384]{2,1,0:T(8,128)(2,1)S(1)}, u32[]{:S(2)}, u32[]{:S(2)}) collective-permute-start(bf16[2,128,384]{2,1,0:T(8,128)(2,1)S(1)} %get-tuple-element.51.refs_7_), channel_id=1, source_target_pairs={{0,16},{8,24},{16,0},{24,8},{32,48},{40,56},{48,32},{56,40},{64,80... | collective-permute-start | bytes 589832 | tf_op jit(solution)/shard_map/ppermute | solution.py:497
  12.0 10.4 %collective-permute-start = (bf16[2,128,384]{2,1,0:T(8,128)(2,1)S(1)}, bf16[2,128,384]{2,1,0:T(8,128)(2,1)}, u32[]{:S(2)}, u32[]{:S(2)}) collective-permute-start(bf16[2,128,384]{2,1,0:T(8,128)(2,1)S(1)} %get-tuple-element.51.refs_7_), channel_id=1, source_target_pairs={{0,8},{8,0},{16,24},{24,16},{32,40},{40,32},{48,56},{56,48},{64,72... | collective-permute-start | bytes 589832 | tf_op jit(solution)/shard_map/ppermute | solution.py:497
  21.0 0.7 copy-start.5
  21.7 0.7 copy-start.6
  22.5 11.2 %collective-permute-start.6 = (bf16[2,256,384]{2,1,0:T(8,128)(2,1)S(1)}, bf16[2,256,384]{2,1,0:T(8,128)(2,1)S(1)}, u32[]{:S(2)}, u32[]{:S(2)}) collective-permute-start(bf16[2,256,384]{2,1,0:T(8,128)(2,1)S(1)} %get-tuple-element.48.refs_3_), channel_id=1, source_target_pairs={{0,24},{8,16},{16,8},{24,0},{32,56},{40,48},{48,40},{56,32},{64,88... | collective-permute-start | bytes 1179656 | tf_op jit(solution)/shard_map/ppermute | solution.py:497
  25.2 9.6 %collective-permute-start.5 = (bf16[2,256,384]{2,1,0:T(8,128)(2,1)S(1)}, bf16[2,256,384]{2,1,0:T(8,128)(2,1)S(1)}, u32[]{:S(2)}, u32[]{:S(2)}) collective-permute-start(bf16[2,256,384]{2,1,0:T(8,128)(2,1)S(1)} %get-tuple-element.48.refs_3_), channel_id=1, source_target_pairs={{0,8},{8,0},{16,24},{24,16},{32,40},{40,32},{48,56},{56,48},{64,72... | collective-permute-start | bytes 1179656 | tf_op jit(solution)/shard_map/ppermute | solution.py:497
  25.2 23.2 %collective-permute-start.4 = (bf16[2,384,384]{2,1,0:T(8,128)(2,1)S(1)}, bf16[2,384,384]{2,1,0:T(8,128)(2,1)S(1)}, u32[]{:S(2)}, u32[]{:S(2)}) collective-permute-start(bf16[2,384,384]{2,1,0:T(8,128)(2,1)S(1)} %get-tuple-element.57.refs_0_.refs_5_), channel_id=1, source_target_pairs={{0,96},{8,104},{16,112},{24,120},{32,64},{40,72},{48,80},{56,88},{... | collective-permute-start | bytes 1769480 | tf_op jit(solution)/shard_map/ppermute | solution.py:497
  29.0 19.5 %collective-permute-start.3 = (bf16[2,384,384]{2,1,0:T(8,128)(2,1)S(1)}, bf16[2,384,384]{2,1,0:T(8,128)(2,1)S(1)}, u32[]{:S(2)}, u32[]{:S(2)}) collective-permute-start(bf16[2,384,384]{2,1,0:T(8,128)(2,1)S(1)} %get-tuple-element.57.refs_0_.refs_5_), channel_id=1, source_target_pairs={{0,32},{8,40},{16,48},{24,56},{32,0},{40,8},{48,16},{56,24},{64,96... | collective-permute-start | bytes 1769480 | tf_op jit(solution)/shard_map/ppermute | solution.py:497
  34.8 23.4 %collective-permute-start.8 = (bf16[2,384,384]{2,1,0:T(8,128)(2,1)S(1)}, bf16[2,384,384]{2,1,0:T(8,128)(2,1)S(1)}, u32[]{:S(2)}, u32[]{:S(2)}) collective-permute-start(bf16[2,384,384]{2,1,0:T(8,128)(2,1)S(1)} %get-tuple-element.57.refs_0_.refs_5_), channel_id=1, source_target_pairs={{0,64},{8,72},{16,80},{24,88},{32,96},{40,104},{48,112},{56,120},{... | collective-permute-start | bytes 1769480 | tf_op jit(solution)/shard_map/ppermute | solution.py:497
  38.4 10.0 %collective-permute-start.7 = (bf16[2,256,384]{2,1,0:T(8,128)(2,1)S(1)}, bf16[2,256,384]{2,1,0:T(8,128)(2,1)}, u32[]{:S(2)}, u32[]{:S(2)}) collective-permute-start(bf16[2,256,384]{2,1,0:T(8,128)(2,1)S(1)} %get-tuple-element.48.refs_3_), channel_id=1, source_target_pairs={{0,16},{8,24},{16,0},{24,8},{32,48},{40,56},{48,32},{56,40},{64,80... | collective-permute-start | bytes 1179656 | tf_op jit(solution)/shard_map/ppermute | solution.py:497
  61.3 4.8 %collective-permute-start.11 = (f32[2,3,1536]{2,1,0:T(4,128)S(1)}, f32[2,3,1536]{2,1,0:T(4,128)S(1)}, u32[]{:S(2)}, u32[]{:S(2)}) collective-permute-start(f32[2,3,1536]{2,1,0:T(4,128)S(1)} %stats_last.1.refs_4_), channel_id=1, source_target_pairs={{0,24},{8,16},{16,8},{24,0},{32,56},{40,48},{48,40},{56,32},{64,88... | collective-permute-start | bytes 110600 | tf_op jit(solution)/shard_map/ppermute | solution.py:497
  61.4 4.7 %collective-permute-start.10 = (f32[2,3,1536]{2,1,0:T(4,128)S(1)}, f32[2,3,1536]{2,1,0:T(4,128)S(1)}, u32[]{:S(2)}, u32[]{:S(2)}) collective-permute-start(f32[2,3,1536]{2,1,0:T(4,128)S(1)} %stats_last.1.refs_4_), channel_id=1, source_target_pairs={{0,16},{8,24},{16,0},{24,8},{32,48},{40,56},{48,32},{56,40},{64,80... | collective-permute-start | bytes 110600 | tf_op jit(solution)/shard_map/ppermute | solution.py:497
  63.3 3.3 %collective-permute-start.9 = (f32[2,3,1536]{2,1,0:T(4,128)S(1)}, f32[2,3,1536]{2,1,0:T(4,128)S(1)}, u32[]{:S(2)}, u32[]{:S(2)}) collective-permute-start(f32[2,3,1536]{2,1,0:T(4,128)S(1)} %stats_last.1.refs_4_), channel_id=1, source_target_pairs={{0,8},{8,0},{16,24},{24,16},{32,40},{40,32},{48,56},{56,48},{64,72... | collective-permute-start | bytes 110600 | tf_op jit(solution)/shard_map/ppermute | solution.py:497
  74.6 16.6 %collective-permute-start.12 = (bf16[2,384,384]{2,1,0:T(8,128)(2,1)S(1)}, bf16[2,384,384]{2,1,0:T(8,128)(2,1)S(1)}, u32[]{:S(2)}, u32[]{:S(2)}) collective-permute-start(bf16[2,384,384]{2,1,0:T(8,128)(2,1)S(1)} %get-tuple-element.65), channel_id=1, source_target_pairs={{0,32},{8,40},{16,48},{24,56},{32,0},{40,8},{48,16},{56,24},{64,96... | collective-permute-start | bytes 1769480 | tf_op jit(solution)/shard_map/ppermute | solution.py:497
  78.1 17.2 %collective-permute-start.17 = (bf16[2,384,384]{2,1,0:T(8,128)(2,1)S(1)}, bf16[2,384,384]{2,1,0:T(8,128)(2,1)S(1)}, u32[]{:S(2)}, u32[]{:S(2)}) collective-permute-start(bf16[2,384,384]{2,1,0:T(8,128)(2,1)S(1)} %get-tuple-element.74), channel_id=1, source_target_pairs={{0,96},{8,104},{16,112},{24,120},{32,64},{40,72},{48,80},{56,88},{... | collective-permute-start | bytes 1769480 | tf_op jit(solution)/shard_map/ppermute | solution.py:497
  91.2 11.6 %collective-permute-start.16 = (bf16[2,384,384]{2,1,0:T(8,128)(2,1)S(1)}, bf16[2,384,384]{2,1,0:T(8,128)(2,1)S(1)}, u32[]{:S(2)}, u32[]{:S(2)}) collective-permute-start(bf16[2,384,384]{2,1,0:T(8,128)(2,1)S(1)} %get-tuple-element.73), channel_id=1, source_target_pairs={{0,64},{8,72},{16,80},{24,88},{32,96},{40,104},{48,112},{56,120},{... | collective-permute-start | bytes 1769480 | tf_op jit(solution)/shard_map/ppermute | solution.py:497
  91.3 5.7 %collective-permute-start.13 = (bf16[3,128,384]{2,1,0:T(8,128)(2,1)S(1)}, bf16[3,128,384]{2,1,0:T(8,128)(2,1)S(1)}, u32[]{:S(2)}, u32[]{:S(2)}) collective-permute-start(bf16[3,128,384]{2,1,0:T(8,128)(2,1)S(1)} %get-tuple-element.68), channel_id=1, source_target_pairs={{0,8},{8,0},{16,24},{24,16},{32,40},{40,32},{48,56},{56,48},{64,72... | collective-permute-start | bytes 884744 | tf_op jit(solution)/shard_map/ppermute | solution.py:497
  92.4 7.9 %collective-permute-start.14 = (bf16[3,128,384]{2,1,0:T(8,128)(2,1)S(1)}, bf16[3,128,384]{2,1,0:T(8,128)(2,1)S(1)}, u32[]{:S(2)}, u32[]{:S(2)}) collective-permute-start(bf16[3,128,384]{2,1,0:T(8,128)(2,1)S(1)} %get-tuple-element.69), channel_id=1, source_target_pairs={{0,16},{8,24},{16,0},{24,8},{32,48},{40,56},{48,32},{56,40},{64,80... | collective-permute-start | bytes 884744 | tf_op jit(solution)/shard_map/ppermute | solution.py:497
  92.6 10.3 %collective-permute-start.15 = (bf16[3,128,384]{2,1,0:T(8,128)(2,1)S(1)}, bf16[3,128,384]{2,1,0:T(8,128)(2,1)S(1)}, u32[]{:S(2)}, u32[]{:S(2)}) collective-permute-start(bf16[3,128,384]{2,1,0:T(8,128)(2,1)S(1)} %get-tuple-element.70), channel_id=1, source_target_pairs={{0,24},{8,16},{16,8},{24,0},{32,56},{40,48},{48,40},{56,32},{64,88... | collective-permute-start | bytes 884744 | tf_op jit(solution)/shard_map/ppermute | solution.py:497

commit v4 on v3

--- a/solution.py
+++ b/solution.py
@@ -26,7 +26,7 @@
 LOW = -1e30
 F32 = jnp.float32
 BF16 = jnp.bfloat16
-VMEM_LIMIT = 24 * 1024 * 1024
+VMEM_LIMIT = 16 * 1024 * 1024
 
 
 def dot_nt(a, b):
@@ -146,10 +146,7 @@
         return row < self.caption_ref[shot]
 
 
-def stage_queries(labels, qg, text_qg, q_all, g_all):
-    for j in range(SIDE):
-        q_all[j] = qg[j][0]
-        g_all[j] = qg[j][1]
+def stage_text_queries(labels, text_qg, q_all, g_all):
     for u in range(SIDE):
         p, rows = u // 2, slice(u % 2 * HALF, (u % 2 + 1) * HALF)
         q_all[SIDE + p, rows] = text_qg[u][0]
@@ -157,12 +154,12 @@
         g_all[SIDE + p, rows] = jnp.where(live, text_qg[u][1], jnp.zeros((HALF, WIDTH), BF16))
 
 
-def stage_keys(kv, k_all, v_all, tk_all, tv_all):
-    for i, ref in enumerate(kv):
-        k_all[i] = ref[0, :BLOCK]
-        v_all[i] = ref[1, :BLOCK]
-        tk_all[i] = ref[0, BLOCK:]
-        tv_all[i] = ref[1, BLOCK:]
+VIDEO_PART = slice(0, BLOCK)
+TEXT_PART = slice(BLOCK, BLOCK + HALF)
+
+
+def joined(kv, which, c):
+    return jnp.concatenate([ref[which, VIDEO_PART, c] for ref in kv], 0)
 
 
 def loop(count, step):
@@ -173,37 +170,43 @@
     return sum(jnp.where(n == m, block, 0) for m, block in enumerate(blocks))
 
 
-def text_keys(labels, blocks, visit):
-    def step(n):
-        t, j = n // SIDE, n % SIDE
-        shot, base = labels.key_shot(chosen(blocks, t)), labels.query_base(j)
+def text_keys(labels, blocks, queries, visit):
+    for n, block in enumerate(blocks):
+        shot = labels.key_shot(block)
         begin, end = labels.span(shot)
 
-        @pl.when(jnp.logical_and(begin < base + BLOCK, end > base))
-        def _():
-            row = base + lax.broadcasted_iota(jnp.int32, (1, BLOCK), 1)
-            same = jnp.logical_and(row >= begin, row < end)
-            visit(t, j, jnp.logical_and(labels.live(shot, labels.y % 2), same))
-
-    loop(len(blocks) * SIDE, step)
-    if 0 in blocks:
-        live = labels.live(labels.key_shot(0), labels.y % 2)
-        visit(blocks.index(0), SIDE, jnp.broadcast_to(live, (HALF, BLOCK)))
+        def step(m, n=n, shot=shot, begin=begin, end=end):
+            j = queries[0] if len(queries) == 1 else chosen(queries, m)
+            base = labels.query_base(j)
+
+            @pl.when(jnp.logical_and(begin < base + BLOCK, end > base))
+            def _():
+                row = base + lax.broadcasted_iota(jnp.int32, (1, BLOCK), 1)
+                same = jnp.logical_and(row >= begin, row < end)
+                visit(n, j, jnp.logical_and(labels.live(shot, labels.y % 2), same))
+
+        loop(len(queries), step)
+
+
+def own_text(labels, n, visit):
+    live = labels.live(labels.key_shot(0), labels.y % 2)
+    visit(n, SIDE, jnp.broadcast_to(live, (HALF, BLOCK)))
 
 
 def text_queries(labels, blocks, visit):
-    def step(n):
-        i, p = n // 2, n % 2
-        base = labels.key_base(chosen(blocks, i))
-        begin, end = labels.span(labels.query_shot(p))
-
-        @pl.when(jnp.logical_and(begin < base + BLOCK, end > base))
-        def _():
-            row = base + lax.broadcasted_iota(jnp.int32, (BLOCK, 1), 0)
-            same = jnp.logical_and(row >= begin, row < end)
-            visit(i, p, jnp.broadcast_to(same, (BLOCK, BLOCK)))
-
-    loop(2 * len(blocks), step)
+    for n, block in enumerate(blocks):
+        base = labels.key_base(block)
+
+        def step(p, n=n, base=base):
+            begin, end = labels.span(labels.query_shot(p))
+
+            @pl.when(jnp.logical_and(begin < base + BLOCK, end > base))
+            def _():
+                row = base + lax.broadcasted_iota(jnp.int32, (BLOCK, 1), 0)
+                same = jnp.logical_and(row >= begin, row < end)
+                visit(n, SIDE + p, jnp.broadcast_to(same, (BLOCK, BLOCK)))
+
+        loop(2, step)
 
 
 def head_ds(h):
@@ -218,41 +221,23 @@
     return slice(j * BLOCK, (j + 1) * BLOCK)
 
 
-def stats_kernel(blocks, last, length_ref, caption_ref, place_ref, *refs):
-    kv, refs = refs[: len(blocks)], refs[len(blocks) :]
-    labels = Labels(length_ref, caption_ref, place_ref)
-    if last:
-        acc_in, q_all, g_all, out_ref, k_all, v_all, tk_all, tv_all, *scratch = refs
-    else:
-        qg, text_qg = refs[:SIDE], refs[SIDE : 2 * SIDE]
-        out_ref, q_all, g_all, k_all, v_all, tk_all, tv_all, *scratch = refs[2 * SIDE :]
-        stage_queries(labels, qg, text_qg, q_all, g_all)
-    stage_keys(kv, k_all, v_all, tk_all, tv_all)
-    if last:
-        acc = scratch[0]
-        acc[...] = acc_in[...]
-    else:
-        acc = out_ref
-        acc[0] = jnp.full((HEADS_LOCAL, ROWS), LOW, F32)
-        acc[1:3] = jnp.zeros((2, HEADS_LOCAL, ROWS), F32)
-
+def video_stats(acc, q_all, g_all, kv, queries, fresh):
     def head(h):
         c, row = head_ds(h), pl.ds(h, 1)
-        keys = k_all[:, :, c].reshape(len(blocks) * BLOCK, HDIM)
-        values = v_all[:, :, c].reshape(len(blocks) * BLOCK, HDIM)
-        for j in range(SIDE):
+        keys, values = joined(kv, 0, c), joined(kv, 1, c)
+        for j in queries:
             cols = query_cols(j)
             scores = dot_nt(keys, q_all[j, :, c])
             dprob = dot_nt(values, g_all[j, :, c])
             top = jnp.max(scores, axis=0, keepdims=True) * TO_LOG2
-            if last:
+            if not fresh:
                 before = acc[0, row, cols]
                 top = jnp.maximum(before, top)
                 shrink = jnp.exp2(before - top)
             weight = jnp.exp2(scores * TO_LOG2 - top)
             total = jnp.sum(weight, axis=0, keepdims=True)
             weighted = jnp.sum(weight * dprob, axis=0, keepdims=True)
-            if last:
+            if not fresh:
                 total += acc[1, row, cols] * shrink
                 weighted += acc[2, row, cols] * shrink
             acc[0, row, cols] = top
@@ -261,36 +246,68 @@
 
     loop(HEADS_LOCAL, head)
 
-    def visit(keys_ref, values_ref, n, j, mask):
-        cols = rows_ds(j)
-        results = []
-        for h in range(HEADS_LOCAL):
-            c = head_cols(h)
-            scores = jnp.where(mask, dot_nt(keys_ref[n, :, c], q_all[j, :, c]) * TO_LOG2, LOW)
-            dprob = dot_nt(values_ref[n, :, c], g_all[j, :, c])
-            before = acc[0, h : h + 1, cols]
-            top = jnp.maximum(before, jnp.max(scores, axis=0, keepdims=True))
-            weight = jnp.where(mask, jnp.exp2(scores - top), 0.0)
-            shrink = jnp.exp2(before - top)
-            results.append(
-                (
-                    top,
-                    acc[1, h : h + 1, cols] * shrink + jnp.sum(weight, axis=0, keepdims=True),
-                    acc[2, h : h + 1, cols] * shrink + jnp.sum(weight * dprob, axis=0, keepdims=True),
-                )
+
+def visit_stats(acc, q_all, g_all, kv, part, n, j, mask):
+    cols = rows_ds(j)
+    results = []
+    for h in range(HEADS_LOCAL):
+        c = head_cols(h)
+        scores = jnp.where(mask, dot_nt(kv[n][0, part, c], q_all[j, :, c]) * TO_LOG2, LOW)
+        dprob = dot_nt(kv[n][1, part, c], g_all[j, :, c])
+        before = acc[0, h : h + 1, cols]
+        top = jnp.maximum(before, jnp.max(scores, axis=0, keepdims=True))
+        weight = jnp.where(mask, jnp.exp2(scores - top), 0.0)
+        shrink = jnp.exp2(before - top)
+        results.append(
+            (
+                top,
+                acc[1, h : h + 1, cols] * shrink + jnp.sum(weight, axis=0, keepdims=True),
+                acc[2, h : h + 1, cols] * shrink + jnp.sum(weight * dprob, axis=0, keepdims=True),
             )
-        for h in range(HEADS_LOCAL):
-            for n in range(3):
-                acc[n, h : h + 1, cols] = results[h][n]
-
-    text_keys(labels, blocks, lambda t, j, mask: visit(tk_all, tv_all, t, j, mask))
-    text_queries(labels, blocks, lambda i, p, mask: visit(k_all, v_all, i, SIDE + p, mask))
-    if last:
-        total = acc[1]
-        some = total > 0.0
-        total = jnp.where(some, total, 1.0)
-        out_ref[0] = jnp.where(some, acc[0] + jnp.log2(total), LOW)
-        out_ref[1] = acc[2] / total
+        )
+    for h in range(HEADS_LOCAL):
+        for m in range(3):
+            acc[m, h : h + 1, cols] = results[h][m]
+
+
+NEAR = (0, 1, 3)
+FAR = 2
+
+
+def stats_first_kernel(length_ref, caption_ref, place_ref, *refs):
+    kv, qg, text_qg, (acc, q_all, g_all) = refs[:3], refs[3:6], refs[6 : SIDE + 6], refs[SIDE + 6 :]
+    labels = Labels(length_ref, caption_ref, place_ref)
+    for j, ref in zip(NEAR, qg):
+        q_all[j] = ref[0]
+        g_all[j] = ref[1]
+    stage_text_queries(labels, text_qg, q_all, g_all)
+    acc[0] = jnp.full((HEADS_LOCAL, ROWS), LOW, F32)
+    acc[1:3] = jnp.zeros((2, HEADS_LOCAL, ROWS), F32)
+    video_stats(acc, q_all, g_all, kv, NEAR, True)
+    visit = functools.partial(visit_stats, acc, q_all, g_all, kv)
+    text_keys(labels, NEAR, NEAR, functools.partial(visit, TEXT_PART))
+    own_text(labels, 0, functools.partial(visit, TEXT_PART))
+    text_queries(labels, NEAR, functools.partial(visit, VIDEO_PART))
+
+
+def stats_last_kernel(length_ref, caption_ref, place_ref, *refs):
+    kv, far_kv, (acc_in, q_in, g_in, far_qg, out_ref, q_all, g_all, acc) = refs[:3], refs[3:4], refs[4:]
+    labels = Labels(length_ref, caption_ref, place_ref)
+    for j in range(SIDE + 2):
+        q_all[j] = far_qg[0] if j == FAR else q_in[j]
+        g_all[j] = far_qg[1] if j == FAR else g_in[j]
+    acc[...] = acc_in[...]
+    video_stats(acc, q_all, g_all, kv, (FAR,), True)
+    video_stats(acc, q_all, g_all, far_kv, range(SIDE), False)
+    visit = functools.partial(visit_stats, acc, q_all, g_all)
+    text_keys(labels, NEAR, (FAR,), functools.partial(visit, kv, TEXT_PART))
+    text_keys(labels, (FAR,), tuple(range(SIDE)), functools.partial(visit, far_kv, TEXT_PART))
+    text_queries(labels, (FAR,), functools.partial(visit, far_kv, VIDEO_PART))
+    total = acc[1]
+    some = total > 0.0
+    total = jnp.where(some, total, 1.0)
+    out_ref[0] = jnp.where(some, acc[0] + jnp.log2(total), LOW)
+    out_ref[1] = acc[2] / total
 
 
 def normalize(stats, norm):
@@ -315,16 +332,13 @@
 
 def key_grads(labels, blocks, fresh, q_all, g_all, kv, dkv_out, norm, dq_t, scratch):
     count = len(blocks)
-    k_all, v_all, tk_all, tv_all, dk, dv, text_dk, text_dv, p_all, ds_all = scratch
-    stage_keys(kv, k_all, v_all, tk_all, tv_all)
+    dk, dv, text_dk, text_dv, p_all, ds_all = scratch
     text_dk[...] = jnp.zeros((count, HEADS_LOCAL, HALF, HDIM), F32)
     text_dv[...] = jnp.zeros((count, HEADS_LOCAL, HALF, HDIM), F32)
-    rows = count * BLOCK
 
     def head(h):
         c, row = head_ds(h), pl.ds(h, 1)
-        keys = k_all[:, :, c].reshape(rows, HDIM)
-        values = v_all[:, :, c].reshape(rows, HDIM)
+        keys, values = joined(kv, 0, c), joined(kv, 1, c)
         keys_t = jnp.transpose(keys)
         for j in range(SIDE):
             cols = query_cols(j)
@@ -344,14 +358,14 @@
 
     loop(HEADS_LOCAL, head)
 
-    def visit(keys_ref, values_ref, n, j, mask, add):
+    def visit(part, add, n, j, mask):
         cols = rows_ds(j)
         results = []
         for h in range(HEADS_LOCAL):
             c = head_cols(h)
-            keys, queries, grads = keys_ref[n, :, c], q_all[j, :, c], g_all[j, :, c]
+            keys, queries, grads = kv[n][0, part, c], q_all[j, :, c], g_all[j, :, c]
             scores = dot_nt(keys, queries) * TO_LOG2
-            dprob = dot_nt(values_ref[n, :, c], grads)
+            dprob = dot_nt(kv[n][1, part, c], grads)
             probs = jnp.where(mask, jnp.exp2(jnp.where(mask, scores, LOW) - norm[0, h : h + 1, cols]), 0.0)
             low = probs.astype(BF16)
             dscore = (probs * (dprob - norm[1, h : h + 1, cols])).astype(BF16)
@@ -365,11 +379,14 @@
         text_dv[n, h] += value_part
 
     def add_video(n, h, key_part, value_part):
-        dk[h, rows_ds(n)] += key_part
-        dv[h, rows_ds(n)] += value_part
-
-    text_keys(labels, blocks, lambda t, j, mask: visit(tk_all, tv_all, t, j, mask, add_text))
-    text_queries(labels, blocks, lambda i, p, mask: visit(k_all, v_all, i, SIDE + p, mask, add_video))
+        dk[h, query_cols(n)] += key_part
+        dv[h, query_cols(n)] += value_part
+
+    visit_text = functools.partial(visit, TEXT_PART, add_text)
+    text_keys(labels, blocks, tuple(range(SIDE)), visit_text)
+    if 0 in blocks:
+        own_text(labels, blocks.index(0), visit_text)
+    text_queries(labels, blocks, functools.partial(visit, VIDEO_PART, add_video))
 
     for i in range(count):
         for h in range(HEADS_LOCAL):
@@ -413,14 +430,9 @@
 KEY_MESSAGE = jax.ShapeDtypeStruct((2, BLOCK + HALF, WIDTH), BF16)
 
 
-def staged(count):
-    return [pltpu.VMEM((count, BLOCK, WIDTH), BF16)] * 2 + [pltpu.VMEM((count, HALF, WIDTH), BF16)] * 2
-
-
 def grads_scratch(count):
     return (
-        staged(count)
-        + [pltpu.VMEM((HEADS_LOCAL, count * BLOCK, HDIM), F32)] * 2
+        [pltpu.VMEM((HEADS_LOCAL, count * BLOCK, HDIM), F32)] * 2
         + [pltpu.VMEM((count, HEADS_LOCAL, HALF, HDIM), F32)] * 2
         + [pltpu.VMEM((count * BLOCK, VIDEO_ROWS), BF16)] * 2
     )
@@ -435,30 +447,30 @@
     return pl.CostEstimate(flops=2 * HDIM * matmuls * pairs, bytes_accessed=8 * 1024 * 1024, transcendentals=pairs)
 
 
-def stats_first_call(blocks, scalars, qg, kv, text_qg):
+def stats_first_call(scalars, qg, kv, text_qg):
+    near_kv, near_qg = [kv[i] for i in NEAR], [qg[j] for j in NEAR]
     return pl.pallas_call(
-        functools.partial(stats_kernel, blocks, False),
-        in_specs=[SMEM_SPEC] * 3 + [VMEM_SPEC] * (2 * SIDE + len(blocks)),
+        stats_first_kernel,
+        in_specs=[SMEM_SPEC] * 3 + [VMEM_SPEC] * (SIDE + 6),
         out_specs=[VMEM_SPEC] * 3,
         out_shape=[jax.ShapeDtypeStruct(STATS, F32), STAGED_QUERIES, STAGED_QUERIES],
-        scratch_shapes=staged(len(blocks)),
         compiler_params=PARAMS,
-        cost_estimate=cost(len(blocks), 2),
+        cost_estimate=cost(3, 2),
         name="stats_first",
-    )(*scalars, *placed([kv[i] for i in blocks] + qg), *placed(text_qg, pltpu.HBM))
-
-
-def stats_last_call(blocks, scalars, acc, queries, kv):
+    )(*scalars, *placed(near_kv), *placed([*near_qg, *text_qg], pltpu.HBM))
+
+
+def stats_last_call(scalars, acc, queries, qg, kv):
     return pl.pallas_call(
-        functools.partial(stats_kernel, blocks, True),
-        in_specs=[SMEM_SPEC] * 3 + [VMEM_SPEC] * (3 + len(blocks)),
-        out_specs=VMEM_SPEC,
-        out_shape=jax.ShapeDtypeStruct((2, HEADS_LOCAL, ROWS), F32),
-        scratch_shapes=staged(len(blocks)) + [pltpu.VMEM(STATS, F32)],
+        stats_last_kernel,
+        in_specs=[SMEM_SPEC] * 3 + [VMEM_SPEC] * (SIDE + 4),
+        out_specs=[VMEM_SPEC] * 3,
+        out_shape=[jax.ShapeDtypeStruct((2, HEADS_LOCAL, ROWS), F32), STAGED_QUERIES, STAGED_QUERIES],
+        scratch_shapes=[pltpu.VMEM(STATS, F32)],
         compiler_params=PARAMS,
-        cost_estimate=cost(len(blocks), 2),
+        cost_estimate=cost(2, 2),
         name="stats_last",
-    )(*scalars, *placed([*[kv[i] for i in blocks], acc, *queries]))
+    )(*scalars, *placed([*[kv[i] for i in NEAR], kv[FAR], acc, *queries, qg[FAR]]))
 
 
 def grads_first_call(blocks, scalars, queries, kv, stats):
@@ -520,13 +532,16 @@
     arrived = lax.all_to_all(packed, "head", split_axis=0, concat_axis=0)
     arrived, text_qg = lax.optimization_barrier((arrived, text_qg))
     qg, kv = assemble(arrived, text_key, text_value)
-    qg = gathered(qg, "y")
+    qg1, qg3 = swap(qg, "y", 1), swap(qg, "y", 3)
     kv1, kv3 = swap(kv, "z", 1), swap(kv, "z", 3)
-    later, qg[1], qg[3] = lax.optimization_barrier((kv, qg[1], qg[3]))
-    kv = [kv, kv1, swap(later, "z", 2), kv3]
-
-    acc, *queries = stats_first_call((0, 1, 3), scalars, qg, kv, text_qg)
-    stats = gathered(stats_last_call((2,), scalars, acc, queries, kv), "y")
+    qg2 = swap(qg, "y", FAR)
+    far_kv, qg1, qg3 = lax.optimization_barrier((kv, qg1, qg3))
+    qg = [qg, qg1, qg2, qg3]
+    kv = [kv, kv1, swap(far_kv, "z", FAR), kv3]
+
+    acc, *queries = stats_first_call(scalars, qg, kv, text_qg)
+    stats, *queries = stats_last_call(scalars, acc, queries, qg, kv)
+    stats = gathered(stats, "y")
     (dkv1, dkv3), dq_t, norm = grads_first_call((1, 3), scalars, queries, kv, stats)
     dq, (dkv2, dkv0) = grads_last_call((2, 0), scalars, queries, kv, dq_t, norm)
 

time: 127 us -> 126 us (level); the launches traced: 126 us -> 127 us
  blocking collectives: 21.2 us -> 17.4 us
  starting transfers between devices: 30.2 us -> 33.8 us
  waiting for transfers between devices: 34.2 us -> 37.8 us
  Pallas kernels: 38.4 us -> 35.7 us
    all_to_all x1, blocking collectives: 21.2 us -> 17.4 us  [on_device(): lax.all_to_all(video, 'head', split_axis=0, concat_axis=0)]
    ppermute x18, waiting for transfers between devices: 34.2 us -> 37.8 us  [swap(): lax.ppermute(array, 'seq', [(i, i ^ shift) for i in range(SIDE * SIDE)])]
    ppermute x18, starting transfers between devices: 24.3 us -> 27.8 us  [swap(): lax.ppermute(array, 'seq', [(i, i ^ shift) for i in range(SIDE * SIDE)])]
    pallas_call x1, Pallas kernels: 13.1 us -> 11.2 us  [grads_last_call(): pl.pallas_call(functools.partial(grads_last_kernel, blocks), in_specs=[SM...]
  transfers between devices with their start and end apart: 19 -> 19, of which waited for: 9 -> 12; matrix products, arithmetic and copies ran while one was open for 0% -> 0% of each run, Pallas kernels for 18% -> 15%
where the time goes in v4:
time: 126 us; the launch traced here: 127 us
  waiting for transfers between devices  37.8 us (30%)
  Pallas kernels  35.7 us (28%)
  starting transfers between devices  33.8 us (27%)
  blocking collectives  17.4 us (14%)
    ppermute x18, waiting for transfers between devices, swap(): lax.ppermute(array, 'seq', [(i, i ^ shift) for i in range(SIDE * SIDE)])  37.8 us
    ppermute x18, starting transfers between devices, swap(): lax.ppermute(array, 'seq', [(i, i ^ shift) for i in range(SIDE * SIDE)])  27.8 us
    all_to_all x1, blocking collectives, on_device(): lax.all_to_all(video, 'head', split_axis=0, concat_axis=0)  17.4 us
    pallas_call x1, Pallas kernels, grads_last_call(): pl.pallas_call(functools.partial(grads_last_kernel, blocks), in_specs=[SM...  11.2 us
    pallas_call x1, Pallas kernels, grads_first_call(): pl.pallas_call(functools.partial(grads_first_kernel, blocks), in_specs=[S...  7.59 us
    pallas_call x1, Pallas kernels, stats_first_call(): pl.pallas_call(stats_first_kernel, in_specs=[SMEM_SPEC] * 3 + [VMEM_SPEC]...  7.28 us
    all_to_all x1, starting transfers between devices, on_device(): arrived = lax.all_to_all(packed, 'head', split_axis=0, concat_axis=0)  5.94 us
    pallas_call x1, Pallas kernels, stats_last_call(): pl.pallas_call(stats_last_kernel, in_specs=[SMEM_SPEC] * 3 + [VMEM_SPEC]...  5.18 us
  transfers between devices with their start and end apart: 19, of which 12 were waited for; matrix products, arithmetic and copies ran while one was open for 0% of the time, Pallas kernels for 15%

profile of v4, /device:TPU:1, one launch (start us, length us, event | category | flops | bytes accessed | tf_op | source)
XLA Modules:
  0.0 126.6 jit_solution(2326915946667059112)
XLA Ops:
  0.6 0.0 copy-start.1
  0.6 0.0 copy-start
  0.7 2.3 %pack_inputs.1 = (bf16[8,4,32,384]{3,2,1,0:T(8,128)(2,1)}, bf16[2,128,384]{2,1,0:T(8,128)(2,1)S(1)}) custom-call(bf16[32,3072]{1,0:T(8,128)(2,1)} %q_ref.1, bf16[32,3072]{1,0:T(8,128)(2,1)} %k_ref.1, bf16[32,3072]{1,0:T(8,128)(2,1)} %v_ref.1, bf16[32,3072]{1,0:T(8,128)(2,1)} %g_ref.1, bf16[128,384]{1,0:T(8,128)(2,1)} %tq_ref.1, bf16[128,384]{1,0:T(8,128)(2,1)} %tg_ref.1), custom_call_target="tpu_custom_call" | custom-call | tf_op jit(solution)/shard_map/pack_inputs/pallas_call | solution.py:53
  2.9 0.0 copy-start.5
  2.9 0.0 copy-start.2
  2.9 0.0 copy-start.3
  2.9 5.9 %all-to-all-start = ((bf16[8,4,32,384]{3,2,1,0:T(8,128)(2,1)}), bf16[8,4,32,384]{3,2,1,0:T(8,128)(2,1)S(1)}, u32[]{:S(2)}, u32[]{:S(2)}) async-start(bf16[8,4,32,384]{3,2,1,0:T(8,128)(2,1)} %get-tuple-element.47), calls=%async_computation | async-start | bytes 1572864 | tf_op jit(solution)/shard_map/all_to_all | solution.py:532
  8.9 2.7 %collective-permute-start.2 = (bf16[2,128,384]{2,1,0:T(8,128)(2,1)S(1)}, bf16[2,128,384]{2,1,0:T(8,128)(2,1)S(1)}, u32[]{:S(2)}, u32[]{:S(2)}) collective-permute-start(bf16[2,128,384]{2,1,0:T(8,128)(2,1)S(1)} %get-tuple-element.55.refs_6_), channel_id=1, source_target_pairs={{0,24},{8,16},{16,8},{24,0},{32,56},{40,48},{48,40},{56,32},{64,88... | collective-permute-start | bytes 589832 | tf_op jit(solution)/shard_map/ppermute | solution.py:509
  11.6 0.3 collective-permute-start.1
  12.0 0.2 collective-permute-start
  12.2 8.8 %collective-permute-done.2.refs_9_ = bf16[2,128,384]{2,1,0:T(8,128)(2,1)S(1)} collective-permute-done((bf16[2,128,384]{2,1,0:T(8,128)(2,1)S(1)}, bf16[2,128,384]{2,1,0:T(8,128)(2,1)S(1)}, u32[]{:S(2)}, u32[]{:S(2)}) %collective-permute-start.2) | collective-permute-done | bytes 196640 | tf_op jit(solution)/shard_map/ppermute | solution.py:509
  21.0 0.0 collective-permute-done.1.refs_8_
  21.0 0.3 collective-permute-done.refs_7_
  21.3 0.4 copy-done.8
  21.6 0.1 copy-done.9
  21.7 0.7 copy-done.10
  22.4 0.0 all-to-all-done.in_ref
  22.4 0.0 copy-done.1
  22.4 0.0 copy-done
  22.4 0.1 assemble_blocks.1
  22.5 0.0 copy-done.5
  22.5 0.0 copy-start.4
  22.5 2.7 %collective-permute-start.6 = (bf16[2,256,384]{2,1,0:T(8,128)(2,1)S(1)}, bf16[2,256,384]{2,1,0:T(8,128)(2,1)S(1)}, u32[]{:S(2)}, u32[]{:S(2)}) collective-permute-start(bf16[2,256,384]{2,1,0:T(8,128)(2,1)S(1)} %get-tuple-element.51.refs_3_), channel_id=1, source_target_pairs={{0,24},{8,16},{16,8},{24,0},{32,56},{40,48},{48,40},{56,32},{64,88... | collective-permute-start | bytes 1179656 | tf_op jit(solution)/shard_map/ppermute | solution.py:509
  25.3 0.0 collective-permute-start.5
  25.3 3.8 %collective-permute-start.4 = (bf16[2,384,384]{2,1,0:T(8,128)(2,1)S(1)}, bf16[2,384,384]{2,1,0:T(8,128)(2,1)S(1)}, u32[]{:S(2)}, u32[]{:S(2)}) collective-permute-start(bf16[2,384,384]{2,1,0:T(8,128)(2,1)S(1)} %get-tuple-element.52.refs_0_.refs_5_), channel_id=1, source_target_pairs={{0,96},{8,104},{16,112},{24,120},{32,64},{40,72},{48,80},{56,88},{... | collective-permute-start | bytes 1769480 | tf_op jit(solution)/shard_map/ppermute | solution.py:509
  29.0 0.0 collective-permute-start.3
  29.0 4.7 %collective-permute-done.6.refs_5_ = bf16[2,256,384]{2,1,0:T(8,128)(2,1)S(1)} collective-permute-done((bf16[2,256,384]{2,1,0:T(8,128)(2,1)S(1)}, bf16[2,256,384]{2,1,0:T(8,128)(2,1)S(1)}, u32[]{:S(2)}, u32[]{:S(2)}) %collective-permute-start.6) | collective-permute-done | bytes 393248 | tf_op jit(solution)/shard_map/ppermute | solution.py:509
  33.7 1.1 collective-permute-done.5.refs_4_
  34.9 0.0 copy-done.6
  34.9 3.6 %collective-permute-start.7 = (bf16[2,384,384]{2,1,0:T(8,128)(2,1)S(1)}, bf16[2,384,384]{2,1,0:T(8,128)(2,1)S(1)}, u32[]{:S(2)}, u32[]{:S(2)}) collective-permute-start(bf16[2,384,384]{2,1,0:T(8,128)(2,1)S(1)} %get-tuple-element.52.refs_0_.refs_5_), channel_id=1, source_target_pairs={{0,64},{8,72},{16,80},{24,88},{32,96},{40,104},{48,112},{56,120},{... | collective-permute-start | bytes 1769480 | tf_op jit(solution)/shard_map/ppermute | solution.py:509
  38.5 0.0 copy-done.7
  38.5 0.3 collective-permute-start.8
  38.8 2.9 %collective-permute-done.4.refs_2_.refs_3_ = bf16[2,384,384]{2,1,0:T(8,128)(2,1)S(1)} collective-permute-done((bf16[2,384,384]{2,1,0:T(8,128)(2,1)S(1)}, bf16[2,384,384]{2,1,0:T(8,128)(2,1)S(1)}, u32[]{:S(2)}, u32[]{:S(2)}) %collective-permute-start.4) | collective-permute-done | bytes 589856 | tf_op jit(solution)/shard_map/ppermute | solution.py:509
  41.7 0.9 collective-permute-done.3.refs_1_.refs_2_
  42.5 0.0 copy-done.4
  42.5 0.0 copy-done.2
  42.5 0.0 copy-done.3
  42.5 7.3 %stats_first.1 = (f32[3,3,1536]{2,1,0:T(4,128)S(1)}, bf16[6,256,384]{2,1,0:T(8,128)(2,1)S(1)}, bf16[6,256,384]{2,1,0:T(8,128)(2,1)S(1)}) custom-call(s32[8]{0:T(128)S(1)} %copy-done.2, s32[8]{0:T(128)S(1)} %copy-done.3, s32[1]{0:T(128)} %bitcast.place_ref, bf16[2,384,384]{2,1,0:T(8,128)(2,1)S(1)} %get-tuple-element.52.refs_0_.refs_5_, ...), custom_call_target="tpu_custom_call" | custom-call | flops 1207959552 | bytes 8388608 | tf_op jit(solution)/shard_map/stats_first/pallas_call | solution.py:452
  49.8 0.0 collective-permute-done.8.refs_7_
  49.8 5.3 %collective-permute-done.7.refs_3_.refs_4_ = bf16[2,384,384]{2,1,0:T(8,128)(2,1)S(1)} collective-permute-done((bf16[2,384,384]{2,1,0:T(8,128)(2,1)S(1)}, bf16[2,384,384]{2,1,0:T(8,128)(2,1)S(1)}, u32[]{:S(2)}, u32[]{:S(2)}) %collective-permute-start.7) | collective-permute-done | bytes 589856 | tf_op jit(solution)/shard_map/ppermute | solution.py:509
  55.2 5.2 %stats_last.1 = (f32[2,3,1536]{2,1,0:T(4,128)S(1)}, bf16[6,256,384]{2,1,0:T(8,128)(2,1)S(1)}, bf16[6,256,384]{2,1,0:T(8,128)(2,1)S(1)}) custom-call(s32[8]{0:T(128)S(1)} %copy-done.2, s32[8]{0:T(128)S(1)} %copy-done.3, s32[1]{0:T(128)} %bitcast.place_ref, bf16[2,384,384]{2,1,0:T(8,128)(2,1)S(1)} %get-tuple-element.52.refs_0_.refs_5_, ...), custom_call_target="tpu_custom_call" | custom-call | flops 805306368 | bytes 8388608 | tf_op jit(solution)/shard_map/stats_last/pallas_call | solution.py:464
  60.4 0.1 collective-permute-start.11
  60.4 2.6 %collective-permute-start.10 = (f32[2,3,1536]{2,1,0:T(4,128)S(1)}, f32[2,3,1536]{2,1,0:T(4,128)S(1)}, u32[]{:S(2)}, u32[]{:S(2)}) collective-permute-start(f32[2,3,1536]{2,1,0:T(4,128)S(1)} %get-tuple-element.64.refs_4_), channel_id=1, source_target_pairs={{0,16},{8,24},{16,0},{24,8},{32,48},{40,56},{48,32},{56,40},{64,80... | collective-permute-start | bytes 110600 | tf_op jit(solution)/shard_map/ppermute | solution.py:509
  63.1 0.6 collective-permute-start.9
  63.7 1.4 %collective-permute-done.11.refs_7_ = f32[2,3,1536]{2,1,0:T(4,128)S(1)} collective-permute-done((f32[2,3,1536]{2,1,0:T(4,128)S(1)}, f32[2,3,1536]{2,1,0:T(4,128)S(1)}, u32[]{:S(2)}, u32[]{:S(2)}) %collective-permute-start.11) | collective-permute-done | bytes 36896 | tf_op jit(solution)/shard_map/ppermute | solution.py:509
  65.1 0.0 collective-permute-done.10.refs_6_
  65.1 0.9 collective-permute-done.9.refs_5_
  66.0 7.6 %grads_first.1 = (bf16[2,384,384]{2,1,0:T(8,128)(2,1)S(1)}, bf16[2,384,384]{2,1,0:T(8,128)(2,1)S(1)}, f32[3,128,1536]{2,1,0:T(8,128)S(1)}, f32[2,3,1536]{2,1,0:T(4,128)S(1)}) custom-call(s32[8]{0:T(128)S(1)} %copy-done.2, s32[8]{0:T(128)S(1)} %copy-done.3, s32[1]{0:T(128)} %bitcast.place_ref, bf16[6,256,384]{2,1,0:T(8,128)(2,1)S(1)} %get-tuple-element.62.refs_0_.refs_2_, ...), custom_call_target="tpu_custom_call" | custom-call | flops 2013265920 | bytes 8388608 | tf_op jit(solution)/shard_map/grads_first/pallas_call | solution.py:478
  73.6 0.6 collective-permute-start.12
  74.3 4.8 %collective-permute-start.17 = (bf16[2,384,384]{2,1,0:T(8,128)(2,1)S(1)}, bf16[2,384,384]{2,1,0:T(8,128)(2,1)S(1)}, u32[]{:S(2)}, u32[]{:S(2)}) collective-permute-start(bf16[2,384,384]{2,1,0:T(8,128)(2,1)S(1)} %get-tuple-element.80), channel_id=1, source_target_pairs={{0,96},{8,104},{16,112},{24,120},{32,64},{40,72},{48,80},{56,88},{... | collective-permute-start | bytes 1769480 | tf_op jit(solution)/shard_map/ppermute | solution.py:509
  79.0 11.2 %grads_last.1 = (bf16[3,128,384]{2,1,0:T(8,128)(2,1)S(1)}, bf16[3,128,384]{2,1,0:T(8,128)(2,1)S(1)}, bf16[3,128,384]{2,1,0:T(8,128)(2,1)S(1)}, bf16[3,128,384]{2...) custom-call(s32[8]{0:T(128)S(1)} %copy-done.2, s32[8]{0:T(128)S(1)} %copy-done.3, ...), custom_call_target="tpu_custom_call" | custom-call | flops 2013265920 | bytes 8388608 | tf_op jit(solution)/shard_map/grads_last/pallas_call | solution.py:494
  90.2 0.0 collective-permute-done.12.refs_5_
  90.2 0.1 collective-permute-start.16
  90.3 2.8 %collective-permute-start.13 = (bf16[3,128,384]{2,1,0:T(8,128)(2,1)S(1)}, bf16[3,128,384]{2,1,0:T(8,128)(2,1)S(1)}, u32[]{:S(2)}, u32[]{:S(2)}) collective-permute-start(bf16[3,128,384]{2,1,0:T(8,128)(2,1)S(1)} %get-tuple-element.74), channel_id=1, source_target_pairs={{0,8},{8,0},{16,24},{24,16},{32,40},{40,32},{48,56},{56,48},{64,72... | collective-permute-start | bytes 884744 | tf_op jit(solution)/shard_map/ppermute | solution.py:509
  93.1 0.0 collective-permute-start.14
  93.1 2.5 %collective-permute-start.15 = (bf16[3,128,384]{2,1,0:T(8,128)(2,1)S(1)}, bf16[3,128,384]{2,1,0:T(8,128)(2,1)S(1)}, u32[]{:S(2)}, u32[]{:S(2)}) collective-permute-start(bf16[3,128,384]{2,1,0:T(8,128)(2,1)S(1)} %get-tuple-element.76), channel_id=1, source_target_pairs={{0,24},{8,16},{16,8},{24,0},{32,56},{40,48},{48,40},{56,32},{64,88... | collective-permute-start | bytes 884744 | tf_op jit(solution)/shard_map/ppermute | solution.py:509
  95.5 0.0 collective-permute-done.17.refs_7_
  95.5 1.6 %collective-permute-done.13.refs_1_ = bf16[3,128,384]{2,1,0:T(8,128)(2,1)S(1)} collective-permute-done((bf16[3,128,384]{2,1,0:T(8,128)(2,1)S(1)}, bf16[3,128,384]{2,1,0:T(8,128)(2,1)S(1)}, u32[]{:S(2)}, u32[]{:S(2)}) %collective-permute-start.13) | collective-permute-done | bytes 294944 | tf_op jit(solution)/shard_map/ppermute | solution.py:509
  97.2 5.4 %collective-permute-done.14.refs_2_ = bf16[3,128,384]{2,1,0:T(8,128)(2,1)S(1)} collective-permute-done((bf16[3,128,384]{2,1,0:T(8,128)(2,1)S(1)}, bf16[3,128,384]{2,1,0:T(8,128)(2,1)S(1)}, u32[]{:S(2)}, u32[]{:S(2)}) %collective-permute-start.14) | collective-permute-done | bytes 294944 | tf_op jit(solution)/shard_map/ppermute | solution.py:509
  102.6 4.5 %collective-permute-done.15.refs_3_ = bf16[3,128,384]{2,1,0:T(8,128)(2,1)S(1)} collective-permute-done((bf16[3,128,384]{2,1,0:T(8,128)(2,1)S(1)}, bf16[3,128,384]{2,1,0:T(8,128)(2,1)S(1)}, u32[]{:S(2)}, u32[]{:S(2)}) %collective-permute-start.15) | collective-permute-done | bytes 294944 | tf_op jit(solution)/shard_map/ppermute | solution.py:509
  107.1 0.0 collective-permute-done.16.refs_6_
  107.1 1.2 sum_terms.1
  108.3 17.4 %all_to_all.10.in_ref = bf16[8,3,32,384]{3,2,1,0:T(8,128)(2,1)S(1)} all-to-all(bf16[8,3,32,384]{3,2,1,0:T(8,128)(2,1)S(1)} %get-tuple-element.81), channel_id=1, replica_groups=mesh['seq'=16,'head'=8] {'head'}, dimensions={0} | all-to-all | bytes 1179648 | tf_op jit(solution)/shard_map/all_to_all | solution.py:553
  125.7 0.9 unpack_video.1
  (5 shorter events, 0.0 us)
Async XLA Ops:
  0.6 21.7 %copy-start.1 = (bf16[128,384]{1,0:T(8,128)(2,1)S(1)}, bf16[128,384]{1,0:T(8,128)(2,1)}, u32[]{:S(2)}) copy-start(bf16[128,384]{1,0:T(8,128)(2,1)} %tv_ref.1) | copy-start | bytes 294916
  0.6 21.7 %copy-start = (bf16[128,384]{1,0:T(8,128)(2,1)S(1)}, bf16[128,384]{1,0:T(8,128)(2,1)}, u32[]{:S(2)}) copy-start(bf16[128,384]{1,0:T(8,128)(2,1)} %tk_ref.1) | copy-start | bytes 294916
  2.9 19.6 %copy-start.5 = (bf16[2,128,384]{2,1,0:T(8,128)(2,1)}, bf16[2,128,384]{2,1,0:T(8,128)(2,1)S(1)}, u32[]{:S(2)}) copy-start(bf16[2,128,384]{2,1,0:T(8,128)(2,1)S(1)} %get-tuple-element.55.refs_6_) | copy-start | bytes 589828
  2.9 39.6 %copy-start.2 = (s32[8]{0:T(128)S(1)}, s32[8]{0:T(128)}, u32[]{:S(2)}) copy-start(s32[8]{0:T(128)} %length_ref.7) | copy-start | bytes 100
  2.9 39.6 %copy-start.3 = (s32[8]{0:T(128)S(1)}, s32[8]{0:T(128)}, u32[]{:S(2)}) copy-start(s32[8]{0:T(128)} %caption_ref.7) | copy-start | bytes 100
  2.9 19.5 %all-to-all-start = ((bf16[8,4,32,384]{3,2,1,0:T(8,128)(2,1)}), bf16[8,4,32,384]{3,2,1,0:T(8,128)(2,1)S(1)}, u32[]{:S(2)}, u32[]{:S(2)}) async-start(bf16[8,4,32,384]{3,2,1,0:T(8,128)(2,1)} %get-tuple-element.47), calls=%async_computation | async-start | bytes 1572864 | tf_op jit(solution)/shard_map/all_to_all | solution.py:532
  8.9 12.1 %collective-permute-start.2 = (bf16[2,128,384]{2,1,0:T(8,128)(2,1)S(1)}, bf16[2,128,384]{2,1,0:T(8,128)(2,1)S(1)}, u32[]{:S(2)}, u32[]{:S(2)}) collective-permute-start(bf16[2,128,384]{2,1,0:T(8,128)(2,1)S(1)} %get-tuple-element.55.refs_6_), channel_id=1, source_target_pairs={{0,24},{8,16},{16,8},{24,0},{32,56},{40,48},{48,40},{56,32},{64,88... | collective-permute-start | bytes 589832 | tf_op jit(solution)/shard_map/ppermute | solution.py:509
  11.6 9.4 %collective-permute-start.1 = (bf16[2,128,384]{2,1,0:T(8,128)(2,1)S(1)}, bf16[2,128,384]{2,1,0:T(8,128)(2,1)S(1)}, u32[]{:S(2)}, u32[]{:S(2)}) collective-permute-start(bf16[2,128,384]{2,1,0:T(8,128)(2,1)S(1)} %get-tuple-element.55.refs_6_), channel_id=1, source_target_pairs={{0,16},{8,24},{16,0},{24,8},{32,48},{40,56},{48,32},{56,40},{64,80... | collective-permute-start | bytes 589832 | tf_op jit(solution)/shard_map/ppermute | solution.py:509
  12.0 9.3 %collective-permute-start = (bf16[2,128,384]{2,1,0:T(8,128)(2,1)S(1)}, bf16[2,128,384]{2,1,0:T(8,128)(2,1)S(1)}, u32[]{:S(2)}, u32[]{:S(2)}) collective-permute-start(bf16[2,128,384]{2,1,0:T(8,128)(2,1)S(1)} %get-tuple-element.55.refs_6_), channel_id=1, source_target_pairs={{0,8},{8,0},{16,24},{24,16},{32,40},{40,32},{48,56},{56,48},{64,72... | collective-permute-start | bytes 589832 | tf_op jit(solution)/shard_map/ppermute | solution.py:509
  21.0 0.7 copy-start.8
  21.0 0.7 copy-start.9
  21.7 0.7 copy-start.10
  22.5 20.0 %copy-start.4 = (bf16[2,256,384]{2,1,0:T(8,128)(2,1)}, bf16[2,256,384]{2,1,0:T(8,128)(2,1)S(1)}, u32[]{:S(2)}) copy-start(bf16[2,256,384]{2,1,0:T(8,128)(2,1)S(1)} %get-tuple-element.51.refs_3_) | copy-start | bytes 1179652
  22.5 11.2 %collective-permute-start.6 = (bf16[2,256,384]{2,1,0:T(8,128)(2,1)S(1)}, bf16[2,256,384]{2,1,0:T(8,128)(2,1)S(1)}, u32[]{:S(2)}, u32[]{:S(2)}) collective-permute-start(bf16[2,256,384]{2,1,0:T(8,128)(2,1)S(1)} %get-tuple-element.51.refs_3_), channel_id=1, source_target_pairs={{0,24},{8,16},{16,8},{24,0},{32,56},{40,48},{48,40},{56,32},{64,88... | collective-permute-start | bytes 1179656 | tf_op jit(solution)/shard_map/ppermute | solution.py:509
  25.3 9.6 %collective-permute-start.5 = (bf16[2,256,384]{2,1,0:T(8,128)(2,1)S(1)}, bf16[2,256,384]{2,1,0:T(8,128)(2,1)S(1)}, u32[]{:S(2)}, u32[]{:S(2)}) collective-permute-start(bf16[2,256,384]{2,1,0:T(8,128)(2,1)S(1)} %get-tuple-element.51.refs_3_), channel_id=1, source_target_pairs={{0,8},{8,0},{16,24},{24,16},{32,40},{40,32},{48,56},{56,48},{64,72... | collective-permute-start | bytes 1179656 | tf_op jit(solution)/shard_map/ppermute | solution.py:509
  25.3 16.4 %collective-permute-start.4 = (bf16[2,384,384]{2,1,0:T(8,128)(2,1)S(1)}, bf16[2,384,384]{2,1,0:T(8,128)(2,1)S(1)}, u32[]{:S(2)}, u32[]{:S(2)}) collective-permute-start(bf16[2,384,384]{2,1,0:T(8,128)(2,1)S(1)} %get-tuple-element.52.refs_0_.refs_5_), channel_id=1, source_target_pairs={{0,96},{8,104},{16,112},{24,120},{32,64},{40,72},{48,80},{56,88},{... | collective-permute-start | bytes 1769480 | tf_op jit(solution)/shard_map/ppermute | solution.py:509
  29.0 13.5 %collective-permute-start.3 = (bf16[2,384,384]{2,1,0:T(8,128)(2,1)S(1)}, bf16[2,384,384]{2,1,0:T(8,128)(2,1)S(1)}, u32[]{:S(2)}, u32[]{:S(2)}) collective-permute-start(bf16[2,384,384]{2,1,0:T(8,128)(2,1)S(1)} %get-tuple-element.52.refs_0_.refs_5_), channel_id=1, source_target_pairs={{0,32},{8,40},{16,48},{24,56},{32,0},{40,8},{48,16},{56,24},{64,96... | collective-permute-start | bytes 1769480 | tf_op jit(solution)/shard_map/ppermute | solution.py:509
  33.7 1.1 copy-start.6
  34.9 3.6 %copy-start.7 = (bf16[2,256,384]{2,1,0:T(8,128)(2,1)}, bf16[2,256,384]{2,1,0:T(8,128)(2,1)S(1)}, u32[]{:S(2)}) copy-start(bf16[2,256,384]{2,1,0:T(8,128)(2,1)S(1)} %collective-permute-done.5.refs_4_) | copy-start | bytes 1179652
  34.9 20.3 %collective-permute-start.7 = (bf16[2,384,384]{2,1,0:T(8,128)(2,1)S(1)}, bf16[2,384,384]{2,1,0:T(8,128)(2,1)S(1)}, u32[]{:S(2)}, u32[]{:S(2)}) collective-permute-start(bf16[2,384,384]{2,1,0:T(8,128)(2,1)S(1)} %get-tuple-element.52.refs_0_.refs_5_), channel_id=1, source_target_pairs={{0,64},{8,72},{16,80},{24,88},{32,96},{40,104},{48,112},{56,120},{... | collective-permute-start | bytes 1769480 | tf_op jit(solution)/shard_map/ppermute | solution.py:509
  38.5 11.4 %collective-permute-start.8 = (bf16[2,256,384]{2,1,0:T(8,128)(2,1)S(1)}, bf16[2,256,384]{2,1,0:T(8,128)(2,1)S(1)}, u32[]{:S(2)}, u32[]{:S(2)}) collective-permute-start(bf16[2,256,384]{2,1,0:T(8,128)(2,1)S(1)} %get-tuple-element.51.refs_3_), channel_id=1, source_target_pairs={{0,16},{8,24},{16,0},{24,8},{32,48},{40,56},{48,32},{56,40},{64,80... | collective-permute-start | bytes 1179656 | tf_op jit(solution)/shard_map/ppermute | solution.py:509
  60.4 4.8 %collective-permute-start.11 = (f32[2,3,1536]{2,1,0:T(4,128)S(1)}, f32[2,3,1536]{2,1,0:T(4,128)S(1)}, u32[]{:S(2)}, u32[]{:S(2)}) collective-permute-start(f32[2,3,1536]{2,1,0:T(4,128)S(1)} %get-tuple-element.64.refs_4_), channel_id=1, source_target_pairs={{0,24},{8,16},{16,8},{24,0},{32,56},{40,48},{48,40},{56,32},{64,88... | collective-permute-start | bytes 110600 | tf_op jit(solution)/shard_map/ppermute | solution.py:509
  60.4 4.7 %collective-permute-start.10 = (f32[2,3,1536]{2,1,0:T(4,128)S(1)}, f32[2,3,1536]{2,1,0:T(4,128)S(1)}, u32[]{:S(2)}, u32[]{:S(2)}) collective-permute-start(f32[2,3,1536]{2,1,0:T(4,128)S(1)} %get-tuple-element.64.refs_4_), channel_id=1, source_target_pairs={{0,16},{8,24},{16,0},{24,8},{32,48},{40,56},{48,32},{56,40},{64,80... | collective-permute-start | bytes 110600 | tf_op jit(solution)/shard_map/ppermute | solution.py:509
  63.1 2.9 %collective-permute-start.9 = (f32[2,3,1536]{2,1,0:T(4,128)S(1)}, f32[2,3,1536]{2,1,0:T(4,128)S(1)}, u32[]{:S(2)}, u32[]{:S(2)}) collective-permute-start(f32[2,3,1536]{2,1,0:T(4,128)S(1)} %get-tuple-element.64.refs_4_), channel_id=1, source_target_pairs={{0,8},{8,0},{16,24},{24,16},{32,40},{40,32},{48,56},{56,48},{64,72... | collective-permute-start | bytes 110600 | tf_op jit(solution)/shard_map/ppermute | solution.py:509
  73.6 16.6 %collective-permute-start.12 = (bf16[2,384,384]{2,1,0:T(8,128)(2,1)S(1)}, bf16[2,384,384]{2,1,0:T(8,128)(2,1)S(1)}, u32[]{:S(2)}, u32[]{:S(2)}) collective-permute-start(bf16[2,384,384]{2,1,0:T(8,128)(2,1)S(1)} %get-tuple-element.71), channel_id=1, source_target_pairs={{0,32},{8,40},{16,48},{24,56},{32,0},{40,8},{48,16},{56,24},{64,96... | collective-permute-start | bytes 1769480 | tf_op jit(solution)/shard_map/ppermute | solution.py:509
  74.3 21.3 %collective-permute-start.17 = (bf16[2,384,384]{2,1,0:T(8,128)(2,1)S(1)}, bf16[2,384,384]{2,1,0:T(8,128)(2,1)S(1)}, u32[]{:S(2)}, u32[]{:S(2)}) collective-permute-start(bf16[2,384,384]{2,1,0:T(8,128)(2,1)S(1)} %get-tuple-element.80), channel_id=1, source_target_pairs={{0,96},{8,104},{16,112},{24,120},{32,64},{40,72},{48,80},{56,88},{... | collective-permute-start | bytes 1769480 | tf_op jit(solution)/shard_map/ppermute | solution.py:509
  90.2 16.9 %collective-permute-start.16 = (bf16[2,384,384]{2,1,0:T(8,128)(2,1)S(1)}, bf16[2,384,384]{2,1,0:T(8,128)(2,1)S(1)}, u32[]{:S(2)}, u32[]{:S(2)}) collective-permute-start(bf16[2,384,384]{2,1,0:T(8,128)(2,1)S(1)} %get-tuple-element.79), channel_id=1, source_target_pairs={{0,64},{8,72},{16,80},{24,88},{32,96},{40,104},{48,112},{56,120},{... | collective-permute-start | bytes 1769480 | tf_op jit(solution)/shard_map/ppermute | solution.py:509
  90.3 6.9 %collective-permute-start.13 = (bf16[3,128,384]{2,1,0:T(8,128)(2,1)S(1)}, bf16[3,128,384]{2,1,0:T(8,128)(2,1)S(1)}, u32[]{:S(2)}, u32[]{:S(2)}) collective-permute-start(bf16[3,128,384]{2,1,0:T(8,128)(2,1)S(1)} %get-tuple-element.74), channel_id=1, source_target_pairs={{0,8},{8,0},{16,24},{24,16},{32,40},{40,32},{48,56},{56,48},{64,72... | collective-permute-start | bytes 884744 | tf_op jit(solution)/shard_map/ppermute | solution.py:509
  93.1 9.5 %collective-permute-start.14 = (bf16[3,128,384]{2,1,0:T(8,128)(2,1)S(1)}, bf16[3,128,384]{2,1,0:T(8,128)(2,1)S(1)}, u32[]{:S(2)}, u32[]{:S(2)}) collective-permute-start(bf16[3,128,384]{2,1,0:T(8,128)(2,1)S(1)} %get-tuple-element.75), channel_id=1, source_target_pairs={{0,16},{8,24},{16,0},{24,8},{32,48},{40,56},{48,32},{56,40},{64,80... | collective-permute-start | bytes 884744 | tf_op jit(solution)/shard_map/ppermute | solution.py:509
  93.1 14.0 %collective-permute-start.15 = (bf16[3,128,384]{2,1,0:T(8,128)(2,1)S(1)}, bf16[3,128,384]{2,1,0:T(8,128)(2,1)S(1)}, u32[]{:S(2)}, u32[]{:S(2)}) collective-permute-start(bf16[3,128,384]{2,1,0:T(8,128)(2,1)S(1)} %get-tuple-element.76), channel_id=1, source_target_pairs={{0,24},{8,16},{16,8},{24,0},{32,56},{40,48},{48,40},{56,32},{64,88... | collective-permute-start | bytes 884744 | tf_op jit(solution)/shard_map/ppermute | solution.py:509

commit v5 on v4

--- a/solution.py
+++ b/solution.py
@@ -37,37 +37,40 @@
     return lax.dot_general(a, b, (((1,), (0,)), ((), ())), preferred_element_type=F32)
 
 
-def pack_kernel(q_ref, k_ref, v_ref, g_ref, tq_ref, tg_ref, out_ref, text_qg_ref):
+def pack_kernel(q_ref, k_ref, v_ref, g_ref, tq_ref, tg_ref, tk_ref, tv_ref, out_ref, text_qg_ref, text_kv_ref):
     for d in range(GROUP):
         cols = slice(d * WIDTH, (d + 1) * WIDTH)
         for n, ref in enumerate((q_ref, g_ref, k_ref, v_ref)):
             out_ref[d, n] = ref[:, cols]
     text_qg_ref[0] = tq_ref[...]
     text_qg_ref[1] = tg_ref[...]
+    text_kv_ref[0] = tk_ref[...]
+    text_kv_ref[1] = tv_ref[...]
 
 
 def pack(*arrays):
     video = jax.ShapeDtypeStruct((GROUP, 4, OWN, WIDTH), BF16)
     text = jax.ShapeDtypeStruct((2, HALF, WIDTH), BF16)
-    call = pl.pallas_call(pack_kernel, out_shape=(video, text), compiler_params=SMALL, name="pack_inputs")
+    call = pl.pallas_call(pack_kernel, out_shape=(video, text, text), compiler_params=SMALL, name="pack_inputs")
     return call(*placed(arrays, pltpu.HBM))
 
 
-def assemble_kernel(in_ref, tk_ref, tv_ref, qg_ref, kv_ref):
+def assemble_kernel(in_ref, text_ref, qg_ref, kv_ref, far_ref):
     for n in range(2):
         qg_ref[n] = in_ref[:, n].reshape(BLOCK, WIDTH)
-        kv_ref[n, :BLOCK] = in_ref[:, 2 + n].reshape(BLOCK, WIDTH)
-    kv_ref[0, BLOCK:] = tk_ref[...]
-    kv_ref[1, BLOCK:] = tv_ref[...]
-
-
-def assemble(arrived, text_key, text_value):
+        rows = in_ref[:, 2 + n].reshape(BLOCK, WIDTH)
+        kv_ref[n] = rows
+        far_ref[n, :BLOCK] = rows
+        far_ref[n, BLOCK:] = text_ref[n]
+
+
+def assemble(arrived, text_kv):
     return pl.pallas_call(
         assemble_kernel,
-        out_shape=(QUERY_MESSAGE, KEY_MESSAGE),
+        out_shape=(VIDEO_MESSAGE, VIDEO_MESSAGE, KEY_MESSAGE),
         compiler_params=SMALL,
         name="assemble_blocks",
-    )(*placed([arrived]), text_key, text_value)
+    )(*placed([arrived]), *placed([text_kv], pltpu.HBM))
 
 
 def unpack_kernel(in_ref, q_ref, k_ref, v_ref):
@@ -154,12 +157,24 @@
         g_all[SIDE + p, rows] = jnp.where(live, text_qg[u][1], jnp.zeros((HALF, WIDTH), BF16))
 
 
-VIDEO_PART = slice(0, BLOCK)
-TEXT_PART = slice(BLOCK, BLOCK + HALF)
+class Keys:
+    def __init__(self, video_ref, text_ref, text_at):
+        self.video_ref, self.text_ref, self.text_rows = video_ref, text_ref, slice(text_at, text_at + HALF)
+
+    def rows(self, is_text, which, c):
+        return self.text_ref[which, self.text_rows, c] if is_text else self.video_ref[which, :BLOCK, c]
+
+
+def near_keys(video_refs, text_refs):
+    return [Keys(video, text, 0) for video, text in zip(video_refs, text_refs)]
+
+
+def far_keys(ref):
+    return Keys(ref, ref, BLOCK)
 
 
 def joined(kv, which, c):
-    return jnp.concatenate([ref[which, VIDEO_PART, c] for ref in kv], 0)
+    return jnp.concatenate([block.rows(False, which, c) for block in kv], 0)
 
 
 def loop(count, step):
@@ -227,14 +242,14 @@
         keys, values = joined(kv, 0, c), joined(kv, 1, c)
         for j in queries:
             cols = query_cols(j)
-            scores = dot_nt(keys, q_all[j, :, c])
+            scores = dot_nt(keys, q_all[j, :, c]) * TO_LOG2
             dprob = dot_nt(values, g_all[j, :, c])
-            top = jnp.max(scores, axis=0, keepdims=True) * TO_LOG2
+            top = jnp.max(scores, axis=0, keepdims=True)
             if not fresh:
                 before = acc[0, row, cols]
                 top = jnp.maximum(before, top)
                 shrink = jnp.exp2(before - top)
-            weight = jnp.exp2(scores * TO_LOG2 - top)
+            weight = jnp.exp2(scores - top)
             total = jnp.sum(weight, axis=0, keepdims=True)
             weighted = jnp.sum(weight * dprob, axis=0, keepdims=True)
             if not fresh:
@@ -247,17 +262,18 @@
     loop(HEADS_LOCAL, head)
 
 
-def visit_stats(acc, q_all, g_all, kv, part, n, j, mask):
+def visit_stats(acc, q_all, g_all, kv, is_text, n, j, mask):
     cols = rows_ds(j)
     results = []
     for h in range(HEADS_LOCAL):
         c = head_cols(h)
-        scores = jnp.where(mask, dot_nt(kv[n][0, part, c], q_all[j, :, c]) * TO_LOG2, LOW)
-        dprob = dot_nt(kv[n][1, part, c], g_all[j, :, c])
+        scores = jnp.where(mask, dot_nt(kv[n].rows(is_text, 0, c), q_all[j, :, c]) * TO_LOG2, LOW)
+        dprob = dot_nt(kv[n].rows(is_text, 1, c), g_all[j, :, c])
         before = acc[0, h : h + 1, cols]
         top = jnp.maximum(before, jnp.max(scores, axis=0, keepdims=True))
-        weight = jnp.where(mask, jnp.exp2(scores - top), 0.0)
-        shrink = jnp.exp2(before - top)
+        floor = jnp.maximum(top, 0.5 * LOW)
+        weight = jnp.exp2(scores - floor)
+        shrink = jnp.exp2(before - floor)
         results.append(
             (
                 top,
@@ -275,7 +291,8 @@
 
 
 def stats_first_kernel(length_ref, caption_ref, place_ref, *refs):
-    kv, qg, text_qg, (acc, q_all, g_all) = refs[:3], refs[3:6], refs[6 : SIDE + 6], refs[SIDE + 6 :]
+    kv, refs = near_keys(refs[:3], refs[3:6]), refs[6:]
+    qg, text_qg, (acc, q_all, g_all) = refs[:3], refs[3 : SIDE + 3], refs[SIDE + 3 :]
     labels = Labels(length_ref, caption_ref, place_ref)
     for j, ref in zip(NEAR, qg):
         q_all[j] = ref[0]
@@ -285,13 +302,14 @@
     acc[1:3] = jnp.zeros((2, HEADS_LOCAL, ROWS), F32)
     video_stats(acc, q_all, g_all, kv, NEAR, True)
     visit = functools.partial(visit_stats, acc, q_all, g_all, kv)
-    text_keys(labels, NEAR, NEAR, functools.partial(visit, TEXT_PART))
-    own_text(labels, 0, functools.partial(visit, TEXT_PART))
-    text_queries(labels, NEAR, functools.partial(visit, VIDEO_PART))
+    text_keys(labels, NEAR, NEAR, functools.partial(visit, True))
+    own_text(labels, 0, functools.partial(visit, True))
+    text_queries(labels, NEAR, functools.partial(visit, False))
 
 
 def stats_last_kernel(length_ref, caption_ref, place_ref, *refs):
-    kv, far_kv, (acc_in, q_in, g_in, far_qg, out_ref, q_all, g_all, acc) = refs[:3], refs[3:4], refs[4:]
+    kv, far_kv = near_keys(refs[:3], refs[3:6]), [far_keys(refs[6])]
+    acc_in, q_in, g_in, far_qg, out_ref, q_all, g_all, acc = refs[7:]
     labels = Labels(length_ref, caption_ref, place_ref)
     for j in range(SIDE + 2):
         q_all[j] = far_qg[0] if j == FAR else q_in[j]
@@ -300,9 +318,9 @@
     video_stats(acc, q_all, g_all, kv, (FAR,), True)
     video_stats(acc, q_all, g_all, far_kv, range(SIDE), False)
     visit = functools.partial(visit_stats, acc, q_all, g_all)
-    text_keys(labels, NEAR, (FAR,), functools.partial(visit, kv, TEXT_PART))
-    text_keys(labels, (FAR,), tuple(range(SIDE)), functools.partial(visit, far_kv, TEXT_PART))
-    text_queries(labels, (FAR,), functools.partial(visit, far_kv, VIDEO_PART))
+    text_keys(labels, NEAR, (FAR,), functools.partial(visit, kv, True))
+    text_keys(labels, (FAR,), tuple(range(SIDE)), functools.partial(visit, far_kv, True))
+    text_queries(labels, (FAR,), functools.partial(visit, far_kv, False))
     total = acc[1]
     some = total > 0.0
     total = jnp.where(some, total, 1.0)
@@ -330,7 +348,7 @@
         norm[1, :, query_cols(j)] = delta
 
 
-def key_grads(labels, blocks, fresh, q_all, g_all, kv, dkv_out, norm, dq_t, scratch):
+def key_grads(labels, blocks, dq_in, q_all, g_all, kv, dkv_out, norm, dq_t, scratch):
     count = len(blocks)
     dk, dv, text_dk, text_dv, p_all, ds_all = scratch
     text_dk[...] = jnp.zeros((count, HEADS_LOCAL, HALF, HDIM), F32)
@@ -348,25 +366,22 @@
             dscore = (probs * (dprob - norm[1, row, cols])).astype(BF16)
             p_all[:, cols] = probs.astype(BF16)
             ds_all[:, cols] = dscore
-            part = dot_nn(keys_t, dscore)
-            if fresh:
-                dq_t[h, :, cols] = part
-            else:
-                dq_t[h, :, cols] += part
         dv[h] = dot_nn(p_all[...], g_all[:SIDE, :, c].reshape(VIDEO_ROWS, HDIM))
         dk[h] = dot_nn(ds_all[...], q_all[:SIDE, :, c].reshape(VIDEO_ROWS, HDIM))
+        part = dot_nn(keys_t, ds_all[...])
+        dq_t[h, :, :VIDEO_ROWS] = part if dq_in is None else dq_in[h, :, :VIDEO_ROWS] + part
 
     loop(HEADS_LOCAL, head)
 
-    def visit(part, add, n, j, mask):
+    def visit(is_text, add, n, j, mask):
         cols = rows_ds(j)
         results = []
         for h in range(HEADS_LOCAL):
             c = head_cols(h)
-            keys, queries, grads = kv[n][0, part, c], q_all[j, :, c], g_all[j, :, c]
+            keys, queries, grads = kv[n].rows(is_text, 0, c), q_all[j, :, c], g_all[j, :, c]
             scores = dot_nt(keys, queries) * TO_LOG2
-            dprob = dot_nt(kv[n][1, part, c], grads)
-            probs = jnp.where(mask, jnp.exp2(jnp.where(mask, scores, LOW) - norm[0, h : h + 1, cols]), 0.0)
+            dprob = dot_nt(kv[n].rows(is_text, 1, c), grads)
+            probs = jnp.exp2(jnp.where(mask, scores, LOW) - norm[0, h : h + 1, cols])
             low = probs.astype(BF16)
             dscore = (probs * (dprob - norm[1, h : h + 1, cols])).astype(BF16)
             results.append((dot_nn(dscore, queries), dot_nn(low, grads), dot_nn(jnp.transpose(keys), dscore)))
@@ -382,11 +397,11 @@
         dk[h, query_cols(n)] += key_part
         dv[h, query_cols(n)] += value_part
 
-    visit_text = functools.partial(visit, TEXT_PART, add_text)
+    visit_text = functools.partial(visit, True, add_text)
     text_keys(labels, blocks, tuple(range(SIDE)), visit_text)
     if 0 in blocks:
         own_text(labels, blocks.index(0), visit_text)
-    text_queries(labels, blocks, functools.partial(visit, VIDEO_PART, add_video))
+    text_queries(labels, blocks, functools.partial(visit, False, add_video))
 
     for i in range(count):
         for h in range(HEADS_LOCAL):
@@ -397,23 +412,22 @@
             dkv_out[i][1, BLOCK:, c] = text_dv[i, h].astype(BF16)
 
 
-def grads_first_kernel(blocks, length_ref, caption_ref, place_ref, *refs):
-    count = len(blocks)
-    q_all, g_all, kv, refs = refs[0], refs[1], refs[2 : 2 + count], refs[2 + count :]
-    stats, dkv_out, (dq_t, norm, *scratch) = refs[:SIDE], refs[SIDE : SIDE + count], refs[SIDE + count :]
+def grads_first_kernel(length_ref, caption_ref, place_ref, *refs):
+    q_all, g_all, kv, refs = refs[0], refs[1], near_keys(refs[2:4], refs[4:6]), refs[6:]
+    stats, dkv_out, (dq_t, norm, *scratch) = refs[:SIDE], refs[SIDE : SIDE + 2], refs[SIDE + 2 :]
     labels = Labels(length_ref, caption_ref, place_ref)
     normalize(stats, norm)
     dq_t[:, :, VIDEO_ROWS:] = jnp.zeros((HEADS_LOCAL, HDIM, TEXT_ROWS), F32)
-    key_grads(labels, blocks, True, q_all, g_all, kv, dkv_out, norm, dq_t, scratch)
-
-
-def grads_last_kernel(blocks, length_ref, caption_ref, place_ref, *refs):
-    count = len(blocks)
-    norm, dq_in, q_all, g_all, kv, refs = *refs[:4], refs[4 : 4 + count], refs[4 + count :]
-    dq_out, dkv_out, (dq_t, *scratch) = refs[:SIDE], refs[SIDE : SIDE + count], refs[SIDE + count :]
+    key_grads(labels, (1, 3), None, q_all, g_all, kv, dkv_out, norm, dq_t, scratch)
+
+
+def grads_last_kernel(length_ref, caption_ref, place_ref, *refs):
+    norm, dq_in, q_all, g_all = refs[:4]
+    kv, refs = [far_keys(refs[4]), Keys(refs[5], refs[6], 0)], refs[7:]
+    dq_out, dkv_out, (dq_t, *scratch) = refs[:SIDE], refs[SIDE : SIDE + 2], refs[SIDE + 2 :]
     labels = Labels(length_ref, caption_ref, place_ref)
-    dq_t[...] = dq_in[...]
-    key_grads(labels, blocks, False, q_all, g_all, kv, dkv_out, norm, dq_t, scratch)
+    dq_t[:, :, VIDEO_ROWS:] = dq_in[:, :, VIDEO_ROWS:]
+    key_grads(labels, (FAR, 0), dq_in, q_all, g_all, kv, dkv_out, norm, dq_t, scratch)
     for n in range(SIDE):
         dq_out[n][:, :, :BLOCK] = (dq_t[:, :, query_cols(n)] * SCALE).astype(BF16)
         dq_out[n][:, :, BLOCK:] = (dq_t[:, :, VIDEO_ROWS + n * HALF : VIDEO_ROWS + (n + 1) * HALF] * SCALE).astype(BF16)
@@ -426,7 +440,7 @@
 DQ_T = (HEADS_LOCAL, HDIM, ROWS)
 STATS = (3, HEADS_LOCAL, ROWS)
 STAGED_QUERIES = jax.ShapeDtypeStruct((SIDE + 2, BLOCK, WIDTH), BF16)
-QUERY_MESSAGE = jax.ShapeDtypeStruct((2, BLOCK, WIDTH), BF16)
+VIDEO_MESSAGE = jax.ShapeDtypeStruct((2, BLOCK, WIDTH), BF16)
 KEY_MESSAGE = jax.ShapeDtypeStruct((2, BLOCK + HALF, WIDTH), BF16)
 
 
@@ -447,60 +461,66 @@
     return pl.CostEstimate(flops=2 * HDIM * matmuls * pairs, bytes_accessed=8 * 1024 * 1024, transcendentals=pairs)
 
 
-def stats_first_call(scalars, qg, kv, text_qg):
-    near_kv, near_qg = [kv[i] for i in NEAR], [qg[j] for j in NEAR]
+def stats_first_call(scalars, qg, kv, text_qg, text_kv):
     return pl.pallas_call(
         stats_first_kernel,
-        in_specs=[SMEM_SPEC] * 3 + [VMEM_SPEC] * (SIDE + 6),
+        in_specs=[SMEM_SPEC] * 3 + [VMEM_SPEC] * (SIDE + 9),
         out_specs=[VMEM_SPEC] * 3,
         out_shape=[jax.ShapeDtypeStruct(STATS, F32), STAGED_QUERIES, STAGED_QUERIES],
         compiler_params=PARAMS,
         cost_estimate=cost(3, 2),
         name="stats_first",
-    )(*scalars, *placed(near_kv), *placed([*near_qg, *text_qg], pltpu.HBM))
-
-
-def stats_last_call(scalars, acc, queries, qg, kv):
+    )(
+        *scalars,
+        *placed([kv[i] for i in NEAR]),
+        *placed([*[text_kv[i] for i in NEAR], *[qg[j] for j in NEAR], *text_qg], pltpu.HBM),
+    )
+
+
+def stats_last_call(scalars, acc, queries, qg, kv, text_kv):
     return pl.pallas_call(
         stats_last_kernel,
-        in_specs=[SMEM_SPEC] * 3 + [VMEM_SPEC] * (SIDE + 4),
+        in_specs=[SMEM_SPEC] * 3 + [VMEM_SPEC] * 11,
         out_specs=[VMEM_SPEC] * 3,
         out_shape=[jax.ShapeDtypeStruct((2, HEADS_LOCAL, ROWS), F32), STAGED_QUERIES, STAGED_QUERIES],
         scratch_shapes=[pltpu.VMEM(STATS, F32)],
         compiler_params=PARAMS,
         cost_estimate=cost(2, 2),
         name="stats_last",
-    )(*scalars, *placed([*[kv[i] for i in NEAR], kv[FAR], acc, *queries, qg[FAR]]))
-
-
-def grads_first_call(blocks, scalars, queries, kv, stats):
-    count = len(blocks)
+    )(
+        *scalars,
+        *placed([kv[i] for i in NEAR]),
+        *placed([text_kv[i] for i in NEAR], pltpu.HBM),
+        *placed([kv[FAR], acc, *queries, qg[FAR]]),
+    )
+
+
+def grads_first_call(scalars, queries, kv, text_kv, stats):
     *dkv, dq_t, norm = pl.pallas_call(
-        functools.partial(grads_first_kernel, blocks),
-        in_specs=[SMEM_SPEC] * 3 + [VMEM_SPEC] * (2 + SIDE + count),
-        out_specs=[VMEM_SPEC] * (count + 2),
-        out_shape=[KEY_MESSAGE] * count
+        grads_first_kernel,
+        in_specs=[SMEM_SPEC] * 3 + [VMEM_SPEC] * (6 + SIDE),
+        out_specs=[VMEM_SPEC] * 4,
+        out_shape=[KEY_MESSAGE] * 2
         + [jax.ShapeDtypeStruct(DQ_T, F32), jax.ShapeDtypeStruct((2, HEADS_LOCAL, ROWS), F32)],
-        scratch_shapes=grads_scratch(count),
+        scratch_shapes=grads_scratch(2),
         compiler_params=PARAMS,
-        cost_estimate=cost(count, 5),
+        cost_estimate=cost(2, 5),
         name="grads_first",
-    )(*scalars, *placed([*queries, *[kv[i] for i in blocks], *stats]))
+    )(*scalars, *placed([*queries, kv[1], kv[3]]), *placed([text_kv[1], text_kv[3]], pltpu.HBM), *placed(stats))
     return dkv, dq_t, norm
 
 
-def grads_last_call(blocks, scalars, queries, kv, dq_t, norm):
-    count = len(blocks)
+def grads_last_call(scalars, queries, kv, text_kv, dq_t, norm):
     out = pl.pallas_call(
-        functools.partial(grads_last_kernel, blocks),
-        in_specs=[SMEM_SPEC] * 3 + [VMEM_SPEC] * (4 + count),
-        out_specs=[VMEM_SPEC] * (SIDE + count),
-        out_shape=[jax.ShapeDtypeStruct((HEADS_LOCAL, HDIM, BLOCK + HALF), BF16)] * SIDE + [KEY_MESSAGE] * count,
-        scratch_shapes=[pltpu.VMEM(DQ_T, F32)] + grads_scratch(count),
+        grads_last_kernel,
+        in_specs=[SMEM_SPEC] * 3 + [VMEM_SPEC] * 7,
+        out_specs=[VMEM_SPEC] * (SIDE + 2),
+        out_shape=[jax.ShapeDtypeStruct((HEADS_LOCAL, HDIM, BLOCK + HALF), BF16)] * SIDE + [KEY_MESSAGE] * 2,
+        scratch_shapes=[pltpu.VMEM(DQ_T, F32)] + grads_scratch(2),
         compiler_params=PARAMS,
-        cost_estimate=cost(count, 5),
+        cost_estimate=cost(2, 5),
         name="grads_last",
-    )(*scalars, *placed([norm]), dq_t, *placed([*queries, *[kv[i] for i in blocks]]))
+    )(*scalars, *placed([norm]), dq_t, *placed([*queries, kv[FAR], kv[0]]), *placed([text_kv[0]], pltpu.HBM))
     return out[:SIDE], out[SIDE:]
 
 
@@ -527,23 +547,26 @@
 ):
     place = lax.axis_index("seq").astype(jnp.int32)
     scalars = (shot_length, caption_length, place.reshape(1))
-    packed, text_qg = pack(video_query, video_key, video_value, video_grad, text_query, text_grad)
+    packed, text_qg, text_kv = pack(
+        video_query, video_key, video_value, video_grad, text_query, text_grad, text_key, text_value
+    )
     text_qg = gathered(text_qg, "y")
+    text_kv = {0: text_kv, 1: swap(text_kv, "z", 1), 3: swap(text_kv, "z", 3)}
     arrived = lax.all_to_all(packed, "head", split_axis=0, concat_axis=0)
-    arrived, text_qg = lax.optimization_barrier((arrived, text_qg))
-    qg, kv = assemble(arrived, text_key, text_value)
+    arrived, text_qg, text_kv = lax.optimization_barrier((arrived, text_qg, text_kv))
+    qg, kv, far_kv = assemble(arrived, text_kv[0])
     qg1, qg3 = swap(qg, "y", 1), swap(qg, "y", 3)
     kv1, kv3 = swap(kv, "z", 1), swap(kv, "z", 3)
     qg2 = swap(qg, "y", FAR)
-    far_kv, qg1, qg3 = lax.optimization_barrier((kv, qg1, qg3))
+    far_kv, qg1, qg3, kv1, kv3 = lax.optimization_barrier((far_kv, qg1, qg3, kv1, kv3))
     qg = [qg, qg1, qg2, qg3]
     kv = [kv, kv1, swap(far_kv, "z", FAR), kv3]
 
-    acc, *queries = stats_first_call(scalars, qg, kv, text_qg)
-    stats, *queries = stats_last_call(scalars, acc, queries, qg, kv)
+    acc, *queries = stats_first_call(scalars, qg, kv, text_qg, text_kv)
+    stats, *queries = stats_last_call(scalars, acc, queries, qg, kv, text_kv)
     stats = gathered(stats, "y")
-    (dkv1, dkv3), dq_t, norm = grads_first_call((1, 3), scalars, queries, kv, stats)
-    dq, (dkv2, dkv0) = grads_last_call((2, 0), scalars, queries, kv, dq_t, norm)
+    (dkv1, dkv3), dq_t, norm = grads_first_call(scalars, queries, kv, text_kv, stats)
+    dq, (dkv2, dkv0) = grads_last_call(scalars, queries, kv, text_kv, dq_t, norm)
 
     dkv1, dkv3 = swap(dkv1, "z", 1), swap(dkv3, "z", 3)
     dq, dkv1, dkv2 = lax.optimization_barrier((dq, dkv1, dkv2))

time: 126 us -> 124 us (0.984)
  waiting for transfers between devices: 37.8 us -> 30.7 us
  blocking collectives: 17.4 us -> 21.2 us
  Pallas kernels: 35.7 us -> 37.1 us
    ppermute x18 -> x20, waiting for transfers between devices: 37.8 us -> 30.7 us  [swap(): lax.ppermute(array, 'seq', [(i, i ^ shift) for i in range(SIDE * SIDE)])]
    all_to_all x1, blocking collectives: 17.4 us -> 21.2 us  [on_device(): lax.all_to_all(video, 'head', split_axis=0, concat_axis=0)]
    ppermute x18 -> x20, starting transfers between devices: 27.8 us -> 27 us  [swap(): lax.ppermute(array, 'seq', [(i, i ^ shift) for i in range(SIDE * SIDE)])]
  transfers between devices with their start and end apart: 19 -> 21, of which waited for: 12 -> 15; matrix products, arithmetic and copies ran while one was open for 0% -> 0% of each run, Pallas kernels for 15% -> 14%
where the time goes in v5:
time: 124 us; the launch traced here: 123 us
  Pallas kernels  37.1 us (30%)
  starting transfers between devices  32.9 us (27%)
  waiting for transfers between devices  30.7 us (25%)
  blocking collectives  21.2 us (17%)
    ppermute x20, waiting for transfers between devices, swap(): lax.ppermute(array, 'seq', [(i, i ^ shift) for i in range(SIDE * SIDE)])  30.7 us
    ppermute x20, starting transfers between devices, swap(): lax.ppermute(array, 'seq', [(i, i ^ shift) for i in range(SIDE * SIDE)])  27 us
    all_to_all x1, blocking collectives, on_device(): lax.all_to_all(video, 'head', split_axis=0, concat_axis=0)  21.2 us
    pallas_call x1, Pallas kernels, grads_last_call(): pl.pallas_call(grads_last_kernel, in_specs=[SMEM_SPEC] * 3 + [VMEM_SPEC]...  9.28 us
    pallas_call x1, Pallas kernels, grads_first_call(): pl.pallas_call(grads_first_kernel, in_specs=[SMEM_SPEC] * 3 + [VMEM_SPEC]...  8.87 us
    pallas_call x1, Pallas kernels, stats_first_call(): pl.pallas_call(stats_first_kernel, in_specs=[SMEM_SPEC] * 3 + [VMEM_SPEC]...  8.25 us
    all_to_all x1, starting transfers between devices, on_device(): arrived = lax.all_to_all(packed, 'head', split_axis=0, concat_axis=0)  5.94 us
    pallas_call x1, Pallas kernels, stats_last_call(): pl.pallas_call(stats_last_kernel, in_specs=[SMEM_SPEC] * 3 + [VMEM_SPEC]...  5.26 us
  transfers between devices with their start and end apart: 21, of which 15 were waited for; matrix products, arithmetic and copies ran while one was open for 0% of the time, Pallas kernels for 14%

profile of v5, /device:TPU:1, one launch (start us, length us, event | category | flops | bytes accessed | tf_op | source)
XLA Modules:
  0.0 123.5 jit_solution(2251519024791020715)
XLA Ops:
  0.6 2.3 %pack_inputs.1 = (bf16[8,4,32,384]{3,2,1,0:T(8,128)(2,1)}, bf16[2,128,384]{2,1,0:T(8,128)(2,1)S(1)}, bf16[2,128,384]{2,1,0:T(8,128)(2,1)S(1)}) custom-call(bf16[32,3072]{1,0:T(8,128)(2,1)} %q_ref.1, bf16[32,3072]{1,0:T(8,128)(2,1)} %k_ref.1, bf16[32,3072]{1,0:T(8,128)(2,1)} %v_ref.1, bf16[32,3072]{1,0:T(8,128)(2,1)} %g_ref.1, bf16[128,384]{1,0:T(8,128)(2,1)} %tq_ref.1, ...), custom_call_target="tpu_custom_call" | custom-call | tf_op jit(solution)/shard_map/pack_inputs/pallas_call | solution.py:55
  3.0 0.0 copy-start.2
  3.0 5.9 %all-to-all-start = ((bf16[8,4,32,384]{3,2,1,0:T(8,128)(2,1)}), bf16[8,4,32,384]{3,2,1,0:T(8,128)(2,1)S(1)}, u32[]{:S(2)}, u32[]{:S(2)}) async-start(bf16[8,4,32,384]{3,2,1,0:T(8,128)(2,1)} %get-tuple-element.54), calls=%async_computation | async-start | bytes 1572864 | tf_op jit(solution)/shard_map/all_to_all | solution.py:555
  8.9 3.8 %collective-permute-start.4 = (bf16[2,128,384]{2,1,0:T(8,128)(2,1)S(1)}, bf16[2,128,384]{2,1,0:T(8,128)(2,1)S(1)}, u32[]{:S(2)}, u32[]{:S(2)}) collective-permute-start(bf16[2,128,384]{2,1,0:T(8,128)(2,1)S(1)} %get-tuple-element.58.text_ref.refs_3_.refs_6_), channel_id=1, source_target_pairs={{0,96},{8,104},{16,112},{24,120},{32,64},{40,72},{48,80},{56,88},{... | collective-permute-start | bytes 589832 | tf_op jit(solution)/shard_map/ppermute | solution.py:529
  12.7 0.0 collective-permute-start.3
  12.7 2.7 %collective-permute-start.2 = (bf16[2,128,384]{2,1,0:T(8,128)(2,1)S(1)}, bf16[2,128,384]{2,1,0:T(8,128)(2,1)S(1)}, u32[]{:S(2)}, u32[]{:S(2)}) collective-permute-start(bf16[2,128,384]{2,1,0:T(8,128)(2,1)S(1)} %get-tuple-element.69.refs_9_), channel_id=1, source_target_pairs={{0,24},{8,16},{16,8},{24,0},{32,56},{40,48},{48,40},{56,32},{64,88... | collective-permute-start | bytes 589832 | tf_op jit(solution)/shard_map/ppermute | solution.py:529
  15.4 0.3 collective-permute-start.1
  15.8 0.2 collective-permute-start
  16.0 2.0 %collective-permute-done.4.refs_5_ = bf16[2,128,384]{2,1,0:T(8,128)(2,1)S(1)} collective-permute-done((bf16[2,128,384]{2,1,0:T(8,128)(2,1)S(1)}, bf16[2,128,384]{2,1,0:T(8,128)(2,1)S(1)}, u32[]{:S(2)}, u32[]{:S(2)}) %collective-permute-start.4) | collective-permute-done | bytes 196640 | tf_op jit(solution)/shard_map/ppermute | solution.py:529
  17.9 0.9 collective-permute-done.3.refs_4_
  18.9 5.1 %collective-permute-done.2.refs_12_ = bf16[2,128,384]{2,1,0:T(8,128)(2,1)S(1)} collective-permute-done((bf16[2,128,384]{2,1,0:T(8,128)(2,1)S(1)}, bf16[2,128,384]{2,1,0:T(8,128)(2,1)S(1)}, u32[]{:S(2)}, u32[]{:S(2)}) %collective-permute-start.2) | collective-permute-done | bytes 196640 | tf_op jit(solution)/shard_map/ppermute | solution.py:529
  24.0 0.0 collective-permute-done.1.refs_11_
  24.0 0.7 collective-permute-done.refs_10_
  24.7 0.0 copy-done.6
  24.8 0.0 copy-done.9
  24.8 0.0 copy-done.10
  24.8 0.7 copy-done.11
  25.5 0.0 all-to-all-done.in_ref
  25.5 0.0 copy-done
  25.5 1.0 assemble_blocks.1
  26.5 0.0 copy-done.4
  26.5 0.0 copy-start.3
  26.5 3.5 %collective-permute-start.6 = (bf16[2,256,384]{2,1,0:T(8,128)(2,1)S(1)}, bf16[2,256,384]{2,1,0:T(8,128)(2,1)S(1)}, u32[]{:S(2)}, u32[]{:S(2)}) collective-permute-start(bf16[2,256,384]{2,1,0:T(8,128)(2,1)S(1)} %get-tuple-element.61.refs_6_), channel_id=1, source_target_pairs={{0,24},{8,16},{16,8},{24,0},{32,56},{40,48},{48,40},{56,32},{64,88... | collective-permute-start | bytes 1179656 | tf_op jit(solution)/shard_map/ppermute | solution.py:529
  30.0 0.0 collective-permute-start.5
  30.0 0.1 collective-permute-start.8
  30.1 1.3 %collective-permute-start.7 = (bf16[2,256,384]{2,1,0:T(8,128)(2,1)S(1)}, bf16[2,256,384]{2,1,0:T(8,128)(2,1)S(1)}, u32[]{:S(2)}, u32[]{:S(2)}) collective-permute-start(bf16[2,256,384]{2,1,0:T(8,128)(2,1)S(1)} %get-tuple-element.59.refs_0_.refs_5_), channel_id=1, source_target_pairs={{0,32},{8,40},{16,48},{24,56},{32,0},{40,8},{48,16},{56,24},{64,96... | collective-permute-start | bytes 1179656 | tf_op jit(solution)/shard_map/ppermute | solution.py:529
  31.4 7.0 %collective-permute-done.6.refs_8_ = bf16[2,256,384]{2,1,0:T(8,128)(2,1)S(1)} collective-permute-done((bf16[2,256,384]{2,1,0:T(8,128)(2,1)S(1)}, bf16[2,256,384]{2,1,0:T(8,128)(2,1)S(1)}, u32[]{:S(2)}, u32[]{:S(2)}) %collective-permute-start.6) | collective-permute-done | bytes 393248 | tf_op jit(solution)/shard_map/ppermute | solution.py:529
  38.4 1.1 collective-permute-done.5.refs_7_
  39.6 1.2 collective-permute-done.8.refs_2_.refs_3_
  40.8 0.0 collective-permute-done.7.refs_1_.refs_2_
  40.8 0.0 copy-done.7
  40.8 1.7 %collective-permute-start.9 = (bf16[2,384,384]{2,1,0:T(8,128)(2,1)S(1)}, bf16[2,384,384]{2,1,0:T(8,128)(2,1)S(1)}, u32[]{:S(2)}, u32[]{:S(2)}) collective-permute-start(bf16[2,384,384]{2,1,0:T(8,128)(2,1)S(1)} %get-tuple-element.66), channel_id=1, source_target_pairs={{0,64},{8,72},{16,80},{24,88},{32,96},{40,104},{48,112},{56,120},{... | collective-permute-start | bytes 1769480 | tf_op jit(solution)/shard_map/ppermute | solution.py:529
  42.4 0.0 copy-done.8
  42.4 1.1 collective-permute-start.10
  43.5 0.0 copy-done.5
  43.5 0.0 copy-done.3
  43.5 0.0 copy-done.1
  43.5 8.3 %stats_first.1 = (f32[3,3,1536]{2,1,0:T(4,128)S(1)}, bf16[6,256,384]{2,1,0:T(8,128)(2,1)S(1)}, bf16[6,256,384]{2,1,0:T(8,128)(2,1)S(1)}) custom-call(s32[8]{0:T(128)S(1)} %copy-done.1, s32[8]{0:T(128)S(1)} %copy-done.2, s32[1]{0:T(128)} %bitcast.place_ref, bf16[2,256,384]{2,1,0:T(8,128)(2,1)S(1)} %get-tuple-element.59.refs_0_.refs_5_, ...), custom_call_target="tpu_custom_call" | custom-call | flops 1207959552 | bytes 8388608 | tf_op jit(solution)/shard_map/stats_first/pallas_call | solution.py:465
  51.8 0.2 collective-permute-done.10.refs_10_
  52.0 3.1 %collective-permute-done.9.refs_6_.refs_4_ = bf16[2,384,384]{2,1,0:T(8,128)(2,1)S(1)} collective-permute-done((bf16[2,384,384]{2,1,0:T(8,128)(2,1)S(1)}, bf16[2,384,384]{2,1,0:T(8,128)(2,1)S(1)}, u32[]{:S(2)}, u32[]{:S(2)}) %collective-permute-start.9) | collective-permute-done | bytes 589856 | tf_op jit(solution)/shard_map/ppermute | solution.py:529
  55.1 5.3 %stats_last.1 = (f32[2,3,1536]{2,1,0:T(4,128)S(1)}, bf16[6,256,384]{2,1,0:T(8,128)(2,1)S(1)}, bf16[6,256,384]{2,1,0:T(8,128)(2,1)S(1)}) custom-call(s32[8]{0:T(128)S(1)} %copy-done.1, s32[8]{0:T(128)S(1)} %copy-done.2, s32[1]{0:T(128)} %bitcast.place_ref, bf16[2,256,384]{2,1,0:T(8,128)(2,1)S(1)} %get-tuple-element.59.refs_0_.refs_5_, ...), custom_call_target="tpu_custom_call" | custom-call | flops 805306368 | bytes 8388608 | tf_op jit(solution)/shard_map/stats_last/pallas_call | solution.py:481
  60.4 1.2 collective-permute-start.13
  61.5 1.7 %collective-permute-start.12 = (f32[2,3,1536]{2,1,0:T(4,128)S(1)}, f32[2,3,1536]{2,1,0:T(4,128)S(1)}, u32[]{:S(2)}, u32[]{:S(2)}) collective-permute-start(f32[2,3,1536]{2,1,0:T(4,128)S(1)} %get-tuple-element.78.refs_6_), channel_id=1, source_target_pairs={{0,16},{8,24},{16,0},{24,8},{32,48},{40,56},{48,32},{56,40},{64,80... | collective-permute-start | bytes 110600 | tf_op jit(solution)/shard_map/ppermute | solution.py:529
  63.2 0.5 collective-permute-start.11
  63.7 0.9 collective-permute-done.13.refs_9_
  64.6 1.4 %collective-permute-done.12.refs_8_ = f32[2,3,1536]{2,1,0:T(4,128)S(1)} collective-permute-done((f32[2,3,1536]{2,1,0:T(4,128)S(1)}, f32[2,3,1536]{2,1,0:T(4,128)S(1)}, u32[]{:S(2)}, u32[]{:S(2)}) %collective-permute-start.12) | collective-permute-done | bytes 36896 | tf_op jit(solution)/shard_map/ppermute | solution.py:529
  66.0 0.1 collective-permute-done.11.refs_7_
  66.1 8.9 %grads_first.1 = (bf16[2,384,384]{2,1,0:T(8,128)(2,1)S(1)}, bf16[2,384,384]{2,1,0:T(8,128)(2,1)S(1)}, f32[3,128,1536]{2,1,0:T(8,128)S(1)}, f32[2,3,1536]{2,1,0:T(4,128)S(1)}) custom-call(s32[8]{0:T(128)S(1)} %copy-done.1, s32[8]{0:T(128)S(1)} %copy-done.2, s32[1]{0:T(128)} %bitcast.place_ref, bf16[6,256,384]{2,1,0:T(8,128)(2,1)S(1)} %get-tuple-element.76.refs_0_.refs_2_, ...), custom_call_target="tpu_custom_call" | custom-call | flops 2013265920 | bytes 8388608 | tf_op jit(solution)/shard_map/grads_first/pallas_call | solution.py:499
  75.0 1.8 %collective-permute-start.14 = (bf16[2,384,384]{2,1,0:T(8,128)(2,1)S(1)}, bf16[2,384,384]{2,1,0:T(8,128)(2,1)S(1)}, u32[]{:S(2)}, u32[]{:S(2)}) collective-permute-start(bf16[2,384,384]{2,1,0:T(8,128)(2,1)S(1)} %get-tuple-element.85), channel_id=1, source_target_pairs={{0,32},{8,40},{16,48},{24,56},{32,0},{40,8},{48,16},{56,24},{64,96... | collective-permute-start | bytes 1769480 | tf_op jit(solution)/shard_map/ppermute | solution.py:529
  76.8 0.0 collective-permute-start.19
  76.8 9.3 %grads_last.1 = (bf16[3,128,384]{2,1,0:T(8,128)(2,1)S(1)}, bf16[3,128,384]{2,1,0:T(8,128)(2,1)S(1)}, bf16[3,128,384]{2,1,0:T(8,128)(2,1)S(1)}, bf16[3,128,384]{2...) custom-call(s32[8]{0:T(128)S(1)} %copy-done.1, s32[8]{0:T(128)S(1)} %copy-done.2, ...), custom_call_target="tpu_custom_call" | custom-call | flops 2013265920 | bytes 8388608 | tf_op jit(solution)/shard_map/grads_last/pallas_call | solution.py:514
  86.1 0.0 collective-permute-done.14.refs_5_
  86.1 3.3 %collective-permute-start.18 = (bf16[2,384,384]{2,1,0:T(8,128)(2,1)S(1)}, bf16[2,384,384]{2,1,0:T(8,128)(2,1)S(1)}, u32[]{:S(2)}, u32[]{:S(2)}) collective-permute-start(bf16[2,384,384]{2,1,0:T(8,128)(2,1)S(1)} %get-tuple-element.93), channel_id=1, source_target_pairs={{0,64},{8,72},{16,80},{24,88},{32,96},{40,104},{48,112},{56,120},{... | collective-permute-start | bytes 1769480 | tf_op jit(solution)/shard_map/ppermute | solution.py:529
  89.4 0.2 collective-permute-start.15
  89.6 0.0 collective-permute-start.16
  89.6 3.6 %collective-permute-start.17 = (bf16[3,128,384]{2,1,0:T(8,128)(2,1)S(1)}, bf16[3,128,384]{2,1,0:T(8,128)(2,1)S(1)}, u32[]{:S(2)}, u32[]{:S(2)}) collective-permute-start(bf16[3,128,384]{2,1,0:T(8,128)(2,1)S(1)} %get-tuple-element.90), channel_id=1, source_target_pairs={{0,24},{8,16},{16,8},{24,0},{32,56},{40,48},{48,40},{56,32},{64,88... | collective-permute-start | bytes 884744 | tf_op jit(solution)/shard_map/ppermute | solution.py:529
  93.2 0.0 collective-permute-done.19.refs_7_
  93.2 2.0 %collective-permute-done.15.refs_1_ = bf16[3,128,384]{2,1,0:T(8,128)(2,1)S(1)} collective-permute-done((bf16[3,128,384]{2,1,0:T(8,128)(2,1)S(1)}, bf16[3,128,384]{2,1,0:T(8,128)(2,1)S(1)}, u32[]{:S(2)}, u32[]{:S(2)}) %collective-permute-start.15) | collective-permute-done | bytes 294944 | tf_op jit(solution)/shard_map/ppermute | solution.py:529
  95.3 3.9 %collective-permute-done.16.refs_2_ = bf16[3,128,384]{2,1,0:T(8,128)(2,1)S(1)} collective-permute-done((bf16[3,128,384]{2,1,0:T(8,128)(2,1)S(1)}, bf16[3,128,384]{2,1,0:T(8,128)(2,1)S(1)}, u32[]{:S(2)}, u32[]{:S(2)}) %collective-permute-start.16) | collective-permute-done | bytes 294944 | tf_op jit(solution)/shard_map/ppermute | solution.py:529
  99.2 1.0 collective-permute-done.17.refs_3_
  100.2 0.0 collective-permute-done.18.refs_6_
  100.2 1.2 %sum_terms.1 = (bf16[8,3,32,384]{3,2,1,0:T(8,128)(2,1)S(1)}, bf16[128,384]{1,0:T(8,128)(2,1)}, bf16[128,384]{1,0:T(8,128)(2,1)}, bf16[128,384]{1,0:T(8,128)(2,1)}) custom-call(bf16[3,128,384]{2,1,0:T(8,128)(2,1)S(1)} %get-tuple-element.87.refs_0_, bf16[3,128,384]{2,1,0:T(8,128)(2,1)S(1)} %collective-permute-done.15.refs_1_, ...), custom_call_target="tpu_custom_call" | custom-call | tf_op jit(solution)/shard_map/sum_terms/pallas_call | solution.py:107
  101.4 21.2 %all_to_all.10.in_ref = bf16[8,3,32,384]{3,2,1,0:T(8,128)(2,1)S(1)} all-to-all(bf16[8,3,32,384]{3,2,1,0:T(8,128)(2,1)S(1)} %get-tuple-element.95), channel_id=1, replica_groups=mesh['seq'=16,'head'=8] {'head'}, dimensions={0} | all-to-all | bytes 1179648 | tf_op jit(solution)/shard_map/all_to_all | solution.py:576
  122.6 0.9 unpack_video.1
  (11 shorter events, 0.0 us)
Async XLA Ops:
  2.9 22.5 %copy-start = (bf16[2,128,384]{2,1,0:T(8,128)(2,1)}, bf16[2,128,384]{2,1,0:T(8,128)(2,1)S(1)}, u32[]{:S(2)}) copy-start(bf16[2,128,384]{2,1,0:T(8,128)(2,1)S(1)} %get-tuple-element.58.text_ref.refs_3_.refs_6_) | copy-start | bytes 589828
  3.0 23.6 %copy-start.4 = (bf16[2,128,384]{2,1,0:T(8,128)(2,1)}, bf16[2,128,384]{2,1,0:T(8,128)(2,1)S(1)}, u32[]{:S(2)}) copy-start(bf16[2,128,384]{2,1,0:T(8,128)(2,1)S(1)} %get-tuple-element.69.refs_9_) | copy-start | bytes 589828
  3.0 40.6 %copy-start.1 = (s32[8]{0:T(128)S(1)}, s32[8]{0:T(128)}, u32[]{:S(2)}) copy-start(s32[8]{0:T(128)} %length_ref.7) | copy-start | bytes 100
  3.0 40.6 %copy-start.2 = (s32[8]{0:T(128)S(1)}, s32[8]{0:T(128)}, u32[]{:S(2)}) copy-start(s32[8]{0:T(128)} %caption_ref.7) | copy-start | bytes 100
  3.0 22.5 %all-to-all-start = ((bf16[8,4,32,384]{3,2,1,0:T(8,128)(2,1)}), bf16[8,4,32,384]{3,2,1,0:T(8,128)(2,1)S(1)}, u32[]{:S(2)}, u32[]{:S(2)}) async-start(bf16[8,4,32,384]{3,2,1,0:T(8,128)(2,1)} %get-tuple-element.54), calls=%async_computation | async-start | bytes 1572864 | tf_op jit(solution)/shard_map/all_to_all | solution.py:555
  8.9 9.0 %collective-permute-start.4 = (bf16[2,128,384]{2,1,0:T(8,128)(2,1)S(1)}, bf16[2,128,384]{2,1,0:T(8,128)(2,1)S(1)}, u32[]{:S(2)}, u32[]{:S(2)}) collective-permute-start(bf16[2,128,384]{2,1,0:T(8,128)(2,1)S(1)} %get-tuple-element.58.text_ref.refs_3_.refs_6_), channel_id=1, source_target_pairs={{0,96},{8,104},{16,112},{24,120},{32,64},{40,72},{48,80},{56,88},{... | collective-permute-start | bytes 589832 | tf_op jit(solution)/shard_map/ppermute | solution.py:529
  12.7 6.2 %collective-permute-start.3 = (bf16[2,128,384]{2,1,0:T(8,128)(2,1)S(1)}, bf16[2,128,384]{2,1,0:T(8,128)(2,1)S(1)}, u32[]{:S(2)}, u32[]{:S(2)}) collective-permute-start(bf16[2,128,384]{2,1,0:T(8,128)(2,1)S(1)} %get-tuple-element.58.text_ref.refs_3_.refs_6_), channel_id=1, source_target_pairs={{0,32},{8,40},{16,48},{24,56},{32,0},{40,8},{48,16},{56,24},{64,96... | collective-permute-start | bytes 589832 | tf_op jit(solution)/shard_map/ppermute | solution.py:529
  12.7 11.3 %collective-permute-start.2 = (bf16[2,128,384]{2,1,0:T(8,128)(2,1)S(1)}, bf16[2,128,384]{2,1,0:T(8,128)(2,1)S(1)}, u32[]{:S(2)}, u32[]{:S(2)}) collective-permute-start(bf16[2,128,384]{2,1,0:T(8,128)(2,1)S(1)} %get-tuple-element.69.refs_9_), channel_id=1, source_target_pairs={{0,24},{8,16},{16,8},{24,0},{32,56},{40,48},{48,40},{56,32},{64,88... | collective-permute-start | bytes 589832 | tf_op jit(solution)/shard_map/ppermute | solution.py:529
  15.4 8.6 %collective-permute-start.1 = (bf16[2,128,384]{2,1,0:T(8,128)(2,1)S(1)}, bf16[2,128,384]{2,1,0:T(8,128)(2,1)S(1)}, u32[]{:S(2)}, u32[]{:S(2)}) collective-permute-start(bf16[2,128,384]{2,1,0:T(8,128)(2,1)S(1)} %get-tuple-element.69.refs_9_), channel_id=1, source_target_pairs={{0,16},{8,24},{16,0},{24,8},{32,48},{40,56},{48,32},{56,40},{64,80... | collective-permute-start | bytes 589832 | tf_op jit(solution)/shard_map/ppermute | solution.py:529
  15.8 9.0 %collective-permute-start = (bf16[2,128,384]{2,1,0:T(8,128)(2,1)S(1)}, bf16[2,128,384]{2,1,0:T(8,128)(2,1)S(1)}, u32[]{:S(2)}, u32[]{:S(2)}) collective-permute-start(bf16[2,128,384]{2,1,0:T(8,128)(2,1)S(1)} %get-tuple-element.69.refs_9_), channel_id=1, source_target_pairs={{0,8},{8,0},{16,24},{24,16},{32,40},{40,32},{48,56},{56,48},{64,72... | collective-permute-start | bytes 589832 | tf_op jit(solution)/shard_map/ppermute | solution.py:529
  17.9 25.6 %copy-start.5 = (bf16[2,128,384]{2,1,0:T(8,128)(2,1)}, bf16[2,128,384]{2,1,0:T(8,128)(2,1)S(1)}, u32[]{:S(2)}) copy-start(bf16[2,128,384]{2,1,0:T(8,128)(2,1)S(1)} %collective-permute-done.4.refs_5_) | copy-start | bytes 589828
  18.9 5.9 %copy-start.6 = (bf16[2,128,384]{2,1,0:T(8,128)(2,1)}, bf16[2,128,384]{2,1,0:T(8,128)(2,1)S(1)}, u32[]{:S(2)}) copy-start(bf16[2,128,384]{2,1,0:T(8,128)(2,1)S(1)} %collective-permute-done.3.refs_4_) | copy-start | bytes 589828
  24.0 0.7 copy-start.9
  24.0 0.7 copy-start.10
  24.8 0.7 copy-start.11
  26.5 17.0 %copy-start.3 = (bf16[2,256,384]{2,1,0:T(8,128)(2,1)}, bf16[2,256,384]{2,1,0:T(8,128)(2,1)S(1)}, u32[]{:S(2)}) copy-start(bf16[2,256,384]{2,1,0:T(8,128)(2,1)S(1)} %get-tuple-element.61.refs_6_) | copy-start | bytes 1179652
  26.5 11.9 %collective-permute-start.6 = (bf16[2,256,384]{2,1,0:T(8,128)(2,1)S(1)}, bf16[2,256,384]{2,1,0:T(8,128)(2,1)S(1)}, u32[]{:S(2)}, u32[]{:S(2)}) collective-permute-start(bf16[2,256,384]{2,1,0:T(8,128)(2,1)S(1)} %get-tuple-element.61.refs_6_), channel_id=1, source_target_pairs={{0,24},{8,16},{16,8},{24,0},{32,56},{40,48},{48,40},{56,32},{64,88... | collective-permute-start | bytes 1179656 | tf_op jit(solution)/shard_map/ppermute | solution.py:529
  30.0 9.6 %collective-permute-start.5 = (bf16[2,256,384]{2,1,0:T(8,128)(2,1)S(1)}, bf16[2,256,384]{2,1,0:T(8,128)(2,1)S(1)}, u32[]{:S(2)}, u32[]{:S(2)}) collective-permute-start(bf16[2,256,384]{2,1,0:T(8,128)(2,1)S(1)} %get-tuple-element.61.refs_6_), channel_id=1, source_target_pairs={{0,8},{8,0},{16,24},{24,16},{32,40},{40,32},{48,56},{56,48},{64,72... | collective-permute-start | bytes 1179656 | tf_op jit(solution)/shard_map/ppermute | solution.py:529
  30.0 10.8 %collective-permute-start.8 = (bf16[2,256,384]{2,1,0:T(8,128)(2,1)S(1)}, bf16[2,256,384]{2,1,0:T(8,128)(2,1)S(1)}, u32[]{:S(2)}, u32[]{:S(2)}) collective-permute-start(bf16[2,256,384]{2,1,0:T(8,128)(2,1)S(1)} %get-tuple-element.59.refs_0_.refs_5_), channel_id=1, source_target_pairs={{0,96},{8,104},{16,112},{24,120},{32,64},{40,72},{48,80},{56,88},{... | collective-permute-start | bytes 1179656 | tf_op jit(solution)/shard_map/ppermute | solution.py:529
  30.1 10.6 %collective-permute-start.7 = (bf16[2,256,384]{2,1,0:T(8,128)(2,1)S(1)}, bf16[2,256,384]{2,1,0:T(8,128)(2,1)S(1)}, u32[]{:S(2)}, u32[]{:S(2)}) collective-permute-start(bf16[2,256,384]{2,1,0:T(8,128)(2,1)S(1)} %get-tuple-element.59.refs_0_.refs_5_), channel_id=1, source_target_pairs={{0,32},{8,40},{16,48},{24,56},{32,0},{40,8},{48,16},{56,24},{64,96... | collective-permute-start | bytes 1179656 | tf_op jit(solution)/shard_map/ppermute | solution.py:529
  38.4 2.3 %copy-start.7 = (bf16[2,256,384]{2,1,0:T(8,128)(2,1)}, bf16[2,256,384]{2,1,0:T(8,128)(2,1)S(1)}, u32[]{:S(2)}) copy-start(bf16[2,256,384]{2,1,0:T(8,128)(2,1)S(1)} %collective-permute-done.6.refs_8_) | copy-start | bytes 1179652
  39.6 2.9 %copy-start.8 = (bf16[2,256,384]{2,1,0:T(8,128)(2,1)}, bf16[2,256,384]{2,1,0:T(8,128)(2,1)S(1)}, u32[]{:S(2)}) copy-start(bf16[2,256,384]{2,1,0:T(8,128)(2,1)S(1)} %collective-permute-done.5.refs_7_) | copy-start | bytes 1179652
  40.8 14.3 %collective-permute-start.9 = (bf16[2,384,384]{2,1,0:T(8,128)(2,1)S(1)}, bf16[2,384,384]{2,1,0:T(8,128)(2,1)S(1)}, u32[]{:S(2)}, u32[]{:S(2)}) collective-permute-start(bf16[2,384,384]{2,1,0:T(8,128)(2,1)S(1)} %get-tuple-element.66), channel_id=1, source_target_pairs={{0,64},{8,72},{16,80},{24,88},{32,96},{40,104},{48,112},{56,120},{... | collective-permute-start | bytes 1769480 | tf_op jit(solution)/shard_map/ppermute | solution.py:529
  42.4 9.5 %collective-permute-start.10 = (bf16[2,256,384]{2,1,0:T(8,128)(2,1)S(1)}, bf16[2,256,384]{2,1,0:T(8,128)(2,1)S(1)}, u32[]{:S(2)}, u32[]{:S(2)}) collective-permute-start(bf16[2,256,384]{2,1,0:T(8,128)(2,1)S(1)} %get-tuple-element.61.refs_6_), channel_id=1, source_target_pairs={{0,16},{8,24},{16,0},{24,8},{32,48},{40,56},{48,32},{56,40},{64,80... | collective-permute-start | bytes 1179656 | tf_op jit(solution)/shard_map/ppermute | solution.py:529
  60.4 4.2 %collective-permute-start.13 = (f32[2,3,1536]{2,1,0:T(4,128)S(1)}, f32[2,3,1536]{2,1,0:T(4,128)S(1)}, u32[]{:S(2)}, u32[]{:S(2)}) collective-permute-start(f32[2,3,1536]{2,1,0:T(4,128)S(1)} %get-tuple-element.78.refs_6_), channel_id=1, source_target_pairs={{0,24},{8,16},{16,8},{24,0},{32,56},{40,48},{48,40},{56,32},{64,88... | collective-permute-start | bytes 110600 | tf_op jit(solution)/shard_map/ppermute | solution.py:529
  61.5 4.4 %collective-permute-start.12 = (f32[2,3,1536]{2,1,0:T(4,128)S(1)}, f32[2,3,1536]{2,1,0:T(4,128)S(1)}, u32[]{:S(2)}, u32[]{:S(2)}) collective-permute-start(f32[2,3,1536]{2,1,0:T(4,128)S(1)} %get-tuple-element.78.refs_6_), channel_id=1, source_target_pairs={{0,16},{8,24},{16,0},{24,8},{32,48},{40,56},{48,32},{56,40},{64,80... | collective-permute-start | bytes 110600 | tf_op jit(solution)/shard_map/ppermute | solution.py:529
  63.2 2.9 %collective-permute-start.11 = (f32[2,3,1536]{2,1,0:T(4,128)S(1)}, f32[2,3,1536]{2,1,0:T(4,128)S(1)}, u32[]{:S(2)}, u32[]{:S(2)}) collective-permute-start(f32[2,3,1536]{2,1,0:T(4,128)S(1)} %get-tuple-element.78.refs_6_), channel_id=1, source_target_pairs={{0,8},{8,0},{16,24},{24,16},{32,40},{40,32},{48,56},{56,48},{64,72... | collective-permute-start | bytes 110600 | tf_op jit(solution)/shard_map/ppermute | solution.py:529
  75.0 11.0 %collective-permute-start.14 = (bf16[2,384,384]{2,1,0:T(8,128)(2,1)S(1)}, bf16[2,384,384]{2,1,0:T(8,128)(2,1)S(1)}, u32[]{:S(2)}, u32[]{:S(2)}) collective-permute-start(bf16[2,384,384]{2,1,0:T(8,128)(2,1)S(1)} %get-tuple-element.85), channel_id=1, source_target_pairs={{0,32},{8,40},{16,48},{24,56},{32,0},{40,8},{48,16},{56,24},{64,96... | collective-permute-start | bytes 1769480 | tf_op jit(solution)/shard_map/ppermute | solution.py:529
  76.8 16.5 %collective-permute-start.19 = (bf16[2,384,384]{2,1,0:T(8,128)(2,1)S(1)}, bf16[2,384,384]{2,1,0:T(8,128)(2,1)S(1)}, u32[]{:S(2)}, u32[]{:S(2)}) collective-permute-start(bf16[2,384,384]{2,1,0:T(8,128)(2,1)S(1)} %get-tuple-element.94), channel_id=1, source_target_pairs={{0,96},{8,104},{16,112},{24,120},{32,64},{40,72},{48,80},{56,88},{... | collective-permute-start | bytes 1769480 | tf_op jit(solution)/shard_map/ppermute | solution.py:529
  86.1 14.1 %collective-permute-start.18 = (bf16[2,384,384]{2,1,0:T(8,128)(2,1)S(1)}, bf16[2,384,384]{2,1,0:T(8,128)(2,1)S(1)}, u32[]{:S(2)}, u32[]{:S(2)}) collective-permute-start(bf16[2,384,384]{2,1,0:T(8,128)(2,1)S(1)} %get-tuple-element.93), channel_id=1, source_target_pairs={{0,64},{8,72},{16,80},{24,88},{32,96},{40,104},{48,112},{56,120},{... | collective-permute-start | bytes 1769480 | tf_op jit(solution)/shard_map/ppermute | solution.py:529
  89.4 5.9 %collective-permute-start.15 = (bf16[3,128,384]{2,1,0:T(8,128)(2,1)S(1)}, bf16[3,128,384]{2,1,0:T(8,128)(2,1)S(1)}, u32[]{:S(2)}, u32[]{:S(2)}) collective-permute-start(bf16[3,128,384]{2,1,0:T(8,128)(2,1)S(1)} %get-tuple-element.88), channel_id=1, source_target_pairs={{0,8},{8,0},{16,24},{24,16},{32,40},{40,32},{48,56},{56,48},{64,72... | collective-permute-start | bytes 884744 | tf_op jit(solution)/shard_map/ppermute | solution.py:529
  89.6 9.6 %collective-permute-start.16 = (bf16[3,128,384]{2,1,0:T(8,128)(2,1)S(1)}, bf16[3,128,384]{2,1,0:T(8,128)(2,1)S(1)}, u32[]{:S(2)}, u32[]{:S(2)}) collective-permute-start(bf16[3,128,384]{2,1,0:T(8,128)(2,1)S(1)} %get-tuple-element.89), channel_id=1, source_target_pairs={{0,16},{8,24},{16,0},{24,8},{32,48},{40,56},{48,32},{56,40},{64,80... | collective-permute-start | bytes 884744 | tf_op jit(solution)/shard_map/ppermute | solution.py:529
  89.6 10.5 %collective-permute-start.17 = (bf16[3,128,384]{2,1,0:T(8,128)(2,1)S(1)}, bf16[3,128,384]{2,1,0:T(8,128)(2,1)S(1)}, u32[]{:S(2)}, u32[]{:S(2)}) collective-permute-start(bf16[3,128,384]{2,1,0:T(8,128)(2,1)S(1)} %get-tuple-element.90), channel_id=1, source_target_pairs={{0,24},{8,16},{16,8},{24,0},{32,56},{40,48},{48,40},{56,32},{64,88... | collective-permute-start | bytes 884744 | tf_op jit(solution)/shard_map/ppermute | solution.py:529

commit v6 on v5

--- a/solution.py
+++ b/solution.py
@@ -55,22 +55,22 @@
     return call(*placed(arrays, pltpu.HBM))
 
 
-def assemble_kernel(in_ref, text_ref, qg_ref, kv_ref, far_ref):
+def assemble_kernel(in_ref, text_qg_ref, text_kv_ref, qg_ref, kv_ref, far_qg_ref, far_kv_ref):
     for n in range(2):
-        qg_ref[n] = in_ref[:, n].reshape(BLOCK, WIDTH)
-        rows = in_ref[:, 2 + n].reshape(BLOCK, WIDTH)
-        kv_ref[n] = rows
-        far_ref[n, :BLOCK] = rows
-        far_ref[n, BLOCK:] = text_ref[n]
-
-
-def assemble(arrived, text_kv):
+        for at, text, near, far in ((0, text_qg_ref, qg_ref, far_qg_ref), (2, text_kv_ref, kv_ref, far_kv_ref)):
+            rows = in_ref[:, at + n].reshape(BLOCK, WIDTH)
+            near[n] = rows
+            far[n, :BLOCK] = rows
+            far[n, BLOCK:] = text[n]
+
+
+def assemble(arrived, text_qg, text_kv):
     return pl.pallas_call(
         assemble_kernel,
-        out_shape=(VIDEO_MESSAGE, VIDEO_MESSAGE, KEY_MESSAGE),
+        out_shape=(VIDEO_MESSAGE, VIDEO_MESSAGE, KEY_MESSAGE, KEY_MESSAGE),
         compiler_params=SMALL,
         name="assemble_blocks",
-    )(*placed([arrived]), *placed([text_kv], pltpu.HBM))
+    )(*placed([arrived]), *placed([text_qg, text_kv], pltpu.HBM))
 
 
 def unpack_kernel(in_ref, q_ref, k_ref, v_ref):
@@ -149,12 +149,13 @@
         return row < self.caption_ref[shot]
 
 
-def stage_text_queries(labels, text_qg, q_all, g_all):
-    for u in range(SIDE):
-        p, rows = u // 2, slice(u % 2 * HALF, (u % 2 + 1) * HALF)
-        q_all[SIDE + p, rows] = text_qg[u][0]
-        live = labels.live(labels.query_shot(p), (labels.y ^ u) % 2)
-        g_all[SIDE + p, rows] = jnp.where(live, text_qg[u][1], jnp.zeros((HALF, WIDTH), BF16))
+def stage_text_queries(labels, p, parts, q_all, g_all):
+    shot = labels.query_shot(p)
+    for e, (ref, at) in enumerate(parts):
+        rows, source = slice(e * HALF, (e + 1) * HALF), slice(at, at + HALF)
+        q_all[SIDE + p, rows] = ref[0, source]
+        live = labels.live(shot, (labels.y ^ e) % 2)
+        g_all[SIDE + p, rows] = jnp.where(live, ref[1, source], jnp.zeros((HALF, WIDTH), BF16))
 
 
 class Keys:
@@ -208,7 +209,7 @@
     visit(n, SIDE, jnp.broadcast_to(live, (HALF, BLOCK)))
 
 
-def text_queries(labels, blocks, visit):
+def text_queries(labels, blocks, pairs, visit):
     for n, block in enumerate(blocks):
         base = labels.key_base(block)
 
@@ -221,7 +222,8 @@
                 same = jnp.logical_and(row >= begin, row < end)
                 visit(n, SIDE + p, jnp.broadcast_to(same, (BLOCK, BLOCK)))
 
-        loop(2, step)
+        for p in pairs:
+            step(p)
 
 
 def head_ds(h):
@@ -292,35 +294,37 @@
 
 def stats_first_kernel(length_ref, caption_ref, place_ref, *refs):
     kv, refs = near_keys(refs[:3], refs[3:6]), refs[6:]
-    qg, text_qg, (acc, q_all, g_all) = refs[:3], refs[3 : SIDE + 3], refs[SIDE + 3 :]
+    qg, text_qg, (acc, q_all, g_all) = refs[:3], refs[3:5], refs[5:]
     labels = Labels(length_ref, caption_ref, place_ref)
     for j, ref in zip(NEAR, qg):
         q_all[j] = ref[0]
         g_all[j] = ref[1]
-    stage_text_queries(labels, text_qg, q_all, g_all)
+    stage_text_queries(labels, 0, [(ref, 0) for ref in text_qg], q_all, g_all)
     acc[0] = jnp.full((HEADS_LOCAL, ROWS), LOW, F32)
     acc[1:3] = jnp.zeros((2, HEADS_LOCAL, ROWS), F32)
     video_stats(acc, q_all, g_all, kv, NEAR, True)
     visit = functools.partial(visit_stats, acc, q_all, g_all, kv)
     text_keys(labels, NEAR, NEAR, functools.partial(visit, True))
     own_text(labels, 0, functools.partial(visit, True))
-    text_queries(labels, NEAR, functools.partial(visit, False))
+    text_queries(labels, NEAR, (0,), functools.partial(visit, False))
 
 
 def stats_last_kernel(length_ref, caption_ref, place_ref, *refs):
     kv, far_kv = near_keys(refs[:3], refs[3:6]), [far_keys(refs[6])]
-    acc_in, q_in, g_in, far_qg, out_ref, q_all, g_all, acc = refs[7:]
+    acc_in, q_in, g_in, far_qg, text_qg, out_ref, q_all, g_all, acc = refs[7:]
     labels = Labels(length_ref, caption_ref, place_ref)
-    for j in range(SIDE + 2):
-        q_all[j] = far_qg[0] if j == FAR else q_in[j]
-        g_all[j] = far_qg[1] if j == FAR else g_in[j]
+    for j in range(SIDE + 1):
+        q_all[j] = far_qg[0, :BLOCK] if j == FAR else q_in[j]
+        g_all[j] = far_qg[1, :BLOCK] if j == FAR else g_in[j]
+    stage_text_queries(labels, 1, [(far_qg, BLOCK), (text_qg, 0)], q_all, g_all)
     acc[...] = acc_in[...]
     video_stats(acc, q_all, g_all, kv, (FAR,), True)
     video_stats(acc, q_all, g_all, far_kv, range(SIDE), False)
     visit = functools.partial(visit_stats, acc, q_all, g_all)
     text_keys(labels, NEAR, (FAR,), functools.partial(visit, kv, True))
     text_keys(labels, (FAR,), tuple(range(SIDE)), functools.partial(visit, far_kv, True))
-    text_queries(labels, (FAR,), functools.partial(visit, far_kv, False))
+    text_queries(labels, NEAR, (1,), functools.partial(visit, kv, False))
+    text_queries(labels, (FAR,), (0, 1), functools.partial(visit, far_kv, False))
     total = acc[1]
     some = total > 0.0
     total = jnp.where(some, total, 1.0)
@@ -401,7 +405,7 @@
     text_keys(labels, blocks, tuple(range(SIDE)), visit_text)
     if 0 in blocks:
         own_text(labels, blocks.index(0), visit_text)
-    text_queries(labels, blocks, functools.partial(visit, False, add_video))
+    text_queries(labels, blocks, (0, 1), functools.partial(visit, False, add_video))
 
     for i in range(count):
         for h in range(HEADS_LOCAL):
@@ -464,7 +468,7 @@
 def stats_first_call(scalars, qg, kv, text_qg, text_kv):
     return pl.pallas_call(
         stats_first_kernel,
-        in_specs=[SMEM_SPEC] * 3 + [VMEM_SPEC] * (SIDE + 9),
+        in_specs=[SMEM_SPEC] * 3 + [VMEM_SPEC] * 11,
         out_specs=[VMEM_SPEC] * 3,
         out_shape=[jax.ShapeDtypeStruct(STATS, F32), STAGED_QUERIES, STAGED_QUERIES],
         compiler_params=PARAMS,
@@ -473,14 +477,14 @@
     )(
         *scalars,
         *placed([kv[i] for i in NEAR]),
-        *placed([*[text_kv[i] for i in NEAR], *[qg[j] for j in NEAR], *text_qg], pltpu.HBM),
+        *placed([*[text_kv[i] for i in NEAR], *[qg[j] for j in NEAR], text_qg[0], text_qg[1]], pltpu.HBM),
     )
 
 
-def stats_last_call(scalars, acc, queries, qg, kv, text_kv):
+def stats_last_call(scalars, acc, queries, qg, kv, text_qg, text_kv):
     return pl.pallas_call(
         stats_last_kernel,
-        in_specs=[SMEM_SPEC] * 3 + [VMEM_SPEC] * 11,
+        in_specs=[SMEM_SPEC] * 3 + [VMEM_SPEC] * 12,
         out_specs=[VMEM_SPEC] * 3,
         out_shape=[jax.ShapeDtypeStruct((2, HEADS_LOCAL, ROWS), F32), STAGED_QUERIES, STAGED_QUERIES],
         scratch_shapes=[pltpu.VMEM(STATS, F32)],
@@ -492,6 +496,7 @@
         *placed([kv[i] for i in NEAR]),
         *placed([text_kv[i] for i in NEAR], pltpu.HBM),
         *placed([kv[FAR], acc, *queries, qg[FAR]]),
+        *placed([text_qg[3]], pltpu.HBM),
     )
 
 
@@ -550,20 +555,19 @@
     packed, text_qg, text_kv = pack(
         video_query, video_key, video_value, video_grad, text_query, text_grad, text_key, text_value
     )
-    text_qg = gathered(text_qg, "y")
+    text_qg = {0: text_qg, 1: swap(text_qg, "y", 1), 3: swap(text_qg, "y", 3)}
     text_kv = {0: text_kv, 1: swap(text_kv, "z", 1), 3: swap(text_kv, "z", 3)}
     arrived = lax.all_to_all(packed, "head", split_axis=0, concat_axis=0)
     arrived, text_qg, text_kv = lax.optimization_barrier((arrived, text_qg, text_kv))
-    qg, kv, far_kv = assemble(arrived, text_kv[0])
+    qg, kv, far_qg, far_kv = assemble(arrived, text_qg[0], text_kv[0])
     qg1, qg3 = swap(qg, "y", 1), swap(qg, "y", 3)
     kv1, kv3 = swap(kv, "z", 1), swap(kv, "z", 3)
-    qg2 = swap(qg, "y", FAR)
-    far_kv, qg1, qg3, kv1, kv3 = lax.optimization_barrier((far_kv, qg1, qg3, kv1, kv3))
-    qg = [qg, qg1, qg2, qg3]
+    far_qg, far_kv, qg1, qg3, kv1, kv3 = lax.optimization_barrier((far_qg, far_kv, qg1, qg3, kv1, kv3))
+    qg = [qg, qg1, swap(far_qg, "y", FAR), qg3]
     kv = [kv, kv1, swap(far_kv, "z", FAR), kv3]
 
     acc, *queries = stats_first_call(scalars, qg, kv, text_qg, text_kv)
-    stats, *queries = stats_last_call(scalars, acc, queries, qg, kv, text_kv)
+    stats, *queries = stats_last_call(scalars, acc, queries, qg, kv, text_qg, text_kv)
     stats = gathered(stats, "y")
     (dkv1, dkv3), dq_t, norm = grads_first_call(scalars, queries, kv, text_kv, stats)
     dq, (dkv2, dkv0) = grads_last_call(scalars, queries, kv, text_kv, dq_t, norm)

time: 124 us -> 121 us (0.976)
  blocking collectives: 21.2 us -> 19.7 us
  Pallas kernels: 37.1 us -> 35.7 us
    pallas_call x1, Pallas kernels: 8.87 us -> 6.53 us  [grads_first_call(): pl.pallas_call(grads_first_kernel, in_specs=[SMEM_SPEC] * 3 + [VMEM_SPEC]...]
    pallas_call x1, Pallas kernels: 8.25 us -> 6.45 us  [stats_first_call(): pl.pallas_call(stats_first_kernel, in_specs=[SMEM_SPEC] * 3 + [VMEM_SPEC]...]
    all_to_all x1, blocking collectives: 21.2 us -> 19.7 us  [on_device(): lax.all_to_all(video, 'head', split_axis=0, concat_axis=0)]
    ppermute x20 -> x19, waiting for transfers between devices: 30.7 us -> 31.1 us  [swap(): lax.ppermute(array, 'seq', [(i, i ^ shift) for i in range(SIDE * SIDE)])]
    ppermute x20 -> x19, starting transfers between devices: 27 us -> 27.1 us  [swap(): lax.ppermute(array, 'seq', [(i, i ^ shift) for i in range(SIDE * SIDE)])]
  transfers between devices with their start and end apart: 21 -> 20, of which waited for: 15 -> 15; matrix products, arithmetic and copies ran while one was open for 0% -> 0% of each run, Pallas kernels for 14% -> 14%
where the time goes in v6:
time: 121 us
  Pallas kernels  35.7 us (30%)
  starting transfers between devices  33 us (27%)
  waiting for transfers between devices  31.1 us (26%)
  blocking collectives  19.7 us (16%)
    ppermute x19, waiting for transfers between devices, swap(): lax.ppermute(array, 'seq', [(i, i ^ shift) for i in range(SIDE * SIDE)])  31.1 us
    ppermute x19, starting transfers between devices, swap(): lax.ppermute(array, 'seq', [(i, i ^ shift) for i in range(SIDE * SIDE)])  27.1 us
    all_to_all x1, blocking collectives, on_device(): lax.all_to_all(video, 'head', split_axis=0, concat_axis=0)  19.7 us
    pallas_call x1, Pallas kernels, grads_last_call(): pl.pallas_call(grads_last_kernel, in_specs=[SMEM_SPEC] * 3 + [VMEM_SPEC]...  10.2 us
    pallas_call x1, Pallas kernels, grads_first_call(): pl.pallas_call(grads_first_kernel, in_specs=[SMEM_SPEC] * 3 + [VMEM_SPEC]...  6.53 us
    pallas_call x1, Pallas kernels, stats_first_call(): pl.pallas_call(stats_first_kernel, in_specs=[SMEM_SPEC] * 3 + [VMEM_SPEC]...  6.45 us
    pallas_call x1, Pallas kernels, stats_last_call(): pl.pallas_call(stats_last_kernel, in_specs=[SMEM_SPEC] * 3 + [VMEM_SPEC]...  6.18 us
    all_to_all x1, starting transfers between devices, on_device(): arrived = lax.all_to_all(packed, 'head', split_axis=0, concat_axis=0)  5.94 us
  transfers between devices with their start and end apart: 20, of which 15 were waited for; matrix products, arithmetic and copies ran while one was open for 0% of the time, Pallas kernels for 14%

profile of v6, /device:TPU:1, one launch (start us, length us, event | category | flops | bytes accessed | tf_op | source)
XLA Modules:
  0.0 121.0 jit_solution(6682862040494336075)
XLA Ops:
  0.6 2.3 %pack_inputs.1 = (bf16[8,4,32,384]{3,2,1,0:T(8,128)(2,1)}, bf16[2,128,384]{2,1,0:T(8,128)(2,1)S(1)}, bf16[2,128,384]{2,1,0:T(8,128)(2,1)S(1)}) custom-call(bf16[32,3072]{1,0:T(8,128)(2,1)} %q_ref.1, bf16[32,3072]{1,0:T(8,128)(2,1)} %k_ref.1, bf16[32,3072]{1,0:T(8,128)(2,1)} %v_ref.1, bf16[32,3072]{1,0:T(8,128)(2,1)} %g_ref.1, bf16[128,384]{1,0:T(8,128)(2,1)} %tq_ref.1, ...), custom_call_target="tpu_custom_call" | custom-call | tf_op jit(solution)/shard_map/pack_inputs/pallas_call | solution.py:55
  2.9 0.0 copy-start
  2.9 0.0 copy-start.1
  2.9 0.0 copy-start.2
  3.0 0.0 copy-start.3
  3.0 5.9 %all-to-all-start = ((bf16[8,4,32,384]{3,2,1,0:T(8,128)(2,1)}), bf16[8,4,32,384]{3,2,1,0:T(8,128)(2,1)S(1)}, u32[]{:S(2)}, u32[]{:S(2)}) async-start(bf16[8,4,32,384]{3,2,1,0:T(8,128)(2,1)} %get-tuple-element.55), calls=%async_computation | async-start | bytes 1572864 | tf_op jit(solution)/shard_map/all_to_all | solution.py:560
  8.9 2.7 %collective-permute-start.1 = (bf16[2,128,384]{2,1,0:T(8,128)(2,1)S(1)}, bf16[2,128,384]{2,1,0:T(8,128)(2,1)S(1)}, u32[]{:S(2)}, u32[]{:S(2)}) collective-permute-start(bf16[2,128,384]{2,1,0:T(8,128)(2,1)S(1)} %get-tuple-element.59.text_qg_ref.refs_9_), channel_id=1, source_target_pairs={{0,24},{8,16},{16,8},{24,0},{32,56},{40,48},{48,40},{56,32},{64,88... | collective-permute-start | bytes 589832 | tf_op jit(solution)/shard_map/ppermute | solution.py:534
  11.6 0.0 collective-permute-start
  11.6 3.8 %collective-permute-start.3 = (bf16[2,128,384]{2,1,0:T(8,128)(2,1)S(1)}, bf16[2,128,384]{2,1,0:T(8,128)(2,1)S(1)}, u32[]{:S(2)}, u32[]{:S(2)}) collective-permute-start(bf16[2,128,384]{2,1,0:T(8,128)(2,1)S(1)} %get-tuple-element.60.text_kv_ref.refs_3_.refs_6_), channel_id=1, source_target_pairs={{0,96},{8,104},{16,112},{24,120},{32,64},{40,72},{48,80},{56,88},{... | collective-permute-start | bytes 589832 | tf_op jit(solution)/shard_map/ppermute | solution.py:534
  15.4 0.0 collective-permute-start.2
  15.4 1.4 %collective-permute-done.1.refs_11_ = bf16[2,128,384]{2,1,0:T(8,128)(2,1)S(1)} collective-permute-done((bf16[2,128,384]{2,1,0:T(8,128)(2,1)S(1)}, bf16[2,128,384]{2,1,0:T(8,128)(2,1)S(1)}, u32[]{:S(2)}, u32[]{:S(2)}) %collective-permute-start.1) | collective-permute-done | bytes 196640 | tf_op jit(solution)/shard_map/ppermute | solution.py:534
  16.8 1.1 collective-permute-done.refs_10_
  17.9 2.5 %collective-permute-done.3.refs_5_ = bf16[2,128,384]{2,1,0:T(8,128)(2,1)S(1)} collective-permute-done((bf16[2,128,384]{2,1,0:T(8,128)(2,1)S(1)}, bf16[2,128,384]{2,1,0:T(8,128)(2,1)S(1)}, u32[]{:S(2)}, u32[]{:S(2)}) %collective-permute-start.3) | collective-permute-done | bytes 196640 | tf_op jit(solution)/shard_map/ppermute | solution.py:534
  20.3 0.8 collective-permute-done.2.refs_4_
  21.1 0.0 copy-done.7
  21.1 0.7 copy-done.6
  21.8 0.0 all-to-all-done.in_ref
  21.8 0.0 copy-done
  21.8 0.0 copy-done.1
  21.8 2.0 %assemble_blocks.1 = (bf16[2,256,384]{2,1,0:T(8,128)(2,1)S(1)}, bf16[2,256,384]{2,1,0:T(8,128)(2,1)S(1)}, bf16[2,384,384]{2,1,0:T(8,128)(2,1)S(1)}, bf16[2,384,384]{2,1,0:T(8,128)(2,1)}) custom-call(bf16[8,4,32,384]{3,2,1,0:T(8,128)(2,1)S(1)} %all-to-all-done.in_ref, bf16[2,128,384]{2,1,0:T(8,128)(2,1)} %copy-done.1, bf16[2,128,384]{2,1,0:T(8,128)(2,1)} %copy-done), custom_call_target="tpu_custom_call" | custom-call | tf_op jit(solution)/shard_map/assemble_blocks/pallas_call | solution.py:68
  23.8 2.1 %collective-permute-start.5 = (bf16[2,256,384]{2,1,0:T(8,128)(2,1)S(1)}, bf16[2,256,384]{2,1,0:T(8,128)(2,1)S(1)}, u32[]{:S(2)}, u32[]{:S(2)}) collective-permute-start(bf16[2,256,384]{2,1,0:T(8,128)(2,1)S(1)} %get-tuple-element.64.refs_6_), channel_id=1, source_target_pairs={{0,24},{8,16},{16,8},{24,0},{32,56},{40,48},{48,40},{56,32},{64,88... | collective-permute-start | bytes 1179656 | tf_op jit(solution)/shard_map/ppermute | solution.py:534
  25.9 0.0 collective-permute-start.4
  25.9 0.0 copy-done.10
  25.9 3.8 %collective-permute-start.7 = (bf16[2,256,384]{2,1,0:T(8,128)(2,1)S(1)}, bf16[2,256,384]{2,1,0:T(8,128)(2,1)S(1)}, u32[]{:S(2)}, u32[]{:S(2)}) collective-permute-start(bf16[2,256,384]{2,1,0:T(8,128)(2,1)S(1)} %get-tuple-element.61.refs_0_.refs_5_), channel_id=1, source_target_pairs={{0,96},{8,104},{16,112},{24,120},{32,64},{40,72},{48,80},{56,88},{... | collective-permute-start | bytes 1179656 | tf_op jit(solution)/shard_map/ppermute | solution.py:534
  29.7 0.0 collective-permute-start.6
  29.7 4.4 %collective-permute-done.5.refs_8_ = bf16[2,256,384]{2,1,0:T(8,128)(2,1)S(1)} collective-permute-done((bf16[2,256,384]{2,1,0:T(8,128)(2,1)S(1)}, bf16[2,256,384]{2,1,0:T(8,128)(2,1)S(1)}, u32[]{:S(2)}, u32[]{:S(2)}) %collective-permute-start.5) | collective-permute-done | bytes 393248 | tf_op jit(solution)/shard_map/ppermute | solution.py:534
  34.0 1.3 %collective-permute-done.4.refs_7_ = bf16[2,256,384]{2,1,0:T(8,128)(2,1)S(1)} collective-permute-done((bf16[2,256,384]{2,1,0:T(8,128)(2,1)S(1)}, bf16[2,256,384]{2,1,0:T(8,128)(2,1)S(1)}, u32[]{:S(2)}, u32[]{:S(2)}) %collective-permute-start.4) | collective-permute-done | bytes 393248 | tf_op jit(solution)/shard_map/ppermute | solution.py:534
  35.4 2.4 %collective-permute-done.7.refs_2_.refs_3_ = bf16[2,256,384]{2,1,0:T(8,128)(2,1)S(1)} collective-permute-done((bf16[2,256,384]{2,1,0:T(8,128)(2,1)S(1)}, bf16[2,256,384]{2,1,0:T(8,128)(2,1)S(1)}, u32[]{:S(2)}, u32[]{:S(2)}) %collective-permute-start.7) | collective-permute-done | bytes 393248 | tf_op jit(solution)/shard_map/ppermute | solution.py:534
  37.8 0.9 collective-permute-done.6.refs_1_.refs_2_
  38.7 0.0 copy-done.5
  38.7 0.3 collective-permute-start.8
  39.1 0.9 collective-permute-start.9
  39.9 0.0 copy-done.8
  39.9 0.0 copy-done.9
  39.9 0.0 copy-done.4
  39.9 0.0 copy-done.2
  39.9 0.0 copy-done.3
  40.0 6.5 %stats_first.1 = (f32[3,3,1536]{2,1,0:T(4,128)S(1)}, bf16[6,256,384]{2,1,0:T(8,128)(2,1)S(1)}, bf16[6,256,384]{2,1,0:T(8,128)(2,1)S(1)}) custom-call(s32[8]{0:T(128)S(1)} %copy-done.2, s32[8]{0:T(128)S(1)} %copy-done.3, s32[1]{0:T(128)} %bitcast.place_ref, bf16[2,256,384]{2,1,0:T(8,128)(2,1)S(1)} %get-tuple-element.61.refs_0_.refs_5_, ...), custom_call_target="tpu_custom_call" | custom-call | flops 1207959552 | bytes 8388608 | tf_op jit(solution)/shard_map/stats_first/pallas_call | solution.py:469
  46.4 6.3 %collective-permute-done.8.refs_6_.refs_4_ = bf16[2,384,384]{2,1,0:T(8,128)(2,1)S(1)} collective-permute-done((bf16[2,384,384]{2,1,0:T(8,128)(2,1)}, bf16[2,384,384]{2,1,0:T(8,128)(2,1)S(1)}, u32[]{:S(2)}, u32[]{:S(2)}) %collective-permute-start.8) | collective-permute-done | bytes 589856 | tf_op jit(solution)/shard_map/ppermute | solution.py:534
  52.8 0.3 collective-permute-done.9.refs_10_
  53.0 6.2 %stats_last.1 = (f32[2,3,1536]{2,1,0:T(4,128)S(1)}, bf16[6,256,384]{2,1,0:T(8,128)(2,1)S(1)}, bf16[6,256,384]{2,1,0:T(8,128)(2,1)S(1)}) custom-call(s32[8]{0:T(128)S(1)} %copy-done.2, s32[8]{0:T(128)S(1)} %copy-done.3, s32[1]{0:T(128)} %bitcast.place_ref, bf16[2,256,384]{2,1,0:T(8,128)(2,1)S(1)} %get-tuple-element.61.refs_0_.refs_5_, ...), custom_call_target="tpu_custom_call" | custom-call | flops 805306368 | bytes 8388608 | tf_op jit(solution)/shard_map/stats_last/pallas_call | solution.py:485
  59.2 1.3 %collective-permute-start.12 = (f32[2,3,1536]{2,1,0:T(4,128)S(1)}, f32[2,3,1536]{2,1,0:T(4,128)S(1)}, u32[]{:S(2)}, u32[]{:S(2)}) collective-permute-start(f32[2,3,1536]{2,1,0:T(4,128)S(1)} %get-tuple-element.80.refs_6_), channel_id=1, source_target_pairs={{0,24},{8,16},{16,8},{24,0},{32,56},{40,48},{48,40},{56,32},{64,88... | collective-permute-start | bytes 110600 | tf_op jit(solution)/shard_map/ppermute | solution.py:534
  60.5 1.3 %collective-permute-start.11 = (f32[2,3,1536]{2,1,0:T(4,128)S(1)}, f32[2,3,1536]{2,1,0:T(4,128)S(1)}, u32[]{:S(2)}, u32[]{:S(2)}) collective-permute-start(f32[2,3,1536]{2,1,0:T(4,128)S(1)} %get-tuple-element.80.refs_6_), channel_id=1, source_target_pairs={{0,16},{8,24},{16,0},{24,8},{32,48},{40,56},{48,32},{56,40},{64,80... | collective-permute-start | bytes 110600 | tf_op jit(solution)/shard_map/ppermute | solution.py:534
  61.8 0.9 collective-permute-start.10
  62.7 0.9 collective-permute-done.12.refs_9_
  63.6 1.3 %collective-permute-done.11.refs_8_ = f32[2,3,1536]{2,1,0:T(4,128)S(1)} collective-permute-done((f32[2,3,1536]{2,1,0:T(4,128)S(1)}, f32[2,3,1536]{2,1,0:T(4,128)S(1)}, u32[]{:S(2)}, u32[]{:S(2)}) %collective-permute-start.11) | collective-permute-done | bytes 36896 | tf_op jit(solution)/shard_map/ppermute | solution.py:534
  64.9 0.0 collective-permute-done.10.refs_7_
  64.9 6.5 %grads_first.1 = (bf16[2,384,384]{2,1,0:T(8,128)(2,1)S(1)}, bf16[2,384,384]{2,1,0:T(8,128)(2,1)S(1)}, f32[3,128,1536]{2,1,0:T(8,128)S(1)}, f32[2,3,1536]{2,1,0:T(4,128)S(1)}) custom-call(s32[8]{0:T(128)S(1)} %copy-done.2, s32[8]{0:T(128)S(1)} %copy-done.3, s32[1]{0:T(128)} %bitcast.place_ref, bf16[6,256,384]{2,1,0:T(8,128)(2,1)S(1)} %get-tuple-element.78.refs_0_.refs_2_, ...), custom_call_target="tpu_custom_call" | custom-call | flops 2013265920 | bytes 8388608 | tf_op jit(solution)/shard_map/grads_first/pallas_call | solution.py:504
  71.5 3.6 %collective-permute-start.13 = (bf16[2,384,384]{2,1,0:T(8,128)(2,1)S(1)}, bf16[2,384,384]{2,1,0:T(8,128)(2,1)S(1)}, u32[]{:S(2)}, u32[]{:S(2)}) collective-permute-start(bf16[2,384,384]{2,1,0:T(8,128)(2,1)S(1)} %get-tuple-element.87), channel_id=1, source_target_pairs={{0,32},{8,40},{16,48},{24,56},{32,0},{40,8},{48,16},{56,24},{64,96... | collective-permute-start | bytes 1769480 | tf_op jit(solution)/shard_map/ppermute | solution.py:534
  75.1 0.2 collective-permute-start.18
  75.2 10.2 %grads_last.1 = (bf16[3,128,384]{2,1,0:T(8,128)(2,1)S(1)}, bf16[3,128,384]{2,1,0:T(8,128)(2,1)S(1)}, bf16[3,128,384]{2,1,0:T(8,128)(2,1)S(1)}, bf16[3,128,384]{2...) custom-call(s32[8]{0:T(128)S(1)} %copy-done.2, s32[8]{0:T(128)S(1)} %copy-done.3, ...), custom_call_target="tpu_custom_call" | custom-call | flops 2013265920 | bytes 8388608 | tf_op jit(solution)/shard_map/grads_last/pallas_call | solution.py:519
  85.4 0.0 collective-permute-done.13.refs_5_
  85.4 2.4 %collective-permute-start.17 = (bf16[2,384,384]{2,1,0:T(8,128)(2,1)S(1)}, bf16[2,384,384]{2,1,0:T(8,128)(2,1)S(1)}, u32[]{:S(2)}, u32[]{:S(2)}) collective-permute-start(bf16[2,384,384]{2,1,0:T(8,128)(2,1)S(1)} %get-tuple-element.95), channel_id=1, source_target_pairs={{0,64},{8,72},{16,80},{24,88},{32,96},{40,104},{48,112},{56,120},{... | collective-permute-start | bytes 1769480 | tf_op jit(solution)/shard_map/ppermute | solution.py:534
  87.8 0.5 collective-permute-start.14
  88.4 0.5 collective-permute-start.15
  88.9 2.8 %collective-permute-start.16 = (bf16[3,128,384]{2,1,0:T(8,128)(2,1)S(1)}, bf16[3,128,384]{2,1,0:T(8,128)(2,1)S(1)}, u32[]{:S(2)}, u32[]{:S(2)}) collective-permute-start(bf16[3,128,384]{2,1,0:T(8,128)(2,1)S(1)} %get-tuple-element.92), channel_id=1, source_target_pairs={{0,24},{8,16},{16,8},{24,0},{32,56},{40,48},{48,40},{56,32},{64,88... | collective-permute-start | bytes 884744 | tf_op jit(solution)/shard_map/ppermute | solution.py:534
  91.7 0.0 collective-permute-done.18.refs_7_
  91.7 2.0 %collective-permute-done.14.refs_1_ = bf16[3,128,384]{2,1,0:T(8,128)(2,1)S(1)} collective-permute-done((bf16[3,128,384]{2,1,0:T(8,128)(2,1)S(1)}, bf16[3,128,384]{2,1,0:T(8,128)(2,1)S(1)}, u32[]{:S(2)}, u32[]{:S(2)}) %collective-permute-start.14) | collective-permute-done | bytes 294944 | tf_op jit(solution)/shard_map/ppermute | solution.py:534
  93.7 3.1 %collective-permute-done.15.refs_2_ = bf16[3,128,384]{2,1,0:T(8,128)(2,1)S(1)} collective-permute-done((bf16[3,128,384]{2,1,0:T(8,128)(2,1)S(1)}, bf16[3,128,384]{2,1,0:T(8,128)(2,1)S(1)}, u32[]{:S(2)}, u32[]{:S(2)}) %collective-permute-start.15) | collective-permute-done | bytes 294944 | tf_op jit(solution)/shard_map/ppermute | solution.py:534
  96.8 2.5 %collective-permute-done.16.refs_3_ = bf16[3,128,384]{2,1,0:T(8,128)(2,1)S(1)} collective-permute-done((bf16[3,128,384]{2,1,0:T(8,128)(2,1)S(1)}, bf16[3,128,384]{2,1,0:T(8,128)(2,1)S(1)}, u32[]{:S(2)}, u32[]{:S(2)}) %collective-permute-start.16) | collective-permute-done | bytes 294944 | tf_op jit(solution)/shard_map/ppermute | solution.py:534
  99.3 0.0 collective-permute-done.17.refs_6_
  99.3 1.2 %sum_terms.1 = (bf16[8,3,32,384]{3,2,1,0:T(8,128)(2,1)S(1)}, bf16[128,384]{1,0:T(8,128)(2,1)}, bf16[128,384]{1,0:T(8,128)(2,1)}, bf16[128,384]{1,0:T(8,128)(2,1)}) custom-call(bf16[3,128,384]{2,1,0:T(8,128)(2,1)S(1)} %get-tuple-element.89.refs_0_, bf16[3,128,384]{2,1,0:T(8,128)(2,1)S(1)} %collective-permute-done.14.refs_1_, ...), custom_call_target="tpu_custom_call" | custom-call | tf_op jit(solution)/shard_map/sum_terms/pallas_call | solution.py:107
  100.5 19.7 %all_to_all.10.in_ref = bf16[8,3,32,384]{3,2,1,0:T(8,128)(2,1)S(1)} all-to-all(bf16[8,3,32,384]{3,2,1,0:T(8,128)(2,1)S(1)} %get-tuple-element.97), channel_id=1, replica_groups=mesh['seq'=16,'head'=8] {'head'}, dimensions={0} | all-to-all | bytes 1179648 | tf_op jit(solution)/shard_map/all_to_all | solution.py:580
  120.2 0.9 unpack_video.1
  (7 shorter events, 0.0 us)
Async XLA Ops:
  2.9 18.9 %copy-start = (bf16[2,128,384]{2,1,0:T(8,128)(2,1)}, bf16[2,128,384]{2,1,0:T(8,128)(2,1)S(1)}, u32[]{:S(2)}) copy-start(bf16[2,128,384]{2,1,0:T(8,128)(2,1)S(1)} %get-tuple-element.60.text_kv_ref.refs_3_.refs_6_) | copy-start | bytes 589828
  2.9 18.9 %copy-start.1 = (bf16[2,128,384]{2,1,0:T(8,128)(2,1)}, bf16[2,128,384]{2,1,0:T(8,128)(2,1)S(1)}, u32[]{:S(2)}) copy-start(bf16[2,128,384]{2,1,0:T(8,128)(2,1)S(1)} %get-tuple-element.59.text_qg_ref.refs_9_) | copy-start | bytes 589828
  2.9 37.0 %copy-start.2 = (s32[8]{0:T(128)S(1)}, s32[8]{0:T(128)}, u32[]{:S(2)}) copy-start(s32[8]{0:T(128)} %length_ref.7) | copy-start | bytes 100
  3.0 37.0 %copy-start.3 = (s32[8]{0:T(128)S(1)}, s32[8]{0:T(128)}, u32[]{:S(2)}) copy-start(s32[8]{0:T(128)} %caption_ref.7) | copy-start | bytes 100
  3.0 18.9 %all-to-all-start = ((bf16[8,4,32,384]{3,2,1,0:T(8,128)(2,1)}), bf16[8,4,32,384]{3,2,1,0:T(8,128)(2,1)S(1)}, u32[]{:S(2)}, u32[]{:S(2)}) async-start(bf16[8,4,32,384]{3,2,1,0:T(8,128)(2,1)} %get-tuple-element.55), calls=%async_computation | async-start | bytes 1572864 | tf_op jit(solution)/shard_map/all_to_all | solution.py:560
  8.9 7.9 %collective-permute-start.1 = (bf16[2,128,384]{2,1,0:T(8,128)(2,1)S(1)}, bf16[2,128,384]{2,1,0:T(8,128)(2,1)S(1)}, u32[]{:S(2)}, u32[]{:S(2)}) collective-permute-start(bf16[2,128,384]{2,1,0:T(8,128)(2,1)S(1)} %get-tuple-element.59.text_qg_ref.refs_9_), channel_id=1, source_target_pairs={{0,24},{8,16},{16,8},{24,0},{32,56},{40,48},{48,40},{56,32},{64,88... | collective-permute-start | bytes 589832 | tf_op jit(solution)/shard_map/ppermute | solution.py:534
  11.6 6.2 %collective-permute-start = (bf16[2,128,384]{2,1,0:T(8,128)(2,1)S(1)}, bf16[2,128,384]{2,1,0:T(8,128)(2,1)S(1)}, u32[]{:S(2)}, u32[]{:S(2)}) collective-permute-start(bf16[2,128,384]{2,1,0:T(8,128)(2,1)S(1)} %get-tuple-element.59.text_qg_ref.refs_9_), channel_id=1, source_target_pairs={{0,8},{8,0},{16,24},{24,16},{32,40},{40,32},{48,56},{56,48},{64,72... | collective-permute-start | bytes 589832 | tf_op jit(solution)/shard_map/ppermute | solution.py:534
  11.6 8.7 %collective-permute-start.3 = (bf16[2,128,384]{2,1,0:T(8,128)(2,1)S(1)}, bf16[2,128,384]{2,1,0:T(8,128)(2,1)S(1)}, u32[]{:S(2)}, u32[]{:S(2)}) collective-permute-start(bf16[2,128,384]{2,1,0:T(8,128)(2,1)S(1)} %get-tuple-element.60.text_kv_ref.refs_3_.refs_6_), channel_id=1, source_target_pairs={{0,96},{8,104},{16,112},{24,120},{32,64},{40,72},{48,80},{56,88},{... | collective-permute-start | bytes 589832 | tf_op jit(solution)/shard_map/ppermute | solution.py:534
  15.4 5.7 %collective-permute-start.2 = (bf16[2,128,384]{2,1,0:T(8,128)(2,1)S(1)}, bf16[2,128,384]{2,1,0:T(8,128)(2,1)S(1)}, u32[]{:S(2)}, u32[]{:S(2)}) collective-permute-start(bf16[2,128,384]{2,1,0:T(8,128)(2,1)S(1)} %get-tuple-element.60.text_kv_ref.refs_3_.refs_6_), channel_id=1, source_target_pairs={{0,32},{8,40},{16,48},{24,56},{32,0},{40,8},{48,16},{56,24},{64,96... | collective-permute-start | bytes 589832 | tf_op jit(solution)/shard_map/ppermute | solution.py:534
  16.8 4.4 %copy-start.7 = (bf16[2,128,384]{2,1,0:T(8,128)(2,1)}, bf16[2,128,384]{2,1,0:T(8,128)(2,1)S(1)}, u32[]{:S(2)}) copy-start(bf16[2,128,384]{2,1,0:T(8,128)(2,1)S(1)} %collective-permute-done.1.refs_11_) | copy-start | bytes 589828
  17.9 8.0 %copy-start.10 = (bf16[2,128,384]{2,1,0:T(8,128)(2,1)}, bf16[2,128,384]{2,1,0:T(8,128)(2,1)S(1)}, u32[]{:S(2)}) copy-start(bf16[2,128,384]{2,1,0:T(8,128)(2,1)S(1)} %collective-permute-done.refs_10_) | copy-start | bytes 589828
  20.3 18.4 %copy-start.5 = (bf16[2,128,384]{2,1,0:T(8,128)(2,1)}, bf16[2,128,384]{2,1,0:T(8,128)(2,1)S(1)}, u32[]{:S(2)}) copy-start(bf16[2,128,384]{2,1,0:T(8,128)(2,1)S(1)} %collective-permute-done.3.refs_5_) | copy-start | bytes 589828
  21.1 0.7 copy-start.6
  23.8 16.1 %copy-start.4 = (bf16[2,256,384]{2,1,0:T(8,128)(2,1)}, bf16[2,256,384]{2,1,0:T(8,128)(2,1)S(1)}, u32[]{:S(2)}) copy-start(bf16[2,256,384]{2,1,0:T(8,128)(2,1)S(1)} %get-tuple-element.64.refs_6_) | copy-start | bytes 1179652
  23.8 10.2 %collective-permute-start.5 = (bf16[2,256,384]{2,1,0:T(8,128)(2,1)S(1)}, bf16[2,256,384]{2,1,0:T(8,128)(2,1)S(1)}, u32[]{:S(2)}, u32[]{:S(2)}) collective-permute-start(bf16[2,256,384]{2,1,0:T(8,128)(2,1)S(1)} %get-tuple-element.64.refs_6_), channel_id=1, source_target_pairs={{0,24},{8,16},{16,8},{24,0},{32,56},{40,48},{48,40},{56,32},{64,88... | collective-permute-start | bytes 1179656 | tf_op jit(solution)/shard_map/ppermute | solution.py:534
  25.9 9.5 %collective-permute-start.4 = (bf16[2,256,384]{2,1,0:T(8,128)(2,1)S(1)}, bf16[2,256,384]{2,1,0:T(8,128)(2,1)S(1)}, u32[]{:S(2)}, u32[]{:S(2)}) collective-permute-start(bf16[2,256,384]{2,1,0:T(8,128)(2,1)S(1)} %get-tuple-element.64.refs_6_), channel_id=1, source_target_pairs={{0,8},{8,0},{16,24},{24,16},{32,40},{40,32},{48,56},{56,48},{64,72... | collective-permute-start | bytes 1179656 | tf_op jit(solution)/shard_map/ppermute | solution.py:534
  25.9 11.9 %collective-permute-start.7 = (bf16[2,256,384]{2,1,0:T(8,128)(2,1)S(1)}, bf16[2,256,384]{2,1,0:T(8,128)(2,1)S(1)}, u32[]{:S(2)}, u32[]{:S(2)}) collective-permute-start(bf16[2,256,384]{2,1,0:T(8,128)(2,1)S(1)} %get-tuple-element.61.refs_0_.refs_5_), channel_id=1, source_target_pairs={{0,96},{8,104},{16,112},{24,120},{32,64},{40,72},{48,80},{56,88},{... | collective-permute-start | bytes 1179656 | tf_op jit(solution)/shard_map/ppermute | solution.py:534
  29.7 9.0 %collective-permute-start.6 = (bf16[2,256,384]{2,1,0:T(8,128)(2,1)S(1)}, bf16[2,256,384]{2,1,0:T(8,128)(2,1)S(1)}, u32[]{:S(2)}, u32[]{:S(2)}) collective-permute-start(bf16[2,256,384]{2,1,0:T(8,128)(2,1)S(1)} %get-tuple-element.61.refs_0_.refs_5_), channel_id=1, source_target_pairs={{0,32},{8,40},{16,48},{24,56},{32,0},{40,8},{48,16},{56,24},{64,96... | collective-permute-start | bytes 1179656 | tf_op jit(solution)/shard_map/ppermute | solution.py:534
  34.0 5.9 %copy-start.8 = (bf16[2,256,384]{2,1,0:T(8,128)(2,1)}, bf16[2,256,384]{2,1,0:T(8,128)(2,1)S(1)}, u32[]{:S(2)}) copy-start(bf16[2,256,384]{2,1,0:T(8,128)(2,1)S(1)} %collective-permute-done.5.refs_8_) | copy-start | bytes 1179652
  35.4 4.6 %copy-start.9 = (bf16[2,256,384]{2,1,0:T(8,128)(2,1)}, bf16[2,256,384]{2,1,0:T(8,128)(2,1)S(1)}, u32[]{:S(2)}) copy-start(bf16[2,256,384]{2,1,0:T(8,128)(2,1)S(1)} %collective-permute-done.4.refs_7_) | copy-start | bytes 1179652
  38.7 14.0 %collective-permute-start.8 = (bf16[2,384,384]{2,1,0:T(8,128)(2,1)}, bf16[2,384,384]{2,1,0:T(8,128)(2,1)S(1)}, u32[]{:S(2)}, u32[]{:S(2)}) collective-permute-start(bf16[2,384,384]{2,1,0:T(8,128)(2,1)} %get-tuple-element.69), channel_id=1, source_target_pairs={{0,64},{8,72},{16,80},{24,88},{32,96},{40,104},{48,112},{56,120},{... | collective-permute-start | bytes 1769480 | tf_op jit(solution)/shard_map/ppermute | solution.py:534
  39.1 14.0 %collective-permute-start.9 = (bf16[2,384,384]{2,1,0:T(8,128)(2,1)S(1)}, bf16[2,384,384]{2,1,0:T(8,128)(2,1)S(1)}, u32[]{:S(2)}, u32[]{:S(2)}) collective-permute-start(bf16[2,384,384]{2,1,0:T(8,128)(2,1)S(1)} %get-tuple-element.76), channel_id=1, source_target_pairs={{0,16},{8,24},{16,0},{24,8},{32,48},{40,56},{48,32},{56,40},{64,80... | collective-permute-start | bytes 1769480 | tf_op jit(solution)/shard_map/ppermute | solution.py:534
  59.2 4.4 %collective-permute-start.12 = (f32[2,3,1536]{2,1,0:T(4,128)S(1)}, f32[2,3,1536]{2,1,0:T(4,128)S(1)}, u32[]{:S(2)}, u32[]{:S(2)}) collective-permute-start(f32[2,3,1536]{2,1,0:T(4,128)S(1)} %get-tuple-element.80.refs_6_), channel_id=1, source_target_pairs={{0,24},{8,16},{16,8},{24,0},{32,56},{40,48},{48,40},{56,32},{64,88... | collective-permute-start | bytes 110600 | tf_op jit(solution)/shard_map/ppermute | solution.py:534
  60.5 4.4 %collective-permute-start.11 = (f32[2,3,1536]{2,1,0:T(4,128)S(1)}, f32[2,3,1536]{2,1,0:T(4,128)S(1)}, u32[]{:S(2)}, u32[]{:S(2)}) collective-permute-start(f32[2,3,1536]{2,1,0:T(4,128)S(1)} %get-tuple-element.80.refs_6_), channel_id=1, source_target_pairs={{0,16},{8,24},{16,0},{24,8},{32,48},{40,56},{48,32},{56,40},{64,80... | collective-permute-start | bytes 110600 | tf_op jit(solution)/shard_map/ppermute | solution.py:534
  61.8 3.1 %collective-permute-start.10 = (f32[2,3,1536]{2,1,0:T(4,128)S(1)}, f32[2,3,1536]{2,1,0:T(4,128)S(1)}, u32[]{:S(2)}, u32[]{:S(2)}) collective-permute-start(f32[2,3,1536]{2,1,0:T(4,128)S(1)} %get-tuple-element.80.refs_6_), channel_id=1, source_target_pairs={{0,8},{8,0},{16,24},{24,16},{32,40},{40,32},{48,56},{56,48},{64,72... | collective-permute-start | bytes 110600 | tf_op jit(solution)/shard_map/ppermute | solution.py:534
  71.5 14.0 %collective-permute-start.13 = (bf16[2,384,384]{2,1,0:T(8,128)(2,1)S(1)}, bf16[2,384,384]{2,1,0:T(8,128)(2,1)S(1)}, u32[]{:S(2)}, u32[]{:S(2)}) collective-permute-start(bf16[2,384,384]{2,1,0:T(8,128)(2,1)S(1)} %get-tuple-element.87), channel_id=1, source_target_pairs={{0,32},{8,40},{16,48},{24,56},{32,0},{40,8},{48,16},{56,24},{64,96... | collective-permute-start | bytes 1769480 | tf_op jit(solution)/shard_map/ppermute | solution.py:534
  75.1 16.6 %collective-permute-start.18 = (bf16[2,384,384]{2,1,0:T(8,128)(2,1)S(1)}, bf16[2,384,384]{2,1,0:T(8,128)(2,1)S(1)}, u32[]{:S(2)}, u32[]{:S(2)}) collective-permute-start(bf16[2,384,384]{2,1,0:T(8,128)(2,1)S(1)} %get-tuple-element.96), channel_id=1, source_target_pairs={{0,96},{8,104},{16,112},{24,120},{32,64},{40,72},{48,80},{56,88},{... | collective-permute-start | bytes 1769480 | tf_op jit(solution)/shard_map/ppermute | solution.py:534
  85.4 13.8 %collective-permute-start.17 = (bf16[2,384,384]{2,1,0:T(8,128)(2,1)S(1)}, bf16[2,384,384]{2,1,0:T(8,128)(2,1)S(1)}, u32[]{:S(2)}, u32[]{:S(2)}) collective-permute-start(bf16[2,384,384]{2,1,0:T(8,128)(2,1)S(1)} %get-tuple-element.95), channel_id=1, source_target_pairs={{0,64},{8,72},{16,80},{24,88},{32,96},{40,104},{48,112},{56,120},{... | collective-permute-start | bytes 1769480 | tf_op jit(solution)/shard_map/ppermute | solution.py:534
  87.8 5.9 %collective-permute-start.14 = (bf16[3,128,384]{2,1,0:T(8,128)(2,1)S(1)}, bf16[3,128,384]{2,1,0:T(8,128)(2,1)S(1)}, u32[]{:S(2)}, u32[]{:S(2)}) collective-permute-start(bf16[3,128,384]{2,1,0:T(8,128)(2,1)S(1)} %get-tuple-element.90), channel_id=1, source_target_pairs={{0,8},{8,0},{16,24},{24,16},{32,40},{40,32},{48,56},{56,48},{64,72... | collective-permute-start | bytes 884744 | tf_op jit(solution)/shard_map/ppermute | solution.py:534
  88.4 8.4 %collective-permute-start.15 = (bf16[3,128,384]{2,1,0:T(8,128)(2,1)S(1)}, bf16[3,128,384]{2,1,0:T(8,128)(2,1)S(1)}, u32[]{:S(2)}, u32[]{:S(2)}) collective-permute-start(bf16[3,128,384]{2,1,0:T(8,128)(2,1)S(1)} %get-tuple-element.91), channel_id=1, source_target_pairs={{0,16},{8,24},{16,0},{24,8},{32,48},{40,56},{48,32},{56,40},{64,80... | collective-permute-start | bytes 884744 | tf_op jit(solution)/shard_map/ppermute | solution.py:534
  88.9 10.4 %collective-permute-start.16 = (bf16[3,128,384]{2,1,0:T(8,128)(2,1)S(1)}, bf16[3,128,384]{2,1,0:T(8,128)(2,1)S(1)}, u32[]{:S(2)}, u32[]{:S(2)}) collective-permute-start(bf16[3,128,384]{2,1,0:T(8,128)(2,1)S(1)} %get-tuple-element.92), channel_id=1, source_target_pairs={{0,24},{8,16},{16,8},{24,0},{32,56},{40,48},{48,40},{56,32},{64,88... | collective-permute-start | bytes 884744 | tf_op jit(solution)/shard_map/ppermute | solution.py:534

commit v7 on v6

--- a/solution.py
+++ b/solution.py
@@ -55,22 +55,35 @@
     return call(*placed(arrays, pltpu.HBM))
 
 
-def assemble_kernel(in_ref, text_qg_ref, text_kv_ref, qg_ref, kv_ref, far_qg_ref, far_kv_ref):
+def assemble_kernel(in_ref, qg_ref, kv_ref):
     for n in range(2):
-        for at, text, near, far in ((0, text_qg_ref, qg_ref, far_qg_ref), (2, text_kv_ref, kv_ref, far_kv_ref)):
-            rows = in_ref[:, at + n].reshape(BLOCK, WIDTH)
-            near[n] = rows
-            far[n, :BLOCK] = rows
-            far[n, BLOCK:] = text[n]
-
-
-def assemble(arrived, text_qg, text_kv):
+        qg_ref[n] = in_ref[:, n].reshape(BLOCK, WIDTH)
+        kv_ref[n] = in_ref[:, 2 + n].reshape(BLOCK, WIDTH)
+
+
+def assemble(arrived):
     return pl.pallas_call(
         assemble_kernel,
-        out_shape=(VIDEO_MESSAGE, VIDEO_MESSAGE, KEY_MESSAGE, KEY_MESSAGE),
+        out_shape=(VIDEO_MESSAGE, VIDEO_MESSAGE),
         compiler_params=SMALL,
         name="assemble_blocks",
-    )(*placed([arrived]), *placed([text_qg, text_kv], pltpu.HBM))
+    )(*placed([arrived]))
+
+
+def hand_on_kernel(*refs):
+    video, text, outs = refs[:4], refs[4:8], refs[8:]
+    for n in range(4):
+        outs[n][:BLOCK] = video[n][n % 2]
+        outs[n][BLOCK:] = text[n][n % 2]
+
+
+def hand_on(video, text):
+    return pl.pallas_call(
+        hand_on_kernel,
+        out_shape=[HALF_MESSAGE] * 4,
+        compiler_params=SMALL,
+        name="hand_on",
+    )(*placed(video), *placed(text, pltpu.HBM))
 
 
 def unpack_kernel(in_ref, q_ref, k_ref, v_ref):
@@ -151,27 +164,27 @@
 
 def stage_text_queries(labels, p, parts, q_all, g_all):
     shot = labels.query_shot(p)
-    for e, (ref, at) in enumerate(parts):
-        rows, source = slice(e * HALF, (e + 1) * HALF), slice(at, at + HALF)
-        q_all[SIDE + p, rows] = ref[0, source]
+    for e, (queries, grads) in enumerate(parts):
+        rows = slice(e * HALF, (e + 1) * HALF)
+        q_all[SIDE + p, rows] = queries
         live = labels.live(shot, (labels.y ^ e) % 2)
-        g_all[SIDE + p, rows] = jnp.where(live, ref[1, source], jnp.zeros((HALF, WIDTH), BF16))
+        g_all[SIDE + p, rows] = jnp.where(live, grads, jnp.zeros((HALF, WIDTH), BF16))
 
 
 class Keys:
-    def __init__(self, video_ref, text_ref, text_at):
-        self.video_ref, self.text_ref, self.text_rows = video_ref, text_ref, slice(text_at, text_at + HALF)
+    def __init__(self, video, text, text_at):
+        self.video, self.text, self.text_rows = video, text, slice(text_at, text_at + HALF)
 
     def rows(self, is_text, which, c):
-        return self.text_ref[which, self.text_rows, c] if is_text else self.video_ref[which, :BLOCK, c]
+        return self.text[which][self.text_rows, c] if is_text else self.video[which][:BLOCK, c]
 
 
 def near_keys(video_refs, text_refs):
-    return [Keys(video, text, 0) for video, text in zip(video_refs, text_refs)]
-
-
-def far_keys(ref):
-    return Keys(ref, ref, BLOCK)
+    return [Keys((v.at[0], v.at[1]), (t.at[0], t.at[1]), 0) for v, t in zip(video_refs, text_refs)]
+
+
+def far_keys(refs):
+    return [Keys(refs, refs, BLOCK)]
 
 
 def joined(kv, which, c):
@@ -299,7 +312,7 @@
     for j, ref in zip(NEAR, qg):
         q_all[j] = ref[0]
         g_all[j] = ref[1]
-    stage_text_queries(labels, 0, [(ref, 0) for ref in text_qg], q_all, g_all)
+    stage_text_queries(labels, 0, [(ref[0], ref[1]) for ref in text_qg], q_all, g_all)
     acc[0] = jnp.full((HEADS_LOCAL, ROWS), LOW, F32)
     acc[1:3] = jnp.zeros((2, HEADS_LOCAL, ROWS), F32)
     video_stats(acc, q_all, g_all, kv, NEAR, True)
@@ -310,13 +323,13 @@
 
 
 def stats_last_kernel(length_ref, caption_ref, place_ref, *refs):
-    kv, far_kv = near_keys(refs[:3], refs[3:6]), [far_keys(refs[6])]
-    acc_in, q_in, g_in, far_qg, text_qg, out_ref, q_all, g_all, acc = refs[7:]
+    kv, far_kv = near_keys(refs[:3], refs[3:6]), far_keys(refs[6:8])
+    acc_in, q_in, g_in, far_q, far_g, text_qg, out_ref, q_all, g_all, acc = refs[8:]
     labels = Labels(length_ref, caption_ref, place_ref)
     for j in range(SIDE + 1):
-        q_all[j] = far_qg[0, :BLOCK] if j == FAR else q_in[j]
-        g_all[j] = far_qg[1, :BLOCK] if j == FAR else g_in[j]
-    stage_text_queries(labels, 1, [(far_qg, BLOCK), (text_qg, 0)], q_all, g_all)
+        q_all[j] = far_q[:BLOCK] if j == FAR else q_in[j]
+        g_all[j] = far_g[:BLOCK] if j == FAR else g_in[j]
+    stage_text_queries(labels, 1, [(far_q[BLOCK:], far_g[BLOCK:]), (text_qg[0], text_qg[1])], q_all, g_all)
     acc[...] = acc_in[...]
     video_stats(acc, q_all, g_all, kv, (FAR,), True)
     video_stats(acc, q_all, g_all, far_kv, range(SIDE), False)
@@ -352,32 +365,47 @@
         norm[1, :, query_cols(j)] = delta
 
 
-def key_grads(labels, blocks, dq_in, q_all, g_all, kv, dkv_out, norm, dq_t, scratch):
-    count = len(blocks)
-    dk, dv, text_dk, text_dv, p_all, ds_all = scratch
-    text_dk[...] = jnp.zeros((count, HEADS_LOCAL, HALF, HDIM), F32)
-    text_dv[...] = jnp.zeros((count, HEADS_LOCAL, HALF, HDIM), F32)
+class Terms:
+    def __init__(self, refs):
+        self.dk, self.dv, self.text_dk, self.text_dv = refs
+
+    def clear(self):
+        for ref in (self.dk, self.dv, self.text_dk, self.text_dv):
+            ref[...] = jnp.zeros(ref.shape, F32)
+
+    def write(self, n, out):
+        rows = query_cols(n)
+        for h in range(HEADS_LOCAL):
+            c = head_cols(h)
+            out[0, :BLOCK, c] = (self.dk[h, rows] * SCALE).astype(BF16)
+            out[1, :BLOCK, c] = self.dv[h, rows].astype(BF16)
+            out[0, BLOCK:, c] = (self.text_dk[n, h] * SCALE).astype(BF16)
+            out[1, BLOCK:, c] = self.text_dv[n, h].astype(BF16)
+
+
+def key_grads(labels, blocks, queries, pairs, q_all, g_all, kv, norm, dq_in, dq_t, terms, work):
+    p_all, ds_all = work
 
     def head(h):
         c, row = head_ds(h), pl.ds(h, 1)
         keys, values = joined(kv, 0, c), joined(kv, 1, c)
-        keys_t = jnp.transpose(keys)
-        for j in range(SIDE):
-            cols = query_cols(j)
+        for n, j in enumerate(queries):
+            cols, at = query_cols(j), query_cols(n)
             scores = dot_nt(keys, q_all[j, :, c])
             dprob = dot_nt(values, g_all[j, :, c])
             probs = jnp.exp2(scores * TO_LOG2 - norm[0, row, cols])
-            dscore = (probs * (dprob - norm[1, row, cols])).astype(BF16)
-            p_all[:, cols] = probs.astype(BF16)
-            ds_all[:, cols] = dscore
-        dv[h] = dot_nn(p_all[...], g_all[:SIDE, :, c].reshape(VIDEO_ROWS, HDIM))
-        dk[h] = dot_nn(ds_all[...], q_all[:SIDE, :, c].reshape(VIDEO_ROWS, HDIM))
-        part = dot_nn(keys_t, ds_all[...])
-        dq_t[h, :, :VIDEO_ROWS] = part if dq_in is None else dq_in[h, :, :VIDEO_ROWS] + part
+            p_all[:, at] = probs.astype(BF16)
+            ds_all[:, at] = (probs * (dprob - norm[1, row, cols])).astype(BF16)
+        terms.dv[h] += dot_nn(p_all[...], jnp.concatenate([g_all[j, :, c] for j in queries], 0))
+        terms.dk[h] += dot_nn(ds_all[...], jnp.concatenate([q_all[j, :, c] for j in queries], 0))
+        part = dot_nn(jnp.transpose(keys), ds_all[...])
+        for n, j in enumerate(queries):
+            cols, piece = query_cols(j), part[:, query_cols(n)]
+            dq_t[h, :, cols] = piece if dq_in is None else dq_in[h, :, cols] + piece
 
     loop(HEADS_LOCAL, head)
 
-    def visit(is_text, add, n, j, mask):
+    def visit(is_text, n, j, mask):
         cols = rows_ds(j)
         results = []
         for h in range(HEADS_LOCAL):
@@ -390,51 +418,69 @@
             dscore = (probs * (dprob - norm[1, h : h + 1, cols])).astype(BF16)
             results.append((dot_nn(dscore, queries), dot_nn(low, grads), dot_nn(jnp.transpose(keys), dscore)))
         for h in range(HEADS_LOCAL):
-            add(n, h, results[h][0], results[h][1])
+            if is_text:
+                terms.text_dk[n, h] += results[h][0]
+                terms.text_dv[n, h] += results[h][1]
+            else:
+                terms.dk[h, query_cols(n)] += results[h][0]
+                terms.dv[h, query_cols(n)] += results[h][1]
             dq_t[h, :, cols] += results[h][2]
 
-    def add_text(n, h, key_part, value_part):
-        text_dk[n, h] += key_part
-        text_dv[n, h] += value_part
-
-    def add_video(n, h, key_part, value_part):
-        dk[h, query_cols(n)] += key_part
-        dv[h, query_cols(n)] += value_part
-
-    visit_text = functools.partial(visit, True, add_text)
-    text_keys(labels, blocks, tuple(range(SIDE)), visit_text)
-    if 0 in blocks:
+    visit_text = functools.partial(visit, True)
+    text_keys(labels, blocks, queries, visit_text)
+    if 0 in blocks and 0 in pairs:
         own_text(labels, blocks.index(0), visit_text)
-    text_queries(labels, blocks, (0, 1), functools.partial(visit, False, add_video))
-
-    for i in range(count):
-        for h in range(HEADS_LOCAL):
-            c = head_cols(h)
-            dkv_out[i][0, :BLOCK, c] = (dk[h, query_cols(i)] * SCALE).astype(BF16)
-            dkv_out[i][1, :BLOCK, c] = dv[h, query_cols(i)].astype(BF16)
-            dkv_out[i][0, BLOCK:, c] = (text_dk[i, h] * SCALE).astype(BF16)
-            dkv_out[i][1, BLOCK:, c] = text_dv[i, h].astype(BF16)
-
-
-def grads_first_kernel(length_ref, caption_ref, place_ref, *refs):
-    q_all, g_all, kv, refs = refs[0], refs[1], near_keys(refs[2:4], refs[4:6]), refs[6:]
-    stats, dkv_out, (dq_t, norm, *scratch) = refs[:SIDE], refs[SIDE : SIDE + 2], refs[SIDE + 2 :]
+    text_queries(labels, blocks, pairs, functools.partial(visit, False))
+
+
+def write_queries(dq_t, j, out):
+    out[:, :, :BLOCK] = (dq_t[:, :, query_cols(j)] * SCALE).astype(BF16)
+    out[:, :, BLOCK:] = (dq_t[:, :, VIDEO_ROWS + j * HALF : VIDEO_ROWS + (j + 1) * HALF] * SCALE).astype(BF16)
+
+
+ALL = (0, 1, 2, 3)
+
+
+def grads_far_kernel(length_ref, caption_ref, place_ref, *refs):
+    q_all, g_all, kv, stats = refs[0], refs[1], far_keys(refs[2:4]), refs[4 : SIDE + 4]
+    dkv_out, dq_t, norm, *scratch = refs[SIDE + 4 :]
     labels = Labels(length_ref, caption_ref, place_ref)
     normalize(stats, norm)
     dq_t[:, :, VIDEO_ROWS:] = jnp.zeros((HEADS_LOCAL, HDIM, TEXT_ROWS), F32)
-    key_grads(labels, (1, 3), None, q_all, g_all, kv, dkv_out, norm, dq_t, scratch)
-
-
-def grads_last_kernel(length_ref, caption_ref, place_ref, *refs):
-    norm, dq_in, q_all, g_all = refs[:4]
-    kv, refs = [far_keys(refs[4]), Keys(refs[5], refs[6], 0)], refs[7:]
-    dq_out, dkv_out, (dq_t, *scratch) = refs[:SIDE], refs[SIDE : SIDE + 2], refs[SIDE + 2 :]
+    terms = Terms(scratch[:4])
+    terms.clear()
+    key_grads(labels, (FAR,), ALL, (0, 1), q_all, g_all, kv, norm, None, dq_t, terms, scratch[4:])
+    terms.write(0, dkv_out)
+
+
+def grads_near_kernel(length_ref, caption_ref, place_ref, *refs):
+    q_all, g_all, dq_in, norm = refs[:4]
+    kv, own, refs = near_keys(refs[4:6], refs[6:8]), near_keys(refs[8:9], refs[9:10]), refs[10:]
+    dkv_out, (dq_out, dq_t), own_terms, scratch = refs[:2], refs[2:4], Terms(refs[4:8]), refs[8:]
     labels = Labels(length_ref, caption_ref, place_ref)
     dq_t[:, :, VIDEO_ROWS:] = dq_in[:, :, VIDEO_ROWS:]
-    key_grads(labels, (FAR, 0), dq_in, q_all, g_all, kv, dkv_out, norm, dq_t, scratch)
-    for n in range(SIDE):
-        dq_out[n][:, :, :BLOCK] = (dq_t[:, :, query_cols(n)] * SCALE).astype(BF16)
-        dq_out[n][:, :, BLOCK:] = (dq_t[:, :, VIDEO_ROWS + n * HALF : VIDEO_ROWS + (n + 1) * HALF] * SCALE).astype(BF16)
+    terms = Terms(scratch[:4])
+    terms.clear()
+    own_terms.clear()
+    key_grads(labels, (1, 3), ALL, (0, 1), q_all, g_all, kv, norm, dq_in, dq_t, terms, scratch[4:6])
+    key_grads(labels, (0,), (FAR,), (1,), q_all, g_all, own, norm, dq_t, dq_t, own_terms, scratch[6:])
+    for n in range(2):
+        terms.write(n, dkv_out[n])
+    write_queries(dq_t, FAR, dq_out)
+
+
+def grads_own_kernel(length_ref, caption_ref, place_ref, *refs):
+    q_all, g_all, dq_in, norm, kv, refs = *refs[:4], near_keys(refs[4:5], refs[5:6]), refs[6:]
+    before, dq_out, dkv_out, dq_t, scratch = refs[:4], refs[4:7], refs[7], refs[8], refs[9:]
+    labels = Labels(length_ref, caption_ref, place_ref)
+    dq_t[:, :, VIDEO_ROWS:] = dq_in[:, :, VIDEO_ROWS:]
+    terms = Terms(scratch[:4])
+    for ref, source in zip(scratch[:4], before):
+        ref[...] = source[...]
+    key_grads(labels, (0,), NEAR, (0,), q_all, g_all, kv, norm, dq_in, dq_t, terms, scratch[4:])
+    for n, j in enumerate(NEAR):
+        write_queries(dq_t, j, dq_out[n])
+    terms.write(0, dkv_out)
 
 
 SMEM_SPEC = pl.BlockSpec(memory_space=pltpu.SMEM)
@@ -445,15 +491,20 @@
 STATS = (3, HEADS_LOCAL, ROWS)
 STAGED_QUERIES = jax.ShapeDtypeStruct((SIDE + 2, BLOCK, WIDTH), BF16)
 VIDEO_MESSAGE = jax.ShapeDtypeStruct((2, BLOCK, WIDTH), BF16)
+HALF_MESSAGE = jax.ShapeDtypeStruct((BLOCK + HALF, WIDTH), BF16)
 KEY_MESSAGE = jax.ShapeDtypeStruct((2, BLOCK + HALF, WIDTH), BF16)
 
 
-def grads_scratch(count):
-    return (
-        [pltpu.VMEM((HEADS_LOCAL, count * BLOCK, HDIM), F32)] * 2
-        + [pltpu.VMEM((count, HEADS_LOCAL, HALF, HDIM), F32)] * 2
-        + [pltpu.VMEM((count * BLOCK, VIDEO_ROWS), BF16)] * 2
-    )
+def terms_shapes(count):
+    return [(HEADS_LOCAL, count * BLOCK, HDIM)] * 2 + [(count, HEADS_LOCAL, HALF, HDIM)] * 2
+
+
+def terms_scratch(count):
+    return [pltpu.VMEM(shape, F32) for shape in terms_shapes(count)]
+
+
+def work_scratch(count, queries):
+    return [pltpu.VMEM((count * BLOCK, queries * BLOCK), BF16)] * 2
 
 
 def placed(arrays, space=pltpu.VMEM):
@@ -484,7 +535,7 @@
 def stats_last_call(scalars, acc, queries, qg, kv, text_qg, text_kv):
     return pl.pallas_call(
         stats_last_kernel,
-        in_specs=[SMEM_SPEC] * 3 + [VMEM_SPEC] * 12,
+        in_specs=[SMEM_SPEC] * 3 + [VMEM_SPEC] * 14,
         out_specs=[VMEM_SPEC] * 3,
         out_shape=[jax.ShapeDtypeStruct((2, HEADS_LOCAL, ROWS), F32), STAGED_QUERIES, STAGED_QUERIES],
         scratch_shapes=[pltpu.VMEM(STATS, F32)],
@@ -495,38 +546,63 @@
         *scalars,
         *placed([kv[i] for i in NEAR]),
         *placed([text_kv[i] for i in NEAR], pltpu.HBM),
-        *placed([kv[FAR], acc, *queries, qg[FAR]]),
+        *placed([*kv[FAR], acc, *queries, *qg[FAR]]),
         *placed([text_qg[3]], pltpu.HBM),
     )
 
 
-def grads_first_call(scalars, queries, kv, text_kv, stats):
-    *dkv, dq_t, norm = pl.pallas_call(
-        grads_first_kernel,
-        in_specs=[SMEM_SPEC] * 3 + [VMEM_SPEC] * (6 + SIDE),
-        out_specs=[VMEM_SPEC] * 4,
+DQ_MESSAGE = jax.ShapeDtypeStruct((HEADS_LOCAL, HDIM, BLOCK + HALF), BF16)
+
+
+def grads_far_call(scalars, queries, kv, stats):
+    return pl.pallas_call(
+        grads_far_kernel,
+        in_specs=[SMEM_SPEC] * 3 + [VMEM_SPEC] * (4 + SIDE),
+        out_specs=[VMEM_SPEC] * 3,
+        out_shape=[KEY_MESSAGE, jax.ShapeDtypeStruct(DQ_T, F32), jax.ShapeDtypeStruct((2, HEADS_LOCAL, ROWS), F32)],
+        scratch_shapes=terms_scratch(1) + work_scratch(1, SIDE),
+        compiler_params=PARAMS,
+        cost_estimate=cost(1, 5),
+        name="grads_far",
+    )(*scalars, *placed([*queries, *kv[FAR], *stats]))
+
+
+def grads_near_call(scalars, queries, dq_t, norm, kv, text_kv):
+    out = pl.pallas_call(
+        grads_near_kernel,
+        in_specs=[SMEM_SPEC] * 3 + [VMEM_SPEC] * 10,
+        out_specs=[VMEM_SPEC] * 8,
         out_shape=[KEY_MESSAGE] * 2
-        + [jax.ShapeDtypeStruct(DQ_T, F32), jax.ShapeDtypeStruct((2, HEADS_LOCAL, ROWS), F32)],
-        scratch_shapes=grads_scratch(2),
+        + [DQ_MESSAGE, jax.ShapeDtypeStruct(DQ_T, F32)]
+        + [jax.ShapeDtypeStruct(shape, F32) for shape in terms_shapes(1)],
+        scratch_shapes=terms_scratch(2) + work_scratch(2, SIDE) + work_scratch(1, 1),
         compiler_params=PARAMS,
         cost_estimate=cost(2, 5),
-        name="grads_first",
-    )(*scalars, *placed([*queries, kv[1], kv[3]]), *placed([text_kv[1], text_kv[3]], pltpu.HBM), *placed(stats))
-    return dkv, dq_t, norm
-
-
-def grads_last_call(scalars, queries, kv, text_kv, dq_t, norm):
+        name="grads_near",
+    )(
+        *scalars,
+        *placed(queries),
+        dq_t,
+        *placed([norm, kv[1], kv[3]]),
+        *placed([text_kv[1], text_kv[3]], pltpu.HBM),
+        *placed([kv[0]]),
+        *placed([text_kv[0]], pltpu.HBM),
+    )
+    return out[:2], out[2], out[3], out[4:]
+
+
+def grads_own_call(scalars, queries, dq_t, norm, kv, text_kv, terms):
     out = pl.pallas_call(
-        grads_last_kernel,
-        in_specs=[SMEM_SPEC] * 3 + [VMEM_SPEC] * 7,
-        out_specs=[VMEM_SPEC] * (SIDE + 2),
-        out_shape=[jax.ShapeDtypeStruct((HEADS_LOCAL, HDIM, BLOCK + HALF), BF16)] * SIDE + [KEY_MESSAGE] * 2,
-        scratch_shapes=[pltpu.VMEM(DQ_T, F32)] + grads_scratch(2),
+        grads_own_kernel,
+        in_specs=[SMEM_SPEC] * 3 + [VMEM_SPEC] * 10,
+        out_specs=[VMEM_SPEC] * 4,
+        out_shape=[DQ_MESSAGE] * 3 + [KEY_MESSAGE],
+        scratch_shapes=[pltpu.VMEM(DQ_T, F32)] + terms_scratch(1) + work_scratch(1, 3),
         compiler_params=PARAMS,
-        cost_estimate=cost(2, 5),
-        name="grads_last",
-    )(*scalars, *placed([norm]), dq_t, *placed([*queries, kv[FAR], kv[0]]), *placed([text_kv[0]], pltpu.HBM))
-    return out[:SIDE], out[SIDE:]
+        cost_estimate=cost(1, 5),
+        name="grads_own",
+    )(*scalars, *placed(queries), dq_t, *placed([norm, kv[0]]), *placed([text_kv[0]], pltpu.HBM), *terms)
+    return out[:3], out[3]
 
 
 def swap(array, axis, step):
@@ -559,23 +635,24 @@
     text_kv = {0: text_kv, 1: swap(text_kv, "z", 1), 3: swap(text_kv, "z", 3)}
     arrived = lax.all_to_all(packed, "head", split_axis=0, concat_axis=0)
     arrived, text_qg, text_kv = lax.optimization_barrier((arrived, text_qg, text_kv))
-    qg, kv, far_qg, far_kv = assemble(arrived, text_qg[0], text_kv[0])
+    qg, kv = assemble(arrived)
     qg1, qg3 = swap(qg, "y", 1), swap(qg, "y", 3)
     kv1, kv3 = swap(kv, "z", 1), swap(kv, "z", 3)
-    far_qg, far_kv, qg1, qg3, kv1, kv3 = lax.optimization_barrier((far_qg, far_kv, qg1, qg3, kv1, kv3))
-    qg = [qg, qg1, swap(far_qg, "y", FAR), qg3]
-    kv = [kv, kv1, swap(far_kv, "z", FAR), kv3]
+    q1, g3, k1, v3 = hand_on([qg1, qg3, kv1, kv3], [text_qg[1], text_qg[3], text_kv[1], text_kv[3]])
+    qg = [qg, qg1, (swap(q1, "y", 3), swap(g3, "y", 1)), qg3]
+    kv = [kv, kv1, (swap(k1, "z", 3), swap(v3, "z", 1)), kv3]
 
     acc, *queries = stats_first_call(scalars, qg, kv, text_qg, text_kv)
     stats, *queries = stats_last_call(scalars, acc, queries, qg, kv, text_qg, text_kv)
     stats = gathered(stats, "y")
-    (dkv1, dkv3), dq_t, norm = grads_first_call(scalars, queries, kv, text_kv, stats)
-    dq, (dkv2, dkv0) = grads_last_call(scalars, queries, kv, text_kv, dq_t, norm)
-
-    dkv1, dkv3 = swap(dkv1, "z", 1), swap(dkv3, "z", 3)
-    dq, dkv1, dkv2 = lax.optimization_barrier((dq, dkv1, dkv2))
-    dq = [dq[0]] + [swap(dq[step], "y", step) for step in range(1, SIDE)]
-    dkv = [dkv0, dkv1, swap(dkv2, "z", 2), dkv3]
+    dkv2, dq_t, norm = grads_far_call(scalars, queries, kv, stats)
+    (dkv1, dkv3), dq2, dq_t, terms = grads_near_call(scalars, queries, dq_t, norm, kv, text_kv)
+    (dq0, dq1, dq3), dkv0 = grads_own_call(scalars, queries, dq_t, norm, kv, text_kv, terms)
+
+    dkv2, dq2 = swap(dkv2, "z", FAR), swap(dq2, "y", FAR)
+    dq1, dq3, dkv2, dq2 = lax.optimization_barrier((dq1, dq3, dkv2, dq2))
+    dq = [dq0, swap(dq1, "y", 1), dq2, swap(dq3, "y", 3)]
+    dkv = [dkv0, swap(dkv1, "z", 1), dkv2, swap(dkv3, "z", 3)]
     video, *text = sum_terms(dq, dkv)
     video_back = unpack(lax.all_to_all(video, "head", split_axis=0, concat_axis=0))
     return (*video_back, *text)

time: 121 us -> 117 us (0.967)
  waiting for transfers between devices: 31.1 us -> 24 us
  starting transfers between devices: 33 us -> 34.8 us
  Pallas kernels: 35.7 us -> 37.4 us
    ppermute x19 -> x21, waiting for transfers between devices: 31.1 us -> 23.9 us  [swap(): lax.ppermute(array, 'seq', [(i, i ^ shift) for i in range(SIDE * SIDE)])]
    ppermute x19 -> x21, starting transfers between devices: 27.1 us -> 29 us  [swap(): lax.ppermute(array, 'seq', [(i, i ^ shift) for i in range(SIDE * SIDE)])]
    pallas_call x3 -> x5, Pallas kernels: 18.7 us -> 20.5 us  [the longest x1 8.52 us: grads_near_call(): pl.pallas_call(grads_near_kernel, in_specs=[SMEM_SPEC] * 3 + [VMEM_SPEC]...]
  transfers between devices with their start and end apart: 20 -> 22, of which waited for: 15 -> 12; matrix products, arithmetic and copies ran while one was open for 0% -> 0% of each run, Pallas kernels for 14% -> 19%
where the time goes in v7:
time: 117 us; the launch traced here: 116 us
  Pallas kernels  37.4 us (32%)
  starting transfers between devices  34.8 us (30%)
  waiting for transfers between devices  24 us (21%)
  blocking collectives  19.5 us (17%)
    ppermute x21, starting transfers between devices, swap(): lax.ppermute(array, 'seq', [(i, i ^ shift) for i in range(SIDE * SIDE)])  29 us
    ppermute x21, waiting for transfers between devices, swap(): lax.ppermute(array, 'seq', [(i, i ^ shift) for i in range(SIDE * SIDE)])  23.9 us
    all_to_all x1, blocking collectives, on_device(): lax.all_to_all(video, 'head', split_axis=0, concat_axis=0)  19.5 us
    pallas_call x1, Pallas kernels, grads_near_call(): pl.pallas_call(grads_near_kernel, in_specs=[SMEM_SPEC] * 3 + [VMEM_SPEC]...  8.52 us
    pallas_call x1, Pallas kernels, stats_first_call(): pl.pallas_call(stats_first_kernel, in_specs=[SMEM_SPEC] * 3 + [VMEM_SPEC]...  6.78 us
    pallas_call x1, Pallas kernels, grads_own_call(): pl.pallas_call(grads_own_kernel, in_specs=[SMEM_SPEC] * 3 + [VMEM_SPEC] *...  6.51 us
    all_to_all x1, starting transfers between devices, on_device(): arrived = lax.all_to_all(packed, 'head', split_axis=0, concat_axis=0)  5.8 us
    pallas_call x1, Pallas kernels, stats_last_call(): pl.pallas_call(stats_last_kernel, in_specs=[SMEM_SPEC] * 3 + [VMEM_SPEC]...  5.7 us
  transfers between devices with their start and end apart: 22, of which 12 were waited for; matrix products, arithmetic and copies ran while one was open for 0% of the time, Pallas kernels for 19%

profile of v7, /device:TPU:1, one launch (start us, length us, event | category | flops | bytes accessed | tf_op | source)
XLA Modules:
  0.0 116.4 jit_solution(11875590605977574529)
XLA Ops:
  0.6 2.3 %pack_inputs.1 = (bf16[8,4,32,384]{3,2,1,0:T(8,128)(2,1)}, bf16[2,128,384]{2,1,0:T(8,128)(2,1)S(1)}, bf16[2,128,384]{2,1,0:T(8,128)(2,1)S(1)}) custom-call(bf16[32,3072]{1,0:T(8,128)(2,1)} %q_ref.1, bf16[32,3072]{1,0:T(8,128)(2,1)} %k_ref.1, bf16[32,3072]{1,0:T(8,128)(2,1)} %v_ref.1, bf16[32,3072]{1,0:T(8,128)(2,1)} %g_ref.1, bf16[128,384]{1,0:T(8,128)(2,1)} %tq_ref.1, ...), custom_call_target="tpu_custom_call" | custom-call | tf_op jit(solution)/shard_map/pack_inputs/pallas_call | solution.py:55
  3.0 5.8 %all-to-all-start = ((bf16[8,4,32,384]{3,2,1,0:T(8,128)(2,1)}), bf16[8,4,32,384]{3,2,1,0:T(8,128)(2,1)S(1)}, u32[]{:S(2)}, u32[]{:S(2)}) async-start(bf16[8,4,32,384]{3,2,1,0:T(8,128)(2,1)} %get-tuple-element.54), calls=%async_computation | async-start | bytes 1572864 | tf_op jit(solution)/shard_map/all_to_all | solution.py:636
  8.8 2.7 %collective-permute-start.1 = (bf16[2,128,384]{2,1,0:T(8,128)(2,1)S(1)}, bf16[2,128,384]{2,1,0:T(8,128)(2,1)S(1)}, u32[]{:S(2)}, u32[]{:S(2)}) collective-permute-start(bf16[2,128,384]{2,1,0:T(8,128)(2,1)S(1)} %get-tuple-element.67.refs_9_), channel_id=1, source_target_pairs={{0,24},{8,16},{16,8},{24,0},{32,56},{40,48},{48,40},{56,32},{64,88... | collective-permute-start | bytes 589832 | tf_op jit(solution)/shard_map/ppermute | solution.py:610
  11.5 0.0 collective-permute-start
  11.5 3.8 %collective-permute-start.3 = (bf16[2,128,384]{2,1,0:T(8,128)(2,1)S(1)}, bf16[2,128,384]{2,1,0:T(8,128)(2,1)S(1)}, u32[]{:S(2)}, u32[]{:S(2)}) collective-permute-start(bf16[2,128,384]{2,1,0:T(8,128)(2,1)S(1)} %get-tuple-element.59.refs_3_.refs_9_.refs_5_), channel_id=1, source_target_pairs={{0,96},{8,104},{16,112},{24,120},{32,64},{40,72},{48,80},{56,88},{... | collective-permute-start | bytes 589832 | tf_op jit(solution)/shard_map/ppermute | solution.py:610
  15.3 0.0 collective-permute-start.2
  15.3 1.4 %collective-permute-done.1.refs_5_.refs_13_ = bf16[2,128,384]{2,1,0:T(8,128)(2,1)S(1)} collective-permute-done((bf16[2,128,384]{2,1,0:T(8,128)(2,1)S(1)}, bf16[2,128,384]{2,1,0:T(8,128)(2,1)S(1)}, u32[]{:S(2)}, u32[]{:S(2)}) %collective-permute-start.1) | collective-permute-done | bytes 196640 | tf_op jit(solution)/shard_map/ppermute | solution.py:610
  16.6 1.1 collective-permute-done.refs_4_.refs_10_
  17.7 2.5 %collective-permute-done.3.refs_7_.refs_5_ = bf16[2,128,384]{2,1,0:T(8,128)(2,1)S(1)} collective-permute-done((bf16[2,128,384]{2,1,0:T(8,128)(2,1)S(1)}, bf16[2,128,384]{2,1,0:T(8,128)(2,1)S(1)}, u32[]{:S(2)}, u32[]{:S(2)}) %collective-permute-start.3) | collective-permute-done | bytes 196640 | tf_op jit(solution)/shard_map/ppermute | solution.py:610
  20.2 0.8 collective-permute-done.2.refs_6_.refs_4_
  21.0 0.0 copy-done.6
  21.0 0.0 copy-done.10
  21.0 0.0 all-to-all-done.in_ref
  21.1 0.1 assemble_blocks.1
  21.1 0.0 copy-done
  21.1 0.0 copy-start.5
  21.1 2.8 %collective-permute-start.7 = (bf16[2,256,384]{2,1,0:T(8,128)(2,1)S(1)}, bf16[2,256,384]{2,1,0:T(8,128)(2,1)S(1)}, u32[]{:S(2)}, u32[]{:S(2)}) collective-permute-start(bf16[2,256,384]{2,1,0:T(8,128)(2,1)S(1)} %get-tuple-element.62.refs_6_), channel_id=1, source_target_pairs={{0,24},{8,16},{16,8},{24,0},{32,56},{40,48},{48,40},{56,32},{64,88... | collective-permute-start | bytes 1179656 | tf_op jit(solution)/shard_map/ppermute | solution.py:610
  24.0 0.0 collective-permute-start.6
  24.0 3.8 %collective-permute-start.5 = (bf16[2,256,384]{2,1,0:T(8,128)(2,1)S(1)}, bf16[2,256,384]{2,1,0:T(8,128)(2,1)S(1)}, u32[]{:S(2)}, u32[]{:S(2)}) collective-permute-start(bf16[2,256,384]{2,1,0:T(8,128)(2,1)S(1)} %get-tuple-element.58.refs_0_.refs_8_.refs_4_), channel_id=1, source_target_pairs={{0,96},{8,104},{16,112},{24,120},{32,64},{40,72},{48,80},{56,88},{... | collective-permute-start | bytes 1179656 | tf_op jit(solution)/shard_map/ppermute | solution.py:610
  27.7 0.0 collective-permute-start.4
  27.7 3.9 %collective-permute-done.7.refs_1_.refs_8_ = bf16[2,256,384]{2,1,0:T(8,128)(2,1)S(1)} collective-permute-done((bf16[2,256,384]{2,1,0:T(8,128)(2,1)S(1)}, bf16[2,256,384]{2,1,0:T(8,128)(2,1)S(1)}, u32[]{:S(2)}, u32[]{:S(2)}) %collective-permute-start.7) | collective-permute-done | bytes 393248 | tf_op jit(solution)/shard_map/ppermute | solution.py:610
  31.6 1.8 %collective-permute-done.6.refs_0_.refs_7_ = bf16[2,256,384]{2,1,0:T(8,128)(2,1)S(1)} collective-permute-done((bf16[2,256,384]{2,1,0:T(8,128)(2,1)S(1)}, bf16[2,256,384]{2,1,0:T(8,128)(2,1)S(1)}, u32[]{:S(2)}, u32[]{:S(2)}) %collective-permute-start.6) | collective-permute-done | bytes 393248 | tf_op jit(solution)/shard_map/ppermute | solution.py:610
  33.4 2.4 %collective-permute-done.5.refs_3_.refs_2_.refs_5_ = bf16[2,256,384]{2,1,0:T(8,128)(2,1)S(1)} collective-permute-done((bf16[2,256,384]{2,1,0:T(8,128)(2,1)S(1)}, bf16[2,256,384]{2,1,0:T(8,128)(2,1)S(1)}, u32[]{:S(2)}, u32[]{:S(2)}) %collective-permute-start.5) | collective-permute-done | bytes 393248 | tf_op jit(solution)/shard_map/ppermute | solution.py:610
  35.9 0.9 collective-permute-done.4.refs_2_.refs_1_.refs_4_
  36.8 0.0 copy-done.9
  36.8 0.0 copy-done.7
  36.8 0.0 copy-done.8
  36.8 2.1 %hand_on.1 = (bf16[384,384]{1,0:T(8,128)(2,1)S(1)}, bf16[384,384]{1,0:T(8,128)(2,1)S(1)}, bf16[384,384]{1,0:T(8,128)(2,1)}, bf16[384,384]{1,0:T(8,128)(2,1)}) custom-call(bf16[2,256,384]{2,1,0:T(8,128)(2,1)S(1)} %collective-permute-done.6.refs_0_.refs_7_, bf16[2,256,384]{2,1,0:T(8,128)(2,1)S(1)} %collective-permute-done.7.refs_1_.refs_8_, ...), custom_call_target="tpu_custom_call" | custom-call | tf_op jit(solution)/shard_map/hand_on/pallas_call | solution.py:81
  38.9 0.0 copy-done.5
  38.9 0.0 copy-done.1
  38.9 1.6 %collective-permute-start.8 = (bf16[384,384]{1,0:T(8,128)(2,1)}, bf16[384,384]{1,0:T(8,128)(2,1)S(1)}, u32[]{:S(2)}, u32[]{:S(2)}) collective-permute-start(bf16[384,384]{1,0:T(8,128)(2,1)} %get-tuple-element.65), channel_id=1, source_target_pairs={{0,96},{8,104},{16,112},{24,120},{32,64},{40,72},{48,80},{56,88},{... | collective-permute-start | bytes 884744 | tf_op jit(solution)/shard_map/ppermute | solution.py:610
  40.5 0.0 collective-permute-start.9
  40.5 0.7 collective-permute-start.10
  41.2 0.6 collective-permute-start.11
  41.8 6.8 %stats_first.1 = (f32[3,3,1536]{2,1,0:T(4,128)S(1)}, bf16[6,256,384]{2,1,0:T(8,128)(2,1)S(1)}, bf16[6,256,384]{2,1,0:T(8,128)(2,1)S(1)}) custom-call(s32[8]{0:T(128)S(1)} %copy-done.3, s32[8]{0:T(128)S(1)} %copy-done.4, s32[1]{0:T(128)} %bitcast.place_ref, bf16[2,256,384]{2,1,0:T(8,128)(2,1)S(1)} %get-tuple-element.58.refs_0_.refs_8_.refs_4_, ...), custom_call_target="tpu_custom_call" | custom-call | flops 1207959552 | bytes 8388608 | tf_op jit(solution)/shard_map/stats_first/pallas_call | solution.py:520
  48.6 0.0 collective-permute-done.8.refs_6_.refs_2_
  48.6 0.0 collective-permute-done.9.refs_7_.refs_3_
  48.6 0.0 collective-permute-done.10.refs_11_
  48.6 0.0 collective-permute-done.11.refs_12_
  48.6 5.7 %stats_last.1 = (f32[2,3,1536]{2,1,0:T(4,128)S(1)}, bf16[6,256,384]{2,1,0:T(8,128)(2,1)S(1)}, bf16[6,256,384]{2,1,0:T(8,128)(2,1)S(1)}) custom-call(s32[8]{0:T(128)S(1)} %copy-done.3, s32[8]{0:T(128)S(1)} %copy-done.4, s32[1]{0:T(128)} %bitcast.place_ref, bf16[2,256,384]{2,1,0:T(8,128)(2,1)S(1)} %get-tuple-element.58.refs_0_.refs_8_.refs_4_, ...), custom_call_target="tpu_custom_call" | custom-call | flops 805306368 | bytes 8388608 | tf_op jit(solution)/shard_map/stats_last/pallas_call | solution.py:536
  54.3 2.0 %collective-permute-start.14 = (f32[2,3,1536]{2,1,0:T(4,128)S(1)}, f32[2,3,1536]{2,1,0:T(4,128)S(1)}, u32[]{:S(2)}, u32[]{:S(2)}) collective-permute-start(f32[2,3,1536]{2,1,0:T(4,128)S(1)} %get-tuple-element.75.refs_4_), channel_id=1, source_target_pairs={{0,24},{8,16},{16,8},{24,0},{32,56},{40,48},{48,40},{56,32},{64,88... | collective-permute-start | bytes 110600 | tf_op jit(solution)/shard_map/ppermute | solution.py:610
  56.3 0.7 collective-permute-start.13
  57.0 0.6 collective-permute-start.12
  57.7 0.9 collective-permute-done.14.refs_7_
  58.6 2.2 %collective-permute-done.13.refs_6_ = f32[2,3,1536]{2,1,0:T(4,128)S(1)} collective-permute-done((f32[2,3,1536]{2,1,0:T(4,128)S(1)}, f32[2,3,1536]{2,1,0:T(4,128)S(1)}, u32[]{:S(2)}, u32[]{:S(2)}) %collective-permute-start.13) | collective-permute-done | bytes 36896 | tf_op jit(solution)/shard_map/ppermute | solution.py:610
  60.8 0.0 collective-permute-done.12.refs_5_
  60.8 3.3 %grads_far.1 = (bf16[2,384,384]{2,1,0:T(8,128)(2,1)S(1)}, f32[3,128,1536]{2,1,0:T(8,128)S(1)}, f32[2,3,1536]{2,1,0:T(4,128)S(1)}) custom-call(s32[8]{0:T(128)S(1)} %copy-done.3, s32[8]{0:T(128)S(1)} %copy-done.4, s32[1]{0:T(128)} %bitcast.place_ref, bf16[6,256,384]{2,1,0:T(8,128)(2,1)S(1)} %get-tuple-element.73.refs_0_, ...), custom_call_target="tpu_custom_call" | custom-call | flops 1006632960 | bytes 8388608 | tf_op jit(solution)/shard_map/grads_far/pallas_call | solution.py:558
  64.1 3.3 %collective-permute-start.15 = (bf16[2,384,384]{2,1,0:T(8,128)(2,1)S(1)}, bf16[2,384,384]{2,1,0:T(8,128)(2,1)S(1)}, u32[]{:S(2)}, u32[]{:S(2)}) collective-permute-start(bf16[2,384,384]{2,1,0:T(8,128)(2,1)S(1)} %get-tuple-element.86), channel_id=1, source_target_pairs={{0,64},{8,72},{16,80},{24,88},{32,96},{40,104},{48,112},{56,120},{... | collective-permute-start | bytes 1769480 | tf_op jit(solution)/shard_map/ppermute | solution.py:610
  67.3 8.5 %grads_near.1 = (bf16[2,384,384]{2,1,0:T(8,128)(2,1)S(1)}, bf16[2,384,384]{2,1,0:T(8,128)(2,1)S(1)}, bf16[3,128,384]{2,1,0:T(8,128)(2,1)S(1)}, f32[3,128,1536]{2...) custom-call(s32[8]{0:T(128)S(1)} %copy-done.3, ...), custom_call_target="tpu_custom_call" | custom-call | flops 2013265920 | bytes 8388608 | tf_op jit(solution)/shard_map/grads_near/pallas_call | solution.py:571
  75.8 1.4 %collective-permute-start.16 = (bf16[3,128,384]{2,1,0:T(8,128)(2,1)S(1)}, bf16[3,128,384]{2,1,0:T(8,128)(2,1)S(1)}, u32[]{:S(2)}, u32[]{:S(2)}) collective-permute-start(bf16[3,128,384]{2,1,0:T(8,128)(2,1)S(1)} %get-tuple-element.87), channel_id=1, source_target_pairs={{0,16},{8,24},{16,0},{24,8},{32,48},{40,56},{48,32},{56,40},{64,80... | collective-permute-start | bytes 884744 | tf_op jit(solution)/shard_map/ppermute | solution.py:610
  77.2 1.1 collective-permute-start.19
  78.3 2.7 %collective-permute-start.20 = (bf16[2,384,384]{2,1,0:T(8,128)(2,1)S(1)}, bf16[2,384,384]{2,1,0:T(8,128)(2,1)S(1)}, u32[]{:S(2)}, u32[]{:S(2)}) collective-permute-start(bf16[2,384,384]{2,1,0:T(8,128)(2,1)S(1)} %get-tuple-element.94), channel_id=1, source_target_pairs={{0,96},{8,104},{16,112},{24,120},{32,64},{40,72},{48,80},{56,88},{... | collective-permute-start | bytes 1769480 | tf_op jit(solution)/shard_map/ppermute | solution.py:610
  81.1 6.5 %grads_own.1 = (bf16[3,128,384]{2,1,0:T(8,128)(2,1)S(1)}, bf16[3,128,384]{2,1,0:T(8,128)(2,1)S(1)}, bf16[3,128,384]{2,1,0:T(8,128)(2,1)S(1)}, bf16[2,384,384]{2,1,0:T(8,128)(2,1)S(1)}) custom-call(s32[8]{0:T(128)S(1)} %copy-done.3, s32[8]{0:T(128)S(1)} %copy-done.4, s32[1]{0:T(128)} %bitcast.place_ref, bf16[6,256,384]{2,1,0:T(8,128)(2,1)S(1)} %get-tuple-element.73.refs_0_, ...), custom_call_target="tpu_custom_call" | custom-call | flops 1006632960 | bytes 8388608 | tf_op jit(solution)/shard_map/grads_own/pallas_call | solution.py:595
  87.6 0.0 collective-permute-done.16.refs_2_
  87.6 0.0 collective-permute-done.15.refs_6_
  87.6 0.1 collective-permute-start.17
  87.7 1.1 collective-permute-start.18
  88.8 0.0 collective-permute-done.19.refs_5_
  88.8 0.0 collective-permute-done.20.refs_7_
  88.8 4.7 %collective-permute-done.17.refs_1_ = bf16[3,128,384]{2,1,0:T(8,128)(2,1)S(1)} collective-permute-done((bf16[3,128,384]{2,1,0:T(8,128)(2,1)S(1)}, bf16[3,128,384]{2,1,0:T(8,128)(2,1)S(1)}, u32[]{:S(2)}, u32[]{:S(2)}) %collective-permute-start.17) | collective-permute-done | bytes 294944 | tf_op jit(solution)/shard_map/ppermute | solution.py:610
  93.5 1.3 %collective-permute-done.18.refs_3_ = bf16[3,128,384]{2,1,0:T(8,128)(2,1)S(1)} collective-permute-done((bf16[3,128,384]{2,1,0:T(8,128)(2,1)S(1)}, bf16[3,128,384]{2,1,0:T(8,128)(2,1)S(1)}, u32[]{:S(2)}, u32[]{:S(2)}) %collective-permute-start.18) | collective-permute-done | bytes 294944 | tf_op jit(solution)/shard_map/ppermute | solution.py:610
  94.8 1.2 %sum_terms.1 = (bf16[8,3,32,384]{3,2,1,0:T(8,128)(2,1)S(1)}, bf16[128,384]{1,0:T(8,128)(2,1)}, bf16[128,384]{1,0:T(8,128)(2,1)}, bf16[128,384]{1,0:T(8,128)(2,1)}) custom-call(bf16[3,128,384]{2,1,0:T(8,128)(2,1)S(1)} %get-tuple-element.83.refs_0_, bf16[3,128,384]{2,1,0:T(8,128)(2,1)S(1)} %collective-permute-done.17.refs_1_, ...), custom_call_target="tpu_custom_call" | custom-call | tf_op jit(solution)/shard_map/sum_terms/pallas_call | solution.py:120
  96.1 19.5 %all_to_all.10.in_ref = bf16[8,3,32,384]{3,2,1,0:T(8,128)(2,1)S(1)} all-to-all(bf16[8,3,32,384]{3,2,1,0:T(8,128)(2,1)S(1)} %get-tuple-element.95), channel_id=1, replica_groups=mesh['seq'=16,'head'=8] {'head'}, dimensions={0} | all-to-all | bytes 1179648 | tf_op jit(solution)/shard_map/all_to_all | solution.py:657
  115.6 0.9 unpack_video.1
  (13 shorter events, 0.0 us)
Async XLA Ops:
  3.0 18.0 %copy-start.6 = (bf16[2,128,384]{2,1,0:T(8,128)(2,1)}, bf16[2,128,384]{2,1,0:T(8,128)(2,1)S(1)}, u32[]{:S(2)}) copy-start(bf16[2,128,384]{2,1,0:T(8,128)(2,1)S(1)} %get-tuple-element.67.refs_9_) | copy-start | bytes 589828
  3.0 18.2 %copy-start = (bf16[2,128,384]{2,1,0:T(8,128)(2,1)}, bf16[2,128,384]{2,1,0:T(8,128)(2,1)S(1)}, u32[]{:S(2)}) copy-start(bf16[2,128,384]{2,1,0:T(8,128)(2,1)S(1)} %get-tuple-element.59.refs_3_.refs_9_.refs_5_) | copy-start | bytes 589828
  3.0 18.1 %all-to-all-start = ((bf16[8,4,32,384]{3,2,1,0:T(8,128)(2,1)}), bf16[8,4,32,384]{3,2,1,0:T(8,128)(2,1)S(1)}, u32[]{:S(2)}, u32[]{:S(2)}) async-start(bf16[8,4,32,384]{3,2,1,0:T(8,128)(2,1)} %get-tuple-element.54), calls=%async_computation | async-start | bytes 1572864 | tf_op jit(solution)/shard_map/all_to_all | solution.py:636
  8.8 7.9 %collective-permute-start.1 = (bf16[2,128,384]{2,1,0:T(8,128)(2,1)S(1)}, bf16[2,128,384]{2,1,0:T(8,128)(2,1)S(1)}, u32[]{:S(2)}, u32[]{:S(2)}) collective-permute-start(bf16[2,128,384]{2,1,0:T(8,128)(2,1)S(1)} %get-tuple-element.67.refs_9_), channel_id=1, source_target_pairs={{0,24},{8,16},{16,8},{24,0},{32,56},{40,48},{48,40},{56,32},{64,88... | collective-permute-start | bytes 589832 | tf_op jit(solution)/shard_map/ppermute | solution.py:610
  11.5 6.2 %collective-permute-start = (bf16[2,128,384]{2,1,0:T(8,128)(2,1)S(1)}, bf16[2,128,384]{2,1,0:T(8,128)(2,1)S(1)}, u32[]{:S(2)}, u32[]{:S(2)}) collective-permute-start(bf16[2,128,384]{2,1,0:T(8,128)(2,1)S(1)} %get-tuple-element.67.refs_9_), channel_id=1, source_target_pairs={{0,8},{8,0},{16,24},{24,16},{32,40},{40,32},{48,56},{56,48},{64,72... | collective-permute-start | bytes 589832 | tf_op jit(solution)/shard_map/ppermute | solution.py:610
  11.5 8.7 %collective-permute-start.3 = (bf16[2,128,384]{2,1,0:T(8,128)(2,1)S(1)}, bf16[2,128,384]{2,1,0:T(8,128)(2,1)S(1)}, u32[]{:S(2)}, u32[]{:S(2)}) collective-permute-start(bf16[2,128,384]{2,1,0:T(8,128)(2,1)S(1)} %get-tuple-element.59.refs_3_.refs_9_.refs_5_), channel_id=1, source_target_pairs={{0,96},{8,104},{16,112},{24,120},{32,64},{40,72},{48,80},{56,88},{... | collective-permute-start | bytes 589832 | tf_op jit(solution)/shard_map/ppermute | solution.py:610
  15.3 5.7 %collective-permute-start.2 = (bf16[2,128,384]{2,1,0:T(8,128)(2,1)S(1)}, bf16[2,128,384]{2,1,0:T(8,128)(2,1)S(1)}, u32[]{:S(2)}, u32[]{:S(2)}) collective-permute-start(bf16[2,128,384]{2,1,0:T(8,128)(2,1)S(1)} %get-tuple-element.59.refs_3_.refs_9_.refs_5_), channel_id=1, source_target_pairs={{0,32},{8,40},{16,48},{24,56},{32,0},{40,8},{48,16},{56,24},{64,96... | collective-permute-start | bytes 589832 | tf_op jit(solution)/shard_map/ppermute | solution.py:610
  16.6 20.1 %copy-start.9 = (bf16[2,128,384]{2,1,0:T(8,128)(2,1)}, bf16[2,128,384]{2,1,0:T(8,128)(2,1)S(1)}, u32[]{:S(2)}) copy-start(bf16[2,128,384]{2,1,0:T(8,128)(2,1)S(1)} %collective-permute-done.1.refs_5_.refs_13_) | copy-start | bytes 589828
  17.7 3.3 %copy-start.10 = (bf16[2,128,384]{2,1,0:T(8,128)(2,1)}, bf16[2,128,384]{2,1,0:T(8,128)(2,1)S(1)}, u32[]{:S(2)}) copy-start(bf16[2,128,384]{2,1,0:T(8,128)(2,1)S(1)} %collective-permute-done.refs_4_.refs_10_) | copy-start | bytes 589828
  20.2 16.6 %copy-start.7 = (bf16[2,128,384]{2,1,0:T(8,128)(2,1)}, bf16[2,128,384]{2,1,0:T(8,128)(2,1)S(1)}, u32[]{:S(2)}) copy-start(bf16[2,128,384]{2,1,0:T(8,128)(2,1)S(1)} %collective-permute-done.3.refs_7_.refs_5_) | copy-start | bytes 589828
  21.0 15.8 %copy-start.8 = (bf16[2,128,384]{2,1,0:T(8,128)(2,1)}, bf16[2,128,384]{2,1,0:T(8,128)(2,1)S(1)}, u32[]{:S(2)}) copy-start(bf16[2,128,384]{2,1,0:T(8,128)(2,1)S(1)} %collective-permute-done.2.refs_6_.refs_4_) | copy-start | bytes 589828
  21.1 17.7 %copy-start.5 = (bf16[2,256,384]{2,1,0:T(8,128)(2,1)}, bf16[2,256,384]{2,1,0:T(8,128)(2,1)S(1)}, u32[]{:S(2)}) copy-start(bf16[2,256,384]{2,1,0:T(8,128)(2,1)S(1)} %get-tuple-element.62.refs_6_) | copy-start | bytes 1179652
  21.1 10.5 %collective-permute-start.7 = (bf16[2,256,384]{2,1,0:T(8,128)(2,1)S(1)}, bf16[2,256,384]{2,1,0:T(8,128)(2,1)S(1)}, u32[]{:S(2)}, u32[]{:S(2)}) collective-permute-start(bf16[2,256,384]{2,1,0:T(8,128)(2,1)S(1)} %get-tuple-element.62.refs_6_), channel_id=1, source_target_pairs={{0,24},{8,16},{16,8},{24,0},{32,56},{40,48},{48,40},{56,32},{64,88... | collective-permute-start | bytes 1179656 | tf_op jit(solution)/shard_map/ppermute | solution.py:610
  24.0 9.5 %collective-permute-start.6 = (bf16[2,256,384]{2,1,0:T(8,128)(2,1)S(1)}, bf16[2,256,384]{2,1,0:T(8,128)(2,1)S(1)}, u32[]{:S(2)}, u32[]{:S(2)}) collective-permute-start(bf16[2,256,384]{2,1,0:T(8,128)(2,1)S(1)} %get-tuple-element.62.refs_6_), channel_id=1, source_target_pairs={{0,8},{8,0},{16,24},{24,16},{32,40},{40,32},{48,56},{56,48},{64,72... | collective-permute-start | bytes 1179656 | tf_op jit(solution)/shard_map/ppermute | solution.py:610
  24.0 17.8 %copy-start.3 = (s32[8]{0:T(128)S(1)}, s32[8]{0:T(128)}, u32[]{:S(2)}) copy-start(s32[8]{0:T(128)} %length_ref.9) | copy-start | bytes 100
  24.0 17.8 %copy-start.4 = (s32[8]{0:T(128)S(1)}, s32[8]{0:T(128)}, u32[]{:S(2)}) copy-start(s32[8]{0:T(128)} %caption_ref.9) | copy-start | bytes 100
  24.0 11.9 %collective-permute-start.5 = (bf16[2,256,384]{2,1,0:T(8,128)(2,1)S(1)}, bf16[2,256,384]{2,1,0:T(8,128)(2,1)S(1)}, u32[]{:S(2)}, u32[]{:S(2)}) collective-permute-start(bf16[2,256,384]{2,1,0:T(8,128)(2,1)S(1)} %get-tuple-element.58.refs_0_.refs_8_.refs_4_), channel_id=1, source_target_pairs={{0,96},{8,104},{16,112},{24,120},{32,64},{40,72},{48,80},{56,88},{... | collective-permute-start | bytes 1179656 | tf_op jit(solution)/shard_map/ppermute | solution.py:610
  27.7 9.0 %collective-permute-start.4 = (bf16[2,256,384]{2,1,0:T(8,128)(2,1)S(1)}, bf16[2,256,384]{2,1,0:T(8,128)(2,1)S(1)}, u32[]{:S(2)}, u32[]{:S(2)}) collective-permute-start(bf16[2,256,384]{2,1,0:T(8,128)(2,1)S(1)} %get-tuple-element.58.refs_0_.refs_8_.refs_4_), channel_id=1, source_target_pairs={{0,32},{8,40},{16,48},{24,56},{32,0},{40,8},{48,16},{56,24},{64,96... | collective-permute-start | bytes 1179656 | tf_op jit(solution)/shard_map/ppermute | solution.py:610
  31.6 7.2 %copy-start.1 = (bf16[2,256,384]{2,1,0:T(8,128)(2,1)}, bf16[2,256,384]{2,1,0:T(8,128)(2,1)S(1)}, u32[]{:S(2)}) copy-start(bf16[2,256,384]{2,1,0:T(8,128)(2,1)S(1)} %collective-permute-done.7.refs_1_.refs_8_) | copy-start | bytes 1179652
  33.4 5.5 %copy-start.2 = (bf16[2,256,384]{2,1,0:T(8,128)(2,1)}, bf16[2,256,384]{2,1,0:T(8,128)(2,1)S(1)}, u32[]{:S(2)}) copy-start(bf16[2,256,384]{2,1,0:T(8,128)(2,1)S(1)} %collective-permute-done.6.refs_0_.refs_7_) | copy-start | bytes 1179652
  38.9 9.7 %collective-permute-start.8 = (bf16[384,384]{1,0:T(8,128)(2,1)}, bf16[384,384]{1,0:T(8,128)(2,1)S(1)}, u32[]{:S(2)}, u32[]{:S(2)}) collective-permute-start(bf16[384,384]{1,0:T(8,128)(2,1)} %get-tuple-element.65), channel_id=1, source_target_pairs={{0,96},{8,104},{16,112},{24,120},{32,64},{40,72},{48,80},{56,88},{... | collective-permute-start | bytes 884744 | tf_op jit(solution)/shard_map/ppermute | solution.py:610
  40.5 8.1 %collective-permute-start.9 = (bf16[384,384]{1,0:T(8,128)(2,1)}, bf16[384,384]{1,0:T(8,128)(2,1)S(1)}, u32[]{:S(2)}, u32[]{:S(2)}) collective-permute-start(bf16[384,384]{1,0:T(8,128)(2,1)} %get-tuple-element.66), channel_id=1, source_target_pairs={{0,32},{8,40},{16,48},{24,56},{32,0},{40,8},{48,16},{56,24},{64,96... | collective-permute-start | bytes 884744 | tf_op jit(solution)/shard_map/ppermute | solution.py:610
  40.5 8.1 %collective-permute-start.10 = (bf16[384,384]{1,0:T(8,128)(2,1)S(1)}, bf16[384,384]{1,0:T(8,128)(2,1)S(1)}, u32[]{:S(2)}, u32[]{:S(2)}) collective-permute-start(bf16[384,384]{1,0:T(8,128)(2,1)S(1)} %get-tuple-element.71), channel_id=1, source_target_pairs={{0,24},{8,16},{16,8},{24,0},{32,56},{40,48},{48,40},{56,32},{64,88... | collective-permute-start | bytes 884744 | tf_op jit(solution)/shard_map/ppermute | solution.py:610
  41.2 7.5 %collective-permute-start.11 = (bf16[384,384]{1,0:T(8,128)(2,1)S(1)}, bf16[384,384]{1,0:T(8,128)(2,1)S(1)}, u32[]{:S(2)}, u32[]{:S(2)}) collective-permute-start(bf16[384,384]{1,0:T(8,128)(2,1)S(1)} %get-tuple-element.72), channel_id=1, source_target_pairs={{0,8},{8,0},{16,24},{24,16},{32,40},{40,32},{48,56},{56,48},{64,72... | collective-permute-start | bytes 884744 | tf_op jit(solution)/shard_map/ppermute | solution.py:610
  54.3 4.2 %collective-permute-start.14 = (f32[2,3,1536]{2,1,0:T(4,128)S(1)}, f32[2,3,1536]{2,1,0:T(4,128)S(1)}, u32[]{:S(2)}, u32[]{:S(2)}) collective-permute-start(f32[2,3,1536]{2,1,0:T(4,128)S(1)} %get-tuple-element.75.refs_4_), channel_id=1, source_target_pairs={{0,24},{8,16},{16,8},{24,0},{32,56},{40,48},{48,40},{56,32},{64,88... | collective-permute-start | bytes 110600 | tf_op jit(solution)/shard_map/ppermute | solution.py:610
  56.3 4.4 %collective-permute-start.13 = (f32[2,3,1536]{2,1,0:T(4,128)S(1)}, f32[2,3,1536]{2,1,0:T(4,128)S(1)}, u32[]{:S(2)}, u32[]{:S(2)}) collective-permute-start(f32[2,3,1536]{2,1,0:T(4,128)S(1)} %get-tuple-element.75.refs_4_), channel_id=1, source_target_pairs={{0,16},{8,24},{16,0},{24,8},{32,48},{40,56},{48,32},{56,40},{64,80... | collective-permute-start | bytes 110600 | tf_op jit(solution)/shard_map/ppermute | solution.py:610
  57.0 3.7 %collective-permute-start.12 = (f32[2,3,1536]{2,1,0:T(4,128)S(1)}, f32[2,3,1536]{2,1,0:T(4,128)S(1)}, u32[]{:S(2)}, u32[]{:S(2)}) collective-permute-start(f32[2,3,1536]{2,1,0:T(4,128)S(1)} %get-tuple-element.75.refs_4_), channel_id=1, source_target_pairs={{0,8},{8,0},{16,24},{24,16},{32,40},{40,32},{48,56},{56,48},{64,72... | collective-permute-start | bytes 110600 | tf_op jit(solution)/shard_map/ppermute | solution.py:610
  64.1 23.5 %collective-permute-start.15 = (bf16[2,384,384]{2,1,0:T(8,128)(2,1)S(1)}, bf16[2,384,384]{2,1,0:T(8,128)(2,1)S(1)}, u32[]{:S(2)}, u32[]{:S(2)}) collective-permute-start(bf16[2,384,384]{2,1,0:T(8,128)(2,1)S(1)} %get-tuple-element.86), channel_id=1, source_target_pairs={{0,64},{8,72},{16,80},{24,88},{32,96},{40,104},{48,112},{56,120},{... | collective-permute-start | bytes 1769480 | tf_op jit(solution)/shard_map/ppermute | solution.py:610
  75.8 11.7 %collective-permute-start.16 = (bf16[3,128,384]{2,1,0:T(8,128)(2,1)S(1)}, bf16[3,128,384]{2,1,0:T(8,128)(2,1)S(1)}, u32[]{:S(2)}, u32[]{:S(2)}) collective-permute-start(bf16[3,128,384]{2,1,0:T(8,128)(2,1)S(1)} %get-tuple-element.87), channel_id=1, source_target_pairs={{0,16},{8,24},{16,0},{24,8},{32,48},{40,56},{48,32},{56,40},{64,80... | collective-permute-start | bytes 884744 | tf_op jit(solution)/shard_map/ppermute | solution.py:610
  77.2 11.6 %collective-permute-start.19 = (bf16[2,384,384]{2,1,0:T(8,128)(2,1)S(1)}, bf16[2,384,384]{2,1,0:T(8,128)(2,1)S(1)}, u32[]{:S(2)}, u32[]{:S(2)}) collective-permute-start(bf16[2,384,384]{2,1,0:T(8,128)(2,1)S(1)} %get-tuple-element.92), channel_id=1, source_target_pairs={{0,32},{8,40},{16,48},{24,56},{32,0},{40,8},{48,16},{56,24},{64,96... | collective-permute-start | bytes 1769480 | tf_op jit(solution)/shard_map/ppermute | solution.py:610
  78.3 10.5 %collective-permute-start.20 = (bf16[2,384,384]{2,1,0:T(8,128)(2,1)S(1)}, bf16[2,384,384]{2,1,0:T(8,128)(2,1)S(1)}, u32[]{:S(2)}, u32[]{:S(2)}) collective-permute-start(bf16[2,384,384]{2,1,0:T(8,128)(2,1)S(1)} %get-tuple-element.94), channel_id=1, source_target_pairs={{0,96},{8,104},{16,112},{24,120},{32,64},{40,72},{48,80},{56,88},{... | collective-permute-start | bytes 1769480 | tf_op jit(solution)/shard_map/ppermute | solution.py:610
  87.6 5.9 %collective-permute-start.17 = (bf16[3,128,384]{2,1,0:T(8,128)(2,1)S(1)}, bf16[3,128,384]{2,1,0:T(8,128)(2,1)S(1)}, u32[]{:S(2)}, u32[]{:S(2)}) collective-permute-start(bf16[3,128,384]{2,1,0:T(8,128)(2,1)S(1)} %get-tuple-element.88), channel_id=1, source_target_pairs={{0,8},{8,0},{16,24},{24,16},{32,40},{40,32},{48,56},{56,48},{64,72... | collective-permute-start | bytes 884744 | tf_op jit(solution)/shard_map/ppermute | solution.py:610
  87.7 7.2 %collective-permute-start.18 = (bf16[3,128,384]{2,1,0:T(8,128)(2,1)S(1)}, bf16[3,128,384]{2,1,0:T(8,128)(2,1)S(1)}, u32[]{:S(2)}, u32[]{:S(2)}) collective-permute-start(bf16[3,128,384]{2,1,0:T(8,128)(2,1)S(1)} %get-tuple-element.90), channel_id=1, source_target_pairs={{0,24},{8,16},{16,8},{24,0},{32,56},{40,48},{48,40},{56,32},{64,88... | collective-permute-start | bytes 884744 | tf_op jit(solution)/shard_map/ppermute | solution.py:610

commit v8 on v7

--- a/solution.py
+++ b/solution.py
@@ -495,6 +495,10 @@
 KEY_MESSAGE = jax.ShapeDtypeStruct((2, BLOCK + HALF, WIDTH), BF16)
 
 
+def kept(shapes):
+    return [pltpu.VMEM(shape.shape, shape.dtype) for shape in shapes]
+
+
 def terms_shapes(count):
     return [(HEADS_LOCAL, count * BLOCK, HDIM)] * 2 + [(count, HEADS_LOCAL, HALF, HDIM)] * 2
 
@@ -521,7 +525,7 @@
         stats_first_kernel,
         in_specs=[SMEM_SPEC] * 3 + [VMEM_SPEC] * 11,
         out_specs=[VMEM_SPEC] * 3,
-        out_shape=[jax.ShapeDtypeStruct(STATS, F32), STAGED_QUERIES, STAGED_QUERIES],
+        out_shape=kept([jax.ShapeDtypeStruct(STATS, F32), STAGED_QUERIES, STAGED_QUERIES]),
         compiler_params=PARAMS,
         cost_estimate=cost(3, 2),
         name="stats_first",
@@ -537,7 +541,7 @@
         stats_last_kernel,
         in_specs=[SMEM_SPEC] * 3 + [VMEM_SPEC] * 14,
         out_specs=[VMEM_SPEC] * 3,
-        out_shape=[jax.ShapeDtypeStruct((2, HEADS_LOCAL, ROWS), F32), STAGED_QUERIES, STAGED_QUERIES],
+        out_shape=kept([jax.ShapeDtypeStruct((2, HEADS_LOCAL, ROWS), F32), STAGED_QUERIES, STAGED_QUERIES]),
         scratch_shapes=[pltpu.VMEM(STATS, F32)],
         compiler_params=PARAMS,
         cost_estimate=cost(2, 2),
@@ -559,7 +563,9 @@
         grads_far_kernel,
         in_specs=[SMEM_SPEC] * 3 + [VMEM_SPEC] * (4 + SIDE),
         out_specs=[VMEM_SPEC] * 3,
-        out_shape=[KEY_MESSAGE, jax.ShapeDtypeStruct(DQ_T, F32), jax.ShapeDtypeStruct((2, HEADS_LOCAL, ROWS), F32)],
+        out_shape=kept(
+            [KEY_MESSAGE, jax.ShapeDtypeStruct(DQ_T, F32), jax.ShapeDtypeStruct((2, HEADS_LOCAL, ROWS), F32)]
+        ),
         scratch_shapes=terms_scratch(1) + work_scratch(1, SIDE),
         compiler_params=PARAMS,
         cost_estimate=cost(1, 5),
@@ -572,18 +578,18 @@
         grads_near_kernel,
         in_specs=[SMEM_SPEC] * 3 + [VMEM_SPEC] * 10,
         out_specs=[VMEM_SPEC] * 8,
-        out_shape=[KEY_MESSAGE] * 2
-        + [DQ_MESSAGE, jax.ShapeDtypeStruct(DQ_T, F32)]
-        + [jax.ShapeDtypeStruct(shape, F32) for shape in terms_shapes(1)],
+        out_shape=kept(
+            [KEY_MESSAGE] * 2
+            + [DQ_MESSAGE, jax.ShapeDtypeStruct(DQ_T, F32)]
+            + [jax.ShapeDtypeStruct(shape, F32) for shape in terms_shapes(1)]
+        ),
         scratch_shapes=terms_scratch(2) + work_scratch(2, SIDE) + work_scratch(1, 1),
         compiler_params=PARAMS,
         cost_estimate=cost(2, 5),
         name="grads_near",
     )(
         *scalars,
-        *placed(queries),
-        dq_t,
-        *placed([norm, kv[1], kv[3]]),
+        *placed([*queries, dq_t, norm, kv[1], kv[3]]),
         *placed([text_kv[1], text_kv[3]], pltpu.HBM),
         *placed([kv[0]]),
         *placed([text_kv[0]], pltpu.HBM),
@@ -596,12 +602,12 @@
         grads_own_kernel,
         in_specs=[SMEM_SPEC] * 3 + [VMEM_SPEC] * 10,
         out_specs=[VMEM_SPEC] * 4,
-        out_shape=[DQ_MESSAGE] * 3 + [KEY_MESSAGE],
+        out_shape=kept([DQ_MESSAGE] * 3 + [KEY_MESSAGE]),
         scratch_shapes=[pltpu.VMEM(DQ_T, F32)] + terms_scratch(1) + work_scratch(1, 3),
         compiler_params=PARAMS,
         cost_estimate=cost(1, 5),
         name="grads_own",
-    )(*scalars, *placed(queries), dq_t, *placed([norm, kv[0]]), *placed([text_kv[0]], pltpu.HBM), *terms)
+    )(*scalars, *placed([*queries, dq_t, norm, kv[0]]), *placed([text_kv[0]], pltpu.HBM), *placed(terms))
     return out[:3], out[3]
 
 

time: 117 us -> 117 us (level)
  starting transfers between devices: 34.8 us -> 31.3 us
  Pallas kernels: 37.4 us -> 39.6 us
    ppermute x21, starting transfers between devices: 29 us -> 25.5 us  [swap(): lax.ppermute(array, 'seq', [(i, i ^ shift) for i in range(SIDE * SIDE)])]
    pallas_call x1, Pallas kernels: 8.52 us -> 10.8 us  [grads_near_call(): pl.pallas_call(grads_near_kernel, in_specs=[SMEM_SPEC] * 3 + [VMEM_SPEC]...]
  transfers between devices with their start and end apart: 22 -> 22, of which waited for: 12 -> 15; matrix products, arithmetic and copies ran while one was open for 0% -> 0% of each run, Pallas kernels for 19% -> 20%
where the time goes in v8:
time: 117 us
  Pallas kernels  39.6 us (34%)
  starting transfers between devices  31.3 us (27%)
  waiting for transfers between devices  25.1 us (21%)
  blocking collectives  20.3 us (17%)
    ppermute x21, starting transfers between devices, swap(): lax.ppermute(array, 'seq', [(i, i ^ shift) for i in range(SIDE * SIDE)])  25.5 us
    ppermute x21, waiting for transfers between devices, swap(): lax.ppermute(array, 'seq', [(i, i ^ shift) for i in range(SIDE * SIDE)])  25.1 us
    all_to_all x1, blocking collectives, on_device(): lax.all_to_all(video, 'head', split_axis=0, concat_axis=0)  20.3 us
    pallas_call x1, Pallas kernels, grads_near_call(): pl.pallas_call(grads_near_kernel, in_specs=[SMEM_SPEC] * 3 + [VMEM_SPEC]...  10.8 us
    pallas_call x1, Pallas kernels, stats_first_call(): pl.pallas_call(stats_first_kernel, in_specs=[SMEM_SPEC] * 3 + [VMEM_SPEC]...  7.12 us
    pallas_call x1, Pallas kernels, stats_last_call(): pl.pallas_call(stats_last_kernel, in_specs=[SMEM_SPEC] * 3 + [VMEM_SPEC]...  6.04 us
    all_to_all x1, starting transfers between devices, on_device(): arrived = lax.all_to_all(packed, 'head', split_axis=0, concat_axis=0)  5.8 us
    pallas_call x1, Pallas kernels, grads_own_call(): pl.pallas_call(grads_own_kernel, in_specs=[SMEM_SPEC] * 3 + [VMEM_SPEC] *...  5.75 us
  transfers between devices with their start and end apart: 22, of which 15 were waited for; matrix products, arithmetic and copies ran while one was open for 0% of the time, Pallas kernels for 20%

profile of v8, /device:TPU:1, one launch (start us, length us, event | category | flops | bytes accessed | tf_op | source)
XLA Modules:
  0.0 117.2 jit_solution(11875590605977574529)
XLA Ops:
  0.6 2.3 %pack_inputs.1 = (bf16[8,4,32,384]{3,2,1,0:T(8,128)(2,1)}, bf16[2,128,384]{2,1,0:T(8,128)(2,1)S(1)}, bf16[2,128,384]{2,1,0:T(8,128)(2,1)S(1)}) custom-call(bf16[32,3072]{1,0:T(8,128)(2,1)} %q_ref.1, bf16[32,3072]{1,0:T(8,128)(2,1)} %k_ref.1, bf16[32,3072]{1,0:T(8,128)(2,1)} %v_ref.1, bf16[32,3072]{1,0:T(8,128)(2,1)} %g_ref.1, bf16[128,384]{1,0:T(8,128)(2,1)} %tq_ref.1, ...), custom_call_target="tpu_custom_call" | custom-call | tf_op jit(solution)/shard_map/pack_inputs/pallas_call | solution.py:55
  3.0 5.8 %all-to-all-start = ((bf16[8,4,32,384]{3,2,1,0:T(8,128)(2,1)}), bf16[8,4,32,384]{3,2,1,0:T(8,128)(2,1)S(1)}, u32[]{:S(2)}, u32[]{:S(2)}) async-start(bf16[8,4,32,384]{3,2,1,0:T(8,128)(2,1)} %get-tuple-element.54), calls=%async_computation | async-start | bytes 1572864 | tf_op jit(solution)/shard_map/all_to_all | solution.py:642
  8.8 2.7 %collective-permute-start.1 = (bf16[2,128,384]{2,1,0:T(8,128)(2,1)S(1)}, bf16[2,128,384]{2,1,0:T(8,128)(2,1)S(1)}, u32[]{:S(2)}, u32[]{:S(2)}) collective-permute-start(bf16[2,128,384]{2,1,0:T(8,128)(2,1)S(1)} %get-tuple-element.67.refs_9_), channel_id=1, source_target_pairs={{0,24},{8,16},{16,8},{24,0},{32,56},{40,48},{48,40},{56,32},{64,88... | collective-permute-start | bytes 589832 | tf_op jit(solution)/shard_map/ppermute | solution.py:616
  11.5 0.0 collective-permute-start
  11.5 3.8 %collective-permute-start.3 = (bf16[2,128,384]{2,1,0:T(8,128)(2,1)S(1)}, bf16[2,128,384]{2,1,0:T(8,128)(2,1)S(1)}, u32[]{:S(2)}, u32[]{:S(2)}) collective-permute-start(bf16[2,128,384]{2,1,0:T(8,128)(2,1)S(1)} %get-tuple-element.59.refs_3_.refs_9_.refs_5_), channel_id=1, source_target_pairs={{0,96},{8,104},{16,112},{24,120},{32,64},{40,72},{48,80},{56,88},{... | collective-permute-start | bytes 589832 | tf_op jit(solution)/shard_map/ppermute | solution.py:616
  15.3 0.0 collective-permute-start.2
  15.3 1.4 %collective-permute-done.1.refs_5_.refs_13_ = bf16[2,128,384]{2,1,0:T(8,128)(2,1)S(1)} collective-permute-done((bf16[2,128,384]{2,1,0:T(8,128)(2,1)S(1)}, bf16[2,128,384]{2,1,0:T(8,128)(2,1)S(1)}, u32[]{:S(2)}, u32[]{:S(2)}) %collective-permute-start.1) | collective-permute-done | bytes 196640 | tf_op jit(solution)/shard_map/ppermute | solution.py:616
  16.6 1.1 collective-permute-done.refs_4_.refs_10_
  17.7 2.5 %collective-permute-done.3.refs_7_.refs_5_ = bf16[2,128,384]{2,1,0:T(8,128)(2,1)S(1)} collective-permute-done((bf16[2,128,384]{2,1,0:T(8,128)(2,1)S(1)}, bf16[2,128,384]{2,1,0:T(8,128)(2,1)S(1)}, u32[]{:S(2)}, u32[]{:S(2)}) %collective-permute-start.3) | collective-permute-done | bytes 196640 | tf_op jit(solution)/shard_map/ppermute | solution.py:616
  20.2 0.8 collective-permute-done.2.refs_6_.refs_4_
  21.0 0.0 copy-done.6
  21.0 0.0 copy-done.10
  21.0 0.0 all-to-all-done.in_ref
  21.1 0.1 assemble_blocks.1
  21.1 0.0 copy-done
  21.1 0.0 copy-start.5
  21.1 2.8 %collective-permute-start.7 = (bf16[2,256,384]{2,1,0:T(8,128)(2,1)S(1)}, bf16[2,256,384]{2,1,0:T(8,128)(2,1)S(1)}, u32[]{:S(2)}, u32[]{:S(2)}) collective-permute-start(bf16[2,256,384]{2,1,0:T(8,128)(2,1)S(1)} %get-tuple-element.62.refs_6_), channel_id=1, source_target_pairs={{0,24},{8,16},{16,8},{24,0},{32,56},{40,48},{48,40},{56,32},{64,88... | collective-permute-start | bytes 1179656 | tf_op jit(solution)/shard_map/ppermute | solution.py:616
  24.0 0.0 collective-permute-start.6
  24.0 3.8 %collective-permute-start.5 = (bf16[2,256,384]{2,1,0:T(8,128)(2,1)S(1)}, bf16[2,256,384]{2,1,0:T(8,128)(2,1)S(1)}, u32[]{:S(2)}, u32[]{:S(2)}) collective-permute-start(bf16[2,256,384]{2,1,0:T(8,128)(2,1)S(1)} %get-tuple-element.58.refs_0_.refs_8_.refs_4_), channel_id=1, source_target_pairs={{0,96},{8,104},{16,112},{24,120},{32,64},{40,72},{48,80},{56,88},{... | collective-permute-start | bytes 1179656 | tf_op jit(solution)/shard_map/ppermute | solution.py:616
  27.7 0.0 collective-permute-start.4
  27.7 3.9 %collective-permute-done.7.refs_1_.refs_8_ = bf16[2,256,384]{2,1,0:T(8,128)(2,1)S(1)} collective-permute-done((bf16[2,256,384]{2,1,0:T(8,128)(2,1)S(1)}, bf16[2,256,384]{2,1,0:T(8,128)(2,1)S(1)}, u32[]{:S(2)}, u32[]{:S(2)}) %collective-permute-start.7) | collective-permute-done | bytes 393248 | tf_op jit(solution)/shard_map/ppermute | solution.py:616
  31.6 1.8 %collective-permute-done.6.refs_0_.refs_7_ = bf16[2,256,384]{2,1,0:T(8,128)(2,1)S(1)} collective-permute-done((bf16[2,256,384]{2,1,0:T(8,128)(2,1)S(1)}, bf16[2,256,384]{2,1,0:T(8,128)(2,1)S(1)}, u32[]{:S(2)}, u32[]{:S(2)}) %collective-permute-start.6) | collective-permute-done | bytes 393248 | tf_op jit(solution)/shard_map/ppermute | solution.py:616
  33.4 2.4 %collective-permute-done.5.refs_3_.refs_2_.refs_5_ = bf16[2,256,384]{2,1,0:T(8,128)(2,1)S(1)} collective-permute-done((bf16[2,256,384]{2,1,0:T(8,128)(2,1)S(1)}, bf16[2,256,384]{2,1,0:T(8,128)(2,1)S(1)}, u32[]{:S(2)}, u32[]{:S(2)}) %collective-permute-start.5) | collective-permute-done | bytes 393248 | tf_op jit(solution)/shard_map/ppermute | solution.py:616
  35.9 0.9 collective-permute-done.4.refs_2_.refs_1_.refs_4_
  36.8 0.0 copy-done.9
  36.8 0.0 copy-done.7
  36.8 0.0 copy-done.8
  36.8 2.1 %hand_on.1 = (bf16[384,384]{1,0:T(8,128)(2,1)S(1)}, bf16[384,384]{1,0:T(8,128)(2,1)S(1)}, bf16[384,384]{1,0:T(8,128)(2,1)}, bf16[384,384]{1,0:T(8,128)(2,1)}) custom-call(bf16[2,256,384]{2,1,0:T(8,128)(2,1)S(1)} %collective-permute-done.6.refs_0_.refs_7_, bf16[2,256,384]{2,1,0:T(8,128)(2,1)S(1)} %collective-permute-done.7.refs_1_.refs_8_, ...), custom_call_target="tpu_custom_call" | custom-call | tf_op jit(solution)/shard_map/hand_on/pallas_call | solution.py:81
  38.9 0.0 copy-done.5
  38.9 0.0 copy-done.1
  38.9 1.6 %collective-permute-start.8 = (bf16[384,384]{1,0:T(8,128)(2,1)}, bf16[384,384]{1,0:T(8,128)(2,1)S(1)}, u32[]{:S(2)}, u32[]{:S(2)}) collective-permute-start(bf16[384,384]{1,0:T(8,128)(2,1)} %get-tuple-element.65), channel_id=1, source_target_pairs={{0,96},{8,104},{16,112},{24,120},{32,64},{40,72},{48,80},{56,88},{... | collective-permute-start | bytes 884744 | tf_op jit(solution)/shard_map/ppermute | solution.py:616
  40.5 0.0 collective-permute-start.9
  40.5 0.7 collective-permute-start.10
  41.2 0.6 collective-permute-start.11
  41.8 7.1 %stats_first.1 = (f32[3,3,1536]{2,1,0:T(4,128)S(1)}, bf16[6,256,384]{2,1,0:T(8,128)(2,1)S(1)}, bf16[6,256,384]{2,1,0:T(8,128)(2,1)S(1)}) custom-call(s32[8]{0:T(128)S(1)} %copy-done.3, s32[8]{0:T(128)S(1)} %copy-done.4, s32[1]{0:T(128)} %bitcast.place_ref, bf16[2,256,384]{2,1,0:T(8,128)(2,1)S(1)} %get-tuple-element.58.refs_0_.refs_8_.refs_4_, ...), custom_call_target="tpu_custom_call" | custom-call | flops 1207959552 | bytes 8388608 | tf_op jit(solution)/shard_map/stats_first/pallas_call | solution.py:524
  48.9 0.0 collective-permute-done.8.refs_6_.refs_2_
  48.9 0.0 collective-permute-done.9.refs_7_.refs_3_
  48.9 0.0 collective-permute-done.10.refs_11_
  49.0 0.0 collective-permute-done.11.refs_12_
  49.0 6.0 %stats_last.1 = (f32[2,3,1536]{2,1,0:T(4,128)S(1)}, bf16[6,256,384]{2,1,0:T(8,128)(2,1)S(1)}, bf16[6,256,384]{2,1,0:T(8,128)(2,1)S(1)}) custom-call(s32[8]{0:T(128)S(1)} %copy-done.3, s32[8]{0:T(128)S(1)} %copy-done.4, s32[1]{0:T(128)} %bitcast.place_ref, bf16[2,256,384]{2,1,0:T(8,128)(2,1)S(1)} %get-tuple-element.58.refs_0_.refs_8_.refs_4_, ...), custom_call_target="tpu_custom_call" | custom-call | flops 805306368 | bytes 8388608 | tf_op jit(solution)/shard_map/stats_last/pallas_call | solution.py:540
  55.0 0.5 collective-permute-start.14
  55.5 1.7 %collective-permute-start.13 = (f32[2,3,1536]{2,1,0:T(4,128)S(1)}, f32[2,3,1536]{2,1,0:T(4,128)S(1)}, u32[]{:S(2)}, u32[]{:S(2)}) collective-permute-start(f32[2,3,1536]{2,1,0:T(4,128)S(1)} %get-tuple-element.75.refs_4_), channel_id=1, source_target_pairs={{0,16},{8,24},{16,0},{24,8},{32,48},{40,56},{48,32},{56,40},{64,80... | collective-permute-start | bytes 110600 | tf_op jit(solution)/shard_map/ppermute | solution.py:616
  57.2 1.1 collective-permute-start.12
  58.3 0.9 collective-permute-done.14.refs_7_
  59.2 0.7 collective-permute-done.13.refs_6_
  60.0 0.4 collective-permute-done.12.refs_5_
  60.3 3.3 %grads_far.1 = (bf16[2,384,384]{2,1,0:T(8,128)(2,1)S(1)}, f32[3,128,1536]{2,1,0:T(8,128)S(1)}, f32[2,3,1536]{2,1,0:T(4,128)S(1)}) custom-call(s32[8]{0:T(128)S(1)} %copy-done.3, s32[8]{0:T(128)S(1)} %copy-done.4, s32[1]{0:T(128)} %bitcast.place_ref, bf16[6,256,384]{2,1,0:T(8,128)(2,1)S(1)} %get-tuple-element.73.refs_0_, ...), custom_call_target="tpu_custom_call" | custom-call | flops 1006632960 | bytes 8388608 | tf_op jit(solution)/shard_map/grads_far/pallas_call | solution.py:562
  63.6 2.9 %collective-permute-start.15 = (bf16[2,384,384]{2,1,0:T(8,128)(2,1)S(1)}, bf16[2,384,384]{2,1,0:T(8,128)(2,1)S(1)}, u32[]{:S(2)}, u32[]{:S(2)}) collective-permute-start(bf16[2,384,384]{2,1,0:T(8,128)(2,1)S(1)} %get-tuple-element.86), channel_id=1, source_target_pairs={{0,64},{8,72},{16,80},{24,88},{32,96},{40,104},{48,112},{56,120},{... | collective-permute-start | bytes 1769480 | tf_op jit(solution)/shard_map/ppermute | solution.py:616
  66.5 10.8 %grads_near.1 = (bf16[2,384,384]{2,1,0:T(8,128)(2,1)S(1)}, bf16[2,384,384]{2,1,0:T(8,128)(2,1)S(1)}, bf16[3,128,384]{2,1,0:T(8,128)(2,1)S(1)}, f32[3,128,1536]{2...) custom-call(s32[8]{0:T(128)S(1)} %copy-done.3, ...), custom_call_target="tpu_custom_call" | custom-call | flops 2013265920 | bytes 8388608 | tf_op jit(solution)/shard_map/grads_near/pallas_call | solution.py:577
  77.3 0.1 collective-permute-start.16
  77.4 1.0 collective-permute-start.19
  78.4 2.0 %collective-permute-start.20 = (bf16[2,384,384]{2,1,0:T(8,128)(2,1)S(1)}, bf16[2,384,384]{2,1,0:T(8,128)(2,1)S(1)}, u32[]{:S(2)}, u32[]{:S(2)}) collective-permute-start(bf16[2,384,384]{2,1,0:T(8,128)(2,1)S(1)} %get-tuple-element.94), channel_id=1, source_target_pairs={{0,96},{8,104},{16,112},{24,120},{32,64},{40,72},{48,80},{56,88},{... | collective-permute-start | bytes 1769480 | tf_op jit(solution)/shard_map/ppermute | solution.py:616
  80.5 5.8 %grads_own.1 = (bf16[3,128,384]{2,1,0:T(8,128)(2,1)S(1)}, bf16[3,128,384]{2,1,0:T(8,128)(2,1)S(1)}, bf16[3,128,384]{2,1,0:T(8,128)(2,1)S(1)}, bf16[2,384,384]{2,1,0:T(8,128)(2,1)S(1)}) custom-call(s32[8]{0:T(128)S(1)} %copy-done.3, s32[8]{0:T(128)S(1)} %copy-done.4, s32[1]{0:T(128)} %bitcast.place_ref, bf16[6,256,384]{2,1,0:T(8,128)(2,1)S(1)} %get-tuple-element.73.refs_0_, ...), custom_call_target="tpu_custom_call" | custom-call | flops 1006632960 | bytes 8388608 | tf_op jit(solution)/shard_map/grads_own/pallas_call | solution.py:601
  86.2 0.0 collective-permute-done.16.refs_2_
  86.3 0.0 collective-permute-done.15.refs_6_
  86.3 0.1 collective-permute-start.17
  86.4 0.1 collective-permute-start.18
  86.4 0.6 collective-permute-done.19.refs_5_
  87.1 1.6 %collective-permute-done.20.refs_7_ = bf16[2,384,384]{2,1,0:T(8,128)(2,1)S(1)} collective-permute-done((bf16[2,384,384]{2,1,0:T(8,128)(2,1)S(1)}, bf16[2,384,384]{2,1,0:T(8,128)(2,1)S(1)}, u32[]{:S(2)}, u32[]{:S(2)}) %collective-permute-start.20) | collective-permute-done | bytes 589856 | tf_op jit(solution)/shard_map/ppermute | solution.py:616
  88.7 3.5 %collective-permute-done.17.refs_1_ = bf16[3,128,384]{2,1,0:T(8,128)(2,1)S(1)} collective-permute-done((bf16[3,128,384]{2,1,0:T(8,128)(2,1)S(1)}, bf16[3,128,384]{2,1,0:T(8,128)(2,1)S(1)}, u32[]{:S(2)}, u32[]{:S(2)}) %collective-permute-start.17) | collective-permute-done | bytes 294944 | tf_op jit(solution)/shard_map/ppermute | solution.py:616
  92.2 2.5 %collective-permute-done.18.refs_3_ = bf16[3,128,384]{2,1,0:T(8,128)(2,1)S(1)} collective-permute-done((bf16[3,128,384]{2,1,0:T(8,128)(2,1)S(1)}, bf16[3,128,384]{2,1,0:T(8,128)(2,1)S(1)}, u32[]{:S(2)}, u32[]{:S(2)}) %collective-permute-start.18) | collective-permute-done | bytes 294944 | tf_op jit(solution)/shard_map/ppermute | solution.py:616
  94.7 1.2 %sum_terms.1 = (bf16[8,3,32,384]{3,2,1,0:T(8,128)(2,1)S(1)}, bf16[128,384]{1,0:T(8,128)(2,1)}, bf16[128,384]{1,0:T(8,128)(2,1)}, bf16[128,384]{1,0:T(8,128)(2,1)}) custom-call(bf16[3,128,384]{2,1,0:T(8,128)(2,1)S(1)} %get-tuple-element.83.refs_0_, bf16[3,128,384]{2,1,0:T(8,128)(2,1)S(1)} %collective-permute-done.17.refs_1_, ...), custom_call_target="tpu_custom_call" | custom-call | tf_op jit(solution)/shard_map/sum_terms/pallas_call | solution.py:120
  96.0 20.3 %all_to_all.10.in_ref = bf16[8,3,32,384]{3,2,1,0:T(8,128)(2,1)S(1)} all-to-all(bf16[8,3,32,384]{3,2,1,0:T(8,128)(2,1)S(1)} %get-tuple-element.95), channel_id=1, replica_groups=mesh['seq'=16,'head'=8] {'head'}, dimensions={0} | all-to-all | bytes 1179648 | tf_op jit(solution)/shard_map/all_to_all | solution.py:663
  116.3 0.9 unpack_video.1
  (13 shorter events, 0.0 us)
Async XLA Ops:
  3.0 18.0 %copy-start.6 = (bf16[2,128,384]{2,1,0:T(8,128)(2,1)}, bf16[2,128,384]{2,1,0:T(8,128)(2,1)S(1)}, u32[]{:S(2)}) copy-start(bf16[2,128,384]{2,1,0:T(8,128)(2,1)S(1)} %get-tuple-element.67.refs_9_) | copy-start | bytes 589828
  3.0 18.2 %copy-start = (bf16[2,128,384]{2,1,0:T(8,128)(2,1)}, bf16[2,128,384]{2,1,0:T(8,128)(2,1)S(1)}, u32[]{:S(2)}) copy-start(bf16[2,128,384]{2,1,0:T(8,128)(2,1)S(1)} %get-tuple-element.59.refs_3_.refs_9_.refs_5_) | copy-start | bytes 589828
  3.0 18.1 %all-to-all-start = ((bf16[8,4,32,384]{3,2,1,0:T(8,128)(2,1)}), bf16[8,4,32,384]{3,2,1,0:T(8,128)(2,1)S(1)}, u32[]{:S(2)}, u32[]{:S(2)}) async-start(bf16[8,4,32,384]{3,2,1,0:T(8,128)(2,1)} %get-tuple-element.54), calls=%async_computation | async-start | bytes 1572864 | tf_op jit(solution)/shard_map/all_to_all | solution.py:642
  8.8 7.9 %collective-permute-start.1 = (bf16[2,128,384]{2,1,0:T(8,128)(2,1)S(1)}, bf16[2,128,384]{2,1,0:T(8,128)(2,1)S(1)}, u32[]{:S(2)}, u32[]{:S(2)}) collective-permute-start(bf16[2,128,384]{2,1,0:T(8,128)(2,1)S(1)} %get-tuple-element.67.refs_9_), channel_id=1, source_target_pairs={{0,24},{8,16},{16,8},{24,0},{32,56},{40,48},{48,40},{56,32},{64,88... | collective-permute-start | bytes 589832 | tf_op jit(solution)/shard_map/ppermute | solution.py:616
  11.5 6.2 %collective-permute-start = (bf16[2,128,384]{2,1,0:T(8,128)(2,1)S(1)}, bf16[2,128,384]{2,1,0:T(8,128)(2,1)S(1)}, u32[]{:S(2)}, u32[]{:S(2)}) collective-permute-start(bf16[2,128,384]{2,1,0:T(8,128)(2,1)S(1)} %get-tuple-element.67.refs_9_), channel_id=1, source_target_pairs={{0,8},{8,0},{16,24},{24,16},{32,40},{40,32},{48,56},{56,48},{64,72... | collective-permute-start | bytes 589832 | tf_op jit(solution)/shard_map/ppermute | solution.py:616
  11.5 8.7 %collective-permute-start.3 = (bf16[2,128,384]{2,1,0:T(8,128)(2,1)S(1)}, bf16[2,128,384]{2,1,0:T(8,128)(2,1)S(1)}, u32[]{:S(2)}, u32[]{:S(2)}) collective-permute-start(bf16[2,128,384]{2,1,0:T(8,128)(2,1)S(1)} %get-tuple-element.59.refs_3_.refs_9_.refs_5_), channel_id=1, source_target_pairs={{0,96},{8,104},{16,112},{24,120},{32,64},{40,72},{48,80},{56,88},{... | collective-permute-start | bytes 589832 | tf_op jit(solution)/shard_map/ppermute | solution.py:616
  15.3 5.7 %collective-permute-start.2 = (bf16[2,128,384]{2,1,0:T(8,128)(2,1)S(1)}, bf16[2,128,384]{2,1,0:T(8,128)(2,1)S(1)}, u32[]{:S(2)}, u32[]{:S(2)}) collective-permute-start(bf16[2,128,384]{2,1,0:T(8,128)(2,1)S(1)} %get-tuple-element.59.refs_3_.refs_9_.refs_5_), channel_id=1, source_target_pairs={{0,32},{8,40},{16,48},{24,56},{32,0},{40,8},{48,16},{56,24},{64,96... | collective-permute-start | bytes 589832 | tf_op jit(solution)/shard_map/ppermute | solution.py:616
  16.6 20.1 %copy-start.9 = (bf16[2,128,384]{2,1,0:T(8,128)(2,1)}, bf16[2,128,384]{2,1,0:T(8,128)(2,1)S(1)}, u32[]{:S(2)}) copy-start(bf16[2,128,384]{2,1,0:T(8,128)(2,1)S(1)} %collective-permute-done.1.refs_5_.refs_13_) | copy-start | bytes 589828
  17.7 3.3 %copy-start.10 = (bf16[2,128,384]{2,1,0:T(8,128)(2,1)}, bf16[2,128,384]{2,1,0:T(8,128)(2,1)S(1)}, u32[]{:S(2)}) copy-start(bf16[2,128,384]{2,1,0:T(8,128)(2,1)S(1)} %collective-permute-done.refs_4_.refs_10_) | copy-start | bytes 589828
  20.2 16.6 %copy-start.7 = (bf16[2,128,384]{2,1,0:T(8,128)(2,1)}, bf16[2,128,384]{2,1,0:T(8,128)(2,1)S(1)}, u32[]{:S(2)}) copy-start(bf16[2,128,384]{2,1,0:T(8,128)(2,1)S(1)} %collective-permute-done.3.refs_7_.refs_5_) | copy-start | bytes 589828
  21.0 15.8 %copy-start.8 = (bf16[2,128,384]{2,1,0:T(8,128)(2,1)}, bf16[2,128,384]{2,1,0:T(8,128)(2,1)S(1)}, u32[]{:S(2)}) copy-start(bf16[2,128,384]{2,1,0:T(8,128)(2,1)S(1)} %collective-permute-done.2.refs_6_.refs_4_) | copy-start | bytes 589828
  21.1 17.7 %copy-start.5 = (bf16[2,256,384]{2,1,0:T(8,128)(2,1)}, bf16[2,256,384]{2,1,0:T(8,128)(2,1)S(1)}, u32[]{:S(2)}) copy-start(bf16[2,256,384]{2,1,0:T(8,128)(2,1)S(1)} %get-tuple-element.62.refs_6_) | copy-start | bytes 1179652
  21.1 10.5 %collective-permute-start.7 = (bf16[2,256,384]{2,1,0:T(8,128)(2,1)S(1)}, bf16[2,256,384]{2,1,0:T(8,128)(2,1)S(1)}, u32[]{:S(2)}, u32[]{:S(2)}) collective-permute-start(bf16[2,256,384]{2,1,0:T(8,128)(2,1)S(1)} %get-tuple-element.62.refs_6_), channel_id=1, source_target_pairs={{0,24},{8,16},{16,8},{24,0},{32,56},{40,48},{48,40},{56,32},{64,88... | collective-permute-start | bytes 1179656 | tf_op jit(solution)/shard_map/ppermute | solution.py:616
  24.0 9.5 %collective-permute-start.6 = (bf16[2,256,384]{2,1,0:T(8,128)(2,1)S(1)}, bf16[2,256,384]{2,1,0:T(8,128)(2,1)S(1)}, u32[]{:S(2)}, u32[]{:S(2)}) collective-permute-start(bf16[2,256,384]{2,1,0:T(8,128)(2,1)S(1)} %get-tuple-element.62.refs_6_), channel_id=1, source_target_pairs={{0,8},{8,0},{16,24},{24,16},{32,40},{40,32},{48,56},{56,48},{64,72... | collective-permute-start | bytes 1179656 | tf_op jit(solution)/shard_map/ppermute | solution.py:616
  24.0 17.8 %copy-start.3 = (s32[8]{0:T(128)S(1)}, s32[8]{0:T(128)}, u32[]{:S(2)}) copy-start(s32[8]{0:T(128)} %length_ref.9) | copy-start | bytes 100
  24.0 17.8 %copy-start.4 = (s32[8]{0:T(128)S(1)}, s32[8]{0:T(128)}, u32[]{:S(2)}) copy-start(s32[8]{0:T(128)} %caption_ref.9) | copy-start | bytes 100
  24.0 11.9 %collective-permute-start.5 = (bf16[2,256,384]{2,1,0:T(8,128)(2,1)S(1)}, bf16[2,256,384]{2,1,0:T(8,128)(2,1)S(1)}, u32[]{:S(2)}, u32[]{:S(2)}) collective-permute-start(bf16[2,256,384]{2,1,0:T(8,128)(2,1)S(1)} %get-tuple-element.58.refs_0_.refs_8_.refs_4_), channel_id=1, source_target_pairs={{0,96},{8,104},{16,112},{24,120},{32,64},{40,72},{48,80},{56,88},{... | collective-permute-start | bytes 1179656 | tf_op jit(solution)/shard_map/ppermute | solution.py:616
  27.7 9.0 %collective-permute-start.4 = (bf16[2,256,384]{2,1,0:T(8,128)(2,1)S(1)}, bf16[2,256,384]{2,1,0:T(8,128)(2,1)S(1)}, u32[]{:S(2)}, u32[]{:S(2)}) collective-permute-start(bf16[2,256,384]{2,1,0:T(8,128)(2,1)S(1)} %get-tuple-element.58.refs_0_.refs_8_.refs_4_), channel_id=1, source_target_pairs={{0,32},{8,40},{16,48},{24,56},{32,0},{40,8},{48,16},{56,24},{64,96... | collective-permute-start | bytes 1179656 | tf_op jit(solution)/shard_map/ppermute | solution.py:616
  31.6 7.2 %copy-start.1 = (bf16[2,256,384]{2,1,0:T(8,128)(2,1)}, bf16[2,256,384]{2,1,0:T(8,128)(2,1)S(1)}, u32[]{:S(2)}) copy-start(bf16[2,256,384]{2,1,0:T(8,128)(2,1)S(1)} %collective-permute-done.7.refs_1_.refs_8_) | copy-start | bytes 1179652
  33.4 5.5 %copy-start.2 = (bf16[2,256,384]{2,1,0:T(8,128)(2,1)}, bf16[2,256,384]{2,1,0:T(8,128)(2,1)S(1)}, u32[]{:S(2)}) copy-start(bf16[2,256,384]{2,1,0:T(8,128)(2,1)S(1)} %collective-permute-done.6.refs_0_.refs_7_) | copy-start | bytes 1179652
  38.9 10.0 %collective-permute-start.8 = (bf16[384,384]{1,0:T(8,128)(2,1)}, bf16[384,384]{1,0:T(8,128)(2,1)S(1)}, u32[]{:S(2)}, u32[]{:S(2)}) collective-permute-start(bf16[384,384]{1,0:T(8,128)(2,1)} %get-tuple-element.65), channel_id=1, source_target_pairs={{0,96},{8,104},{16,112},{24,120},{32,64},{40,72},{48,80},{56,88},{... | collective-permute-start | bytes 884744 | tf_op jit(solution)/shard_map/ppermute | solution.py:616
  40.5 8.5 %collective-permute-start.9 = (bf16[384,384]{1,0:T(8,128)(2,1)}, bf16[384,384]{1,0:T(8,128)(2,1)S(1)}, u32[]{:S(2)}, u32[]{:S(2)}) collective-permute-start(bf16[384,384]{1,0:T(8,128)(2,1)} %get-tuple-element.66), channel_id=1, source_target_pairs={{0,32},{8,40},{16,48},{24,56},{32,0},{40,8},{48,16},{56,24},{64,96... | collective-permute-start | bytes 884744 | tf_op jit(solution)/shard_map/ppermute | solution.py:616
  40.5 8.5 %collective-permute-start.10 = (bf16[384,384]{1,0:T(8,128)(2,1)S(1)}, bf16[384,384]{1,0:T(8,128)(2,1)S(1)}, u32[]{:S(2)}, u32[]{:S(2)}) collective-permute-start(bf16[384,384]{1,0:T(8,128)(2,1)S(1)} %get-tuple-element.71), channel_id=1, source_target_pairs={{0,24},{8,16},{16,8},{24,0},{32,56},{40,48},{48,40},{56,32},{64,88... | collective-permute-start | bytes 884744 | tf_op jit(solution)/shard_map/ppermute | solution.py:616
  41.2 7.8 %collective-permute-start.11 = (bf16[384,384]{1,0:T(8,128)(2,1)S(1)}, bf16[384,384]{1,0:T(8,128)(2,1)S(1)}, u32[]{:S(2)}, u32[]{:S(2)}) collective-permute-start(bf16[384,384]{1,0:T(8,128)(2,1)S(1)} %get-tuple-element.72), channel_id=1, source_target_pairs={{0,8},{8,0},{16,24},{24,16},{32,40},{40,32},{48,56},{56,48},{64,72... | collective-permute-start | bytes 884744 | tf_op jit(solution)/shard_map/ppermute | solution.py:616
  55.0 4.2 %collective-permute-start.14 = (f32[2,3,1536]{2,1,0:T(4,128)S(1)}, f32[2,3,1536]{2,1,0:T(4,128)S(1)}, u32[]{:S(2)}, u32[]{:S(2)}) collective-permute-start(f32[2,3,1536]{2,1,0:T(4,128)S(1)} %get-tuple-element.75.refs_4_), channel_id=1, source_target_pairs={{0,24},{8,16},{16,8},{24,0},{32,56},{40,48},{48,40},{56,32},{64,88... | collective-permute-start | bytes 110600 | tf_op jit(solution)/shard_map/ppermute | solution.py:616
  55.5 4.4 %collective-permute-start.13 = (f32[2,3,1536]{2,1,0:T(4,128)S(1)}, f32[2,3,1536]{2,1,0:T(4,128)S(1)}, u32[]{:S(2)}, u32[]{:S(2)}) collective-permute-start(f32[2,3,1536]{2,1,0:T(4,128)S(1)} %get-tuple-element.75.refs_4_), channel_id=1, source_target_pairs={{0,16},{8,24},{16,0},{24,8},{32,48},{40,56},{48,32},{56,40},{64,80... | collective-permute-start | bytes 110600 | tf_op jit(solution)/shard_map/ppermute | solution.py:616
  57.2 3.1 %collective-permute-start.12 = (f32[2,3,1536]{2,1,0:T(4,128)S(1)}, f32[2,3,1536]{2,1,0:T(4,128)S(1)}, u32[]{:S(2)}, u32[]{:S(2)}) collective-permute-start(f32[2,3,1536]{2,1,0:T(4,128)S(1)} %get-tuple-element.75.refs_4_), channel_id=1, source_target_pairs={{0,8},{8,0},{16,24},{24,16},{32,40},{40,32},{48,56},{56,48},{64,72... | collective-permute-start | bytes 110600 | tf_op jit(solution)/shard_map/ppermute | solution.py:616
  63.6 22.6 %collective-permute-start.15 = (bf16[2,384,384]{2,1,0:T(8,128)(2,1)S(1)}, bf16[2,384,384]{2,1,0:T(8,128)(2,1)S(1)}, u32[]{:S(2)}, u32[]{:S(2)}) collective-permute-start(bf16[2,384,384]{2,1,0:T(8,128)(2,1)S(1)} %get-tuple-element.86), channel_id=1, source_target_pairs={{0,64},{8,72},{16,80},{24,88},{32,96},{40,104},{48,112},{56,120},{... | collective-permute-start | bytes 1769480 | tf_op jit(solution)/shard_map/ppermute | solution.py:616
  77.3 8.9 %collective-permute-start.16 = (bf16[3,128,384]{2,1,0:T(8,128)(2,1)S(1)}, bf16[3,128,384]{2,1,0:T(8,128)(2,1)S(1)}, u32[]{:S(2)}, u32[]{:S(2)}) collective-permute-start(bf16[3,128,384]{2,1,0:T(8,128)(2,1)S(1)} %get-tuple-element.87), channel_id=1, source_target_pairs={{0,16},{8,24},{16,0},{24,8},{32,48},{40,56},{48,32},{56,40},{64,80... | collective-permute-start | bytes 884744 | tf_op jit(solution)/shard_map/ppermute | solution.py:616
  77.4 9.7 %collective-permute-start.19 = (bf16[2,384,384]{2,1,0:T(8,128)(2,1)S(1)}, bf16[2,384,384]{2,1,0:T(8,128)(2,1)S(1)}, u32[]{:S(2)}, u32[]{:S(2)}) collective-permute-start(bf16[2,384,384]{2,1,0:T(8,128)(2,1)S(1)} %get-tuple-element.92), channel_id=1, source_target_pairs={{0,32},{8,40},{16,48},{24,56},{32,0},{40,8},{48,16},{56,24},{64,96... | collective-permute-start | bytes 1769480 | tf_op jit(solution)/shard_map/ppermute | solution.py:616
  78.4 10.3 %collective-permute-start.20 = (bf16[2,384,384]{2,1,0:T(8,128)(2,1)S(1)}, bf16[2,384,384]{2,1,0:T(8,128)(2,1)S(1)}, u32[]{:S(2)}, u32[]{:S(2)}) collective-permute-start(bf16[2,384,384]{2,1,0:T(8,128)(2,1)S(1)} %get-tuple-element.94), channel_id=1, source_target_pairs={{0,96},{8,104},{16,112},{24,120},{32,64},{40,72},{48,80},{56,88},{... | collective-permute-start | bytes 1769480 | tf_op jit(solution)/shard_map/ppermute | solution.py:616
  86.3 5.9 %collective-permute-start.17 = (bf16[3,128,384]{2,1,0:T(8,128)(2,1)S(1)}, bf16[3,128,384]{2,1,0:T(8,128)(2,1)S(1)}, u32[]{:S(2)}, u32[]{:S(2)}) collective-permute-start(bf16[3,128,384]{2,1,0:T(8,128)(2,1)S(1)} %get-tuple-element.88), channel_id=1, source_target_pairs={{0,8},{8,0},{16,24},{24,16},{32,40},{40,32},{48,56},{56,48},{64,72... | collective-permute-start | bytes 884744 | tf_op jit(solution)/shard_map/ppermute | solution.py:616
  86.4 8.4 %collective-permute-start.18 = (bf16[3,128,384]{2,1,0:T(8,128)(2,1)S(1)}, bf16[3,128,384]{2,1,0:T(8,128)(2,1)S(1)}, u32[]{:S(2)}, u32[]{:S(2)}) collective-permute-start(bf16[3,128,384]{2,1,0:T(8,128)(2,1)S(1)} %get-tuple-element.90), channel_id=1, source_target_pairs={{0,24},{8,16},{16,8},{24,0},{32,56},{40,48},{48,40},{56,32},{64,88... | collective-permute-start | bytes 884744 | tf_op jit(solution)/shard_map/ppermute | solution.py:616

commit v9 on v8

--- a/solution.py
+++ b/solution.py
@@ -64,7 +64,7 @@
 def assemble(arrived):
     return pl.pallas_call(
         assemble_kernel,
-        out_shape=(VIDEO_MESSAGE, VIDEO_MESSAGE),
+        out_shape=kept([VIDEO_MESSAGE, VIDEO_MESSAGE]),
         compiler_params=SMALL,
         name="assemble_blocks",
     )(*placed([arrived]))
@@ -80,7 +80,7 @@
 def hand_on(video, text):
     return pl.pallas_call(
         hand_on_kernel,
-        out_shape=[HALF_MESSAGE] * 4,
+        out_shape=kept([HALF_MESSAGE] * 4),
         compiler_params=SMALL,
         name="hand_on",
     )(*placed(video), *placed(text, pltpu.HBM))
@@ -119,7 +119,7 @@
 def sum_terms(dq, dkv):
     return pl.pallas_call(
         sum_kernel,
-        out_shape=[jax.ShapeDtypeStruct((GROUP, 3, OWN, WIDTH), BF16)]
+        out_shape=kept([jax.ShapeDtypeStruct((GROUP, 3, OWN, WIDTH), BF16)])
         + [jax.ShapeDtypeStruct((HALF, WIDTH), BF16)] * 3,
         compiler_params=SMALL,
         name="sum_terms",

time: 117 us -> 117 us (level)
  starting transfers between devices: 31.3 us -> 33.6 us
    ppermute x21, starting transfers between devices: 25.5 us -> 27.8 us  [swap(): lax.ppermute(array, 'seq', [(i, i ^ shift) for i in range(SIDE * SIDE)])]
    pallas_call x1, Pallas kernels: 10.8 us -> 8.52 us  [grads_near_call(): pl.pallas_call(grads_near_kernel, in_specs=[SMEM_SPEC] * 3 + [VMEM_SPEC]...]
  transfers between devices with their start and end apart: 22 -> 22, of which waited for: 15 -> 13; matrix products, arithmetic and copies ran while one was open for 0% -> 0% of each run, Pallas kernels for 20% -> 19%
where the time goes in v9:
time: 117 us; the launch traced here: 118 us
  Pallas kernels  38.8 us (33%)
  starting transfers between devices  33.6 us (29%)
  waiting for transfers between devices  24.7 us (21%)
  blocking collectives  19.9 us (17%)
    ppermute x21, starting transfers between devices, swap(): lax.ppermute(array, 'seq', [(i, i ^ shift) for i in range(SIDE * SIDE)])  27.8 us
    ppermute x21, waiting for transfers between devices, swap(): lax.ppermute(array, 'seq', [(i, i ^ shift) for i in range(SIDE * SIDE)])  24.7 us
    all_to_all x1, blocking collectives, on_device(): lax.all_to_all(video, 'head', split_axis=0, concat_axis=0)  19.9 us
    pallas_call x1, Pallas kernels, grads_near_call(): pl.pallas_call(grads_near_kernel, in_specs=[SMEM_SPEC] * 3 + [VMEM_SPEC]...  8.52 us
    pallas_call x1, Pallas kernels, stats_first_call(): pl.pallas_call(stats_first_kernel, in_specs=[SMEM_SPEC] * 3 + [VMEM_SPEC]...  6.78 us
    pallas_call x1, Pallas kernels, grads_own_call(): pl.pallas_call(grads_own_kernel, in_specs=[SMEM_SPEC] * 3 + [VMEM_SPEC] *...  6.51 us
    pallas_call x1, Pallas kernels, stats_last_call(): pl.pallas_call(stats_last_kernel, in_specs=[SMEM_SPEC] * 3 + [VMEM_SPEC]...  6.18 us
    all_to_all x1, starting transfers between devices, on_device(): arrived = lax.all_to_all(packed, 'head', split_axis=0, concat_axis=0)  5.8 us
  transfers between devices with their start and end apart: 22, of which 13 were waited for; matrix products, arithmetic and copies ran while one was open for 0% of the time, Pallas kernels for 19%

profile of v9, /device:TPU:1, one launch (start us, length us, event | category | flops | bytes accessed | tf_op | source)
XLA Modules:
  0.0 117.8 jit_solution(11875590605977574529)
XLA Ops:
  0.6 2.3 %pack_inputs.1 = (bf16[8,4,32,384]{3,2,1,0:T(8,128)(2,1)}, bf16[2,128,384]{2,1,0:T(8,128)(2,1)S(1)}, bf16[2,128,384]{2,1,0:T(8,128)(2,1)S(1)}) custom-call(bf16[32,3072]{1,0:T(8,128)(2,1)} %q_ref.1, bf16[32,3072]{1,0:T(8,128)(2,1)} %k_ref.1, bf16[32,3072]{1,0:T(8,128)(2,1)} %v_ref.1, bf16[32,3072]{1,0:T(8,128)(2,1)} %g_ref.1, bf16[128,384]{1,0:T(8,128)(2,1)} %tq_ref.1, ...), custom_call_target="tpu_custom_call" | custom-call | tf_op jit(solution)/shard_map/pack_inputs/pallas_call | solution.py:55
  3.0 5.8 %all-to-all-start = ((bf16[8,4,32,384]{3,2,1,0:T(8,128)(2,1)}), bf16[8,4,32,384]{3,2,1,0:T(8,128)(2,1)S(1)}, u32[]{:S(2)}, u32[]{:S(2)}) async-start(bf16[8,4,32,384]{3,2,1,0:T(8,128)(2,1)} %get-tuple-element.54), calls=%async_computation | async-start | bytes 1572864 | tf_op jit(solution)/shard_map/all_to_all | solution.py:642
  8.8 2.7 %collective-permute-start.1 = (bf16[2,128,384]{2,1,0:T(8,128)(2,1)S(1)}, bf16[2,128,384]{2,1,0:T(8,128)(2,1)S(1)}, u32[]{:S(2)}, u32[]{:S(2)}) collective-permute-start(bf16[2,128,384]{2,1,0:T(8,128)(2,1)S(1)} %get-tuple-element.67.refs_9_), channel_id=1, source_target_pairs={{0,24},{8,16},{16,8},{24,0},{32,56},{40,48},{48,40},{56,32},{64,88... | collective-permute-start | bytes 589832 | tf_op jit(solution)/shard_map/ppermute | solution.py:616
  11.5 0.0 collective-permute-start
  11.5 3.8 %collective-permute-start.3 = (bf16[2,128,384]{2,1,0:T(8,128)(2,1)S(1)}, bf16[2,128,384]{2,1,0:T(8,128)(2,1)S(1)}, u32[]{:S(2)}, u32[]{:S(2)}) collective-permute-start(bf16[2,128,384]{2,1,0:T(8,128)(2,1)S(1)} %get-tuple-element.59.refs_3_.refs_9_.refs_5_), channel_id=1, source_target_pairs={{0,96},{8,104},{16,112},{24,120},{32,64},{40,72},{48,80},{56,88},{... | collective-permute-start | bytes 589832 | tf_op jit(solution)/shard_map/ppermute | solution.py:616
  15.3 0.0 collective-permute-start.2
  15.3 1.4 %collective-permute-done.1.refs_5_.refs_13_ = bf16[2,128,384]{2,1,0:T(8,128)(2,1)S(1)} collective-permute-done((bf16[2,128,384]{2,1,0:T(8,128)(2,1)S(1)}, bf16[2,128,384]{2,1,0:T(8,128)(2,1)S(1)}, u32[]{:S(2)}, u32[]{:S(2)}) %collective-permute-start.1) | collective-permute-done | bytes 196640 | tf_op jit(solution)/shard_map/ppermute | solution.py:616
  16.6 1.1 collective-permute-done.refs_4_.refs_10_
  17.7 2.5 %collective-permute-done.3.refs_7_.refs_5_ = bf16[2,128,384]{2,1,0:T(8,128)(2,1)S(1)} collective-permute-done((bf16[2,128,384]{2,1,0:T(8,128)(2,1)S(1)}, bf16[2,128,384]{2,1,0:T(8,128)(2,1)S(1)}, u32[]{:S(2)}, u32[]{:S(2)}) %collective-permute-start.3) | collective-permute-done | bytes 196640 | tf_op jit(solution)/shard_map/ppermute | solution.py:616
  20.2 0.8 collective-permute-done.2.refs_6_.refs_4_
  21.0 0.0 copy-done.6
  21.0 0.0 copy-done.10
  21.0 0.0 all-to-all-done.in_ref
  21.1 0.1 assemble_blocks.1
  21.1 0.0 copy-done
  21.1 0.0 copy-start.5
  21.1 2.8 %collective-permute-start.7 = (bf16[2,256,384]{2,1,0:T(8,128)(2,1)S(1)}, bf16[2,256,384]{2,1,0:T(8,128)(2,1)S(1)}, u32[]{:S(2)}, u32[]{:S(2)}) collective-permute-start(bf16[2,256,384]{2,1,0:T(8,128)(2,1)S(1)} %get-tuple-element.62.refs_6_), channel_id=1, source_target_pairs={{0,24},{8,16},{16,8},{24,0},{32,56},{40,48},{48,40},{56,32},{64,88... | collective-permute-start | bytes 1179656 | tf_op jit(solution)/shard_map/ppermute | solution.py:616
  24.0 0.0 collective-permute-start.6
  24.0 3.8 %collective-permute-start.5 = (bf16[2,256,384]{2,1,0:T(8,128)(2,1)S(1)}, bf16[2,256,384]{2,1,0:T(8,128)(2,1)S(1)}, u32[]{:S(2)}, u32[]{:S(2)}) collective-permute-start(bf16[2,256,384]{2,1,0:T(8,128)(2,1)S(1)} %get-tuple-element.58.refs_0_.refs_8_.refs_4_), channel_id=1, source_target_pairs={{0,96},{8,104},{16,112},{24,120},{32,64},{40,72},{48,80},{56,88},{... | collective-permute-start | bytes 1179656 | tf_op jit(solution)/shard_map/ppermute | solution.py:616
  27.7 0.0 collective-permute-start.4
  27.7 3.9 %collective-permute-done.7.refs_1_.refs_8_ = bf16[2,256,384]{2,1,0:T(8,128)(2,1)S(1)} collective-permute-done((bf16[2,256,384]{2,1,0:T(8,128)(2,1)S(1)}, bf16[2,256,384]{2,1,0:T(8,128)(2,1)S(1)}, u32[]{:S(2)}, u32[]{:S(2)}) %collective-permute-start.7) | collective-permute-done | bytes 393248 | tf_op jit(solution)/shard_map/ppermute | solution.py:616
  31.6 1.8 %collective-permute-done.6.refs_0_.refs_7_ = bf16[2,256,384]{2,1,0:T(8,128)(2,1)S(1)} collective-permute-done((bf16[2,256,384]{2,1,0:T(8,128)(2,1)S(1)}, bf16[2,256,384]{2,1,0:T(8,128)(2,1)S(1)}, u32[]{:S(2)}, u32[]{:S(2)}) %collective-permute-start.6) | collective-permute-done | bytes 393248 | tf_op jit(solution)/shard_map/ppermute | solution.py:616
  33.4 2.4 %collective-permute-done.5.refs_3_.refs_2_.refs_5_ = bf16[2,256,384]{2,1,0:T(8,128)(2,1)S(1)} collective-permute-done((bf16[2,256,384]{2,1,0:T(8,128)(2,1)S(1)}, bf16[2,256,384]{2,1,0:T(8,128)(2,1)S(1)}, u32[]{:S(2)}, u32[]{:S(2)}) %collective-permute-start.5) | collective-permute-done | bytes 393248 | tf_op jit(solution)/shard_map/ppermute | solution.py:616
  35.9 0.9 collective-permute-done.4.refs_2_.refs_1_.refs_4_
  36.8 0.0 copy-done.9
  36.8 0.0 copy-done.7
  36.8 0.0 copy-done.8
  36.8 2.1 %hand_on.1 = (bf16[384,384]{1,0:T(8,128)(2,1)S(1)}, bf16[384,384]{1,0:T(8,128)(2,1)S(1)}, bf16[384,384]{1,0:T(8,128)(2,1)}, bf16[384,384]{1,0:T(8,128)(2,1)}) custom-call(bf16[2,256,384]{2,1,0:T(8,128)(2,1)S(1)} %collective-permute-done.6.refs_0_.refs_7_, bf16[2,256,384]{2,1,0:T(8,128)(2,1)S(1)} %collective-permute-done.7.refs_1_.refs_8_, ...), custom_call_target="tpu_custom_call" | custom-call | tf_op jit(solution)/shard_map/hand_on/pallas_call | solution.py:81
  38.9 0.0 copy-done.1
  38.9 1.6 %collective-permute-start.8 = (bf16[384,384]{1,0:T(8,128)(2,1)}, bf16[384,384]{1,0:T(8,128)(2,1)S(1)}, u32[]{:S(2)}, u32[]{:S(2)}) collective-permute-start(bf16[384,384]{1,0:T(8,128)(2,1)} %get-tuple-element.65), channel_id=1, source_target_pairs={{0,96},{8,104},{16,112},{24,120},{32,64},{40,72},{48,80},{56,88},{... | collective-permute-start | bytes 884744 | tf_op jit(solution)/shard_map/ppermute | solution.py:616
  40.5 0.0 collective-permute-start.9
  40.5 0.7 collective-permute-start.10
  41.2 0.6 collective-permute-start.11
  41.8 0.0 copy-done.3
  41.8 6.8 %stats_first.1 = (f32[3,3,1536]{2,1,0:T(4,128)S(1)}, bf16[6,256,384]{2,1,0:T(8,128)(2,1)S(1)}, bf16[6,256,384]{2,1,0:T(8,128)(2,1)S(1)}) custom-call(s32[8]{0:T(128)S(1)} %copy-done.3, s32[8]{0:T(128)S(1)} %copy-done.4, s32[1]{0:T(128)} %bitcast.place_ref, bf16[2,256,384]{2,1,0:T(8,128)(2,1)S(1)} %get-tuple-element.58.refs_0_.refs_8_.refs_4_, ...), custom_call_target="tpu_custom_call" | custom-call | flops 1207959552 | bytes 8388608 | tf_op jit(solution)/shard_map/stats_first/pallas_call | solution.py:524
  48.6 0.0 collective-permute-done.8.refs_6_.refs_2_
  48.6 0.0 collective-permute-done.9.refs_7_.refs_3_
  48.6 0.0 collective-permute-done.10.refs_11_
  48.6 0.0 collective-permute-done.11.refs_12_
  48.6 6.2 %stats_last.1 = (f32[2,3,1536]{2,1,0:T(4,128)S(1)}, bf16[6,256,384]{2,1,0:T(8,128)(2,1)S(1)}, bf16[6,256,384]{2,1,0:T(8,128)(2,1)S(1)}) custom-call(s32[8]{0:T(128)S(1)} %copy-done.3, s32[8]{0:T(128)S(1)} %copy-done.4, s32[1]{0:T(128)} %bitcast.place_ref, bf16[2,256,384]{2,1,0:T(8,128)(2,1)S(1)} %get-tuple-element.58.refs_0_.refs_8_.refs_4_, ...), custom_call_target="tpu_custom_call" | custom-call | flops 805306368 | bytes 8388608 | tf_op jit(solution)/shard_map/stats_last/pallas_call | solution.py:540
  54.8 2.0 %collective-permute-start.14 = (f32[2,3,1536]{2,1,0:T(4,128)S(1)}, f32[2,3,1536]{2,1,0:T(4,128)S(1)}, u32[]{:S(2)}, u32[]{:S(2)}) collective-permute-start(f32[2,3,1536]{2,1,0:T(4,128)S(1)} %get-tuple-element.75.refs_4_), channel_id=1, source_target_pairs={{0,24},{8,16},{16,8},{24,0},{32,56},{40,48},{48,40},{56,32},{64,88... | collective-permute-start | bytes 110600 | tf_op jit(solution)/shard_map/ppermute | solution.py:616
  56.8 1.2 %collective-permute-start.13 = (f32[2,3,1536]{2,1,0:T(4,128)S(1)}, f32[2,3,1536]{2,1,0:T(4,128)S(1)}, u32[]{:S(2)}, u32[]{:S(2)}) collective-permute-start(f32[2,3,1536]{2,1,0:T(4,128)S(1)} %get-tuple-element.75.refs_4_), channel_id=1, source_target_pairs={{0,16},{8,24},{16,0},{24,8},{32,48},{40,56},{48,32},{56,40},{64,80... | collective-permute-start | bytes 110600 | tf_op jit(solution)/shard_map/ppermute | solution.py:616
  58.0 0.2 collective-permute-start.12
  58.2 0.9 collective-permute-done.14.refs_7_
  59.1 2.2 %collective-permute-done.13.refs_6_ = f32[2,3,1536]{2,1,0:T(4,128)S(1)} collective-permute-done((f32[2,3,1536]{2,1,0:T(4,128)S(1)}, f32[2,3,1536]{2,1,0:T(4,128)S(1)}, u32[]{:S(2)}, u32[]{:S(2)}) %collective-permute-start.13) | collective-permute-done | bytes 36896 | tf_op jit(solution)/shard_map/ppermute | solution.py:616
  61.3 0.0 collective-permute-done.12.refs_5_
  61.3 4.2 %grads_far.1 = (bf16[2,384,384]{2,1,0:T(8,128)(2,1)S(1)}, f32[3,128,1536]{2,1,0:T(8,128)S(1)}, f32[2,3,1536]{2,1,0:T(4,128)S(1)}) custom-call(s32[8]{0:T(128)S(1)} %copy-done.3, s32[8]{0:T(128)S(1)} %copy-done.4, s32[1]{0:T(128)} %bitcast.place_ref, bf16[6,256,384]{2,1,0:T(8,128)(2,1)S(1)} %get-tuple-element.73.refs_0_, ...), custom_call_target="tpu_custom_call" | custom-call | flops 1006632960 | bytes 8388608 | tf_op jit(solution)/shard_map/grads_far/pallas_call | solution.py:562
  65.5 2.5 %collective-permute-start.15 = (bf16[2,384,384]{2,1,0:T(8,128)(2,1)S(1)}, bf16[2,384,384]{2,1,0:T(8,128)(2,1)S(1)}, u32[]{:S(2)}, u32[]{:S(2)}) collective-permute-start(bf16[2,384,384]{2,1,0:T(8,128)(2,1)S(1)} %get-tuple-element.86), channel_id=1, source_target_pairs={{0,64},{8,72},{16,80},{24,88},{32,96},{40,104},{48,112},{56,120},{... | collective-permute-start | bytes 1769480 | tf_op jit(solution)/shard_map/ppermute | solution.py:616
  68.0 8.5 %grads_near.1 = (bf16[2,384,384]{2,1,0:T(8,128)(2,1)S(1)}, bf16[2,384,384]{2,1,0:T(8,128)(2,1)S(1)}, bf16[3,128,384]{2,1,0:T(8,128)(2,1)S(1)}, f32[3,128,1536]{2...) custom-call(s32[8]{0:T(128)S(1)} %copy-done.3, ...), custom_call_target="tpu_custom_call" | custom-call | flops 2013265920 | bytes 8388608 | tf_op jit(solution)/shard_map/grads_near/pallas_call | solution.py:577
  76.5 3.1 %collective-permute-start.16 = (bf16[3,128,384]{2,1,0:T(8,128)(2,1)S(1)}, bf16[3,128,384]{2,1,0:T(8,128)(2,1)S(1)}, u32[]{:S(2)}, u32[]{:S(2)}) collective-permute-start(bf16[3,128,384]{2,1,0:T(8,128)(2,1)S(1)} %get-tuple-element.87), channel_id=1, source_target_pairs={{0,16},{8,24},{16,0},{24,8},{32,48},{40,56},{48,32},{56,40},{64,80... | collective-permute-start | bytes 884744 | tf_op jit(solution)/shard_map/ppermute | solution.py:616
  79.6 0.0 collective-permute-start.19
  79.6 1.7 %collective-permute-start.20 = (bf16[2,384,384]{2,1,0:T(8,128)(2,1)S(1)}, bf16[2,384,384]{2,1,0:T(8,128)(2,1)S(1)}, u32[]{:S(2)}, u32[]{:S(2)}) collective-permute-start(bf16[2,384,384]{2,1,0:T(8,128)(2,1)S(1)} %get-tuple-element.94), channel_id=1, source_target_pairs={{0,96},{8,104},{16,112},{24,120},{32,64},{40,72},{48,80},{56,88},{... | collective-permute-start | bytes 1769480 | tf_op jit(solution)/shard_map/ppermute | solution.py:616
  81.3 6.5 %grads_own.1 = (bf16[3,128,384]{2,1,0:T(8,128)(2,1)S(1)}, bf16[3,128,384]{2,1,0:T(8,128)(2,1)S(1)}, bf16[3,128,384]{2,1,0:T(8,128)(2,1)S(1)}, bf16[2,384,384]{2,1,0:T(8,128)(2,1)S(1)}) custom-call(s32[8]{0:T(128)S(1)} %copy-done.3, s32[8]{0:T(128)S(1)} %copy-done.4, s32[1]{0:T(128)} %bitcast.place_ref, bf16[6,256,384]{2,1,0:T(8,128)(2,1)S(1)} %get-tuple-element.73.refs_0_, ...), custom_call_target="tpu_custom_call" | custom-call | flops 1006632960 | bytes 8388608 | tf_op jit(solution)/shard_map/grads_own/pallas_call | solution.py:601
  87.8 0.0 collective-permute-done.16.refs_2_
  87.8 0.0 collective-permute-done.15.refs_6_
  87.8 0.9 collective-permute-start.17
  88.7 0.3 collective-permute-start.18
  89.0 0.0 collective-permute-done.19.refs_5_
  89.0 0.8 collective-permute-done.20.refs_7_
  89.8 3.9 %collective-permute-done.17.refs_1_ = bf16[3,128,384]{2,1,0:T(8,128)(2,1)S(1)} collective-permute-done((bf16[3,128,384]{2,1,0:T(8,128)(2,1)S(1)}, bf16[3,128,384]{2,1,0:T(8,128)(2,1)S(1)}, u32[]{:S(2)}, u32[]{:S(2)}) %collective-permute-start.17) | collective-permute-done | bytes 294944 | tf_op jit(solution)/shard_map/ppermute | solution.py:616
  93.8 2.1 %collective-permute-done.18.refs_3_ = bf16[3,128,384]{2,1,0:T(8,128)(2,1)S(1)} collective-permute-done((bf16[3,128,384]{2,1,0:T(8,128)(2,1)S(1)}, bf16[3,128,384]{2,1,0:T(8,128)(2,1)S(1)}, u32[]{:S(2)}, u32[]{:S(2)}) %collective-permute-start.18) | collective-permute-done | bytes 294944 | tf_op jit(solution)/shard_map/ppermute | solution.py:616
  95.8 1.2 %sum_terms.1 = (bf16[8,3,32,384]{3,2,1,0:T(8,128)(2,1)S(1)}, bf16[128,384]{1,0:T(8,128)(2,1)}, bf16[128,384]{1,0:T(8,128)(2,1)}, bf16[128,384]{1,0:T(8,128)(2,1)}) custom-call(bf16[3,128,384]{2,1,0:T(8,128)(2,1)S(1)} %get-tuple-element.83.refs_0_, bf16[3,128,384]{2,1,0:T(8,128)(2,1)S(1)} %collective-permute-done.17.refs_1_, ...), custom_call_target="tpu_custom_call" | custom-call | tf_op jit(solution)/shard_map/sum_terms/pallas_call | solution.py:120
  97.1 19.9 %all_to_all.10.in_ref = bf16[8,3,32,384]{3,2,1,0:T(8,128)(2,1)S(1)} all-to-all(bf16[8,3,32,384]{3,2,1,0:T(8,128)(2,1)S(1)} %get-tuple-element.95), channel_id=1, replica_groups=mesh['seq'=16,'head'=8] {'head'}, dimensions={0} | all-to-all | bytes 1179648 | tf_op jit(solution)/shard_map/all_to_all | solution.py:663
  116.9 0.9 unpack_video.1
  (13 shorter events, 0.0 us)
Async XLA Ops:
  3.0 18.0 %copy-start.6 = (bf16[2,128,384]{2,1,0:T(8,128)(2,1)}, bf16[2,128,384]{2,1,0:T(8,128)(2,1)S(1)}, u32[]{:S(2)}) copy-start(bf16[2,128,384]{2,1,0:T(8,128)(2,1)S(1)} %get-tuple-element.67.refs_9_) | copy-start | bytes 589828
  3.0 18.2 %copy-start = (bf16[2,128,384]{2,1,0:T(8,128)(2,1)}, bf16[2,128,384]{2,1,0:T(8,128)(2,1)S(1)}, u32[]{:S(2)}) copy-start(bf16[2,128,384]{2,1,0:T(8,128)(2,1)S(1)} %get-tuple-element.59.refs_3_.refs_9_.refs_5_) | copy-start | bytes 589828
  3.0 18.1 %all-to-all-start = ((bf16[8,4,32,384]{3,2,1,0:T(8,128)(2,1)}), bf16[8,4,32,384]{3,2,1,0:T(8,128)(2,1)S(1)}, u32[]{:S(2)}, u32[]{:S(2)}) async-start(bf16[8,4,32,384]{3,2,1,0:T(8,128)(2,1)} %get-tuple-element.54), calls=%async_computation | async-start | bytes 1572864 | tf_op jit(solution)/shard_map/all_to_all | solution.py:642
  8.8 7.9 %collective-permute-start.1 = (bf16[2,128,384]{2,1,0:T(8,128)(2,1)S(1)}, bf16[2,128,384]{2,1,0:T(8,128)(2,1)S(1)}, u32[]{:S(2)}, u32[]{:S(2)}) collective-permute-start(bf16[2,128,384]{2,1,0:T(8,128)(2,1)S(1)} %get-tuple-element.67.refs_9_), channel_id=1, source_target_pairs={{0,24},{8,16},{16,8},{24,0},{32,56},{40,48},{48,40},{56,32},{64,88... | collective-permute-start | bytes 589832 | tf_op jit(solution)/shard_map/ppermute | solution.py:616
  11.5 6.2 %collective-permute-start = (bf16[2,128,384]{2,1,0:T(8,128)(2,1)S(1)}, bf16[2,128,384]{2,1,0:T(8,128)(2,1)S(1)}, u32[]{:S(2)}, u32[]{:S(2)}) collective-permute-start(bf16[2,128,384]{2,1,0:T(8,128)(2,1)S(1)} %get-tuple-element.67.refs_9_), channel_id=1, source_target_pairs={{0,8},{8,0},{16,24},{24,16},{32,40},{40,32},{48,56},{56,48},{64,72... | collective-permute-start | bytes 589832 | tf_op jit(solution)/shard_map/ppermute | solution.py:616
  11.5 8.7 %collective-permute-start.3 = (bf16[2,128,384]{2,1,0:T(8,128)(2,1)S(1)}, bf16[2,128,384]{2,1,0:T(8,128)(2,1)S(1)}, u32[]{:S(2)}, u32[]{:S(2)}) collective-permute-start(bf16[2,128,384]{2,1,0:T(8,128)(2,1)S(1)} %get-tuple-element.59.refs_3_.refs_9_.refs_5_), channel_id=1, source_target_pairs={{0,96},{8,104},{16,112},{24,120},{32,64},{40,72},{48,80},{56,88},{... | collective-permute-start | bytes 589832 | tf_op jit(solution)/shard_map/ppermute | solution.py:616
  15.3 5.7 %collective-permute-start.2 = (bf16[2,128,384]{2,1,0:T(8,128)(2,1)S(1)}, bf16[2,128,384]{2,1,0:T(8,128)(2,1)S(1)}, u32[]{:S(2)}, u32[]{:S(2)}) collective-permute-start(bf16[2,128,384]{2,1,0:T(8,128)(2,1)S(1)} %get-tuple-element.59.refs_3_.refs_9_.refs_5_), channel_id=1, source_target_pairs={{0,32},{8,40},{16,48},{24,56},{32,0},{40,8},{48,16},{56,24},{64,96... | collective-permute-start | bytes 589832 | tf_op jit(solution)/shard_map/ppermute | solution.py:616
  16.6 20.1 %copy-start.9 = (bf16[2,128,384]{2,1,0:T(8,128)(2,1)}, bf16[2,128,384]{2,1,0:T(8,128)(2,1)S(1)}, u32[]{:S(2)}) copy-start(bf16[2,128,384]{2,1,0:T(8,128)(2,1)S(1)} %collective-permute-done.1.refs_5_.refs_13_) | copy-start | bytes 589828
  17.7 3.3 %copy-start.10 = (bf16[2,128,384]{2,1,0:T(8,128)(2,1)}, bf16[2,128,384]{2,1,0:T(8,128)(2,1)S(1)}, u32[]{:S(2)}) copy-start(bf16[2,128,384]{2,1,0:T(8,128)(2,1)S(1)} %collective-permute-done.refs_4_.refs_10_) | copy-start | bytes 589828
  20.2 16.6 %copy-start.7 = (bf16[2,128,384]{2,1,0:T(8,128)(2,1)}, bf16[2,128,384]{2,1,0:T(8,128)(2,1)S(1)}, u32[]{:S(2)}) copy-start(bf16[2,128,384]{2,1,0:T(8,128)(2,1)S(1)} %collective-permute-done.3.refs_7_.refs_5_) | copy-start | bytes 589828
  21.0 15.8 %copy-start.8 = (bf16[2,128,384]{2,1,0:T(8,128)(2,1)}, bf16[2,128,384]{2,1,0:T(8,128)(2,1)S(1)}, u32[]{:S(2)}) copy-start(bf16[2,128,384]{2,1,0:T(8,128)(2,1)S(1)} %collective-permute-done.2.refs_6_.refs_4_) | copy-start | bytes 589828
  21.1 17.7 %copy-start.5 = (bf16[2,256,384]{2,1,0:T(8,128)(2,1)}, bf16[2,256,384]{2,1,0:T(8,128)(2,1)S(1)}, u32[]{:S(2)}) copy-start(bf16[2,256,384]{2,1,0:T(8,128)(2,1)S(1)} %get-tuple-element.62.refs_6_) | copy-start | bytes 1179652
  21.1 10.5 %collective-permute-start.7 = (bf16[2,256,384]{2,1,0:T(8,128)(2,1)S(1)}, bf16[2,256,384]{2,1,0:T(8,128)(2,1)S(1)}, u32[]{:S(2)}, u32[]{:S(2)}) collective-permute-start(bf16[2,256,384]{2,1,0:T(8,128)(2,1)S(1)} %get-tuple-element.62.refs_6_), channel_id=1, source_target_pairs={{0,24},{8,16},{16,8},{24,0},{32,56},{40,48},{48,40},{56,32},{64,88... | collective-permute-start | bytes 1179656 | tf_op jit(solution)/shard_map/ppermute | solution.py:616
  24.0 9.5 %collective-permute-start.6 = (bf16[2,256,384]{2,1,0:T(8,128)(2,1)S(1)}, bf16[2,256,384]{2,1,0:T(8,128)(2,1)S(1)}, u32[]{:S(2)}, u32[]{:S(2)}) collective-permute-start(bf16[2,256,384]{2,1,0:T(8,128)(2,1)S(1)} %get-tuple-element.62.refs_6_), channel_id=1, source_target_pairs={{0,8},{8,0},{16,24},{24,16},{32,40},{40,32},{48,56},{56,48},{64,72... | collective-permute-start | bytes 1179656 | tf_op jit(solution)/shard_map/ppermute | solution.py:616
  24.0 17.8 %copy-start.3 = (s32[8]{0:T(128)S(1)}, s32[8]{0:T(128)}, u32[]{:S(2)}) copy-start(s32[8]{0:T(128)} %length_ref.9) | copy-start | bytes 100
  24.0 17.8 %copy-start.4 = (s32[8]{0:T(128)S(1)}, s32[8]{0:T(128)}, u32[]{:S(2)}) copy-start(s32[8]{0:T(128)} %caption_ref.9) | copy-start | bytes 100
  24.0 11.9 %collective-permute-start.5 = (bf16[2,256,384]{2,1,0:T(8,128)(2,1)S(1)}, bf16[2,256,384]{2,1,0:T(8,128)(2,1)S(1)}, u32[]{:S(2)}, u32[]{:S(2)}) collective-permute-start(bf16[2,256,384]{2,1,0:T(8,128)(2,1)S(1)} %get-tuple-element.58.refs_0_.refs_8_.refs_4_), channel_id=1, source_target_pairs={{0,96},{8,104},{16,112},{24,120},{32,64},{40,72},{48,80},{56,88},{... | collective-permute-start | bytes 1179656 | tf_op jit(solution)/shard_map/ppermute | solution.py:616
  27.7 9.0 %collective-permute-start.4 = (bf16[2,256,384]{2,1,0:T(8,128)(2,1)S(1)}, bf16[2,256,384]{2,1,0:T(8,128)(2,1)S(1)}, u32[]{:S(2)}, u32[]{:S(2)}) collective-permute-start(bf16[2,256,384]{2,1,0:T(8,128)(2,1)S(1)} %get-tuple-element.58.refs_0_.refs_8_.refs_4_), channel_id=1, source_target_pairs={{0,32},{8,40},{16,48},{24,56},{32,0},{40,8},{48,16},{56,24},{64,96... | collective-permute-start | bytes 1179656 | tf_op jit(solution)/shard_map/ppermute | solution.py:616
  31.6 7.2 %copy-start.1 = (bf16[2,256,384]{2,1,0:T(8,128)(2,1)}, bf16[2,256,384]{2,1,0:T(8,128)(2,1)S(1)}, u32[]{:S(2)}) copy-start(bf16[2,256,384]{2,1,0:T(8,128)(2,1)S(1)} %collective-permute-done.7.refs_1_.refs_8_) | copy-start | bytes 1179652
  33.4 5.5 %copy-start.2 = (bf16[2,256,384]{2,1,0:T(8,128)(2,1)}, bf16[2,256,384]{2,1,0:T(8,128)(2,1)S(1)}, u32[]{:S(2)}) copy-start(bf16[2,256,384]{2,1,0:T(8,128)(2,1)S(1)} %collective-permute-done.6.refs_0_.refs_7_) | copy-start | bytes 1179652
  38.9 9.7 %collective-permute-start.8 = (bf16[384,384]{1,0:T(8,128)(2,1)}, bf16[384,384]{1,0:T(8,128)(2,1)S(1)}, u32[]{:S(2)}, u32[]{:S(2)}) collective-permute-start(bf16[384,384]{1,0:T(8,128)(2,1)} %get-tuple-element.65), channel_id=1, source_target_pairs={{0,96},{8,104},{16,112},{24,120},{32,64},{40,72},{48,80},{56,88},{... | collective-permute-start | bytes 884744 | tf_op jit(solution)/shard_map/ppermute | solution.py:616
  40.5 8.1 %collective-permute-start.9 = (bf16[384,384]{1,0:T(8,128)(2,1)}, bf16[384,384]{1,0:T(8,128)(2,1)S(1)}, u32[]{:S(2)}, u32[]{:S(2)}) collective-permute-start(bf16[384,384]{1,0:T(8,128)(2,1)} %get-tuple-element.66), channel_id=1, source_target_pairs={{0,32},{8,40},{16,48},{24,56},{32,0},{40,8},{48,16},{56,24},{64,96... | collective-permute-start | bytes 884744 | tf_op jit(solution)/shard_map/ppermute | solution.py:616
  40.5 8.1 %collective-permute-start.10 = (bf16[384,384]{1,0:T(8,128)(2,1)S(1)}, bf16[384,384]{1,0:T(8,128)(2,1)S(1)}, u32[]{:S(2)}, u32[]{:S(2)}) collective-permute-start(bf16[384,384]{1,0:T(8,128)(2,1)S(1)} %get-tuple-element.71), channel_id=1, source_target_pairs={{0,24},{8,16},{16,8},{24,0},{32,56},{40,48},{48,40},{56,32},{64,88... | collective-permute-start | bytes 884744 | tf_op jit(solution)/shard_map/ppermute | solution.py:616
  41.2 7.5 %collective-permute-start.11 = (bf16[384,384]{1,0:T(8,128)(2,1)S(1)}, bf16[384,384]{1,0:T(8,128)(2,1)S(1)}, u32[]{:S(2)}, u32[]{:S(2)}) collective-permute-start(bf16[384,384]{1,0:T(8,128)(2,1)S(1)} %get-tuple-element.72), channel_id=1, source_target_pairs={{0,8},{8,0},{16,24},{24,16},{32,40},{40,32},{48,56},{56,48},{64,72... | collective-permute-start | bytes 884744 | tf_op jit(solution)/shard_map/ppermute | solution.py:616
  54.8 4.2 %collective-permute-start.14 = (f32[2,3,1536]{2,1,0:T(4,128)S(1)}, f32[2,3,1536]{2,1,0:T(4,128)S(1)}, u32[]{:S(2)}, u32[]{:S(2)}) collective-permute-start(f32[2,3,1536]{2,1,0:T(4,128)S(1)} %get-tuple-element.75.refs_4_), channel_id=1, source_target_pairs={{0,24},{8,16},{16,8},{24,0},{32,56},{40,48},{48,40},{56,32},{64,88... | collective-permute-start | bytes 110600 | tf_op jit(solution)/shard_map/ppermute | solution.py:616
  56.8 4.4 %collective-permute-start.13 = (f32[2,3,1536]{2,1,0:T(4,128)S(1)}, f32[2,3,1536]{2,1,0:T(4,128)S(1)}, u32[]{:S(2)}, u32[]{:S(2)}) collective-permute-start(f32[2,3,1536]{2,1,0:T(4,128)S(1)} %get-tuple-element.75.refs_4_), channel_id=1, source_target_pairs={{0,16},{8,24},{16,0},{24,8},{32,48},{40,56},{48,32},{56,40},{64,80... | collective-permute-start | bytes 110600 | tf_op jit(solution)/shard_map/ppermute | solution.py:616
  58.0 3.3 %collective-permute-start.12 = (f32[2,3,1536]{2,1,0:T(4,128)S(1)}, f32[2,3,1536]{2,1,0:T(4,128)S(1)}, u32[]{:S(2)}, u32[]{:S(2)}) collective-permute-start(f32[2,3,1536]{2,1,0:T(4,128)S(1)} %get-tuple-element.75.refs_4_), channel_id=1, source_target_pairs={{0,8},{8,0},{16,24},{24,16},{32,40},{40,32},{48,56},{56,48},{64,72... | collective-permute-start | bytes 110600 | tf_op jit(solution)/shard_map/ppermute | solution.py:616
  65.5 22.4 %collective-permute-start.15 = (bf16[2,384,384]{2,1,0:T(8,128)(2,1)S(1)}, bf16[2,384,384]{2,1,0:T(8,128)(2,1)S(1)}, u32[]{:S(2)}, u32[]{:S(2)}) collective-permute-start(bf16[2,384,384]{2,1,0:T(8,128)(2,1)S(1)} %get-tuple-element.86), channel_id=1, source_target_pairs={{0,64},{8,72},{16,80},{24,88},{32,96},{40,104},{48,112},{56,120},{... | collective-permute-start | bytes 1769480 | tf_op jit(solution)/shard_map/ppermute | solution.py:616
  76.5 11.3 %collective-permute-start.16 = (bf16[3,128,384]{2,1,0:T(8,128)(2,1)S(1)}, bf16[3,128,384]{2,1,0:T(8,128)(2,1)S(1)}, u32[]{:S(2)}, u32[]{:S(2)}) collective-permute-start(bf16[3,128,384]{2,1,0:T(8,128)(2,1)S(1)} %get-tuple-element.87), channel_id=1, source_target_pairs={{0,16},{8,24},{16,0},{24,8},{32,48},{40,56},{48,32},{56,40},{64,80... | collective-permute-start | bytes 884744 | tf_op jit(solution)/shard_map/ppermute | solution.py:616
  79.6 9.5 %collective-permute-start.19 = (bf16[2,384,384]{2,1,0:T(8,128)(2,1)S(1)}, bf16[2,384,384]{2,1,0:T(8,128)(2,1)S(1)}, u32[]{:S(2)}, u32[]{:S(2)}) collective-permute-start(bf16[2,384,384]{2,1,0:T(8,128)(2,1)S(1)} %get-tuple-element.92), channel_id=1, source_target_pairs={{0,32},{8,40},{16,48},{24,56},{32,0},{40,8},{48,16},{56,24},{64,96... | collective-permute-start | bytes 1769480 | tf_op jit(solution)/shard_map/ppermute | solution.py:616
  79.6 10.2 %collective-permute-start.20 = (bf16[2,384,384]{2,1,0:T(8,128)(2,1)S(1)}, bf16[2,384,384]{2,1,0:T(8,128)(2,1)S(1)}, u32[]{:S(2)}, u32[]{:S(2)}) collective-permute-start(bf16[2,384,384]{2,1,0:T(8,128)(2,1)S(1)} %get-tuple-element.94), channel_id=1, source_target_pairs={{0,96},{8,104},{16,112},{24,120},{32,64},{40,72},{48,80},{56,88},{... | collective-permute-start | bytes 1769480 | tf_op jit(solution)/shard_map/ppermute | solution.py:616
  87.8 5.9 %collective-permute-start.17 = (bf16[3,128,384]{2,1,0:T(8,128)(2,1)S(1)}, bf16[3,128,384]{2,1,0:T(8,128)(2,1)S(1)}, u32[]{:S(2)}, u32[]{:S(2)}) collective-permute-start(bf16[3,128,384]{2,1,0:T(8,128)(2,1)S(1)} %get-tuple-element.88), channel_id=1, source_target_pairs={{0,8},{8,0},{16,24},{24,16},{32,40},{40,32},{48,56},{56,48},{64,72... | collective-permute-start | bytes 884744 | tf_op jit(solution)/shard_map/ppermute | solution.py:616
  88.7 7.1 %collective-permute-start.18 = (bf16[3,128,384]{2,1,0:T(8,128)(2,1)S(1)}, bf16[3,128,384]{2,1,0:T(8,128)(2,1)S(1)}, u32[]{:S(2)}, u32[]{:S(2)}) collective-permute-start(bf16[3,128,384]{2,1,0:T(8,128)(2,1)S(1)} %get-tuple-element.90), channel_id=1, source_target_pairs={{0,24},{8,16},{16,8},{24,0},{32,56},{40,48},{48,40},{56,32},{64,88... | collective-permute-start | bytes 884744 | tf_op jit(solution)/shard_map/ppermute | solution.py:616

commit v10 on v9

--- a/solution.py
+++ b/solution.py
@@ -369,8 +369,8 @@
     def __init__(self, refs):
         self.dk, self.dv, self.text_dk, self.text_dv = refs
 
-    def clear(self):
-        for ref in (self.dk, self.dv, self.text_dk, self.text_dv):
+    def clear_text(self):
+        for ref in (self.text_dk, self.text_dv):
             ref[...] = jnp.zeros(ref.shape, F32)
 
     def write(self, n, out):
@@ -383,7 +383,7 @@
             out[1, BLOCK:, c] = self.text_dv[n, h].astype(BF16)
 
 
-def key_grads(labels, blocks, queries, pairs, q_all, g_all, kv, norm, dq_in, dq_t, terms, work):
+def key_grads(labels, blocks, queries, pairs, q_all, g_all, kv, norm, dq_in, dq_t, terms, work, before=None):
     p_all, ds_all = work
 
     def head(h):
@@ -396,8 +396,10 @@
             probs = jnp.exp2(scores * TO_LOG2 - norm[0, row, cols])
             p_all[:, at] = probs.astype(BF16)
             ds_all[:, at] = (probs * (dprob - norm[1, row, cols])).astype(BF16)
-        terms.dv[h] += dot_nn(p_all[...], jnp.concatenate([g_all[j, :, c] for j in queries], 0))
-        terms.dk[h] += dot_nn(ds_all[...], jnp.concatenate([q_all[j, :, c] for j in queries], 0))
+        value_part = dot_nn(p_all[...], jnp.concatenate([g_all[j, :, c] for j in queries], 0))
+        key_part = dot_nn(ds_all[...], jnp.concatenate([q_all[j, :, c] for j in queries], 0))
+        terms.dv[h] = value_part if before is None else before.dv[h] + value_part
+        terms.dk[h] = key_part if before is None else before.dk[h] + key_part
         part = dot_nn(jnp.transpose(keys), ds_all[...])
         for n, j in enumerate(queries):
             cols, piece = query_cols(j), part[:, query_cols(n)]
@@ -448,7 +450,7 @@
     normalize(stats, norm)
     dq_t[:, :, VIDEO_ROWS:] = jnp.zeros((HEADS_LOCAL, HDIM, TEXT_ROWS), F32)
     terms = Terms(scratch[:4])
-    terms.clear()
+    terms.clear_text()
     key_grads(labels, (FAR,), ALL, (0, 1), q_all, g_all, kv, norm, None, dq_t, terms, scratch[4:])
     terms.write(0, dkv_out)
 
@@ -460,8 +462,8 @@
     labels = Labels(length_ref, caption_ref, place_ref)
     dq_t[:, :, VIDEO_ROWS:] = dq_in[:, :, VIDEO_ROWS:]
     terms = Terms(scratch[:4])
-    terms.clear()
-    own_terms.clear()
+    terms.clear_text()
+    own_terms.clear_text()
     key_grads(labels, (1, 3), ALL, (0, 1), q_all, g_all, kv, norm, dq_in, dq_t, terms, scratch[4:6])
     key_grads(labels, (0,), (FAR,), (1,), q_all, g_all, own, norm, dq_t, dq_t, own_terms, scratch[6:])
     for n in range(2):
@@ -475,9 +477,10 @@
     labels = Labels(length_ref, caption_ref, place_ref)
     dq_t[:, :, VIDEO_ROWS:] = dq_in[:, :, VIDEO_ROWS:]
     terms = Terms(scratch[:4])
-    for ref, source in zip(scratch[:4], before):
-        ref[...] = source[...]
-    key_grads(labels, (0,), NEAR, (0,), q_all, g_all, kv, norm, dq_in, dq_t, terms, scratch[4:])
+    before = Terms(before)
+    terms.text_dk[...] = before.text_dk[...]
+    terms.text_dv[...] = before.text_dv[...]
+    key_grads(labels, (0,), NEAR, (0,), q_all, g_all, kv, norm, dq_in, dq_t, terms, scratch[4:], before)
     for n, j in enumerate(NEAR):
         write_queries(dq_t, j, dq_out[n])
     terms.write(0, dkv_out)

time: 117 us -> 117 us (level)
  blocking collectives: 19.9 us -> 22 us
  starting transfers between devices: 33.6 us -> 32.3 us
    all_to_all x1, blocking collectives: 19.9 us -> 22 us  [on_device(): lax.all_to_all(video, 'head', split_axis=0, concat_axis=0)]
    ppermute x21, starting transfers between devices: 27.8 us -> 26.5 us  [swap(): lax.ppermute(array, 'seq', [(i, i ^ shift) for i in range(SIDE * SIDE)])]
where the time goes in v10:
time: 117 us; the launch traced here: 118 us
  Pallas kernels  38 us (32%)
  starting transfers between devices  32.3 us (28%)
  waiting for transfers between devices  24.4 us (21%)
  blocking collectives  22 us (19%)
    ppermute x21, starting transfers between devices, swap(): lax.ppermute(array, 'seq', [(i, i ^ shift) for i in range(SIDE * SIDE)])  26.5 us
    ppermute x21, waiting for transfers between devices, swap(): lax.ppermute(array, 'seq', [(i, i ^ shift) for i in range(SIDE * SIDE)])  24.4 us
    all_to_all x1, blocking collectives, on_device(): lax.all_to_all(video, 'head', split_axis=0, concat_axis=0)  22 us
    pallas_call x1, Pallas kernels, grads_near_call(): pl.pallas_call(grads_near_kernel, in_specs=[SMEM_SPEC] * 3 + [VMEM_SPEC]...  9.66 us
    pallas_call x1, Pallas kernels, stats_first_call(): pl.pallas_call(stats_first_kernel, in_specs=[SMEM_SPEC] * 3 + [VMEM_SPEC]...  6.78 us
    pallas_call x1, Pallas kernels, stats_last_call(): pl.pallas_call(stats_last_kernel, in_specs=[SMEM_SPEC] * 3 + [VMEM_SPEC]...  6.04 us
    all_to_all x1, starting transfers between devices, on_device(): arrived = lax.all_to_all(packed, 'head', split_axis=0, concat_axis=0)  5.8 us
    pallas_call x1, Pallas kernels, grads_own_call(): pl.pallas_call(grads_own_kernel, in_specs=[SMEM_SPEC] * 3 + [VMEM_SPEC] *...  5.7 us
  transfers between devices with their start and end apart: 22, of which 13 were waited for; matrix products, arithmetic and copies ran while one was open for 0% of the time, Pallas kernels for 19%

profile of v10, /device:TPU:1, one launch (start us, length us, event | category | flops | bytes accessed | tf_op | source)
XLA Modules:
  0.0 117.5 jit_solution(773035199600186653)
XLA Ops:
  0.6 2.3 %pack_inputs.1 = (bf16[8,4,32,384]{3,2,1,0:T(8,128)(2,1)}, bf16[2,128,384]{2,1,0:T(8,128)(2,1)S(1)}, bf16[2,128,384]{2,1,0:T(8,128)(2,1)S(1)}) custom-call(bf16[32,3072]{1,0:T(8,128)(2,1)} %q_ref.1, bf16[32,3072]{1,0:T(8,128)(2,1)} %k_ref.1, bf16[32,3072]{1,0:T(8,128)(2,1)} %v_ref.1, bf16[32,3072]{1,0:T(8,128)(2,1)} %g_ref.1, bf16[128,384]{1,0:T(8,128)(2,1)} %tq_ref.1, ...), custom_call_target="tpu_custom_call" | custom-call | tf_op jit(solution)/shard_map/pack_inputs/pallas_call | solution.py:55
  3.0 5.8 %all-to-all-start = ((bf16[8,4,32,384]{3,2,1,0:T(8,128)(2,1)}), bf16[8,4,32,384]{3,2,1,0:T(8,128)(2,1)S(1)}, u32[]{:S(2)}, u32[]{:S(2)}) async-start(bf16[8,4,32,384]{3,2,1,0:T(8,128)(2,1)} %get-tuple-element.54), calls=%async_computation | async-start | bytes 1572864 | tf_op jit(solution)/shard_map/all_to_all | solution.py:645
  8.8 2.7 %collective-permute-start.1 = (bf16[2,128,384]{2,1,0:T(8,128)(2,1)S(1)}, bf16[2,128,384]{2,1,0:T(8,128)(2,1)S(1)}, u32[]{:S(2)}, u32[]{:S(2)}) collective-permute-start(bf16[2,128,384]{2,1,0:T(8,128)(2,1)S(1)} %get-tuple-element.67.refs_9_), channel_id=1, source_target_pairs={{0,24},{8,16},{16,8},{24,0},{32,56},{40,48},{48,40},{56,32},{64,88... | collective-permute-start | bytes 589832 | tf_op jit(solution)/shard_map/ppermute | solution.py:619
  11.5 0.0 collective-permute-start
  11.5 3.8 %collective-permute-start.3 = (bf16[2,128,384]{2,1,0:T(8,128)(2,1)S(1)}, bf16[2,128,384]{2,1,0:T(8,128)(2,1)S(1)}, u32[]{:S(2)}, u32[]{:S(2)}) collective-permute-start(bf16[2,128,384]{2,1,0:T(8,128)(2,1)S(1)} %get-tuple-element.59.refs_3_.refs_9_.refs_5_), channel_id=1, source_target_pairs={{0,96},{8,104},{16,112},{24,120},{32,64},{40,72},{48,80},{56,88},{... | collective-permute-start | bytes 589832 | tf_op jit(solution)/shard_map/ppermute | solution.py:619
  15.3 0.0 collective-permute-start.2
  15.3 1.4 %collective-permute-done.1.refs_5_.refs_13_ = bf16[2,128,384]{2,1,0:T(8,128)(2,1)S(1)} collective-permute-done((bf16[2,128,384]{2,1,0:T(8,128)(2,1)S(1)}, bf16[2,128,384]{2,1,0:T(8,128)(2,1)S(1)}, u32[]{:S(2)}, u32[]{:S(2)}) %collective-permute-start.1) | collective-permute-done | bytes 196640 | tf_op jit(solution)/shard_map/ppermute | solution.py:619
  16.6 1.1 collective-permute-done.refs_4_.refs_10_
  17.7 2.5 %collective-permute-done.3.refs_7_.refs_5_ = bf16[2,128,384]{2,1,0:T(8,128)(2,1)S(1)} collective-permute-done((bf16[2,128,384]{2,1,0:T(8,128)(2,1)S(1)}, bf16[2,128,384]{2,1,0:T(8,128)(2,1)S(1)}, u32[]{:S(2)}, u32[]{:S(2)}) %collective-permute-start.3) | collective-permute-done | bytes 196640 | tf_op jit(solution)/shard_map/ppermute | solution.py:619
  20.2 0.8 collective-permute-done.2.refs_6_.refs_4_
  21.0 0.0 copy-done.6
  21.0 0.0 copy-done.10
  21.0 0.0 all-to-all-done.in_ref
  21.1 0.1 assemble_blocks.1
  21.1 0.0 copy-done
  21.1 0.0 copy-start.5
  21.1 2.8 %collective-permute-start.7 = (bf16[2,256,384]{2,1,0:T(8,128)(2,1)S(1)}, bf16[2,256,384]{2,1,0:T(8,128)(2,1)S(1)}, u32[]{:S(2)}, u32[]{:S(2)}) collective-permute-start(bf16[2,256,384]{2,1,0:T(8,128)(2,1)S(1)} %get-tuple-element.62.refs_6_), channel_id=1, source_target_pairs={{0,24},{8,16},{16,8},{24,0},{32,56},{40,48},{48,40},{56,32},{64,88... | collective-permute-start | bytes 1179656 | tf_op jit(solution)/shard_map/ppermute | solution.py:619
  24.0 0.0 collective-permute-start.6
  24.0 3.8 %collective-permute-start.5 = (bf16[2,256,384]{2,1,0:T(8,128)(2,1)S(1)}, bf16[2,256,384]{2,1,0:T(8,128)(2,1)S(1)}, u32[]{:S(2)}, u32[]{:S(2)}) collective-permute-start(bf16[2,256,384]{2,1,0:T(8,128)(2,1)S(1)} %get-tuple-element.58.refs_0_.refs_8_.refs_4_), channel_id=1, source_target_pairs={{0,96},{8,104},{16,112},{24,120},{32,64},{40,72},{48,80},{56,88},{... | collective-permute-start | bytes 1179656 | tf_op jit(solution)/shard_map/ppermute | solution.py:619
  27.7 0.0 collective-permute-start.4
  27.7 3.9 %collective-permute-done.7.refs_1_.refs_8_ = bf16[2,256,384]{2,1,0:T(8,128)(2,1)S(1)} collective-permute-done((bf16[2,256,384]{2,1,0:T(8,128)(2,1)S(1)}, bf16[2,256,384]{2,1,0:T(8,128)(2,1)S(1)}, u32[]{:S(2)}, u32[]{:S(2)}) %collective-permute-start.7) | collective-permute-done | bytes 393248 | tf_op jit(solution)/shard_map/ppermute | solution.py:619
  31.6 1.8 %collective-permute-done.6.refs_0_.refs_7_ = bf16[2,256,384]{2,1,0:T(8,128)(2,1)S(1)} collective-permute-done((bf16[2,256,384]{2,1,0:T(8,128)(2,1)S(1)}, bf16[2,256,384]{2,1,0:T(8,128)(2,1)S(1)}, u32[]{:S(2)}, u32[]{:S(2)}) %collective-permute-start.6) | collective-permute-done | bytes 393248 | tf_op jit(solution)/shard_map/ppermute | solution.py:619
  33.4 2.4 %collective-permute-done.5.refs_3_.refs_2_.refs_5_ = bf16[2,256,384]{2,1,0:T(8,128)(2,1)S(1)} collective-permute-done((bf16[2,256,384]{2,1,0:T(8,128)(2,1)S(1)}, bf16[2,256,384]{2,1,0:T(8,128)(2,1)S(1)}, u32[]{:S(2)}, u32[]{:S(2)}) %collective-permute-start.5) | collective-permute-done | bytes 393248 | tf_op jit(solution)/shard_map/ppermute | solution.py:619
  35.9 0.9 collective-permute-done.4.refs_2_.refs_1_.refs_4_
  36.8 0.0 copy-done.9
  36.8 0.0 copy-done.7
  36.8 0.0 copy-done.8
  36.8 2.1 %hand_on.1 = (bf16[384,384]{1,0:T(8,128)(2,1)S(1)}, bf16[384,384]{1,0:T(8,128)(2,1)S(1)}, bf16[384,384]{1,0:T(8,128)(2,1)}, bf16[384,384]{1,0:T(8,128)(2,1)}) custom-call(bf16[2,256,384]{2,1,0:T(8,128)(2,1)S(1)} %collective-permute-done.6.refs_0_.refs_7_, bf16[2,256,384]{2,1,0:T(8,128)(2,1)S(1)} %collective-permute-done.7.refs_1_.refs_8_, ...), custom_call_target="tpu_custom_call" | custom-call | tf_op jit(solution)/shard_map/hand_on/pallas_call | solution.py:81
  38.9 0.0 copy-done.5
  38.9 0.0 copy-done.1
  38.9 1.6 %collective-permute-start.8 = (bf16[384,384]{1,0:T(8,128)(2,1)}, bf16[384,384]{1,0:T(8,128)(2,1)S(1)}, u32[]{:S(2)}, u32[]{:S(2)}) collective-permute-start(bf16[384,384]{1,0:T(8,128)(2,1)} %get-tuple-element.65), channel_id=1, source_target_pairs={{0,96},{8,104},{16,112},{24,120},{32,64},{40,72},{48,80},{56,88},{... | collective-permute-start | bytes 884744 | tf_op jit(solution)/shard_map/ppermute | solution.py:619
  40.5 0.0 collective-permute-start.9
  40.5 0.7 collective-permute-start.10
  41.2 0.6 collective-permute-start.11
  41.8 6.8 %stats_first.1 = (f32[3,3,1536]{2,1,0:T(4,128)S(1)}, bf16[6,256,384]{2,1,0:T(8,128)(2,1)S(1)}, bf16[6,256,384]{2,1,0:T(8,128)(2,1)S(1)}) custom-call(s32[8]{0:T(128)S(1)} %copy-done.3, s32[8]{0:T(128)S(1)} %copy-done.4, s32[1]{0:T(128)} %bitcast.place_ref, bf16[2,256,384]{2,1,0:T(8,128)(2,1)S(1)} %get-tuple-element.58.refs_0_.refs_8_.refs_4_, ...), custom_call_target="tpu_custom_call" | custom-call | flops 1207959552 | bytes 8388608 | tf_op jit(solution)/shard_map/stats_first/pallas_call | solution.py:527
  48.6 0.0 collective-permute-done.8.refs_6_.refs_2_
  48.6 0.0 collective-permute-done.9.refs_7_.refs_3_
  48.6 0.0 collective-permute-done.10.refs_11_
  48.6 0.0 collective-permute-done.11.refs_12_
  48.6 6.0 %stats_last.1 = (f32[2,3,1536]{2,1,0:T(4,128)S(1)}, bf16[6,256,384]{2,1,0:T(8,128)(2,1)S(1)}, bf16[6,256,384]{2,1,0:T(8,128)(2,1)S(1)}) custom-call(s32[8]{0:T(128)S(1)} %copy-done.3, s32[8]{0:T(128)S(1)} %copy-done.4, s32[1]{0:T(128)} %bitcast.place_ref, bf16[2,256,384]{2,1,0:T(8,128)(2,1)S(1)} %get-tuple-element.58.refs_0_.refs_8_.refs_4_, ...), custom_call_target="tpu_custom_call" | custom-call | flops 805306368 | bytes 8388608 | tf_op jit(solution)/shard_map/stats_last/pallas_call | solution.py:543
  54.7 1.5 %collective-permute-start.14 = (f32[2,3,1536]{2,1,0:T(4,128)S(1)}, f32[2,3,1536]{2,1,0:T(4,128)S(1)}, u32[]{:S(2)}, u32[]{:S(2)}) collective-permute-start(f32[2,3,1536]{2,1,0:T(4,128)S(1)} %get-tuple-element.75.refs_4_), channel_id=1, source_target_pairs={{0,24},{8,16},{16,8},{24,0},{32,56},{40,48},{48,40},{56,32},{64,88... | collective-permute-start | bytes 110600 | tf_op jit(solution)/shard_map/ppermute | solution.py:619
  56.2 0.7 collective-permute-start.13
  56.9 1.1 collective-permute-start.12
  58.0 0.9 collective-permute-done.14.refs_7_
  58.9 1.7 %collective-permute-done.13.refs_6_ = f32[2,3,1536]{2,1,0:T(4,128)S(1)} collective-permute-done((f32[2,3,1536]{2,1,0:T(4,128)S(1)}, f32[2,3,1536]{2,1,0:T(4,128)S(1)}, u32[]{:S(2)}, u32[]{:S(2)}) %collective-permute-start.13) | collective-permute-done | bytes 36896 | tf_op jit(solution)/shard_map/ppermute | solution.py:619
  60.6 0.0 collective-permute-done.12.refs_5_
  60.6 3.2 %grads_far.1 = (bf16[2,384,384]{2,1,0:T(8,128)(2,1)S(1)}, f32[3,128,1536]{2,1,0:T(8,128)S(1)}, f32[2,3,1536]{2,1,0:T(4,128)S(1)}) custom-call(s32[8]{0:T(128)S(1)} %copy-done.3, s32[8]{0:T(128)S(1)} %copy-done.4, s32[1]{0:T(128)} %bitcast.place_ref, bf16[6,256,384]{2,1,0:T(8,128)(2,1)S(1)} %get-tuple-element.73.refs_0_, ...), custom_call_target="tpu_custom_call" | custom-call | flops 1006632960 | bytes 8388608 | tf_op jit(solution)/shard_map/grads_far/pallas_call | solution.py:565
  63.9 3.1 %collective-permute-start.15 = (bf16[2,384,384]{2,1,0:T(8,128)(2,1)S(1)}, bf16[2,384,384]{2,1,0:T(8,128)(2,1)S(1)}, u32[]{:S(2)}, u32[]{:S(2)}) collective-permute-start(bf16[2,384,384]{2,1,0:T(8,128)(2,1)S(1)} %get-tuple-element.86), channel_id=1, source_target_pairs={{0,64},{8,72},{16,80},{24,88},{32,96},{40,104},{48,112},{56,120},{... | collective-permute-start | bytes 1769480 | tf_op jit(solution)/shard_map/ppermute | solution.py:619
  67.0 9.7 %grads_near.1 = (bf16[2,384,384]{2,1,0:T(8,128)(2,1)S(1)}, bf16[2,384,384]{2,1,0:T(8,128)(2,1)S(1)}, bf16[3,128,384]{2,1,0:T(8,128)(2,1)S(1)}, f32[3,128,1536]{2...) custom-call(s32[8]{0:T(128)S(1)} %copy-done.3, ...), custom_call_target="tpu_custom_call" | custom-call | flops 2013265920 | bytes 8388608 | tf_op jit(solution)/shard_map/grads_near/pallas_call | solution.py:580
  76.6 0.9 collective-permute-start.16
  77.5 0.2 collective-permute-start.19
  77.7 0.7 collective-permute-start.20
  78.4 5.7 %grads_own.1 = (bf16[3,128,384]{2,1,0:T(8,128)(2,1)S(1)}, bf16[3,128,384]{2,1,0:T(8,128)(2,1)S(1)}, bf16[3,128,384]{2,1,0:T(8,128)(2,1)S(1)}, bf16[2,384,384]{2,1,0:T(8,128)(2,1)S(1)}) custom-call(s32[8]{0:T(128)S(1)} %copy-done.3, s32[8]{0:T(128)S(1)} %copy-done.4, s32[1]{0:T(128)} %bitcast.place_ref, bf16[6,256,384]{2,1,0:T(8,128)(2,1)S(1)} %get-tuple-element.73.refs_0_, ...), custom_call_target="tpu_custom_call" | custom-call | flops 1006632960 | bytes 8388608 | tf_op jit(solution)/shard_map/grads_own/pallas_call | solution.py:604
  84.1 0.0 collective-permute-done.16.refs_2_
  84.1 0.0 collective-permute-done.15.refs_6_
  84.1 0.8 collective-permute-start.17
  85.0 1.5 %collective-permute-start.18 = (bf16[3,128,384]{2,1,0:T(8,128)(2,1)S(1)}, bf16[3,128,384]{2,1,0:T(8,128)(2,1)S(1)}, u32[]{:S(2)}, u32[]{:S(2)}) collective-permute-start(bf16[3,128,384]{2,1,0:T(8,128)(2,1)S(1)} %get-tuple-element.90), channel_id=1, source_target_pairs={{0,24},{8,16},{16,8},{24,0},{32,56},{40,48},{48,40},{56,32},{64,88... | collective-permute-start | bytes 884744 | tf_op jit(solution)/shard_map/ppermute | solution.py:619
  86.4 2.2 %collective-permute-done.19.refs_5_ = bf16[2,384,384]{2,1,0:T(8,128)(2,1)S(1)} collective-permute-done((bf16[2,384,384]{2,1,0:T(8,128)(2,1)S(1)}, bf16[2,384,384]{2,1,0:T(8,128)(2,1)S(1)}, u32[]{:S(2)}, u32[]{:S(2)}) %collective-permute-start.19) | collective-permute-done | bytes 589856 | tf_op jit(solution)/shard_map/ppermute | solution.py:619
  88.6 0.0 collective-permute-done.20.refs_7_
  88.6 3.8 %collective-permute-done.17.refs_1_ = bf16[3,128,384]{2,1,0:T(8,128)(2,1)S(1)} collective-permute-done((bf16[3,128,384]{2,1,0:T(8,128)(2,1)S(1)}, bf16[3,128,384]{2,1,0:T(8,128)(2,1)S(1)}, u32[]{:S(2)}, u32[]{:S(2)}) %collective-permute-start.17) | collective-permute-done | bytes 294944 | tf_op jit(solution)/shard_map/ppermute | solution.py:619
  92.4 1.0 collective-permute-done.18.refs_3_
  93.4 1.2 %sum_terms.1 = (bf16[8,3,32,384]{3,2,1,0:T(8,128)(2,1)S(1)}, bf16[128,384]{1,0:T(8,128)(2,1)}, bf16[128,384]{1,0:T(8,128)(2,1)}, bf16[128,384]{1,0:T(8,128)(2,1)}) custom-call(bf16[3,128,384]{2,1,0:T(8,128)(2,1)S(1)} %get-tuple-element.83.refs_0_, bf16[3,128,384]{2,1,0:T(8,128)(2,1)S(1)} %collective-permute-done.17.refs_1_, ...), custom_call_target="tpu_custom_call" | custom-call | tf_op jit(solution)/shard_map/sum_terms/pallas_call | solution.py:120
  94.7 22.0 %all_to_all.10.in_ref = bf16[8,3,32,384]{3,2,1,0:T(8,128)(2,1)S(1)} all-to-all(bf16[8,3,32,384]{3,2,1,0:T(8,128)(2,1)S(1)} %get-tuple-element.95), channel_id=1, replica_groups=mesh['seq'=16,'head'=8] {'head'}, dimensions={0} | all-to-all | bytes 1179648 | tf_op jit(solution)/shard_map/all_to_all | solution.py:666
  116.7 0.9 unpack_video.1
  (13 shorter events, 0.0 us)
Async XLA Ops:
  3.0 18.0 %copy-start.6 = (bf16[2,128,384]{2,1,0:T(8,128)(2,1)}, bf16[2,128,384]{2,1,0:T(8,128)(2,1)S(1)}, u32[]{:S(2)}) copy-start(bf16[2,128,384]{2,1,0:T(8,128)(2,1)S(1)} %get-tuple-element.67.refs_9_) | copy-start | bytes 589828
  3.0 18.2 %copy-start = (bf16[2,128,384]{2,1,0:T(8,128)(2,1)}, bf16[2,128,384]{2,1,0:T(8,128)(2,1)S(1)}, u32[]{:S(2)}) copy-start(bf16[2,128,384]{2,1,0:T(8,128)(2,1)S(1)} %get-tuple-element.59.refs_3_.refs_9_.refs_5_) | copy-start | bytes 589828
  3.0 18.1 %all-to-all-start = ((bf16[8,4,32,384]{3,2,1,0:T(8,128)(2,1)}), bf16[8,4,32,384]{3,2,1,0:T(8,128)(2,1)S(1)}, u32[]{:S(2)}, u32[]{:S(2)}) async-start(bf16[8,4,32,384]{3,2,1,0:T(8,128)(2,1)} %get-tuple-element.54), calls=%async_computation | async-start | bytes 1572864 | tf_op jit(solution)/shard_map/all_to_all | solution.py:645
  8.8 7.9 %collective-permute-start.1 = (bf16[2,128,384]{2,1,0:T(8,128)(2,1)S(1)}, bf16[2,128,384]{2,1,0:T(8,128)(2,1)S(1)}, u32[]{:S(2)}, u32[]{:S(2)}) collective-permute-start(bf16[2,128,384]{2,1,0:T(8,128)(2,1)S(1)} %get-tuple-element.67.refs_9_), channel_id=1, source_target_pairs={{0,24},{8,16},{16,8},{24,0},{32,56},{40,48},{48,40},{56,32},{64,88... | collective-permute-start | bytes 589832 | tf_op jit(solution)/shard_map/ppermute | solution.py:619
  11.5 6.2 %collective-permute-start = (bf16[2,128,384]{2,1,0:T(8,128)(2,1)S(1)}, bf16[2,128,384]{2,1,0:T(8,128)(2,1)S(1)}, u32[]{:S(2)}, u32[]{:S(2)}) collective-permute-start(bf16[2,128,384]{2,1,0:T(8,128)(2,1)S(1)} %get-tuple-element.67.refs_9_), channel_id=1, source_target_pairs={{0,8},{8,0},{16,24},{24,16},{32,40},{40,32},{48,56},{56,48},{64,72... | collective-permute-start | bytes 589832 | tf_op jit(solution)/shard_map/ppermute | solution.py:619
  11.5 8.7 %collective-permute-start.3 = (bf16[2,128,384]{2,1,0:T(8,128)(2,1)S(1)}, bf16[2,128,384]{2,1,0:T(8,128)(2,1)S(1)}, u32[]{:S(2)}, u32[]{:S(2)}) collective-permute-start(bf16[2,128,384]{2,1,0:T(8,128)(2,1)S(1)} %get-tuple-element.59.refs_3_.refs_9_.refs_5_), channel_id=1, source_target_pairs={{0,96},{8,104},{16,112},{24,120},{32,64},{40,72},{48,80},{56,88},{... | collective-permute-start | bytes 589832 | tf_op jit(solution)/shard_map/ppermute | solution.py:619
  15.3 5.7 %collective-permute-start.2 = (bf16[2,128,384]{2,1,0:T(8,128)(2,1)S(1)}, bf16[2,128,384]{2,1,0:T(8,128)(2,1)S(1)}, u32[]{:S(2)}, u32[]{:S(2)}) collective-permute-start(bf16[2,128,384]{2,1,0:T(8,128)(2,1)S(1)} %get-tuple-element.59.refs_3_.refs_9_.refs_5_), channel_id=1, source_target_pairs={{0,32},{8,40},{16,48},{24,56},{32,0},{40,8},{48,16},{56,24},{64,96... | collective-permute-start | bytes 589832 | tf_op jit(solution)/shard_map/ppermute | solution.py:619
  16.6 20.1 %copy-start.9 = (bf16[2,128,384]{2,1,0:T(8,128)(2,1)}, bf16[2,128,384]{2,1,0:T(8,128)(2,1)S(1)}, u32[]{:S(2)}) copy-start(bf16[2,128,384]{2,1,0:T(8,128)(2,1)S(1)} %collective-permute-done.1.refs_5_.refs_13_) | copy-start | bytes 589828
  17.7 3.3 %copy-start.10 = (bf16[2,128,384]{2,1,0:T(8,128)(2,1)}, bf16[2,128,384]{2,1,0:T(8,128)(2,1)S(1)}, u32[]{:S(2)}) copy-start(bf16[2,128,384]{2,1,0:T(8,128)(2,1)S(1)} %collective-permute-done.refs_4_.refs_10_) | copy-start | bytes 589828
  20.2 16.6 %copy-start.7 = (bf16[2,128,384]{2,1,0:T(8,128)(2,1)}, bf16[2,128,384]{2,1,0:T(8,128)(2,1)S(1)}, u32[]{:S(2)}) copy-start(bf16[2,128,384]{2,1,0:T(8,128)(2,1)S(1)} %collective-permute-done.3.refs_7_.refs_5_) | copy-start | bytes 589828
  21.0 15.8 %copy-start.8 = (bf16[2,128,384]{2,1,0:T(8,128)(2,1)}, bf16[2,128,384]{2,1,0:T(8,128)(2,1)S(1)}, u32[]{:S(2)}) copy-start(bf16[2,128,384]{2,1,0:T(8,128)(2,1)S(1)} %collective-permute-done.2.refs_6_.refs_4_) | copy-start | bytes 589828
  21.1 17.7 %copy-start.5 = (bf16[2,256,384]{2,1,0:T(8,128)(2,1)}, bf16[2,256,384]{2,1,0:T(8,128)(2,1)S(1)}, u32[]{:S(2)}) copy-start(bf16[2,256,384]{2,1,0:T(8,128)(2,1)S(1)} %get-tuple-element.62.refs_6_) | copy-start | bytes 1179652
  21.1 10.5 %collective-permute-start.7 = (bf16[2,256,384]{2,1,0:T(8,128)(2,1)S(1)}, bf16[2,256,384]{2,1,0:T(8,128)(2,1)S(1)}, u32[]{:S(2)}, u32[]{:S(2)}) collective-permute-start(bf16[2,256,384]{2,1,0:T(8,128)(2,1)S(1)} %get-tuple-element.62.refs_6_), channel_id=1, source_target_pairs={{0,24},{8,16},{16,8},{24,0},{32,56},{40,48},{48,40},{56,32},{64,88... | collective-permute-start | bytes 1179656 | tf_op jit(solution)/shard_map/ppermute | solution.py:619
  24.0 9.5 %collective-permute-start.6 = (bf16[2,256,384]{2,1,0:T(8,128)(2,1)S(1)}, bf16[2,256,384]{2,1,0:T(8,128)(2,1)S(1)}, u32[]{:S(2)}, u32[]{:S(2)}) collective-permute-start(bf16[2,256,384]{2,1,0:T(8,128)(2,1)S(1)} %get-tuple-element.62.refs_6_), channel_id=1, source_target_pairs={{0,8},{8,0},{16,24},{24,16},{32,40},{40,32},{48,56},{56,48},{64,72... | collective-permute-start | bytes 1179656 | tf_op jit(solution)/shard_map/ppermute | solution.py:619
  24.0 17.8 %copy-start.3 = (s32[8]{0:T(128)S(1)}, s32[8]{0:T(128)}, u32[]{:S(2)}) copy-start(s32[8]{0:T(128)} %length_ref.9) | copy-start | bytes 100
  24.0 17.8 %copy-start.4 = (s32[8]{0:T(128)S(1)}, s32[8]{0:T(128)}, u32[]{:S(2)}) copy-start(s32[8]{0:T(128)} %caption_ref.9) | copy-start | bytes 100
  24.0 11.9 %collective-permute-start.5 = (bf16[2,256,384]{2,1,0:T(8,128)(2,1)S(1)}, bf16[2,256,384]{2,1,0:T(8,128)(2,1)S(1)}, u32[]{:S(2)}, u32[]{:S(2)}) collective-permute-start(bf16[2,256,384]{2,1,0:T(8,128)(2,1)S(1)} %get-tuple-element.58.refs_0_.refs_8_.refs_4_), channel_id=1, source_target_pairs={{0,96},{8,104},{16,112},{24,120},{32,64},{40,72},{48,80},{56,88},{... | collective-permute-start | bytes 1179656 | tf_op jit(solution)/shard_map/ppermute | solution.py:619
  27.7 9.0 %collective-permute-start.4 = (bf16[2,256,384]{2,1,0:T(8,128)(2,1)S(1)}, bf16[2,256,384]{2,1,0:T(8,128)(2,1)S(1)}, u32[]{:S(2)}, u32[]{:S(2)}) collective-permute-start(bf16[2,256,384]{2,1,0:T(8,128)(2,1)S(1)} %get-tuple-element.58.refs_0_.refs_8_.refs_4_), channel_id=1, source_target_pairs={{0,32},{8,40},{16,48},{24,56},{32,0},{40,8},{48,16},{56,24},{64,96... | collective-permute-start | bytes 1179656 | tf_op jit(solution)/shard_map/ppermute | solution.py:619
  31.6 7.2 %copy-start.1 = (bf16[2,256,384]{2,1,0:T(8,128)(2,1)}, bf16[2,256,384]{2,1,0:T(8,128)(2,1)S(1)}, u32[]{:S(2)}) copy-start(bf16[2,256,384]{2,1,0:T(8,128)(2,1)S(1)} %collective-permute-done.7.refs_1_.refs_8_) | copy-start | bytes 1179652
  33.4 5.5 %copy-start.2 = (bf16[2,256,384]{2,1,0:T(8,128)(2,1)}, bf16[2,256,384]{2,1,0:T(8,128)(2,1)S(1)}, u32[]{:S(2)}) copy-start(bf16[2,256,384]{2,1,0:T(8,128)(2,1)S(1)} %collective-permute-done.6.refs_0_.refs_7_) | copy-start | bytes 1179652
  38.9 9.7 %collective-permute-start.8 = (bf16[384,384]{1,0:T(8,128)(2,1)}, bf16[384,384]{1,0:T(8,128)(2,1)S(1)}, u32[]{:S(2)}, u32[]{:S(2)}) collective-permute-start(bf16[384,384]{1,0:T(8,128)(2,1)} %get-tuple-element.65), channel_id=1, source_target_pairs={{0,96},{8,104},{16,112},{24,120},{32,64},{40,72},{48,80},{56,88},{... | collective-permute-start | bytes 884744 | tf_op jit(solution)/shard_map/ppermute | solution.py:619
  40.5 8.1 %collective-permute-start.9 = (bf16[384,384]{1,0:T(8,128)(2,1)}, bf16[384,384]{1,0:T(8,128)(2,1)S(1)}, u32[]{:S(2)}, u32[]{:S(2)}) collective-permute-start(bf16[384,384]{1,0:T(8,128)(2,1)} %get-tuple-element.66), channel_id=1, source_target_pairs={{0,32},{8,40},{16,48},{24,56},{32,0},{40,8},{48,16},{56,24},{64,96... | collective-permute-start | bytes 884744 | tf_op jit(solution)/shard_map/ppermute | solution.py:619
  40.5 8.1 %collective-permute-start.10 = (bf16[384,384]{1,0:T(8,128)(2,1)S(1)}, bf16[384,384]{1,0:T(8,128)(2,1)S(1)}, u32[]{:S(2)}, u32[]{:S(2)}) collective-permute-start(bf16[384,384]{1,0:T(8,128)(2,1)S(1)} %get-tuple-element.71), channel_id=1, source_target_pairs={{0,24},{8,16},{16,8},{24,0},{32,56},{40,48},{48,40},{56,32},{64,88... | collective-permute-start | bytes 884744 | tf_op jit(solution)/shard_map/ppermute | solution.py:619
  41.2 7.5 %collective-permute-start.11 = (bf16[384,384]{1,0:T(8,128)(2,1)S(1)}, bf16[384,384]{1,0:T(8,128)(2,1)S(1)}, u32[]{:S(2)}, u32[]{:S(2)}) collective-permute-start(bf16[384,384]{1,0:T(8,128)(2,1)S(1)} %get-tuple-element.72), channel_id=1, source_target_pairs={{0,8},{8,0},{16,24},{24,16},{32,40},{40,32},{48,56},{56,48},{64,72... | collective-permute-start | bytes 884744 | tf_op jit(solution)/shard_map/ppermute | solution.py:619
  54.7 4.2 %collective-permute-start.14 = (f32[2,3,1536]{2,1,0:T(4,128)S(1)}, f32[2,3,1536]{2,1,0:T(4,128)S(1)}, u32[]{:S(2)}, u32[]{:S(2)}) collective-permute-start(f32[2,3,1536]{2,1,0:T(4,128)S(1)} %get-tuple-element.75.refs_4_), channel_id=1, source_target_pairs={{0,24},{8,16},{16,8},{24,0},{32,56},{40,48},{48,40},{56,32},{64,88... | collective-permute-start | bytes 110600 | tf_op jit(solution)/shard_map/ppermute | solution.py:619
  56.2 4.4 %collective-permute-start.13 = (f32[2,3,1536]{2,1,0:T(4,128)S(1)}, f32[2,3,1536]{2,1,0:T(4,128)S(1)}, u32[]{:S(2)}, u32[]{:S(2)}) collective-permute-start(f32[2,3,1536]{2,1,0:T(4,128)S(1)} %get-tuple-element.75.refs_4_), channel_id=1, source_target_pairs={{0,16},{8,24},{16,0},{24,8},{32,48},{40,56},{48,32},{56,40},{64,80... | collective-permute-start | bytes 110600 | tf_op jit(solution)/shard_map/ppermute | solution.py:619
  56.9 3.7 %collective-permute-start.12 = (f32[2,3,1536]{2,1,0:T(4,128)S(1)}, f32[2,3,1536]{2,1,0:T(4,128)S(1)}, u32[]{:S(2)}, u32[]{:S(2)}) collective-permute-start(f32[2,3,1536]{2,1,0:T(4,128)S(1)} %get-tuple-element.75.refs_4_), channel_id=1, source_target_pairs={{0,8},{8,0},{16,24},{24,16},{32,40},{40,32},{48,56},{56,48},{64,72... | collective-permute-start | bytes 110600 | tf_op jit(solution)/shard_map/ppermute | solution.py:619
  63.9 20.3 %collective-permute-start.15 = (bf16[2,384,384]{2,1,0:T(8,128)(2,1)S(1)}, bf16[2,384,384]{2,1,0:T(8,128)(2,1)S(1)}, u32[]{:S(2)}, u32[]{:S(2)}) collective-permute-start(bf16[2,384,384]{2,1,0:T(8,128)(2,1)S(1)} %get-tuple-element.86), channel_id=1, source_target_pairs={{0,64},{8,72},{16,80},{24,88},{32,96},{40,104},{48,112},{56,120},{... | collective-permute-start | bytes 1769480 | tf_op jit(solution)/shard_map/ppermute | solution.py:619
  76.6 7.5 %collective-permute-start.16 = (bf16[3,128,384]{2,1,0:T(8,128)(2,1)S(1)}, bf16[3,128,384]{2,1,0:T(8,128)(2,1)S(1)}, u32[]{:S(2)}, u32[]{:S(2)}) collective-permute-start(bf16[3,128,384]{2,1,0:T(8,128)(2,1)S(1)} %get-tuple-element.87), channel_id=1, source_target_pairs={{0,16},{8,24},{16,0},{24,8},{32,48},{40,56},{48,32},{56,40},{64,80... | collective-permute-start | bytes 884744 | tf_op jit(solution)/shard_map/ppermute | solution.py:619
  77.5 11.1 %collective-permute-start.19 = (bf16[2,384,384]{2,1,0:T(8,128)(2,1)S(1)}, bf16[2,384,384]{2,1,0:T(8,128)(2,1)S(1)}, u32[]{:S(2)}, u32[]{:S(2)}) collective-permute-start(bf16[2,384,384]{2,1,0:T(8,128)(2,1)S(1)} %get-tuple-element.92), channel_id=1, source_target_pairs={{0,32},{8,40},{16,48},{24,56},{32,0},{40,8},{48,16},{56,24},{64,96... | collective-permute-start | bytes 1769480 | tf_op jit(solution)/shard_map/ppermute | solution.py:619
  77.7 10.9 %collective-permute-start.20 = (bf16[2,384,384]{2,1,0:T(8,128)(2,1)S(1)}, bf16[2,384,384]{2,1,0:T(8,128)(2,1)S(1)}, u32[]{:S(2)}, u32[]{:S(2)}) collective-permute-start(bf16[2,384,384]{2,1,0:T(8,128)(2,1)S(1)} %get-tuple-element.94), channel_id=1, source_target_pairs={{0,96},{8,104},{16,112},{24,120},{32,64},{40,72},{48,80},{56,88},{... | collective-permute-start | bytes 1769480 | tf_op jit(solution)/shard_map/ppermute | solution.py:619
  84.1 8.3 %collective-permute-start.17 = (bf16[3,128,384]{2,1,0:T(8,128)(2,1)S(1)}, bf16[3,128,384]{2,1,0:T(8,128)(2,1)S(1)}, u32[]{:S(2)}, u32[]{:S(2)}) collective-permute-start(bf16[3,128,384]{2,1,0:T(8,128)(2,1)S(1)} %get-tuple-element.88), channel_id=1, source_target_pairs={{0,8},{8,0},{16,24},{24,16},{32,40},{40,32},{48,56},{56,48},{64,72... | collective-permute-start | bytes 884744 | tf_op jit(solution)/shard_map/ppermute | solution.py:619
  85.0 8.5 %collective-permute-start.18 = (bf16[3,128,384]{2,1,0:T(8,128)(2,1)S(1)}, bf16[3,128,384]{2,1,0:T(8,128)(2,1)S(1)}, u32[]{:S(2)}, u32[]{:S(2)}) collective-permute-start(bf16[3,128,384]{2,1,0:T(8,128)(2,1)S(1)} %get-tuple-element.90), channel_id=1, source_target_pairs={{0,24},{8,16},{16,8},{24,0},{32,56},{40,48},{48,40},{56,32},{64,88... | collective-permute-start | bytes 884744 | tf_op jit(solution)/shard_map/ppermute | solution.py:619
